TPU v7x, 32 devices: a whole 2x2x4 slice. The times are simulated.
32 devices in a mesh: ctx: 8 (over z, y), exp: 2 (over x), rep: 2 (over core).
Axes of the slice: x: 2, y: 2, z: 4, core: 2. Of those that a mesh axis runs over, the one named last changes fastest.
Arguments:
- queries: bfloat16 [1024, 4096], P(('rep', 'ctx'), 'exp'), parts along dimension 0, may hold values from -8 to 8
- key_rows: bfloat16 [1024, 256], P(('rep', 'ctx')), parts along dimension 0, may hold values from -8 to 8
- value_head_rows: bfloat16 [1024, 256], P(('rep', 'ctx')), parts along dimension 0, may hold values from -6 to 6
- block_order: int32 [16], P('rep'), parts along dimension 0, may hold values from 0 to 7, each once
- residual: bfloat16 [1024, 4096], P(('rep', 'ctx'), 'exp'), parts along dimension 0, may hold values from -8 to 8
- norm_gain: float32 [4096], P('exp'), may hold values from 0.25 to 1.75
- expert_ids: int32 [1024, 8], P(('rep', 'ctx')), parts along dimension 0, may hold values from 0 to 15, all different within a row; in each aligned block of 64 rows (0 to 63, 64 to 127, ...) at most 64 rows name the same one
- route_weight: float32 [1024, 8], P(('rep', 'ctx')), parts along dimension 0, may hold values from 0.02 to 0.5
- gate_weight: bfloat16 [16, 4096, 768], P('ctx', 'exp'), may hold values from -0.09375 to 0.09375
- up_weight: bfloat16 [16, 4096, 768], P('ctx', 'exp'), may hold values from -0.09375 to 0.09375
- down_weight: bfloat16 [16, 768, 4096], P('ctx', None, 'exp'), may hold values from -0.21875 to 0.21875
Outputs:
- layer_out: bfloat16 [1024, 4096], P(('rep', 'ctx'), 'exp'), parts along dimension 0
There are 2 independent parts, one for each index of `rep`. A program takes and returns all parts, laid end to end along the dimension named above; an argument that names none is the same for every part. Nothing has to cross between parts.
Inputs may be any that keep to these rules, and one draw needn't show every extreme that they name: `expert_ids`: each row names 8 different experts. In each aligned block of 64 rows no expert is named by more than 64 rows, a bound that some block reaches. `block_order`: each block index appears once.
All inputs are finite; a program needn't handle non-finite values.
Results may differ from a plain program's by a relative error of at most 0.011.
Values may be sent and summed in bfloat16 or wider, within the bound.
No kernel may reach another device: no remote copies, remote signals or barrier semaphores. Data moves between devices by JAX's collectives and lax.ppermute only.
A program may use at most 64 MiB of HBM per device.

v0:
```python
import math

import jax
import jax.numpy as jnp
from jax import lax
from jax.sharding import PartitionSpec as P

D = 4096
QUERY_HEADS = 32
KEY_VALUE_HEADS = 2
HEAD_SIZE = 128
TOPK = 8
EXP_ROW = 2


MASKED_SCORE = -1e30
NORM_EPS = 1e-06


def local(
    queries,
    key_rows,
    value_head_rows,
    block_order,
    residual,
    norm_gain,
    expert_ids,
    route_weight,
    gate_weight,
    up_weight,
    down_weight,
):
    shard_rows = queries.shape[0]
    ctx_count = lax.axis_size("ctx")
    local_head = queries.shape[1] // HEAD_SIZE
    expert_index = lax.axis_index("exp")
    ctx_index = lax.axis_index("ctx")
    key_value_head = expert_index * local_head // (QUERY_HEADS // KEY_VALUE_HEADS)
    my_keys = lax.dynamic_slice_in_dim(key_rows, key_value_head * HEAD_SIZE, HEAD_SIZE, 1)
    my_values = lax.dynamic_slice_in_dim(value_head_rows, key_value_head * HEAD_SIZE, HEAD_SIZE, 1)
    block_ids = jnp.arange(ctx_count, dtype=jnp.int32)
    own_block = jnp.sum(jnp.where(block_ids == ctx_index, block_order, 0))
    local_rows = jnp.arange(shard_rows, dtype=jnp.int32)
    query_pos = jnp.tile(own_block * shard_rows + local_rows, local_head)
    query_flat = (
        queries.reshape(shard_rows, local_head, HEAD_SIZE)
        .transpose(1, 0, 2)
        .reshape(local_head * shard_rows, HEAD_SIZE)
    )
    inv_scale = 1.0 / math.sqrt(HEAD_SIZE)
    query_count = local_head * shard_rows
    running_max = jnp.full((query_count,), MASKED_SCORE, jnp.float32)
    piece_keys = lax.all_gather(my_keys, "ctx", axis=0, tiled=True)
    piece_values = lax.all_gather(my_values, "ctx", axis=0, tiled=True)
    key_index = jnp.arange(piece_keys.shape[0], dtype=jnp.int32)
    owner_shard = key_index // shard_rows
    key_block = jnp.sum(
        jnp.where(owner_shard[:, None] == block_ids[None, :], block_order[None, :], 0), axis=1
    )
    key_pos = key_block * shard_rows + key_index % shard_rows
    visible = key_pos[None, :] <= query_pos[:, None]
    scores = (
        lax.dot_general(
            query_flat, piece_keys, (((1,), (1,)), ((), ())), preferred_element_type=jnp.float32
        )
        * inv_scale
    )
    scores = jnp.where(visible, scores, MASKED_SCORE)
    newest = jnp.maximum(running_max, jnp.max(scores, axis=1))
    weights = jnp.where(visible, jnp.exp(scores - newest[:, None]), 0.0)
    running_sum = jnp.sum(weights, axis=1)
    weighted = jnp.dot(
        weights.astype(jnp.bfloat16), piece_values, preferred_element_type=jnp.float32
    )
    running_max, running_sum, weighted = (newest, running_sum, weighted)
    attention = (
        (weighted / running_sum[:, None])
        .reshape(local_head, shard_rows, HEAD_SIZE)
        .transpose(1, 0, 2)
        .reshape(shard_rows, local_head * HEAD_SIZE)
        .astype(jnp.bfloat16)
    )
    mixed_rows = (residual.astype(jnp.float32) + attention.astype(jnp.float32)).astype(jnp.bfloat16)
    mixed_f = mixed_rows.astype(jnp.float32)
    square_sum = lax.psum(jnp.sum(mixed_f * mixed_f, axis=1), "exp")
    normed = (mixed_f * lax.rsqrt(square_sum[:, None] / D + NORM_EPS) * norm_gain[None, :]).astype(
        jnp.bfloat16
    )
    expert_count = ctx_count * EXP_ROW
    capacity = 2 * shard_rows * TOPK // expert_count
    flat_ids = expert_ids.reshape(-1)
    onehot = (flat_ids[:, None] == jnp.arange(expert_count, dtype=jnp.int32)[None, :]).astype(
        jnp.int32
    )
    slot_rank = jnp.sum((jnp.cumsum(onehot, axis=0) - onehot) * onehot, axis=1)
    slot_index = flat_ids * capacity + slot_rank
    source_rows = jnp.arange(shard_rows * TOPK, dtype=jnp.int32) // TOPK
    outgoing = (
        jnp.zeros((expert_count * capacity, normed.shape[1]), jnp.bfloat16)
        .at[slot_index]
        .set(normed[source_rows])
    )
    outgoing = outgoing.reshape(ctx_count, EXP_ROW, capacity, normed.shape[1])
    incoming = lax.all_to_all(outgoing, "ctx", split_axis=0, concat_axis=0, tiled=True)
    gate_part = jnp.einsum(
        "skcd,kdh->skch", incoming, gate_weight, preferred_element_type=jnp.float32
    ).astype(jnp.bfloat16)
    up_part = jnp.einsum(
        "skcd,kdh->skch", incoming, up_weight, preferred_element_type=jnp.float32
    ).astype(jnp.bfloat16)
    gate_full, up_full = (
        lax.psum(gate_part, "exp").astype(jnp.float32),
        lax.psum(up_part, "exp").astype(jnp.float32),
    )
    hidden = (jax.nn.silu(gate_full) * up_full).astype(jnp.bfloat16)
    expert_out = jnp.einsum(
        "skch,khd->skcd", hidden, down_weight, preferred_element_type=jnp.float32
    ).astype(jnp.bfloat16)
    returned = lax.all_to_all(expert_out, "ctx", split_axis=0, concat_axis=0, tiled=True)
    flat_back = returned.reshape(expert_count * capacity, normed.shape[1])
    picked = flat_back[slot_index].astype(jnp.float32).reshape(shard_rows, TOPK, normed.shape[1])
    routed_sum = jnp.sum(route_weight[:, :, None] * picked, axis=1)
    return (mixed_f + routed_sum).astype(jnp.bfloat16)


def solution(mesh):
    placed = (
        P(("rep", "ctx"), "exp"),
        P(("rep", "ctx"), None),
        P(("rep", "ctx"), None),
        P("rep"),
        P(("rep", "ctx"), "exp"),
        P("exp"),
        P(("rep", "ctx"), None),
        P(("rep", "ctx"), None),
        P("ctx", "exp", None),
        P("ctx", "exp", None),
        P("ctx", None, "exp"),
    )
    return jax.shard_map(
        local, mesh=mesh, in_specs=placed, out_specs=P(("rep", "ctx"), "exp"), check_vma=False
    )
```

profile of v0, /device:TPU:0, one launch (start us, length us, event | category | flops | bytes accessed | tf_op | source)
XLA Modules:
  0.0 404.9 jit_solution(4876694102088402417)
XLA Ops:
  6.5 0.0 copy-start
  6.5 0.0 copy-start.3
  6.5 0.0 all-reduce.3.cloned.1.call-start
  6.5 0.8 copy.45
  7.3 0.1 eq.55
  7.4 0.1 eq.51
  7.5 0.7 broadcast_multiply_fusion
  8.2 0.0 copy-done
  8.3 32.3 %all_gather.6 = bf16[512,128]{1,0:T(8,128)(2,1)S(1)} all-gather(bf16[64,128]{1,0:T(8,128)(2,1)S(1)} %constant_dynamic-slice_fusion.1), channel_id=1, replica_groups=mesh['ctx'=8,'exp'=2,'rep'=2] {'ctx'}, dimensions={0}, use_global_device_ids=true | all-gather | bytes 147456 | tf_op jit(solution)/shard_map/all_gather | solution.py:53
  40.6 1.3 fusion.64
  42.5 0.1 le.16
  42.6 0.7 select_reduce_fusion
  43.4 1.0 copy.56
  44.4 0.1 copy.41
  44.4 0.5 fusion.19
  44.9 0.0 copy-done.3
  44.9 30.5 %all_gather.7 = bf16[512,128]{1,0:T(8,128)(2,1)S(1)} all-gather(bf16[64,128]{1,0:T(8,128)(2,1)S(1)} %constant_dynamic-slice_fusion), channel_id=1, replica_groups=mesh['ctx'=8,'exp'=2,'rep'=2] {'ctx'}, dimensions={0}, use_global_device_ids=true | all-gather | bytes 147456 | tf_op jit(solution)/shard_map/all_gather | solution.py:54
  75.5 0.6 fusion.42
  76.1 0.0 copy-start.1
  76.1 0.0 copy-start.2
  76.1 0.8 fusion.44
  77.0 0.1 copy-done.1
  77.0 0.2 fusion.47
  77.2 5.1 %psum.21 = f32[64]{0:T(128)S(1)} all-reduce(f32[64]{0:T(128)S(1)} %get-tuple-element.7), channel_id=1, replica_groups=mesh['ctx'=8,'exp'=2,'rep'=2] {'exp'}, use_global_device_ids=true, to_apply=%region_8.9 | all-reduce | flops 64 | bytes 512 | tf_op jit(solution)/shard_map/psum | solution.py:85
  82.4 1.2 reduce-window.6
  83.5 0.2 slice_reduce_fusion
  83.8 0.1 copy.44
  83.9 0.1 mul.85
  84.0 0.1 fusion.54
  84.1 0.0 copy-done.2
  84.1 0.1 fusion.49
  84.2 12.8 %scatter_custom_fusion = bf16[1024,2048]{1,0:T(8,128)(2,1)} fusion(s32[512]{0:T(512)S(1)} %bitcast.93, bf16[64,2048]{1,0:T(8,128)(2,1)S(1)} %fusion.49, s32[1024]{0:T(1024)S(1)} %pad_clamp_fusion.1, bf16[]{:T(256)} %constant.93.clone.1), kind=kCustom, calls=%fused_computation.23 | custom fusion | bytes 4194306 | tf_op jit(solution)/shard_map/scatter | solution.py:101
  97.0 85.5 %all_to_all.10 = bf16[8,2,64,2048]{3,2,1,0:T(8,128)(2,1)S(1)} all-to-all(bf16[8,2,64,2048]{3,2,1,0:T(8,128)(2,1)} %bitcast.88), channel_id=1, replica_groups=mesh['ctx'=8,'exp'=2,'rep'=2] {'ctx'}, dimensions={0} | all-to-all | bytes 8388608 | tf_op jit(solution)/shard_map/all_to_all | solution.py:104
  182.6 7.5 %fusion.32 = bf16[8,2,64,768]{3,2,0,1:T(8,128)(2,1)} fusion(bf16[2,2048,768]{2,1,0:T(8,128)(2,1)} %param.20, bf16[8,2,64,2048]{3,2,1,0:T(8,128)(2,1)S(1)} %all_to_all.10), kind=kOutput, calls=%fused_computation.30 | convolution fusion | flops 3222011904 | bytes 12058624 | tf_op jit(solution)/shard_map/skcd,kdh->skch/dot_general | solution.py:108
  190.1 0.0 slice-done
  190.1 0.0 slice-done.1
  190.1 4.6 %fusion.37 = bf16[8,2,64,768]{3,2,0,1:T(8,128)(2,1)} fusion(bf16[2,2048,768]{2,1,0:T(8,128)(2,1)S(1)} %bitcast.98, bf16[8,2,64,2048]{3,2,1,0:T(8,128)(2,1)S(1)} %all_to_all.10), kind=kOutput, calls=%fused_computation.31 | convolution fusion | flops 3222011904 | bytes 12058624 | tf_op jit(solution)/shard_map/skcd,kdh->skch/dot_general | solution.py:105
  194.7 0.0 all-reduce.3.cloned.1.call-update
  194.7 85.0 %all-reduce.3.cloned.1.call-done = (bf16[8,2,64,768]{3,2,0,1:T(8,128)(2,1)}, bf16[8,2,64,768]{3,2,0,1:T(8,128)(2,1)}) async-done(((bf16[8,2,64,768]{3,2,0,1:T(8,128)(2,1)}, bf16[8,2,64,768]{3,2,0,1:T(8,128)(2,1)}), (bf16[8,2,64,768]{3,2,0,1:T(8,128)(2,1)}, bf16[8,2,64,768]{3,2,0,1:T(8,128)(2,1)})) %all-reduce.3.cloned.1.call-update) | async-done | bytes 3145744 | tf_op jit(solution)/shard_map/psum | solution.py:113
  279.7 7.4 %convert_bitcast_fusion = bf16[8,2,64,2048]{3,2,0,1:T(8,128)(2,1)S(1)} fusion(bf16[2,768,2048]{2,1,0:T(8,128)(2,1)} %param.21, bf16[8,2,64,768]{3,2,0,1:T(8,128)(2,1)} %get-tuple-element.5, bf16[8,2,64,768]{3,2,0,1:T(8,128)(2,1)} %get-tuple-element.6), kind=kOutput, calls=%fused_computation.11 | convolution fusion | flops 3229614080 | bytes 13631488 | tf_op jit(solution)/shard_map/skch,khd->skcd/dot_general | solution.py:116
  287.1 2.3 copy.50
  289.3 5.6 %all-to-all-start.1 = ((bf16[8,2,64,2048]{3,2,1,0:T(8,128)(2,1)}), bf16[8,2,64,2048]{3,2,1,0:T(8,128)(2,1)}, u32[]{:S(2)}, u32[]{:S(2)}) async-start(bf16[8,2,64,2048]{3,2,1,0:T(8,128)(2,1)} %copy.50), calls=%async_computation.1 | async-start | bytes 8388608 | tf_op jit(solution)/shard_map/all_to_all | solution.py:119
  295.0 0.0 copy-done.4
  295.0 0.1 copy.43
  295.1 93.2 %all-to-all-done.1 = bf16[8,2,64,2048]{3,2,1,0:T(8,128)(2,1)} async-done(((bf16[8,2,64,2048]{3,2,1,0:T(8,128)(2,1)}), bf16[8,2,64,2048]{3,2,1,0:T(8,128)(2,1)}, u32[]{:S(2)}, u32[]{:S(2)}) %all-to-all-start.1) | async-done | bytes 4194336 | tf_op jit(solution)/shard_map/all_to_all | solution.py:119
  388.3 7.1 %gather_fusion = bf16[512,2048]{1,0:T(8,128)(2,1)S(1)} fusion(bf16[1024,2048]{1,0:T(8,128)(2,1)} %bitcast.19, s32[1024]{0:T(1024)S(1)} %pad_clamp_fusion), kind=kCustom, calls=%fused_computation.1 | custom fusion | bytes 4196352 | tf_op jit(solution)/shard_map/gather | solution.py:121
  395.4 1.8 fusion.6
  397.3 0.8 fusion.50
  (19 shorter events, 0.1 us)
Async XLA Ops:
  6.5 1.7 copy-start
  6.5 38.4 %copy-start.3 = (bf16[64,256]{1,0:T(8,128)(2,1)S(1)}, bf16[64,256]{1,0:T(8,128)(2,1)}, u32[]{:S(2)}) copy-start(bf16[64,256]{1,0:T(8,128)(2,1)} %param.13) | copy-start | bytes 98308
  6.5 273.1 %all-reduce.3.cloned.1.call-start = ((), (), s32[]{:S(2)}) async-start(), calls=%async_computation.2 | async-start | bytes 6291456 | tf_op jit(solution)/shard_map/psum | solution.py:113
  76.1 1.0 copy-start.1
  76.1 8.0 %copy-start.2 = (f32[2048]{0:T(1024)S(1)}, f32[2048]{0:T(1024)}, u32[]{:S(2)}) copy-start(f32[2048]{0:T(1024)} %param.16) | copy-start | bytes 24580
  97.0 93.1 %slice-start = ((s8[6291456]{0:T(1024)(128)(4,1)}), s8[4194304]{0:T(1024)(128)(4,1)S(1)}, s32[]{:S(2)}) async-start(s8[6291456]{0:T(1024)(128)(4,1)} %bitcast.97), calls=%async_computation.3 | async-start | bytes 8388608
  182.6 7.5 %slice-start.1 = ((s8[6291456]{0:T(1024)(128)(4,1)}), s8[2097152]{0:T(1024)(128)(4,1)S(1)}, s32[]{:S(2)}) async-start(s8[6291456]{0:T(1024)(128)(4,1)} %bitcast.97), calls=%async_computation.4 | async-start | bytes 4194304
  289.3 5.7 %copy-start.4 = (f32[64,8]{0,1:T(8,128)S(1)}, f32[64,8]{0,1:T(8,128)}, u32[]{:S(2)}) copy-start(f32[64,8]{0,1:T(8,128)} %param.18) | copy-start | bytes 6148
  289.3 98.9 %all-to-all-start.1 = ((bf16[8,2,64,2048]{3,2,1,0:T(8,128)(2,1)}), bf16[8,2,64,2048]{3,2,1,0:T(8,128)(2,1)}, u32[]{:S(2)}, u32[]{:S(2)}) async-start(bf16[8,2,64,2048]{3,2,1,0:T(8,128)(2,1)} %copy.50), calls=%async_computation.1 | async-start | bytes 8388608 | tf_op jit(solution)/shard_map/all_to_all | solution.py:119
Sparse Core Ops, SparseCore 0:
  194.8 84.7 all-reduce.2
where the time goes:
time: 405 us
  waiting for transfers between devices  178 us (44%)
  blocking collectives  153 us (38%)
  local copies, waits for them, and re-layouts  24.9 us (6%)
  matrix products  20.8 us (5%)
  between operations  14.2 us (4%)
  other arithmetic  7.62 us (2%)
  starting transfers between devices  5.65 us (1%)
    all_to_all x1, waiting for transfers between devices, local(): lax.all_to_all(expert_out, 'ctx', split_axis=0, concat_axis=0, tiled=True)  93.2 us
    all_to_all x1, blocking collectives, local(): lax.all_to_all(outgoing, 'ctx', split_axis=0, concat_axis=0, tiled=True)  85.5 us
    psum x1, waiting for transfers between devices, local(): lax.psum(up_part, 'exp').astype(jnp.float32)  85 us
    all_gather x1, blocking collectives, local(): piece_keys = lax.all_gather(my_keys, 'ctx', axis=0, tiled=True)  32.3 us
    all_gather x1, blocking collectives, local(): piece_values = lax.all_gather(my_values, 'ctx', axis=0, tiled=True)  30.5 us
    scatter x1, local copies, waits for them, and re-layouts, local(): outgoing = jnp.zeros((expert_count * capacity, normed.shape[1]), jnp.bflo...  12.8 us
  transfers between devices with their start and end apart: 2, of which 2 were waited for; matrix products, arithmetic and copies ran while one was open for 0% of the time, Pallas kernels for 0%

commit v1 on v0

v1 whole, which is shorter than its diff:
```python
import math

import jax
import jax.numpy as jnp
from jax import lax
from jax.sharding import PartitionSpec as P

D = 4096
QUERY_HEADS = 32
KEY_VALUE_HEADS = 2
HEAD_SIZE = 128
TOPK = 8

MASKED_SCORE = -1e30
NORM_EPS = 1e-06


def xor_pairs(count, bit):
    return [(i, i ^ bit) for i in range(count)]


def bits_of(count):
    bits = []
    bit = count // 2
    while bit:
        bits.append(bit)
        bit //= 2
    return bits


def gather_rows(block, count):
    for bit in bits_of(count):
        block = jnp.concatenate([block, lax.ppermute(block, "ctx", xor_pairs(count, bit))], axis=0)
    return block


def offsets(count):
    found = [0]
    for bit in bits_of(count):
        found = found + [offset ^ bit for offset in found]
    return found


def scatter_sums(partial, count):
    for bit in reversed(bits_of(count)):
        half = partial.shape[0] // 2
        arrived = lax.ppermute(partial[half:].astype(jnp.bfloat16), "ctx", xor_pairs(count, bit))
        partial = partial[:half] + arrived.astype(jnp.float32)
    return partial


def local(
    queries,
    key_rows,
    value_head_rows,
    block_order,
    residual,
    norm_gain,
    expert_ids,
    route_weight,
    gate_weight,
    up_weight,
    down_weight,
):
    shard_rows = queries.shape[0]
    ctx_count = lax.axis_size("ctx")
    exp_count = lax.axis_size("exp")
    local_head = queries.shape[1] // HEAD_SIZE
    expert_index = lax.axis_index("exp")
    ctx_index = lax.axis_index("ctx")
    own_experts, _, hidden_size = gate_weight.shape
    expert_count = ctx_count * own_experts

    key_value_head = expert_index * local_head // (QUERY_HEADS // KEY_VALUE_HEADS)
    my_keys = lax.dynamic_slice_in_dim(key_rows, key_value_head * HEAD_SIZE, HEAD_SIZE, 1)
    my_values = lax.dynamic_slice_in_dim(value_head_rows, key_value_head * HEAD_SIZE, HEAD_SIZE, 1)
    experts = jnp.arange(expert_count, dtype=jnp.int32)
    route = jnp.sum(
        jnp.where(expert_ids[:, :, None] == experts[None, None, :], route_weight[:, :, None], 0.0),
        axis=1,
    )
    route_high = lax.reduce_precision(route, 8, 7)
    route_low = route - route_high
    packed = jnp.concatenate(
        [my_keys, my_values, route_high.astype(jnp.bfloat16), route_low.astype(jnp.bfloat16)], axis=1
    )
    gathered = gather_rows(packed, ctx_count)
    all_keys = gathered[:, :HEAD_SIZE]
    all_values = gathered[:, HEAD_SIZE : 2 * HEAD_SIZE]
    all_route = gathered[:, 2 * HEAD_SIZE :].astype(jnp.float32)
    all_route = all_route[:, :expert_count] + all_route[:, expert_count:]
    own_route = lax.dynamic_slice_in_dim(all_route, ctx_index * own_experts, own_experts, 1)

    owners = jnp.array(offsets(ctx_count), jnp.int32) ^ ctx_index
    block_ids = jnp.arange(ctx_count, dtype=jnp.int32)
    key_block = jnp.sum(
        jnp.where(owners[:, None] == block_ids[None, :], block_order[None, :], 0), axis=1
    )
    own_block = key_block[0]
    local_rows = jnp.arange(shard_rows, dtype=jnp.int32)
    query_pos = jnp.tile(own_block * shard_rows + local_rows, local_head)
    key_pos = (key_block[:, None] * shard_rows + local_rows[None, :]).reshape(-1)
    query_flat = (
        queries.reshape(shard_rows, local_head, HEAD_SIZE)
        .transpose(1, 0, 2)
        .reshape(local_head * shard_rows, HEAD_SIZE)
    )
    inv_scale = 1.0 / math.sqrt(HEAD_SIZE)
    visible = key_pos[None, :] <= query_pos[:, None]
    scores = (
        lax.dot_general(
            query_flat, all_keys, (((1,), (1,)), ((), ())), preferred_element_type=jnp.float32
        )
        * inv_scale
    )
    scores = jnp.where(visible, scores, MASKED_SCORE)
    newest = jnp.max(scores, axis=1)
    weights = jnp.where(visible, jnp.exp(scores - newest[:, None]), 0.0)
    weight_sum = jnp.sum(weights, axis=1)
    weighted = jnp.dot(weights.astype(jnp.bfloat16), all_values, preferred_element_type=jnp.float32)
    attention = (
        (weighted / weight_sum[:, None])
        .reshape(local_head, shard_rows, HEAD_SIZE)
        .transpose(1, 0, 2)
        .reshape(shard_rows, local_head * HEAD_SIZE)
        .astype(jnp.bfloat16)
    )
    mixed_rows = (residual.astype(jnp.float32) + attention.astype(jnp.float32)).astype(jnp.bfloat16)
    mixed_f = mixed_rows.astype(jnp.float32)
    square_sum = lax.psum(jnp.sum(mixed_f * mixed_f, axis=1), "exp")
    normed = (mixed_f * lax.rsqrt(square_sum[:, None] / D + NORM_EPS) * norm_gain[None, :]).astype(
        jnp.bfloat16
    )

    all_normed = gather_rows(normed, ctx_count)
    total = all_normed.shape[0]
    share = total // exp_count

    def partial_sums(rows):
        terms = []
        for k in range(own_experts):
            for weight in (gate_weight, up_weight):
                terms.append(jnp.dot(rows, weight[k], preferred_element_type=jnp.float32))
        return jnp.concatenate([term.astype(jnp.bfloat16) for term in terms], axis=1)

    if exp_count == 2:
        swap = [(0, 1), (1, 0)]
        others = lax.dynamic_slice_in_dim(all_normed, (1 - expert_index) * share, share, 0)
        mine = lax.dynamic_slice_in_dim(all_normed, expert_index * share, share, 0)
        arrived = lax.ppermute(partial_sums(others), "exp", swap)
        sums = partial_sums(mine).astype(jnp.float32) + arrived.astype(jnp.float32)
    else:
        sums = lax.psum_scatter(
            partial_sums(all_normed), "exp", scatter_dimension=0, tiled=True
        ).astype(jnp.float32)
    my_route = lax.dynamic_slice_in_dim(own_route, expert_index * share, share, 0)
    pieces = []
    for k in range(own_experts):
        gate_sum = sums[:, 2 * k * hidden_size : (2 * k + 1) * hidden_size]
        up_sum = sums[:, (2 * k + 1) * hidden_size : (2 * k + 2) * hidden_size]
        pieces.append((jax.nn.silu(gate_sum) * up_sum * my_route[:, k : k + 1]).astype(jnp.bfloat16))
    hidden = jnp.concatenate(pieces, axis=1)
    if exp_count == 2:
        other_hidden = lax.ppermute(hidden, "exp", swap)
        first = jnp.where(expert_index == 0, hidden, other_hidden)
        second = jnp.where(expert_index == 0, other_hidden, hidden)
        all_hidden = jnp.concatenate([first, second], axis=0)
    else:
        all_hidden = lax.all_gather(hidden, "exp", axis=0, tiled=True)
    down = down_weight.reshape(own_experts * hidden_size, down_weight.shape[2])
    partial = jnp.dot(all_hidden, down, preferred_element_type=jnp.float32)
    routed_sum = scatter_sums(partial, ctx_count)
    return (mixed_f + routed_sum).astype(jnp.bfloat16)


def solution(mesh):
    placed = (
        P(("rep", "ctx"), "exp"),
        P(("rep", "ctx"), None),
        P(("rep", "ctx"), None),
        P("rep"),
        P(("rep", "ctx"), "exp"),
        P("exp"),
        P(("rep", "ctx"), None),
        P(("rep", "ctx"), None),
        P("ctx", "exp", None),
        P("ctx", "exp", None),
        P("ctx", None, "exp"),
    )
    return jax.shard_map(
        local, mesh=mesh, in_specs=placed, out_specs=P(("rep", "ctx"), "exp"), check_vma=False
    )
```

time: 405 us -> 173 us (0.43)
  blocking collectives: 153 us -> 5.11 us
  waiting for transfers between devices: 178 us -> 115 us
  local copies, waits for them, and re-layouts: 24.9 us -> 2.81 us
  starting transfers between devices: 5.65 us -> 22.5 us
  between operations: 14.2 us -> 0.41 us
    ppermute x0 -> x11, waiting for transfers between devices: none -> 115 us  [the longest x6 41.9 us: gather_rows(): lax.ppermute(block, 'ctx', xor_pairs(count, bit))]
    all_to_all x1 -> x0, waiting for transfers between devices: 93.2 us -> none  [local(): lax.all_to_all(expert_out, 'ctx', split_axis=0, concat_axis=0, tiled=True)]
    all_to_all x1 -> x0, blocking collectives: 85.5 us -> none  [local(): lax.all_to_all(outgoing, 'ctx', split_axis=0, concat_axis=0, tiled=True)]
    psum x1 -> x0, waiting for transfers between devices: 85 us -> none  [local(): lax.psum(up_part, 'exp').astype(jnp.float32)]
    all_gather x2 -> x0, blocking collectives: 62.8 us -> none  [the longest x1 32.3 us: local(): piece_keys = lax.all_gather(my_keys, 'ctx', axis=0, tiled=True)]
    ppermute x0 -> x11, starting transfers between devices: none -> 22.5 us  [the longest x6 12.1 us: gather_rows(): lax.ppermute(block, 'ctx', xor_pairs(count, bit))]
    scatter x1 -> x0, local copies, waits for them, and re-layouts: 12.8 us -> none  [local(): outgoing = jnp.zeros((expert_count * capacity, normed.shape[1]), jnp.bflo...]
    gather x1 -> x0, local copies, waits for them, and re-layouts: 7.13 us -> none  [local(): flat_back[slot_index].astype(jnp.float32)]
  transfers between devices with their start and end apart: 2 -> 11, of which waited for: 2 -> 11; matrix products, arithmetic and copies ran while one was open for 0% -> 4% of each run, Pallas kernels for 0% -> 0%
where the time goes in v1:
time: 173 us; the launch traced here: 172 us
  waiting for transfers between devices  115 us (66%)
  starting transfers between devices  22.5 us (13%)
  matrix products  18.6 us (11%)
  other arithmetic  8.01 us (5%)
  blocking collectives  5.11 us (3%)
  local copies, waits for them, and re-layouts  2.81 us (2%)
    ppermute x6, waiting for transfers between devices, gather_rows(): lax.ppermute(block, 'ctx', xor_pairs(count, bit))  41.9 us
    ppermute x3, waiting for transfers between devices, scatter_sums(): lax.ppermute(partial[half:].astype(jnp.bfloat16), 'ctx', xor_pairs(count,...  34.7 us
    ppermute x1, waiting for transfers between devices, local(): arrived = lax.ppermute(partial_sums(others), 'exp', swap)  27.5 us
    ppermute x6, starting transfers between devices, gather_rows(): lax.ppermute(block, 'ctx', xor_pairs(count, bit))  12.1 us
    dot_general x8, matrix products, partial_sums(): terms.append(jnp.dot(rows, weight[k], preferred_element_type=jnp.float32))  11.8 us
    ppermute x1, waiting for transfers between devices, local(): other_hidden = lax.ppermute(hidden, 'exp', swap)  10.8 us
    ppermute x3, starting transfers between devices, scatter_sums(): lax.ppermute(partial[half:].astype(jnp.bfloat16), 'ctx', xor_pairs(count,...  6.85 us
    dot_general x1, matrix products, local(): partial = jnp.dot(all_hidden, down, preferred_element_type=jnp.float32)  5.51 us
  transfers between devices with their start and end apart: 11, of which 11 were waited for; matrix products, arithmetic and copies ran while one was open for 4% of the time, Pallas kernels for 0%

profile of v1, /device:TPU:0, one launch (start us, length us, event | category | flops | bytes accessed | tf_op | source)
XLA Modules:
  0.0 172.3 jit_solution(12822784603896607222)
XLA Ops:
  0.0 0.7 select_reduce_fusion
  0.9 0.7 constant_dynamic-slice_fusion
  1.8 4.0 %collective-permute-start = (bf16[64,288]{1,0:T(8,128)(2,1)S(1)}, bf16[64,288]{1,0:T(8,128)(2,1)S(1)}, u32[]{:S(2)}, u32[]{:S(2)}) collective-permute-start(bf16[64,288]{1,0:T(8,128)(2,1)S(1)} %pad_maximum_fusion.8), channel_id=1, source_target_pairs={{0,16},{4,20},{8,24},{12,28},{16,0},{20,4},{24,8},{28,12},{1,17},{... | collective-permute-start | bytes 110600 | tf_op jit(solution)/shard_map/ppermute | solution.py:33
  5.8 0.7 broadcast_xor_fusion
  6.5 0.8 select_reduce_fusion.1
  7.3 1.1 collective-permute-done
  8.5 1.4 collective-permute-start.1
  9.9 3.2 %collective-permute-done.1 = bf16[128,288]{1,0:T(8,128)(2,1)S(1)} collective-permute-done((bf16[128,288]{1,0:T(8,128)(2,1)S(1)}, bf16[128,288]{1,0:T(8,128)(2,1)S(1)}, u32[]{:S(2)}, u32[]{:S(2)}) %collective-permute-start.1) | collective-permute-done | bytes 73760 | tf_op jit(solution)/shard_map/ppermute | solution.py:33
  13.2 1.7 %collective-permute-start.2 = (bf16[256,288]{1,0:T(8,128)(2,1)S(1)}, bf16[256,288]{1,0:T(8,128)(2,1)S(1)}, u32[]{:S(2)}, u32[]{:S(2)}) collective-permute-start(bf16[256,288]{1,0:T(8,128)(2,1)S(1)} %pad_maximum_fusion.6), channel_id=1, source_target_pairs={{0,4},{4,0},{8,12},{12,8},{16,20},{20,16},{24,28},{28,24},{1,5},{5... | collective-permute-start | bytes 442376 | tf_op jit(solution)/shard_map/ppermute | solution.py:33
  15.2 1.0 copy.28
  16.3 2.6 %collective-permute-done.2 = bf16[256,288]{1,0:T(8,128)(2,1)S(1)} collective-permute-done((bf16[256,288]{1,0:T(8,128)(2,1)S(1)}, bf16[256,288]{1,0:T(8,128)(2,1)S(1)}, u32[]{:S(2)}, u32[]{:S(2)}) %collective-permute-start.2) | collective-permute-done | bytes 147488 | tf_op jit(solution)/shard_map/ppermute | solution.py:33
  19.0 0.5 fusion.24
  19.4 0.6 fusion.53
  20.1 0.9 fusion.55
  21.0 0.2 fusion.70
  21.2 5.1 %psum.7 = f32[64]{0:T(128)S(1)} all-reduce(f32[64]{0:T(128)S(1)} %get-tuple-element.7), channel_id=1, replica_groups=mesh['ctx'=8,'exp'=2,'rep'=2] {'exp'}, use_global_device_ids=true, to_apply=%region_5.6 | all-reduce | flops 64 | bytes 512 | tf_op jit(solution)/shard_map/psum | solution.py:130
  26.5 2.5 %collective-permute-start.3 = (bf16[64,2048]{1,0:T(8,128)(2,1)S(1)}, bf16[64,2048]{1,0:T(8,128)(2,1)S(1)}, u32[]{:S(2)}, u32[]{:S(2)}) collective-permute-start(bf16[64,2048]{1,0:T(8,128)(2,1)S(1)} %fusion.72), channel_id=1, source_target_pairs={{0,16},{4,20},{8,24},{12,28},{16,0},{20,4},{24,8},{28,12},{1,17},{... | collective-permute-start | bytes 786440 | tf_op jit(solution)/shard_map/ppermute | solution.py:33
  29.0 7.7 %collective-permute-done.3 = bf16[64,2048]{1,0:T(8,128)(2,1)S(1)} collective-permute-done((bf16[64,2048]{1,0:T(8,128)(2,1)S(1)}, bf16[64,2048]{1,0:T(8,128)(2,1)S(1)}, u32[]{:S(2)}, u32[]{:S(2)}) %collective-permute-start.3) | collective-permute-done | bytes 262176 | tf_op jit(solution)/shard_map/ppermute | solution.py:33
  36.8 0.6 collective-permute-start.4
  37.4 9.1 %collective-permute-done.4 = bf16[128,2048]{1,0:T(8,128)(2,1)S(1)} collective-permute-done((bf16[128,2048]{1,0:T(8,128)(2,1)S(1)}, bf16[128,2048]{1,0:T(8,128)(2,1)S(1)}, u32[]{:S(2)}, u32[]{:S(2)}) %collective-permute-start.4) | collective-permute-done | bytes 524320 | tf_op jit(solution)/shard_map/ppermute | solution.py:33
  46.6 1.8 %collective-permute-start.5 = (bf16[256,2048]{1,0:T(8,128)(2,1)S(1)}, bf16[256,2048]{1,0:T(8,128)(2,1)}, u32[]{:S(2)}, u32[]{:S(2)}) collective-permute-start(bf16[256,2048]{1,0:T(8,128)(2,1)S(1)} %pad_maximum_fusion.2), channel_id=1, source_target_pairs={{0,4},{4,0},{8,12},{12,8},{16,20},{20,16},{24,28},{28,24},{1,5},{5... | collective-permute-start | bytes 3145736 | tf_op jit(solution)/shard_map/ppermute | solution.py:33
  48.5 18.2 %collective-permute-done.5 = bf16[256,2048]{1,0:T(8,128)(2,1)} collective-permute-done((bf16[256,2048]{1,0:T(8,128)(2,1)S(1)}, bf16[256,2048]{1,0:T(8,128)(2,1)}, u32[]{:S(2)}, u32[]{:S(2)}) %collective-permute-start.5) | collective-permute-done | bytes 1048608 | tf_op jit(solution)/shard_map/ppermute | solution.py:33
  66.7 1.5 pad_maximum_fusion
  68.2 3.0 %fusion.38 = bf16[256,768]{1,0:T(8,128)(2,1)S(1)} fusion(bf16[2,2048,768]{2,1,0:T(8,128)(2,1)} %param.21, bf16[512,2048]{1,0:T(8,128)(2,1)S(1)} %pad_maximum_fusion, s32[]{:T(128)S(6)} %select_n.58), kind=kOutput, calls=%fused_computation.39 | convolution fusion | flops 805502976 | bytes 4587524 | tf_op jit(solution)/shard_map/dot_general | solution.py:143
  71.3 2.9 %fusion.50 = bf16[256,768]{1,0:T(8,128)(2,1)S(1)} fusion(bf16[2,2048,768]{2,1,0:T(8,128)(2,1)} %param.21, bf16[512,2048]{1,0:T(8,128)(2,1)S(1)} %pad_maximum_fusion, s32[]{:T(128)S(6)} %select_n.58), kind=kOutput, calls=%fused_computation.43 | convolution fusion | flops 805502976 | bytes 4587524 | tf_op jit(solution)/shard_map/dot_general | solution.py:143
  74.2 1.0 fusion.44
  75.2 1.0 fusion.32
  76.2 0.2 pad_maximum_fusion.1
  76.4 1.8 %collective-permute-start.6 = (bf16[256,3072]{1,0:T(8,128)(2,1)S(1)}, bf16[256,3072]{1,0:T(8,128)(2,1)S(1)}, u32[]{:S(2)}, u32[]{:S(2)}) collective-permute-start(bf16[256,3072]{1,0:T(8,128)(2,1)S(1)} %pad_maximum_fusion.1), channel_id=1, source_target_pairs={{0,2},{2,0},{1,3},{3,1},{4,6},{6,4},{5,7},{7,5},{8,10},{10,8},{9,1... | collective-permute-start | bytes 4718600 | tf_op jit(solution)/shard_map/ppermute | solution.py:150
  78.3 0.2 slice_reduce_fusion.1
  78.5 1.0 fusion.35
  79.5 1.0 fusion.41
  80.5 1.0 fusion.47
  81.5 1.0 fusion.29
  82.5 27.5 %collective-permute-done.6 = bf16[256,3072]{1,0:T(8,128)(2,1)S(1)} collective-permute-done((bf16[256,3072]{1,0:T(8,128)(2,1)S(1)}, bf16[256,3072]{1,0:T(8,128)(2,1)S(1)}, u32[]{:S(2)}, u32[]{:S(2)}) %collective-permute-start.6) | collective-permute-done | bytes 1572896 | tf_op jit(solution)/shard_map/ppermute | solution.py:150
  110.0 0.4 convert_add_fusion
  110.4 0.4 fusion.61
  110.9 1.8 %collective-permute-start.7 = (bf16[256,1536]{1,0:T(8,128)(2,1)S(1)}, bf16[256,1536]{1,0:T(8,128)(2,1)S(1)}, u32[]{:S(2)}, u32[]{:S(2)}) collective-permute-start(bf16[256,1536]{1,0:T(8,128)(2,1)S(1)} %pad_maximum_fusion.3), channel_id=1, source_target_pairs={{0,2},{2,0},{1,3},{3,1},{4,6},{6,4},{5,7},{7,5},{8,10},{10,8},{9,1... | collective-permute-start | bytes 2359304 | tf_op jit(solution)/shard_map/ppermute | solution.py:164
  112.7 10.8 %collective-permute-done.7 = bf16[256,1536]{1,0:T(8,128)(2,1)S(1)} collective-permute-done((bf16[256,1536]{1,0:T(8,128)(2,1)S(1)}, bf16[256,1536]{1,0:T(8,128)(2,1)S(1)}, u32[]{:S(2)}, u32[]{:S(2)}) %collective-permute-start.7) | collective-permute-done | bytes 786464 | tf_op jit(solution)/shard_map/ppermute | solution.py:164
  123.5 0.3 broadcast_select_fusion.1
  123.8 5.5 %fusion.25 = f32[512,2048]{1,0:T(8,128)S(1)} fusion(bf16[1536,2048]{1,0:T(8,128)(2,1)} %bitcast.76, bf16[256,1536]{1,0:T(8,128)(2,1)S(1)} %get-tuple-element.12, bf16[256,1536]{1,0:T(8,128)(2,1)S(1)} %get-tuple-element.11), kind=kOutput, calls=%fused_computation.32 | convolution fusion | flops 3224371200 | bytes 12058624 | tf_op jit(solution)/shard_map/dot_general | solution.py:171
  129.5 1.8 %collective-permute-start.8 = (bf16[256,2048]{1,0:T(8,128)(2,1)S(1)}, bf16[256,2048]{1,0:T(8,128)(2,1)S(1)}, u32[]{:S(2)}, u32[]{:S(2)}) collective-permute-start(bf16[256,2048]{1,0:T(8,128)(2,1)S(1)} %slice.187), channel_id=1, source_target_pairs={{0,4},{4,0},{8,12},{12,8},{16,20},{20,16},{24,28},{28,24},{1,5},{5... | collective-permute-start | bytes 3145736 | tf_op jit(solution)/shard_map/ppermute | solution.py:47
  131.3 15.5 %collective-permute-done.8 = bf16[256,2048]{1,0:T(8,128)(2,1)S(1)} collective-permute-done((bf16[256,2048]{1,0:T(8,128)(2,1)S(1)}, bf16[256,2048]{1,0:T(8,128)(2,1)S(1)}, u32[]{:S(2)}, u32[]{:S(2)}) %collective-permute-start.8) | collective-permute-done | bytes 1048608 | tf_op jit(solution)/shard_map/ppermute | solution.py:47
  146.8 0.3 slice_add_fusion
  147.2 12.0 %collective-permute-done.9 = bf16[128,2048]{1,0:T(8,128)(2,1)S(1)} collective-permute-done((bf16[128,2048]{1,0:T(8,128)(2,1)S(1)}, bf16[128,2048]{1,0:T(8,128)(2,1)S(1)}, u32[]{:S(2)}, u32[]{:S(2)}) %collective-permute-start.9) | collective-permute-done | bytes 524320 | tf_op jit(solution)/shard_map/ppermute | solution.py:47
  159.4 5.0 %collective-permute-start.10 = (bf16[64,2048]{1,0:T(8,128)(2,1)S(1)}, bf16[64,2048]{1,0:T(8,128)(2,1)S(1)}, u32[]{:S(2)}, u32[]{:S(2)}) collective-permute-start(bf16[64,2048]{1,0:T(8,128)(2,1)S(1)} %slice.189), channel_id=1, source_target_pairs={{0,16},{4,20},{8,24},{12,28},{16,0},{20,4},{24,8},{28,12},{1,17},{... | collective-permute-start | bytes 786440 | tf_op jit(solution)/shard_map/ppermute | solution.py:47
  164.4 7.2 %collective-permute-done.10 = bf16[64,2048]{1,0:T(8,128)(2,1)S(1)} collective-permute-done((bf16[64,2048]{1,0:T(8,128)(2,1)S(1)}, bf16[64,2048]{1,0:T(8,128)(2,1)S(1)}, u32[]{:S(2)}, u32[]{:S(2)}) %collective-permute-start.10) | collective-permute-done | bytes 262176 | tf_op jit(solution)/shard_map/ppermute | solution.py:47
  171.5 0.8 fusion.73
  (41 shorter events, 2.0 us)
Async XLA Ops:
  1.8 6.6 %collective-permute-start = (bf16[64,288]{1,0:T(8,128)(2,1)S(1)}, bf16[64,288]{1,0:T(8,128)(2,1)S(1)}, u32[]{:S(2)}, u32[]{:S(2)}) collective-permute-start(bf16[64,288]{1,0:T(8,128)(2,1)S(1)} %pad_maximum_fusion.8), channel_id=1, source_target_pairs={{0,16},{4,20},{8,24},{12,28},{16,0},{20,4},{24,8},{28,12},{1,17},{... | collective-permute-start | bytes 110600 | tf_op jit(solution)/shard_map/ppermute | solution.py:33
  8.5 4.6 %collective-permute-start.1 = (bf16[128,288]{1,0:T(8,128)(2,1)S(1)}, bf16[128,288]{1,0:T(8,128)(2,1)S(1)}, u32[]{:S(2)}, u32[]{:S(2)}) collective-permute-start(bf16[128,288]{1,0:T(8,128)(2,1)S(1)} %pad_maximum_fusion.7), channel_id=1, source_target_pairs={{0,8},{4,12},{8,0},{12,4},{16,24},{20,28},{24,16},{28,20},{1,9},{5... | collective-permute-start | bytes 221192 | tf_op jit(solution)/shard_map/ppermute | solution.py:33
  13.2 5.7 %collective-permute-start.2 = (bf16[256,288]{1,0:T(8,128)(2,1)S(1)}, bf16[256,288]{1,0:T(8,128)(2,1)S(1)}, u32[]{:S(2)}, u32[]{:S(2)}) collective-permute-start(bf16[256,288]{1,0:T(8,128)(2,1)S(1)} %pad_maximum_fusion.6), channel_id=1, source_target_pairs={{0,4},{4,0},{8,12},{12,8},{16,20},{20,16},{24,28},{28,24},{1,5},{5... | collective-permute-start | bytes 442376 | tf_op jit(solution)/shard_map/ppermute | solution.py:33
  20.1 1.0 copy-start
  20.1 6.3 %copy-start.1 = (f32[2048]{0:T(1024)S(1)}, f32[2048]{0:T(1024)}, u32[]{:S(2)}) copy-start(f32[2048]{0:T(1024)} %param.17) | copy-start | bytes 24580
  26.5 10.2 %collective-permute-start.3 = (bf16[64,2048]{1,0:T(8,128)(2,1)S(1)}, bf16[64,2048]{1,0:T(8,128)(2,1)S(1)}, u32[]{:S(2)}, u32[]{:S(2)}) collective-permute-start(bf16[64,2048]{1,0:T(8,128)(2,1)S(1)} %fusion.72), channel_id=1, source_target_pairs={{0,16},{4,20},{8,24},{12,28},{16,0},{20,4},{24,8},{28,12},{1,17},{... | collective-permute-start | bytes 786440 | tf_op jit(solution)/shard_map/ppermute | solution.py:33
  36.8 9.7 %collective-permute-start.4 = (bf16[128,2048]{1,0:T(8,128)(2,1)S(1)}, bf16[128,2048]{1,0:T(8,128)(2,1)S(1)}, u32[]{:S(2)}, u32[]{:S(2)}) collective-permute-start(bf16[128,2048]{1,0:T(8,128)(2,1)S(1)} %pad_maximum_fusion.4), channel_id=1, source_target_pairs={{0,8},{4,12},{8,0},{12,4},{16,24},{20,28},{24,16},{28,20},{1,9},{5... | collective-permute-start | bytes 1572872 | tf_op jit(solution)/shard_map/ppermute | solution.py:33
  46.6 20.1 %collective-permute-start.5 = (bf16[256,2048]{1,0:T(8,128)(2,1)S(1)}, bf16[256,2048]{1,0:T(8,128)(2,1)}, u32[]{:S(2)}, u32[]{:S(2)}) collective-permute-start(bf16[256,2048]{1,0:T(8,128)(2,1)S(1)} %pad_maximum_fusion.2), channel_id=1, source_target_pairs={{0,4},{4,0},{8,12},{12,8},{16,20},{20,16},{24,28},{28,24},{1,5},{5... | collective-permute-start | bytes 3145736 | tf_op jit(solution)/shard_map/ppermute | solution.py:33
  66.7 7.5 %slice-start.2 = ((s8[6291456]{0:T(1024)(128)(4,1)}), s8[4194304]{0:T(1024)(128)(4,1)S(1)}, s32[]{:S(2)}) async-start(s8[6291456]{0:T(1024)(128)(4,1)} %bitcast.74), calls=%async_computation.2 | async-start | bytes 8388608
  68.2 5.9 %slice-start.3 = ((s8[6291456]{0:T(1024)(128)(4,1)}), s8[2097152]{0:T(1024)(128)(4,1)S(1)}, s32[]{:S(2)}) async-start(s8[6291456]{0:T(1024)(128)(4,1)} %bitcast.74), calls=%async_computation.3 | async-start | bytes 4194304
  74.2 4.3 %slice-start = ((s8[6291456]{0:T(1024)(128)(4,1)}), s8[4194304]{0:T(1024)(128)(4,1)S(1)}, s32[]{:S(2)}) async-start(s8[6291456]{0:T(1024)(128)(4,1)} %bitcast.72), calls=%async_computation | async-start | bytes 8388608
  75.2 3.3 %slice-start.1 = ((s8[6291456]{0:T(1024)(128)(4,1)}), s8[2097152]{0:T(1024)(128)(4,1)S(1)}, s32[]{:S(2)}) async-start(s8[6291456]{0:T(1024)(128)(4,1)} %bitcast.72), calls=%async_computation.1 | async-start | bytes 4194304
  76.4 33.6 %collective-permute-start.6 = (bf16[256,3072]{1,0:T(8,128)(2,1)S(1)}, bf16[256,3072]{1,0:T(8,128)(2,1)S(1)}, u32[]{:S(2)}, u32[]{:S(2)}) collective-permute-start(bf16[256,3072]{1,0:T(8,128)(2,1)S(1)} %pad_maximum_fusion.1), channel_id=1, source_target_pairs={{0,2},{2,0},{1,3},{3,1},{4,6},{6,4},{5,7},{7,5},{8,10},{10,8},{9,1... | collective-permute-start | bytes 4718600 | tf_op jit(solution)/shard_map/ppermute | solution.py:150
  110.9 12.6 %collective-permute-start.7 = (bf16[256,1536]{1,0:T(8,128)(2,1)S(1)}, bf16[256,1536]{1,0:T(8,128)(2,1)S(1)}, u32[]{:S(2)}, u32[]{:S(2)}) collective-permute-start(bf16[256,1536]{1,0:T(8,128)(2,1)S(1)} %pad_maximum_fusion.3), channel_id=1, source_target_pairs={{0,2},{2,0},{1,3},{3,1},{4,6},{6,4},{5,7},{7,5},{8,10},{10,8},{9,1... | collective-permute-start | bytes 2359304 | tf_op jit(solution)/shard_map/ppermute | solution.py:164
  129.5 17.3 %collective-permute-start.8 = (bf16[256,2048]{1,0:T(8,128)(2,1)S(1)}, bf16[256,2048]{1,0:T(8,128)(2,1)S(1)}, u32[]{:S(2)}, u32[]{:S(2)}) collective-permute-start(bf16[256,2048]{1,0:T(8,128)(2,1)S(1)} %slice.187), channel_id=1, source_target_pairs={{0,4},{4,0},{8,12},{12,8},{16,20},{20,16},{24,28},{28,24},{1,5},{5... | collective-permute-start | bytes 3145736 | tf_op jit(solution)/shard_map/ppermute | solution.py:47
  147.1 12.1 %collective-permute-start.9 = (bf16[128,2048]{1,0:T(8,128)(2,1)S(1)}, bf16[128,2048]{1,0:T(8,128)(2,1)S(1)}, u32[]{:S(2)}, u32[]{:S(2)}) collective-permute-start(bf16[128,2048]{1,0:T(8,128)(2,1)S(1)} %slice.188), channel_id=1, source_target_pairs={{0,8},{4,12},{8,0},{12,4},{16,24},{20,28},{24,16},{28,20},{1,9},{5... | collective-permute-start | bytes 1572872 | tf_op jit(solution)/shard_map/ppermute | solution.py:47
  159.4 12.2 %collective-permute-start.10 = (bf16[64,2048]{1,0:T(8,128)(2,1)S(1)}, bf16[64,2048]{1,0:T(8,128)(2,1)S(1)}, u32[]{:S(2)}, u32[]{:S(2)}) collective-permute-start(bf16[64,2048]{1,0:T(8,128)(2,1)S(1)} %slice.189), channel_id=1, source_target_pairs={{0,16},{4,20},{8,24},{12,28},{16,0},{20,4},{24,8},{28,12},{1,17},{... | collective-permute-start | bytes 786440 | tf_op jit(solution)/shard_map/ppermute | solution.py:47

commit v2 on v1

--- a/solution.py
+++ b/solution.py
@@ -1,8 +1,11 @@
+import functools
 import math
 
 import jax
 import jax.numpy as jnp
 from jax import lax
+from jax.experimental import pallas as pl
+from jax.experimental.pallas import tpu as pltpu
 from jax.sharding import PartitionSpec as P
 
 D = 4096
@@ -13,6 +16,9 @@
 
 MASKED_SCORE = -1e30
 NORM_EPS = 1e-06
+LANES = 128
+KERNEL_BYTES = 16 * 1024 * 1024
+CHUNKS = ((0, 4, 1), (2, 5, 6), (3, 7))
 
 
 def xor_pairs(count, bit):
@@ -47,6 +53,164 @@
         arrived = lax.ppermute(partial[half:].astype(jnp.bfloat16), "ctx", xor_pairs(count, bit))
         partial = partial[:half] + arrived.astype(jnp.float32)
     return partial
+
+
+def routed_at_once(mixed_rows, norm_gain, own_route, gate_weight, up_weight, down_weight):
+    ctx_count = lax.axis_size("ctx")
+    own_experts, _, hidden_size = gate_weight.shape
+    mixed_f = mixed_rows.astype(jnp.float32)
+    square_sum = lax.psum(jnp.sum(mixed_f * mixed_f, axis=1), "exp")
+    normed = (mixed_f * lax.rsqrt(square_sum[:, None] / D + NORM_EPS) * norm_gain[None, :]).astype(
+        jnp.bfloat16
+    )
+    all_normed = gather_rows(normed, ctx_count)
+    share = all_normed.shape[0] // lax.axis_size("exp")
+    terms = []
+    for k in range(own_experts):
+        for weight in (gate_weight, up_weight):
+            term = jnp.dot(all_normed, weight[k], preferred_element_type=jnp.float32)
+            terms.append(term.astype(jnp.bfloat16))
+    sums = lax.psum_scatter(
+        jnp.concatenate(terms, axis=1), "exp", scatter_dimension=0, tiled=True
+    ).astype(jnp.float32)
+    my_route = lax.dynamic_slice_in_dim(own_route, lax.axis_index("exp") * share, share, 0)
+    pieces = []
+    for k in range(own_experts):
+        gate_sum = sums[:, 2 * k * hidden_size : (2 * k + 1) * hidden_size]
+        up_sum = sums[:, (2 * k + 1) * hidden_size : (2 * k + 2) * hidden_size]
+        pieces.append((jax.nn.silu(gate_sum) * up_sum * my_route[:, k : k + 1]).astype(jnp.bfloat16))
+    hidden = lax.all_gather(jnp.concatenate(pieces, axis=1), "exp", axis=0, tiled=True)
+    down = down_weight.reshape(own_experts * hidden_size, down_weight.shape[2])
+    partial = jnp.dot(hidden, down, preferred_element_type=jnp.float32)
+    return scatter_sums(partial, ctx_count)
+
+
+def prepared(blocks, gain_ref):
+    rows = jnp.concatenate([block[...] for block in blocks], axis=0).astype(jnp.float32)
+    squares = jnp.sum(rows * rows, axis=1, keepdims=True)
+    return (rows * gain_ref[...]).astype(jnp.bfloat16), squares
+
+
+def first_kernel(blocks, index_ref, gain_ref, gate_ref, up_ref, *rest):
+    out_ref = rest[blocks]
+    k = index_ref[0]
+    size = gate_ref.shape[2]
+    rows, squares = prepared(rest[:blocks], gain_ref)
+    gate = jnp.dot(rows, gate_ref[k], preferred_element_type=jnp.float32)
+    out_ref[:, :size] = gate.astype(jnp.bfloat16)
+    up = jnp.dot(rows, up_ref[k], preferred_element_type=jnp.float32)
+    out_ref[:, size : 2 * size] = up.astype(jnp.bfloat16)
+    high = squares.astype(jnp.bfloat16)
+    low = (squares - high.astype(jnp.float32)).astype(jnp.bfloat16)
+    lane = lax.broadcasted_iota(jnp.int32, (rows.shape[0], LANES), 1)
+    out_ref[:, 2 * size :] = jnp.where(
+        lane == 0, high.astype(jnp.float32), low.astype(jnp.float32)
+    ).astype(jnp.bfloat16)
+
+
+def hidden_kernel(kept_ref, arrived_ref, route_ref, out_ref):
+    size = out_ref.shape[1]
+    tail = kept_ref[:, 2 * size :].astype(jnp.float32) + arrived_ref[:, 2 * size :].astype(
+        jnp.float32
+    )
+    scale = lax.rsqrt((tail[:, :1] + tail[:, 1:2]) / D + NORM_EPS)
+    gate = kept_ref[:, :size].astype(jnp.float32) + arrived_ref[:, :size].astype(jnp.float32)
+    up = kept_ref[:, size : 2 * size].astype(jnp.float32) + arrived_ref[
+        :, size : 2 * size
+    ].astype(jnp.float32)
+    gate = gate * scale
+    up = up * (scale * route_ref[...])
+    out_ref[...] = (gate / (1.0 + jnp.exp(-gate)) * up).astype(jnp.bfloat16)
+
+
+def down_kernel(index_ref, hidden_ref, down_ref, out_ref):
+    out_ref[...] = jnp.dot(
+        hidden_ref[...], down_ref[index_ref[0]], preferred_element_type=jnp.float32
+    )
+
+
+def last_kernel(index_ref, hidden_ref, down_ref, before_ref, *outs):
+    both = before_ref[...] + jnp.dot(
+        hidden_ref[...], down_ref[index_ref[0]], preferred_element_type=jnp.float32
+    )
+    rows = outs[0].shape[0]
+    for i, out_ref in enumerate(outs):
+        out_ref[...] = both[i * rows : (i + 1) * rows].astype(out_ref.dtype)
+
+
+def in_vmem(kernel, out_shape, *args, flops=0):
+    specs = [
+        pl.BlockSpec(memory_space=pltpu.SMEM if arg.dtype == jnp.int32 else pltpu.VMEM)
+        for arg in args
+    ]
+    many = isinstance(out_shape, (list, tuple))
+    out_spec = pl.BlockSpec(memory_space=pltpu.VMEM)
+    return pl.pallas_call(
+        kernel,
+        out_shape=out_shape,
+        in_specs=specs,
+        out_specs=[out_spec] * len(out_shape) if many else out_spec,
+        compiler_params=pltpu.CompilerParams(vmem_limit_bytes=KERNEL_BYTES),
+        cost_estimate=pl.CostEstimate(flops=flops, bytes_accessed=0, transcendentals=0),
+    )(*args)
+
+
+def routed_in_chunks(mixed_rows, norm_gain, own_route, gate_weight, up_weight, down_weight):
+    rows, features = mixed_rows.shape
+    ctx_count = lax.axis_size("ctx")
+    size = gate_weight.shape[2]
+    mine = lax.axis_index("exp").astype(jnp.int32).reshape(1)
+    other = 1 - mine
+    swap = [(0, 1), (1, 0)]
+    gain = norm_gain.reshape(1, features)
+    route_mine = lax.dynamic_index_in_dim(own_route, mine[0], 1, keepdims=True)
+    place = {offset: i for i, offset in enumerate(offsets(ctx_count))}
+
+    def hop(block, offset):
+        return lax.ppermute(block, "ctx", xor_pairs(ctx_count, offset))
+
+    block = {0: mixed_rows}
+    block[4], block[1], block[2] = hop(block[0], 4), hop(block[0], 1), hop(block[0], 2)
+    block[6], block[5] = hop(block[4], 2), hop(block[4], 1)
+    block[3] = hop(block[2], 1)
+    block[7] = hop(block[6], 1)
+
+    total = 0.0
+    for chunk in CHUNKS:
+        blocks = [block[offset] for offset in chunk]
+        count = len(chunk) * rows
+        first = functools.partial(first_kernel, len(chunk))
+        shape = jax.ShapeDtypeStruct((count, 2 * size + LANES), jnp.bfloat16)
+        cost = 4 * count * features * size
+        weights = (gain, gate_weight, up_weight)
+        sent = in_vmem(first, shape, other, *weights, *blocks, flops=cost)
+        arrived = lax.ppermute(sent, "exp", swap)
+        kept = in_vmem(first, shape, mine, *weights, *blocks, flops=cost)
+        route = jnp.concatenate(
+            [route_mine[place[o] * rows : (place[o] + 1) * rows] for o in chunk], axis=0
+        )
+        hidden = in_vmem(
+            hidden_kernel, jax.ShapeDtypeStruct((count, size), jnp.bfloat16), kept, arrived, route
+        )
+        other_hidden = lax.ppermute(hidden, "exp", swap)
+        before = in_vmem(
+            down_kernel,
+            jax.ShapeDtypeStruct((count, features), jnp.float32),
+            mine,
+            hidden,
+            down_weight,
+            flops=cost // 2,
+        )
+        shapes = [
+            jax.ShapeDtypeStruct((rows, features), jnp.bfloat16 if offset else jnp.float32)
+            for offset in chunk
+        ]
+        terms = in_vmem(
+            last_kernel, shapes, other, other_hidden, down_weight, before, flops=cost // 2
+        )
+        for offset, term in zip(chunk, terms):
+            total = total + (hop(term, offset).astype(jnp.float32) if offset else term)
+    return total
 
 
 def local(
@@ -127,49 +291,14 @@
     )
     mixed_rows = (residual.astype(jnp.float32) + attention.astype(jnp.float32)).astype(jnp.bfloat16)
     mixed_f = mixed_rows.astype(jnp.float32)
-    square_sum = lax.psum(jnp.sum(mixed_f * mixed_f, axis=1), "exp")
-    normed = (mixed_f * lax.rsqrt(square_sum[:, None] / D + NORM_EPS) * norm_gain[None, :]).astype(
-        jnp.bfloat16
-    )
-
-    all_normed = gather_rows(normed, ctx_count)
-    total = all_normed.shape[0]
-    share = total // exp_count
-
-    def partial_sums(rows):
-        terms = []
-        for k in range(own_experts):
-            for weight in (gate_weight, up_weight):
-                terms.append(jnp.dot(rows, weight[k], preferred_element_type=jnp.float32))
-        return jnp.concatenate([term.astype(jnp.bfloat16) for term in terms], axis=1)
-
-    if exp_count == 2:
-        swap = [(0, 1), (1, 0)]
-        others = lax.dynamic_slice_in_dim(all_normed, (1 - expert_index) * share, share, 0)
-        mine = lax.dynamic_slice_in_dim(all_normed, expert_index * share, share, 0)
-        arrived = lax.ppermute(partial_sums(others), "exp", swap)
-        sums = partial_sums(mine).astype(jnp.float32) + arrived.astype(jnp.float32)
+    if exp_count == 2 and own_experts == 2 and ctx_count == 8:
+        routed_sum = routed_in_chunks(
+            mixed_rows, norm_gain, own_route, gate_weight, up_weight, down_weight
+        )
     else:
-        sums = lax.psum_scatter(
-            partial_sums(all_normed), "exp", scatter_dimension=0, tiled=True
-        ).astype(jnp.float32)
-    my_route = lax.dynamic_slice_in_dim(own_route, expert_index * share, share, 0)
-    pieces = []
-    for k in range(own_experts):
-        gate_sum = sums[:, 2 * k * hidden_size : (2 * k + 1) * hidden_size]
-        up_sum = sums[:, (2 * k + 1) * hidden_size : (2 * k + 2) * hidden_size]
-        pieces.append((jax.nn.silu(gate_sum) * up_sum * my_route[:, k : k + 1]).astype(jnp.bfloat16))
-    hidden = jnp.concatenate(pieces, axis=1)
-    if exp_count == 2:
-        other_hidden = lax.ppermute(hidden, "exp", swap)
-        first = jnp.where(expert_index == 0, hidden, other_hidden)
-        second = jnp.where(expert_index == 0, other_hidden, hidden)
-        all_hidden = jnp.concatenate([first, second], axis=0)
-    else:
-        all_hidden = lax.all_gather(hidden, "exp", axis=0, tiled=True)
-    down = down_weight.reshape(own_experts * hidden_size, down_weight.shape[2])
-    partial = jnp.dot(all_hidden, down, preferred_element_type=jnp.float32)
-    routed_sum = scatter_sums(partial, ctx_count)
+        routed_sum = routed_at_once(
+            mixed_rows, norm_gain, own_route, gate_weight, up_weight, down_weight
+        )
     return (mixed_f + routed_sum).astype(jnp.bfloat16)
 
 

time: 173 us -> 126 us (0.73)
  waiting for transfers between devices: 115 us -> 65.7 us
  matrix products: 18.6 us -> 1.32 us
  starting transfers between devices: 22.5 us -> 37.1 us
  Pallas kernels: 0 us -> 13.8 us
  blocking collectives: 5.11 us -> 0 us
  other arithmetic: 8.01 us -> 4.73 us
    ppermute x6 -> x3, waiting for transfers between devices: 41.9 us -> 6.91 us  [gather_rows(): lax.ppermute(block, 'ctx', xor_pairs(count, bit))]
    ppermute x5 -> x20, starting transfers between devices: 10.4 us -> 30 us  [the longest x14 21.1 us: hop(): return lax.ppermute(block, 'ctx', xor_pairs(ctx_count, offset))]
    dot_general x9 -> x0, matrix products: 17.3 us -> none  [the longest x8 11.8 us: partial_sums(): terms.append(jnp.dot(rows, weight[k], preferred_element_type=jnp.float32))]
    ppermute x5 -> x20, waiting for transfers between devices: 73 us -> 58.7 us  [the longest x14 40.3 us: hop(): return lax.ppermute(block, 'ctx', xor_pairs(ctx_count, offset))]
    pallas_call x0 -> x15, Pallas kernels: none -> 13.8 us  [in_vmem(): pl.pallas_call(kernel, out_shape=out_shape, in_specs=specs, out_specs=[ou...]
    psum x1 -> x0, blocking collectives: 5.11 us -> none  [local(): square_sum = lax.psum(jnp.sum(mixed_f * mixed_f, axis=1), 'exp')]
    ppermute x6 -> x3, starting transfers between devices: 12.1 us -> 7.18 us  [gather_rows(): lax.ppermute(block, 'ctx', xor_pairs(count, bit))]
  transfers between devices with their start and end apart: 11 -> 23, of which waited for: 11 -> 15; matrix products, arithmetic and copies ran while one was open for 4% -> 3% of each run, Pallas kernels for 0% -> 11%
where the time goes in v2:
time: 126 us
  waiting for transfers between devices  65.7 us (52%)
  starting transfers between devices  37.1 us (29%)
  Pallas kernels  13.8 us (11%)
  other arithmetic  4.73 us (4%)
  local copies, waits for them, and re-layouts  2.47 us (2%)
  matrix products  1.32 us (1%)
    ppermute x14, waiting for transfers between devices, hop(): return lax.ppermute(block, 'ctx', xor_pairs(ctx_count, offset))  40.3 us
    ppermute x14, starting transfers between devices, hop(): return lax.ppermute(block, 'ctx', xor_pairs(ctx_count, offset))  21.1 us
    ppermute x3, waiting for transfers between devices, routed_in_chunks(): arrived = lax.ppermute(sent, 'exp', swap)  16 us
    pallas_call x15, Pallas kernels, in_vmem(): pl.pallas_call(kernel, out_shape=out_shape, in_specs=specs, out_specs=[ou...  13.8 us
    ppermute x3, starting transfers between devices, gather_rows(): lax.ppermute(block, 'ctx', xor_pairs(count, bit))  7.18 us
    ppermute x3, waiting for transfers between devices, gather_rows(): lax.ppermute(block, 'ctx', xor_pairs(count, bit))  6.91 us
    ppermute x3, starting transfers between devices, routed_in_chunks(): other_hidden = lax.ppermute(hidden, 'exp', swap)  4.67 us
    ppermute x3, starting transfers between devices, routed_in_chunks(): arrived = lax.ppermute(sent, 'exp', swap)  4.23 us
  transfers between devices with their start and end apart: 23, of which 15 were waited for; matrix products, arithmetic and copies ran while one was open for 3% of the time, Pallas kernels for 11%

profile of v2, /device:TPU:0, one launch (start us, length us, event | category | flops | bytes accessed | tf_op | source)
XLA Modules:
  0.0 125.5 jit_solution(424232069121854479)
XLA Ops:
  0.0 0.7 select_reduce_fusion
  0.9 0.7 constant_dynamic-slice_fusion
  1.7 4.0 %collective-permute-start = (bf16[64,288]{1,0:T(8,128)(2,1)S(1)}, bf16[64,288]{1,0:T(8,128)(2,1)S(1)}, u32[]{:S(2)}, u32[]{:S(2)}) collective-permute-start(bf16[64,288]{1,0:T(8,128)(2,1)S(1)} %pad_maximum_fusion.5), channel_id=1, source_target_pairs={{0,16},{4,20},{8,24},{12,28},{16,0},{20,4},{24,8},{28,12},{1,17},{... | collective-permute-start | bytes 110600 | tf_op jit(solution)/shard_map/ppermute | solution.py:39
  6.4 0.8 select_reduce_fusion.1
  7.3 1.1 collective-permute-done
  8.5 1.4 %collective-permute-start.1 = (bf16[128,288]{1,0:T(8,128)(2,1)S(1)}, bf16[128,288]{1,0:T(8,128)(2,1)S(1)}, u32[]{:S(2)}, u32[]{:S(2)}) collective-permute-start(bf16[128,288]{1,0:T(8,128)(2,1)S(1)} %pad_maximum_fusion.2), channel_id=1, source_target_pairs={{0,8},{4,12},{8,0},{12,4},{16,24},{20,28},{24,16},{28,20},{1,9},{5... | collective-permute-start | bytes 221192 | tf_op jit(solution)/shard_map/ppermute | solution.py:39
  9.9 3.2 %collective-permute-done.1 = bf16[128,288]{1,0:T(8,128)(2,1)S(1)} collective-permute-done((bf16[128,288]{1,0:T(8,128)(2,1)S(1)}, bf16[128,288]{1,0:T(8,128)(2,1)S(1)}, u32[]{:S(2)}, u32[]{:S(2)}) %collective-permute-start.1) | collective-permute-done | bytes 73760 | tf_op jit(solution)/shard_map/ppermute | solution.py:39
  13.2 1.7 %collective-permute-start.2 = (bf16[256,288]{1,0:T(8,128)(2,1)S(1)}, bf16[256,288]{1,0:T(8,128)(2,1)S(1)}, u32[]{:S(2)}, u32[]{:S(2)}) collective-permute-start(bf16[256,288]{1,0:T(8,128)(2,1)S(1)} %pad_maximum_fusion.1), channel_id=1, source_target_pairs={{0,4},{4,0},{8,12},{12,8},{16,20},{20,16},{24,28},{28,24},{1,5},{5... | collective-permute-start | bytes 442376 | tf_op jit(solution)/shard_map/ppermute | solution.py:39
  15.2 1.0 copy.43
  16.3 2.6 %collective-permute-done.2 = bf16[256,288]{1,0:T(8,128)(2,1)S(1)} collective-permute-done((bf16[256,288]{1,0:T(8,128)(2,1)S(1)}, bf16[256,288]{1,0:T(8,128)(2,1)S(1)}, u32[]{:S(2)}, u32[]{:S(2)}) %collective-permute-start.2) | collective-permute-done | bytes 147488 | tf_op jit(solution)/shard_map/ppermute | solution.py:39
  20.1 0.9 fusion.3
  21.3 1.5 %collective-permute-start.9 = (bf16[64,2048]{1,0:T(8,128)(2,1)S(1)}, bf16[64,2048]{1,0:T(8,128)(2,1)S(1)}, u32[]{:S(2)}, u32[]{:S(2)}) collective-permute-start(bf16[64,2048]{1,0:T(8,128)(2,1)S(1)} %fusion.6.rest_0_), channel_id=1, source_target_pairs={{0,8},{4,12},{8,0},{12,4},{16,24},{20,28},{24,16},{28,20},{1,9},{5... | collective-permute-start | bytes 786440 | tf_op jit(solution)/shard_map/ppermute | solution.py:170
  22.8 1.5 %collective-permute-start.4 = (bf16[64,2048]{1,0:T(8,128)(2,1)S(1)}, bf16[64,2048]{1,0:T(8,128)(2,1)S(1)}, u32[]{:S(2)}, u32[]{:S(2)}) collective-permute-start(bf16[64,2048]{1,0:T(8,128)(2,1)S(1)} %fusion.6.rest_0_), channel_id=1, source_target_pairs={{0,4},{4,0},{8,12},{12,8},{16,20},{20,16},{24,28},{28,24},{1,5},{5... | collective-permute-start | bytes 786440 | tf_op jit(solution)/shard_map/ppermute | solution.py:170
  24.3 3.0 %collective-permute-start.3 = (bf16[64,2048]{1,0:T(8,128)(2,1)S(1)}, bf16[64,2048]{1,0:T(8,128)(2,1)S(1)}, u32[]{:S(2)}, u32[]{:S(2)}) collective-permute-start(bf16[64,2048]{1,0:T(8,128)(2,1)S(1)} %fusion.6.rest_0_), channel_id=1, source_target_pairs={{0,16},{4,20},{8,24},{12,28},{16,0},{20,4},{24,8},{28,12},{1,17},{... | collective-permute-start | bytes 786440 | tf_op jit(solution)/shard_map/ppermute | solution.py:170
  27.7 7.7 %collective-permute-done.3.rest_1_ = bf16[64,2048]{1,0:T(8,128)(2,1)S(1)} collective-permute-done((bf16[64,2048]{1,0:T(8,128)(2,1)S(1)}, bf16[64,2048]{1,0:T(8,128)(2,1)S(1)}, u32[]{:S(2)}, u32[]{:S(2)}) %collective-permute-start.3) | collective-permute-done | bytes 262176 | tf_op jit(solution)/shard_map/ppermute | solution.py:170
  35.3 1.6 %collective-permute-start.10 = (bf16[64,2048]{1,0:T(8,128)(2,1)S(1)}, bf16[64,2048]{1,0:T(8,128)(2,1)S(1)}, u32[]{:S(2)}, u32[]{:S(2)}) collective-permute-start(bf16[64,2048]{1,0:T(8,128)(2,1)S(1)} %collective-permute-done.3.rest_1_), channel_id=1, source_target_pairs={{0,4},{4,0},{8,12},{12,8},{16,20},{20,16},{24,28},{28,24},{1,5},{5... | collective-permute-start | bytes 786440 | tf_op jit(solution)/shard_map/ppermute | solution.py:170
  37.0 1.4 %shard_map.119 = bf16[192,1664]{1,0:T(8,128)(2,1)S(1)} custom-call(s32[1]{0:T(128)S(6)} %sub.22.index_ref, f32[1,2048]{1,0:T(1,128)S(1)} %bitcast.33, bf16[2,2048,768]{2,1,0:T(8,128)(2,1)S(1)} %bitcast.30, bf16[2,2048,768]{2,1,0:T(8,128)(2,1)S(1)} %copy-done, bf16[64,2048]{1,0:T(8,128)(2,1)S(1)} %fusion.6.rest_0_, ...), custom_call_target="tpu_custom_call" | custom-call | flops 1207959552 | tf_op jit(solution)/shard_map/pallas_call | solution.py:148
  38.4 1.6 %collective-permute-start.5 = (bf16[192,1664]{1,0:T(8,128)(2,1)S(1)}, bf16[192,1664]{1,0:T(8,128)(2,1)S(1)}, u32[]{:S(2)}, u32[]{:S(2)}) collective-permute-start(bf16[192,1664]{1,0:T(8,128)(2,1)S(1)} %shard_map.119), channel_id=1, source_target_pairs={{0,2},{2,0},{1,3},{3,1},{4,6},{6,4},{5,7},{7,5},{8,10},{10,8},{9,1... | collective-permute-start | bytes 1916936 | tf_op jit(solution)/shard_map/ppermute | solution.py:187
  40.4 1.3 %collective-permute-done.11.rest_2_ = bf16[64,2048]{1,0:T(8,128)(2,1)S(1)} collective-permute-done((bf16[64,2048]{1,0:T(8,128)(2,1)S(1)}, bf16[64,2048]{1,0:T(8,128)(2,1)S(1)}, u32[]{:S(2)}, u32[]{:S(2)}) %collective-permute-start.11) | collective-permute-done | bytes 262176 | tf_op jit(solution)/shard_map/ppermute | solution.py:170
  41.7 1.4 %shard_map.124 = bf16[192,1664]{1,0:T(8,128)(2,1)S(1)} custom-call(s32[1]{0:T(128)S(6)} %sub.22.index_ref, f32[1,2048]{1,0:T(1,128)S(1)} %bitcast.34, bf16[2,2048,768]{2,1,0:T(8,128)(2,1)S(1)} %bitcast.30, bf16[2,2048,768]{2,1,0:T(8,128)(2,1)S(1)} %copy-done, bf16[64,2048]{1,0:T(8,128)(2,1)S(1)} %collective-permute-done.9.rest_0_, ...), custom_call_target="tpu_custom_call" | custom-call | flops 1207959552 | tf_op jit(solution)/shard_map/pallas_call | solution.py:148
  43.2 2.5 %collective-permute-start.12 = (bf16[192,1664]{1,0:T(8,128)(2,1)S(1)}, bf16[192,1664]{1,0:T(8,128)(2,1)S(1)}, u32[]{:S(2)}, u32[]{:S(2)}) collective-permute-start(bf16[192,1664]{1,0:T(8,128)(2,1)S(1)} %shard_map.124), channel_id=1, source_target_pairs={{0,2},{2,0},{1,3},{3,1},{4,6},{6,4},{5,7},{7,5},{8,10},{10,8},{9,1... | collective-permute-start | bytes 1916936 | tf_op jit(solution)/shard_map/ppermute | solution.py:187
  45.7 2.5 %collective-permute-start.18 = (bf16[64,2048]{1,0:T(8,128)(2,1)S(1)}, bf16[64,2048]{1,0:T(8,128)(2,1)S(1)}, u32[]{:S(2)}, u32[]{:S(2)}) collective-permute-start(bf16[64,2048]{1,0:T(8,128)(2,1)S(1)} %collective-permute-done.11.rest_2_), channel_id=1, source_target_pairs={{0,4},{4,0},{8,12},{12,8},{16,20},{20,16},{24,28},{28,24},{1,5},{5... | collective-permute-start | bytes 786440 | tf_op jit(solution)/shard_map/ppermute | solution.py:170
  48.2 4.3 %collective-permute-done.18.rest_1_ = bf16[64,2048]{1,0:T(8,128)(2,1)S(1)} collective-permute-done((bf16[64,2048]{1,0:T(8,128)(2,1)S(1)}, bf16[64,2048]{1,0:T(8,128)(2,1)S(1)}, u32[]{:S(2)}, u32[]{:S(2)}) %collective-permute-start.18) | collective-permute-done | bytes 262176 | tf_op jit(solution)/shard_map/ppermute | solution.py:170
  52.5 1.0 shard_map.129
  53.7 1.4 %shard_map.118.kept_ref = bf16[192,1664]{1,0:T(8,128)(2,1)S(1)} custom-call(s32[1]{0:T(128)} %bitcast.6.index_ref, f32[1,2048]{1,0:T(1,128)S(1)} %bitcast.36, bf16[2,2048,768]{2,1,0:T(8,128)(2,1)S(1)} %bitcast.30, bf16[2,2048,768]{2,1,0:T(8,128)(2,1)S(1)} %copy-done, bf16[64,2048]{1,0:T(8,128)(2,1)S(1)} %fusion.6.rest_0_, ...), custom_call_target="tpu_custom_call" | custom-call | flops 1207959552 | tf_op jit(solution)/shard_map/pallas_call | solution.py:148
  55.1 0.7 collective-permute-done.5.arrived_ref
  56.2 1.6 %collective-permute-start.6 = (bf16[192,768]{1,0:T(8,128)(2,1)S(1)}, bf16[192,768]{1,0:T(8,128)(2,1)S(1)}, u32[]{:S(2)}, u32[]{:S(2)}) collective-permute-start(bf16[192,768]{1,0:T(8,128)(2,1)S(1)} %shard_map.120.hidden_ref), channel_id=1, source_target_pairs={{0,2},{2,0},{1,3},{3,1},{4,6},{6,4},{5,7},{7,5},{8,10},{10,8},{9,1... | collective-permute-start | bytes 884744 | tf_op jit(solution)/shard_map/ppermute | solution.py:195
  57.8 1.4 %shard_map.123.kept_ref = bf16[192,1664]{1,0:T(8,128)(2,1)S(1)} custom-call(s32[1]{0:T(128)} %bitcast.6.index_ref, f32[1,2048]{1,0:T(1,128)S(1)} %bitcast.37, bf16[2,2048,768]{2,1,0:T(8,128)(2,1)S(1)} %bitcast.30, bf16[2,2048,768]{2,1,0:T(8,128)(2,1)S(1)} %copy-done, bf16[64,2048]{1,0:T(8,128)(2,1)S(1)} %collective-permute-done.9.rest_0_, ...), custom_call_target="tpu_custom_call" | custom-call | flops 1207959552 | tf_op jit(solution)/shard_map/pallas_call | solution.py:148
  59.3 1.0 shard_map.128.kept_ref
  60.3 9.2 %collective-permute-done.12.arrived_ref = bf16[192,1664]{1,0:T(8,128)(2,1)S(1)} collective-permute-done((bf16[192,1664]{1,0:T(8,128)(2,1)S(1)}, bf16[192,1664]{1,0:T(8,128)(2,1)S(1)}, u32[]{:S(2)}, u32[]{:S(2)}) %collective-permute-start.12) | collective-permute-done | bytes 639008 | tf_op jit(solution)/shard_map/ppermute | solution.py:187
  69.9 1.6 %collective-permute-start.13 = (bf16[192,768]{1,0:T(8,128)(2,1)S(1)}, bf16[192,768]{1,0:T(8,128)(2,1)S(1)}, u32[]{:S(2)}, u32[]{:S(2)}) collective-permute-start(bf16[192,768]{1,0:T(8,128)(2,1)S(1)} %shard_map.125.hidden_ref), channel_id=1, source_target_pairs={{0,2},{2,0},{1,3},{3,1},{4,6},{6,4},{5,7},{7,5},{8,10},{10,8},{9,1... | collective-permute-start | bytes 884744 | tf_op jit(solution)/shard_map/ppermute | solution.py:195
  71.5 1.0 shard_map.121.before_ref
  72.5 6.1 %collective-permute-done.19.arrived_ref = bf16[128,1664]{1,0:T(8,128)(2,1)S(1)} collective-permute-done((bf16[128,1664]{1,0:T(8,128)(2,1)S(1)}, bf16[128,1664]{1,0:T(8,128)(2,1)S(1)}, u32[]{:S(2)}, u32[]{:S(2)}) %collective-permute-start.19) | collective-permute-done | bytes 426016 | tf_op jit(solution)/shard_map/ppermute | solution.py:187
  79.0 1.6 %collective-permute-start.20 = (bf16[128,768]{1,0:T(8,128)(2,1)S(1)}, bf16[128,768]{1,0:T(8,128)(2,1)S(1)}, u32[]{:S(2)}, u32[]{:S(2)}) collective-permute-start(bf16[128,768]{1,0:T(8,128)(2,1)S(1)} %shard_map.130.hidden_ref), channel_id=1, source_target_pairs={{0,2},{2,0},{1,3},{3,1},{4,6},{6,4},{5,7},{7,5},{8,10},{10,8},{9,1... | collective-permute-start | bytes 589832 | tf_op jit(solution)/shard_map/ppermute | solution.py:195
  80.5 2.4 %collective-permute-done.6.hidden_ref = bf16[192,768]{1,0:T(8,128)(2,1)S(1)} collective-permute-done((bf16[192,768]{1,0:T(8,128)(2,1)S(1)}, bf16[192,768]{1,0:T(8,128)(2,1)S(1)}, u32[]{:S(2)}, u32[]{:S(2)}) %collective-permute-start.6) | collective-permute-done | bytes 294944 | tf_op jit(solution)/shard_map/ppermute | solution.py:195
  83.0 0.9 shard_map.122
  83.8 2.7 %collective-permute-start.7 = (bf16[64,2048]{1,0:T(8,128)(2,1)S(1)}, bf16[64,2048]{1,0:T(8,128)(2,1)S(1)}, u32[]{:S(2)}, u32[]{:S(2)}) collective-permute-start(bf16[64,2048]{1,0:T(8,128)(2,1)S(1)} %get-tuple-element.14), channel_id=1, source_target_pairs={{0,16},{4,20},{8,24},{12,28},{16,0},{20,4},{24,8},{28,12},{1,17},{... | collective-permute-start | bytes 786440 | tf_op jit(solution)/shard_map/ppermute | solution.py:170
  87.1 0.8 shard_map.126.before_ref
  89.2 2.1 %collective-permute-start.21 = (bf16[64,2048]{1,0:T(8,128)(2,1)S(1)}, bf16[64,2048]{1,0:T(8,128)(2,1)S(1)}, u32[]{:S(2)}, u32[]{:S(2)}) collective-permute-start(bf16[64,2048]{1,0:T(8,128)(2,1)S(1)} %get-tuple-element.19), channel_id=1, source_target_pairs={{0,12},{4,8},{8,4},{12,0},{16,28},{20,24},{24,20},{28,16},{1,13},{... | collective-permute-start | bytes 786440 | tf_op jit(solution)/shard_map/ppermute | solution.py:170
  91.3 2.6 %collective-permute-start.22 = (bf16[64,2048]{1,0:T(8,128)(2,1)S(1)}, bf16[64,2048]{1,0:T(8,128)(2,1)S(1)}, u32[]{:S(2)}, u32[]{:S(2)}) collective-permute-start(bf16[64,2048]{1,0:T(8,128)(2,1)S(1)} %get-tuple-element.20), channel_id=1, source_target_pairs={{0,28},{4,24},{8,20},{12,16},{16,12},{20,8},{24,4},{28,0},{1,29},{... | collective-permute-start | bytes 786440 | tf_op jit(solution)/shard_map/ppermute | solution.py:170
  94.0 0.8 shard_map.127
  94.9 4.9 %collective-permute-done.7 = bf16[64,2048]{1,0:T(8,128)(2,1)S(1)} collective-permute-done((bf16[64,2048]{1,0:T(8,128)(2,1)S(1)}, bf16[64,2048]{1,0:T(8,128)(2,1)S(1)}, u32[]{:S(2)}, u32[]{:S(2)}) %collective-permute-start.7) | collective-permute-done | bytes 262176 | tf_op jit(solution)/shard_map/ppermute | solution.py:170
  99.8 2.5 %collective-permute-start.16 = (bf16[64,2048]{1,0:T(8,128)(2,1)S(1)}, bf16[64,2048]{1,0:T(8,128)(2,1)S(1)}, u32[]{:S(2)}, u32[]{:S(2)}) collective-permute-start(bf16[64,2048]{1,0:T(8,128)(2,1)S(1)} %get-tuple-element.18), channel_id=1, source_target_pairs={{0,24},{4,28},{8,16},{12,20},{16,8},{20,12},{24,0},{28,4},{1,25},{... | collective-permute-start | bytes 786440 | tf_op jit(solution)/shard_map/ppermute | solution.py:170
  102.3 1.3 %collective-permute-done.21 = bf16[64,2048]{1,0:T(8,128)(2,1)S(1)} collective-permute-done((bf16[64,2048]{1,0:T(8,128)(2,1)S(1)}, bf16[64,2048]{1,0:T(8,128)(2,1)S(1)}, u32[]{:S(2)}, u32[]{:S(2)}) %collective-permute-start.21) | collective-permute-done | bytes 262176 | tf_op jit(solution)/shard_map/ppermute | solution.py:170
  103.6 3.8 %collective-permute-done.22 = bf16[64,2048]{1,0:T(8,128)(2,1)S(1)} collective-permute-done((bf16[64,2048]{1,0:T(8,128)(2,1)S(1)}, bf16[64,2048]{1,0:T(8,128)(2,1)S(1)}, u32[]{:S(2)}, u32[]{:S(2)}) %collective-permute-start.22) | collective-permute-done | bytes 262176 | tf_op jit(solution)/shard_map/ppermute | solution.py:170
  107.4 4.5 %collective-permute-done.14 = bf16[64,2048]{1,0:T(8,128)(2,1)S(1)} collective-permute-done((bf16[64,2048]{1,0:T(8,128)(2,1)S(1)}, bf16[64,2048]{1,0:T(8,128)(2,1)S(1)}, u32[]{:S(2)}, u32[]{:S(2)}) %collective-permute-start.14) | collective-permute-done | bytes 262176 | tf_op jit(solution)/shard_map/ppermute | solution.py:170
  111.9 12.6 %collective-permute-done.15 = bf16[64,2048]{1,0:T(8,128)(2,1)S(1)} collective-permute-done((bf16[64,2048]{1,0:T(8,128)(2,1)S(1)}, bf16[64,2048]{1,0:T(8,128)(2,1)S(1)}, u32[]{:S(2)}, u32[]{:S(2)}) %collective-permute-start.15) | collective-permute-done | bytes 262176 | tf_op jit(solution)/shard_map/ppermute | solution.py:170
  124.5 1.1 add_convert_fusion
  (62 shorter events, 7.0 us)
Async XLA Ops:
  1.7 6.6 %collective-permute-start = (bf16[64,288]{1,0:T(8,128)(2,1)S(1)}, bf16[64,288]{1,0:T(8,128)(2,1)S(1)}, u32[]{:S(2)}, u32[]{:S(2)}) collective-permute-start(bf16[64,288]{1,0:T(8,128)(2,1)S(1)} %pad_maximum_fusion.5), channel_id=1, source_target_pairs={{0,16},{4,20},{8,24},{12,28},{16,0},{20,4},{24,8},{28,12},{1,17},{... | collective-permute-start | bytes 110600 | tf_op jit(solution)/shard_map/ppermute | solution.py:39
  8.5 4.6 %collective-permute-start.1 = (bf16[128,288]{1,0:T(8,128)(2,1)S(1)}, bf16[128,288]{1,0:T(8,128)(2,1)S(1)}, u32[]{:S(2)}, u32[]{:S(2)}) collective-permute-start(bf16[128,288]{1,0:T(8,128)(2,1)S(1)} %pad_maximum_fusion.2), channel_id=1, source_target_pairs={{0,8},{4,12},{8,0},{12,4},{16,24},{20,28},{24,16},{28,20},{1,9},{5... | collective-permute-start | bytes 221192 | tf_op jit(solution)/shard_map/ppermute | solution.py:39
  13.2 5.7 %collective-permute-start.2 = (bf16[256,288]{1,0:T(8,128)(2,1)S(1)}, bf16[256,288]{1,0:T(8,128)(2,1)S(1)}, u32[]{:S(2)}, u32[]{:S(2)}) collective-permute-start(bf16[256,288]{1,0:T(8,128)(2,1)S(1)} %pad_maximum_fusion.1), channel_id=1, source_target_pairs={{0,4},{4,0},{8,12},{12,8},{16,20},{20,16},{24,28},{28,24},{1,5},{5... | collective-permute-start | bytes 442376 | tf_op jit(solution)/shard_map/ppermute | solution.py:39
  19.0 2.2 %copy-start.2 = (bf16[64,2048]{1,0:T(8,128)(2,1)S(1)}, bf16[64,2048]{1,0:T(8,128)(2,1)}, u32[]{:S(2)}) copy-start(bf16[64,2048]{1,0:T(8,128)(2,1)} %param.16) | copy-start | bytes 786436
  19.5 17.5 %slice-start = ((s8[6291456]{0:T(1024)(128)(4,1)}), s8[4194304]{0:T(1024)(128)(4,1)S(1)}, s32[]{:S(2)}) async-start(s8[6291456]{0:T(1024)(128)(4,1)} %bitcast.29), calls=%async_computation | async-start | bytes 8388608
  20.1 16.9 %slice-start.1 = ((s8[6291456]{0:T(1024)(128)(4,1)}), s8[2097152]{0:T(1024)(128)(4,1)S(1)}, s32[]{:S(2)}) async-start(s8[6291456]{0:T(1024)(128)(4,1)} %bitcast.29), calls=%async_computation.1 | async-start | bytes 4194304
  20.1 16.9 %copy-start = (bf16[2,2048,768]{2,1,0:T(8,128)(2,1)S(1)}, bf16[2,2048,768]{2,1,0:T(8,128)(2,1)}, u32[]{:S(2)}) copy-start(bf16[2,2048,768]{2,1,0:T(8,128)(2,1)} %up_ref.11) | copy-start | bytes 18874372
  21.0 16.0 %copy-start.1 = (f32[2048]{0:T(1024)S(1)}, f32[2048]{0:T(1024)}, u32[]{:S(2)}) copy-start(f32[2048]{0:T(1024)} %param.17) | copy-start | bytes 24580
  21.3 18.6 %collective-permute-start.9 = (bf16[64,2048]{1,0:T(8,128)(2,1)S(1)}, bf16[64,2048]{1,0:T(8,128)(2,1)S(1)}, u32[]{:S(2)}, u32[]{:S(2)}) collective-permute-start(bf16[64,2048]{1,0:T(8,128)(2,1)S(1)} %fusion.6.rest_0_), channel_id=1, source_target_pairs={{0,8},{4,12},{8,0},{12,4},{16,24},{20,28},{24,16},{28,20},{1,9},{5... | collective-permute-start | bytes 786440 | tf_op jit(solution)/shard_map/ppermute | solution.py:170
  22.8 14.1 %collective-permute-start.4 = (bf16[64,2048]{1,0:T(8,128)(2,1)S(1)}, bf16[64,2048]{1,0:T(8,128)(2,1)S(1)}, u32[]{:S(2)}, u32[]{:S(2)}) collective-permute-start(bf16[64,2048]{1,0:T(8,128)(2,1)S(1)} %fusion.6.rest_0_), channel_id=1, source_target_pairs={{0,4},{4,0},{8,12},{12,8},{16,20},{20,16},{24,28},{28,24},{1,5},{5... | collective-permute-start | bytes 786440 | tf_op jit(solution)/shard_map/ppermute | solution.py:170
  24.3 11.0 %collective-permute-start.3 = (bf16[64,2048]{1,0:T(8,128)(2,1)S(1)}, bf16[64,2048]{1,0:T(8,128)(2,1)S(1)}, u32[]{:S(2)}, u32[]{:S(2)}) collective-permute-start(bf16[64,2048]{1,0:T(8,128)(2,1)S(1)} %fusion.6.rest_0_), channel_id=1, source_target_pairs={{0,16},{4,20},{8,24},{12,28},{16,0},{20,4},{24,8},{28,12},{1,17},{... | collective-permute-start | bytes 786440 | tf_op jit(solution)/shard_map/ppermute | solution.py:170
  35.3 6.4 %collective-permute-start.11 = (bf16[64,2048]{1,0:T(8,128)(2,1)S(1)}, bf16[64,2048]{1,0:T(8,128)(2,1)S(1)}, u32[]{:S(2)}, u32[]{:S(2)}) collective-permute-start(bf16[64,2048]{1,0:T(8,128)(2,1)S(1)} %collective-permute-done.3.rest_1_), channel_id=1, source_target_pairs={{0,8},{4,12},{8,0},{12,4},{16,24},{20,28},{24,16},{28,20},{1,9},{5... | collective-permute-start | bytes 786440 | tf_op jit(solution)/shard_map/ppermute | solution.py:170
  35.3 6.4 %collective-permute-start.10 = (bf16[64,2048]{1,0:T(8,128)(2,1)S(1)}, bf16[64,2048]{1,0:T(8,128)(2,1)S(1)}, u32[]{:S(2)}, u32[]{:S(2)}) collective-permute-start(bf16[64,2048]{1,0:T(8,128)(2,1)S(1)} %collective-permute-done.3.rest_1_), channel_id=1, source_target_pairs={{0,4},{4,0},{8,12},{12,8},{16,20},{20,16},{24,28},{28,24},{1,5},{5... | collective-permute-start | bytes 786440 | tf_op jit(solution)/shard_map/ppermute | solution.py:170
  38.4 17.4 %collective-permute-start.5 = (bf16[192,1664]{1,0:T(8,128)(2,1)S(1)}, bf16[192,1664]{1,0:T(8,128)(2,1)S(1)}, u32[]{:S(2)}, u32[]{:S(2)}) collective-permute-start(bf16[192,1664]{1,0:T(8,128)(2,1)S(1)} %shard_map.119), channel_id=1, source_target_pairs={{0,2},{2,0},{1,3},{3,1},{4,6},{6,4},{5,7},{7,5},{8,10},{10,8},{9,1... | collective-permute-start | bytes 1916936 | tf_op jit(solution)/shard_map/ppermute | solution.py:187
  40.0 8.2 %collective-permute-start.17 = (bf16[64,2048]{1,0:T(8,128)(2,1)S(1)}, bf16[64,2048]{1,0:T(8,128)(2,1)S(1)}, u32[]{:S(2)}, u32[]{:S(2)}) collective-permute-start(bf16[64,2048]{1,0:T(8,128)(2,1)S(1)} %collective-permute-done.9.rest_0_), channel_id=1, source_target_pairs={{0,4},{4,0},{8,12},{12,8},{16,20},{20,16},{24,28},{28,24},{1,5},{5... | collective-permute-start | bytes 786440 | tf_op jit(solution)/shard_map/ppermute | solution.py:170
  43.2 26.3 %collective-permute-start.12 = (bf16[192,1664]{1,0:T(8,128)(2,1)S(1)}, bf16[192,1664]{1,0:T(8,128)(2,1)S(1)}, u32[]{:S(2)}, u32[]{:S(2)}) collective-permute-start(bf16[192,1664]{1,0:T(8,128)(2,1)S(1)} %shard_map.124), channel_id=1, source_target_pairs={{0,2},{2,0},{1,3},{3,1},{4,6},{6,4},{5,7},{7,5},{8,10},{10,8},{9,1... | collective-permute-start | bytes 1916936 | tf_op jit(solution)/shard_map/ppermute | solution.py:187
  45.7 6.8 %collective-permute-start.18 = (bf16[64,2048]{1,0:T(8,128)(2,1)S(1)}, bf16[64,2048]{1,0:T(8,128)(2,1)S(1)}, u32[]{:S(2)}, u32[]{:S(2)}) collective-permute-start(bf16[64,2048]{1,0:T(8,128)(2,1)S(1)} %collective-permute-done.11.rest_2_), channel_id=1, source_target_pairs={{0,4},{4,0},{8,12},{12,8},{16,20},{20,16},{24,28},{28,24},{1,5},{5... | collective-permute-start | bytes 786440 | tf_op jit(solution)/shard_map/ppermute | solution.py:170
  53.6 25.1 %collective-permute-start.19 = (bf16[128,1664]{1,0:T(8,128)(2,1)S(1)}, bf16[128,1664]{1,0:T(8,128)(2,1)S(1)}, u32[]{:S(2)}, u32[]{:S(2)}) collective-permute-start(bf16[128,1664]{1,0:T(8,128)(2,1)S(1)} %shard_map.129), channel_id=1, source_target_pairs={{0,2},{2,0},{1,3},{3,1},{4,6},{6,4},{5,7},{7,5},{8,10},{10,8},{9,1... | collective-permute-start | bytes 1277960 | tf_op jit(solution)/shard_map/ppermute | solution.py:187
  56.2 26.7 %collective-permute-start.6 = (bf16[192,768]{1,0:T(8,128)(2,1)S(1)}, bf16[192,768]{1,0:T(8,128)(2,1)S(1)}, u32[]{:S(2)}, u32[]{:S(2)}) collective-permute-start(bf16[192,768]{1,0:T(8,128)(2,1)S(1)} %shard_map.120.hidden_ref), channel_id=1, source_target_pairs={{0,2},{2,0},{1,3},{3,1},{4,6},{6,4},{5,7},{7,5},{8,10},{10,8},{9,1... | collective-permute-start | bytes 884744 | tf_op jit(solution)/shard_map/ppermute | solution.py:195
  57.8 13.7 %slice-start.2 = ((s8[6291456]{0:T(1024)(128)(4,1)}), s8[4194304]{0:T(1024)(128)(4,1)S(1)}, s32[]{:S(2)}) async-start(s8[6291456]{0:T(1024)(128)(4,1)} %bitcast.31), calls=%async_computation.2 | async-start | bytes 8388608
  59.3 12.2 %slice-start.3 = ((s8[6291456]{0:T(1024)(128)(4,1)}), s8[2097152]{0:T(1024)(128)(4,1)S(1)}, s32[]{:S(2)}) async-start(s8[6291456]{0:T(1024)(128)(4,1)} %bitcast.31), calls=%async_computation.3 | async-start | bytes 4194304
  69.9 24.0 %collective-permute-start.13 = (bf16[192,768]{1,0:T(8,128)(2,1)S(1)}, bf16[192,768]{1,0:T(8,128)(2,1)S(1)}, u32[]{:S(2)}, u32[]{:S(2)}) collective-permute-start(bf16[192,768]{1,0:T(8,128)(2,1)S(1)} %shard_map.125.hidden_ref), channel_id=1, source_target_pairs={{0,2},{2,0},{1,3},{3,1},{4,6},{6,4},{5,7},{7,5},{8,10},{10,8},{9,1... | collective-permute-start | bytes 884744 | tf_op jit(solution)/shard_map/ppermute | solution.py:195
  79.0 9.6 %collective-permute-start.20 = (bf16[128,768]{1,0:T(8,128)(2,1)S(1)}, bf16[128,768]{1,0:T(8,128)(2,1)S(1)}, u32[]{:S(2)}, u32[]{:S(2)}) collective-permute-start(bf16[128,768]{1,0:T(8,128)(2,1)S(1)} %shard_map.130.hidden_ref), channel_id=1, source_target_pairs={{0,2},{2,0},{1,3},{3,1},{4,6},{6,4},{5,7},{7,5},{8,10},{10,8},{9,1... | collective-permute-start | bytes 589832 | tf_op jit(solution)/shard_map/ppermute | solution.py:195
  83.8 16.0 %collective-permute-start.7 = (bf16[64,2048]{1,0:T(8,128)(2,1)S(1)}, bf16[64,2048]{1,0:T(8,128)(2,1)S(1)}, u32[]{:S(2)}, u32[]{:S(2)}) collective-permute-start(bf16[64,2048]{1,0:T(8,128)(2,1)S(1)} %get-tuple-element.14), channel_id=1, source_target_pairs={{0,16},{4,20},{8,24},{12,28},{16,0},{20,4},{24,8},{28,12},{1,17},{... | collective-permute-start | bytes 786440 | tf_op jit(solution)/shard_map/ppermute | solution.py:170
  86.6 13.3 %collective-permute-start.8 = (bf16[64,2048]{1,0:T(8,128)(2,1)S(1)}, bf16[64,2048]{1,0:T(8,128)(2,1)S(1)}, u32[]{:S(2)}, u32[]{:S(2)}) collective-permute-start(bf16[64,2048]{1,0:T(8,128)(2,1)S(1)} %get-tuple-element.15), channel_id=1, source_target_pairs={{0,4},{4,0},{8,12},{12,8},{16,20},{20,16},{24,28},{28,24},{1,5},{5... | collective-permute-start | bytes 786440 | tf_op jit(solution)/shard_map/ppermute | solution.py:170
  89.2 14.4 %collective-permute-start.21 = (bf16[64,2048]{1,0:T(8,128)(2,1)S(1)}, bf16[64,2048]{1,0:T(8,128)(2,1)S(1)}, u32[]{:S(2)}, u32[]{:S(2)}) collective-permute-start(bf16[64,2048]{1,0:T(8,128)(2,1)S(1)} %get-tuple-element.19), channel_id=1, source_target_pairs={{0,12},{4,8},{8,4},{12,0},{16,28},{20,24},{24,20},{28,16},{1,13},{... | collective-permute-start | bytes 786440 | tf_op jit(solution)/shard_map/ppermute | solution.py:170
  91.3 16.1 %collective-permute-start.22 = (bf16[64,2048]{1,0:T(8,128)(2,1)S(1)}, bf16[64,2048]{1,0:T(8,128)(2,1)S(1)}, u32[]{:S(2)}, u32[]{:S(2)}) collective-permute-start(bf16[64,2048]{1,0:T(8,128)(2,1)S(1)} %get-tuple-element.20), channel_id=1, source_target_pairs={{0,28},{4,24},{8,20},{12,16},{16,12},{20,8},{24,4},{28,0},{1,29},{... | collective-permute-start | bytes 786440 | tf_op jit(solution)/shard_map/ppermute | solution.py:170
  94.8 17.1 %collective-permute-start.14 = (bf16[64,2048]{1,0:T(8,128)(2,1)S(1)}, bf16[64,2048]{1,0:T(8,128)(2,1)S(1)}, u32[]{:S(2)}, u32[]{:S(2)}) collective-permute-start(bf16[64,2048]{1,0:T(8,128)(2,1)S(1)} %get-tuple-element.16), channel_id=1, source_target_pairs={{0,8},{4,12},{8,0},{12,4},{16,24},{20,28},{24,16},{28,20},{1,9},{5... | collective-permute-start | bytes 786440 | tf_op jit(solution)/shard_map/ppermute | solution.py:170
  99.8 24.7 %collective-permute-start.15 = (bf16[64,2048]{1,0:T(8,128)(2,1)S(1)}, bf16[64,2048]{1,0:T(8,128)(2,1)S(1)}, u32[]{:S(2)}, u32[]{:S(2)}) collective-permute-start(bf16[64,2048]{1,0:T(8,128)(2,1)S(1)} %get-tuple-element.17), channel_id=1, source_target_pairs={{0,20},{4,16},{8,28},{12,24},{16,4},{20,0},{24,12},{28,8},{1,21},{... | collective-permute-start | bytes 786440 | tf_op jit(solution)/shard_map/ppermute | solution.py:170
  99.8 24.7 %collective-permute-start.16 = (bf16[64,2048]{1,0:T(8,128)(2,1)S(1)}, bf16[64,2048]{1,0:T(8,128)(2,1)S(1)}, u32[]{:S(2)}, u32[]{:S(2)}) collective-permute-start(bf16[64,2048]{1,0:T(8,128)(2,1)S(1)} %get-tuple-element.18), channel_id=1, source_target_pairs={{0,24},{4,28},{8,16},{12,20},{16,8},{20,12},{24,0},{28,4},{1,25},{... | collective-permute-start | bytes 786440 | tf_op jit(solution)/shard_map/ppermute | solution.py:170

commit v3 on v1

--- a/solution.py
+++ b/solution.py
@@ -1,8 +1,11 @@
+import functools
 import math
 
 import jax
 import jax.numpy as jnp
 from jax import lax
+from jax.experimental import pallas as pl
+from jax.experimental.pallas import tpu as pltpu
 from jax.sharding import PartitionSpec as P
 
 D = 4096
@@ -13,6 +16,22 @@
 
 MASKED_SCORE = -1e30
 NORM_EPS = 1e-06
+LANES = 128
+KERNEL_BYTES = 16 * 1024 * 1024
+ROUTE_LANES = 16
+HELD = False
+COST = 2e9
+PACK_COST = 5
+ATT_COST = 5
+HOPS = ((0, 1), (0, 4), (4, 2), (4, 1), (6, 1), (0, 2), (2, 1))
+CHUNKS = ((1,), (6, 5), (7, 4), (2, 3), (0,))
+SENDS = {1: 1, 2: 2, 3: 3, 4: 4, 5: 1, 6: 2, 7: 7}
+STEPS = (
+    ("send", 0), ("keep", 0), ("send", 1), ("hidden", 0), ("keep", 1), ("send", 2),
+    ("both", 0), ("hidden", 1), ("keep", 2), ("hidden", 2), ("send", 3), ("both", 1), ("keep", 3),
+    ("both", 2), ("hidden", 3), ("send", 4), ("keep", 4), ("both", 3), ("hidden", 4), ("own", 4), ("end", 4),
+)
+OWN = {"own": 1, "end": 4}
 
 
 def xor_pairs(count, bit):
@@ -49,7 +68,37 @@
     return partial
 
 
-def local(
+def routed_at_once(mixed_rows, norm_gain, own_route, gate_weight, up_weight, down_weight):
+    ctx_count = lax.axis_size("ctx")
+    own_experts, _, hidden_size = gate_weight.shape
+    mixed_f = mixed_rows.astype(jnp.float32)
+    square_sum = lax.psum(jnp.sum(mixed_f * mixed_f, axis=1), "exp")
+    normed = (mixed_f * lax.rsqrt(square_sum[:, None] / D + NORM_EPS) * norm_gain[None, :]).astype(
+        jnp.bfloat16
+    )
+    all_normed = gather_rows(normed, ctx_count)
+    share = all_normed.shape[0] // lax.axis_size("exp")
+    terms = []
+    for k in range(own_experts):
+        for weight in (gate_weight, up_weight):
+            term = jnp.dot(all_normed, weight[k], preferred_element_type=jnp.float32)
+            terms.append(term.astype(jnp.bfloat16))
+    sums = lax.psum_scatter(
+        jnp.concatenate(terms, axis=1), "exp", scatter_dimension=0, tiled=True
+    ).astype(jnp.float32)
+    my_route = lax.dynamic_slice_in_dim(own_route, lax.axis_index("exp") * share, share, 0)
+    pieces = []
+    for k in range(own_experts):
+        gate_sum = sums[:, 2 * k * hidden_size : (2 * k + 1) * hidden_size]
+        up_sum = sums[:, (2 * k + 1) * hidden_size : (2 * k + 2) * hidden_size]
+        pieces.append((jax.nn.silu(gate_sum) * up_sum * my_route[:, k : k + 1]).astype(jnp.bfloat16))
+    hidden = lax.all_gather(jnp.concatenate(pieces, axis=1), "exp", axis=0, tiled=True)
+    down = down_weight.reshape(own_experts * hidden_size, down_weight.shape[2])
+    partial = jnp.dot(hidden, down, preferred_element_type=jnp.float32)
+    return scatter_sums(partial, ctx_count)
+
+
+def general(
     queries,
     key_rows,
     value_head_rows,
@@ -64,11 +113,10 @@
 ):
     shard_rows = queries.shape[0]
     ctx_count = lax.axis_size("ctx")
-    exp_count = lax.axis_size("exp")
     local_head = queries.shape[1] // HEAD_SIZE
     expert_index = lax.axis_index("exp")
     ctx_index = lax.axis_index("ctx")
-    own_experts, _, hidden_size = gate_weight.shape
+    own_experts = gate_weight.shape[0]
     expert_count = ctx_count * own_experts
 
     key_value_head = expert_index * local_head // (QUERY_HEADS // KEY_VALUE_HEADS)
@@ -127,50 +175,298 @@
     )
     mixed_rows = (residual.astype(jnp.float32) + attention.astype(jnp.float32)).astype(jnp.bfloat16)
     mixed_f = mixed_rows.astype(jnp.float32)
-    square_sum = lax.psum(jnp.sum(mixed_f * mixed_f, axis=1), "exp")
-    normed = (mixed_f * lax.rsqrt(square_sum[:, None] / D + NORM_EPS) * norm_gain[None, :]).astype(
-        jnp.bfloat16
-    )
-
-    all_normed = gather_rows(normed, ctx_count)
-    total = all_normed.shape[0]
-    share = total // exp_count
-
-    def partial_sums(rows):
-        terms = []
-        for k in range(own_experts):
-            for weight in (gate_weight, up_weight):
-                terms.append(jnp.dot(rows, weight[k], preferred_element_type=jnp.float32))
-        return jnp.concatenate([term.astype(jnp.bfloat16) for term in terms], axis=1)
-
-    if exp_count == 2:
-        swap = [(0, 1), (1, 0)]
-        others = lax.dynamic_slice_in_dim(all_normed, (1 - expert_index) * share, share, 0)
-        mine = lax.dynamic_slice_in_dim(all_normed, expert_index * share, share, 0)
-        arrived = lax.ppermute(partial_sums(others), "exp", swap)
-        sums = partial_sums(mine).astype(jnp.float32) + arrived.astype(jnp.float32)
-    else:
-        sums = lax.psum_scatter(
-            partial_sums(all_normed), "exp", scatter_dimension=0, tiled=True
-        ).astype(jnp.float32)
-    my_route = lax.dynamic_slice_in_dim(own_route, expert_index * share, share, 0)
-    pieces = []
-    for k in range(own_experts):
-        gate_sum = sums[:, 2 * k * hidden_size : (2 * k + 1) * hidden_size]
-        up_sum = sums[:, (2 * k + 1) * hidden_size : (2 * k + 2) * hidden_size]
-        pieces.append((jax.nn.silu(gate_sum) * up_sum * my_route[:, k : k + 1]).astype(jnp.bfloat16))
-    hidden = jnp.concatenate(pieces, axis=1)
-    if exp_count == 2:
-        other_hidden = lax.ppermute(hidden, "exp", swap)
-        first = jnp.where(expert_index == 0, hidden, other_hidden)
-        second = jnp.where(expert_index == 0, other_hidden, hidden)
-        all_hidden = jnp.concatenate([first, second], axis=0)
-    else:
-        all_hidden = lax.all_gather(hidden, "exp", axis=0, tiled=True)
-    down = down_weight.reshape(own_experts * hidden_size, down_weight.shape[2])
-    partial = jnp.dot(all_hidden, down, preferred_element_type=jnp.float32)
-    routed_sum = scatter_sums(partial, ctx_count)
+    routed_sum = routed_at_once(
+        mixed_rows, norm_gain, own_route, gate_weight, up_weight, down_weight
+    )
     return (mixed_f + routed_sum).astype(jnp.bfloat16)
+
+
+def pack_kernel(head_ref, key_ref, value_ref, ids_ref, route_ref, out_ref, ids, weights, sems):
+    columns = pl.ds(pl.multiple_of(head_ref[0] * HEAD_SIZE, HEAD_SIZE), HEAD_SIZE)
+    copies = [
+        pltpu.make_async_copy(ids_ref, ids, sems.at[0]),
+        pltpu.make_async_copy(route_ref, weights, sems.at[1]),
+        pltpu.make_async_copy(key_ref.at[:, columns], out_ref.at[:, :HEAD_SIZE], sems.at[2]),
+        pltpu.make_async_copy(
+            value_ref.at[:, columns], out_ref.at[:, HEAD_SIZE : 2 * HEAD_SIZE], sems.at[3]
+        ),
+    ]
+    for copy in copies:
+        copy.start()
+    copies[0].wait()
+    copies[1].wait()
+    rows = out_ref.shape[0]
+    line = lax.broadcasted_iota(jnp.int32, (LANES, rows), 0)
+    expert = line % ROUTE_LANES
+    route = jnp.zeros(line.shape, jnp.float32)
+    for i in range(TOPK):
+        route = route + jnp.where(ids[i : i + 1, :] == expert, weights[i : i + 1, :], 0.0)
+    high = route.astype(jnp.bfloat16).astype(jnp.float32)
+    both = jnp.where(line < ROUTE_LANES, high, route - high)
+    both = jnp.concatenate([both, jnp.zeros((LANES, LANES - rows), jnp.float32)], axis=1)
+    out_ref[:, 2 * HEAD_SIZE :] = jnp.transpose(both)[:rows].astype(jnp.bfloat16)
+    copies[2].wait()
+    copies[3].wait()
+
+
+def attention_kernel(place_ref, order_ref, query_ref, packed_ref, residual_ref, out_ref):
+    rows = query_ref.shape[0]
+    heads = query_ref.shape[1] // HEAD_SIZE
+    count = packed_ref.shape[0]
+    queries = jnp.concatenate(
+        [query_ref[:, h * HEAD_SIZE : (h + 1) * HEAD_SIZE] for h in range(heads)], axis=0
+    )
+    scores = lax.dot_general(
+        queries,
+        packed_ref[:, :HEAD_SIZE],
+        (((1,), (1,)), ((), ())),
+        preferred_element_type=jnp.float32,
+    ) * (1.0 / math.sqrt(HEAD_SIZE))
+    me = place_ref[0]
+    column = lax.broadcasted_iota(jnp.int32, (rows, count), 1)
+    key_pos = column % rows
+    for i, offset in enumerate(offsets(count // rows)):
+        key_pos = key_pos + jnp.where(column // rows == i, order_ref[me ^ offset] * rows, 0)
+    query_pos = order_ref[me] * rows + lax.broadcasted_iota(jnp.int32, (rows, count), 0)
+    visible = jnp.concatenate([key_pos <= query_pos] * heads, axis=0)
+    scores = jnp.where(visible, scores, MASKED_SCORE)
+    largest = jnp.max(scores, axis=1, keepdims=True)
+    weights = jnp.where(visible, jnp.exp(scores - largest), 0.0)
+    weight_sum = jnp.sum(weights, axis=1, keepdims=True)
+    weighted = jnp.dot(
+        weights.astype(jnp.bfloat16),
+        packed_ref[:, HEAD_SIZE : 2 * HEAD_SIZE],
+        preferred_element_type=jnp.float32,
+    )
+    attention = (weighted / weight_sum).astype(jnp.bfloat16)
+    for h in range(heads):
+        columns = slice(h * HEAD_SIZE, (h + 1) * HEAD_SIZE)
+        part = attention[h * rows : (h + 1) * rows].astype(jnp.float32)
+        out_ref[:, columns] = (residual_ref[:, columns].astype(jnp.float32) + part).astype(
+            jnp.bfloat16
+        )
+
+
+def prepared(blocks, gain_ref):
+    rows = jnp.concatenate([block[...] for block in blocks], axis=0).astype(jnp.float32)
+    squares = jnp.sum(rows * rows, axis=1, keepdims=True)
+    return (rows * gain_ref[...]).astype(jnp.bfloat16), squares
+
+
+def first_kernel(index_ref, gain_ref, gate_ref, up_ref, *rest):
+    out_ref = rest[-1]
+    k = index_ref[0]
+    size = gate_ref.shape[2]
+    rows, squares = prepared(rest[:-1], gain_ref)
+    gate = jnp.dot(rows, gate_ref[k], preferred_element_type=jnp.float32)
+    out_ref[:, :size] = gate.astype(jnp.bfloat16)
+    up = jnp.dot(rows, up_ref[k], preferred_element_type=jnp.float32)
+    out_ref[:, size : 2 * size] = up.astype(jnp.bfloat16)
+    high = squares.astype(jnp.bfloat16).astype(jnp.float32)
+    lane = lax.broadcasted_iota(jnp.int32, (rows.shape[0], LANES), 1)
+    out_ref[:, 2 * size :] = jnp.where(lane == 0, high, squares - high).astype(jnp.bfloat16)
+
+
+def hidden_kernel(places, index_ref, kept_ref, arrived_ref, packed_ref, out_ref):
+    size = out_ref.shape[1]
+    rows = out_ref.shape[0] // len(places)
+    tail = kept_ref[:, 2 * size :].astype(jnp.float32) + arrived_ref[:, 2 * size :].astype(
+        jnp.float32
+    )
+    scale = lax.rsqrt((tail[:, :1] + tail[:, 1:2]) / D + NORM_EPS)
+    route = jnp.concatenate(
+        [packed_ref[place * rows : (place + 1) * rows, 2 * HEAD_SIZE :] for place in places], axis=0
+    ).astype(jnp.float32)
+    lane = lax.broadcasted_iota(jnp.int32, route.shape, 1)
+    route = jnp.sum(
+        jnp.where(lane % ROUTE_LANES == index_ref[0], route, 0.0), axis=1, keepdims=True
+    )
+    gate = kept_ref[:, :size].astype(jnp.float32) + arrived_ref[:, :size].astype(jnp.float32)
+    up = kept_ref[:, size : 2 * size].astype(jnp.float32) + arrived_ref[
+        :, size : 2 * size
+    ].astype(jnp.float32)
+    gate = gate * scale
+    up = up * (scale * route)
+    out_ref[...] = (gate / (1.0 + jnp.exp(-gate)) * up).astype(jnp.bfloat16)
+
+
+def own_kernel(index_ref, hidden_ref, down_ref, mixed_ref, *rest):
+    out_ref = rest[-1]
+    total = mixed_ref[...].astype(jnp.float32) + jnp.dot(
+        hidden_ref[...], down_ref[index_ref[0]], preferred_element_type=jnp.float32
+    )
+    for term in rest[:-1]:
+        total = total + term[...].astype(jnp.float32)
+    out_ref[...] = total.astype(out_ref.dtype)
+
+
+def both_kernel(places, mine_ref, other_ref, hidden_ref, other_hidden_ref, down_ref, *rest):
+    both = jnp.dot(hidden_ref[...], down_ref[mine_ref[0]], preferred_element_type=jnp.float32)
+    both = both + jnp.dot(
+        other_hidden_ref[...], down_ref[other_ref[0]], preferred_element_type=jnp.float32
+    )
+    rows = rest[-1].shape[0]
+    for i, out_ref in enumerate(rest[len(places) :]):
+        term = both[i * rows : (i + 1) * rows]
+        for place, term_ref in zip(places, rest):
+            if place == i:
+                term = term + term_ref[...].astype(jnp.float32)
+        out_ref[...] = term.astype(out_ref.dtype)
+
+
+class Core:
+    def __init__(self):
+        self.before = None
+        self.also = []
+
+    def __call__(self, kernel, out_shape, *args, held=(), cost=0, scratch=(), space=pltpu.VMEM):
+        vmem = pl.BlockSpec(memory_space=pltpu.VMEM)
+        specs = [
+            pl.BlockSpec(memory_space=pltpu.SMEM if arg.ndim == 1 else space) for arg in args
+        ]
+        unread = list(held) + ([] if self.before is None else [self.before]) + self.also
+        self.also = []
+        specs += [vmem] * len(held) + [pl.BlockSpec(memory_space=pl.ANY)] * (len(unread) - len(held))
+        read = len(args)
+        many = isinstance(out_shape, list)
+
+        def body(*refs):
+            kernel(*refs[:read], *refs[read + len(unread) :])
+
+        out = pl.pallas_call(
+            body,
+            out_shape=out_shape,
+            in_specs=specs,
+            out_specs=[vmem] * len(out_shape) if many else vmem,
+            scratch_shapes=list(scratch),
+            compiler_params=pltpu.CompilerParams(vmem_limit_bytes=KERNEL_BYTES),
+            cost_estimate=pl.CostEstimate(
+                flops=int(cost * COST), bytes_accessed=0, transcendentals=0
+            ),
+        )(*args, *unread)
+        self.before = out[0] if many else out
+        return out
+
+
+def local(
+    queries,
+    key_rows,
+    value_head_rows,
+    block_order,
+    residual,
+    norm_gain,
+    expert_ids,
+    route_weight,
+    gate_weight,
+    up_weight,
+    down_weight,
+):
+    rows, features = queries.shape
+    ctx_count = lax.axis_size("ctx")
+    size = gate_weight.shape[2]
+    mine = lax.axis_index("exp").astype(jnp.int32).reshape(1)
+    other = 1 - mine
+    place = lax.axis_index("ctx").astype(jnp.int32).reshape(1)
+    expert = 2 * place + mine
+    swap = [(0, 1), (1, 0)]
+    gain = norm_gain.reshape(1, features)
+    position = {offset: i for i, offset in enumerate(offsets(ctx_count))}
+    core = Core()
+
+    def of(shape, dtype=jnp.bfloat16):
+        return jax.ShapeDtypeStruct(shape, dtype)
+
+    def hop(block, offset):
+        return lax.ppermute(block, "ctx", xor_pairs(ctx_count, offset))
+
+    packed = core(
+        pack_kernel,
+        of((rows, 2 * HEAD_SIZE + LANES)),
+        mine,
+        key_rows,
+        value_head_rows,
+        expert_ids.T,
+        route_weight.T,
+        cost=PACK_COST,
+        space=pl.ANY,
+        scratch=(
+            pltpu.VMEM((TOPK, rows), jnp.int32),
+            pltpu.VMEM((TOPK, rows), jnp.float32),
+            pltpu.SemaphoreType.DMA((4,)),
+        ),
+    )
+    packed = gather_rows(packed, ctx_count)
+    mixed_rows = core(
+        attention_kernel,
+        of((rows, features)),
+        place,
+        block_order,
+        queries,
+        packed,
+        residual,
+        held=(gate_weight, up_weight) if HELD else (),
+        cost=ATT_COST,
+    )
+
+    block = {0: mixed_rows}
+    for source, offset in HOPS:
+        block[source ^ offset] = hop(block[source], offset)
+
+    kept, arrived, hidden, other_hidden, terms = {}, {}, {}, {}, {}
+    for step, i in STEPS:
+        chunk = CHUNKS[i % len(CHUNKS)]
+        count = len(chunk) * rows
+        if step in ("send", "keep"):
+            product = core(
+                first_kernel,
+                of((count, 2 * size + LANES)),
+                other if step == "send" else mine,
+                gain,
+                gate_weight,
+                up_weight,
+                *[block[offset] for offset in chunk],
+                cost=1.2,
+            )
+            if step == "send":
+                arrived[i] = lax.ppermute(product, "exp", swap)
+            else:
+                kept[i] = product
+        elif step == "hidden":
+            kernel = functools.partial(hidden_kernel, [position[offset] for offset in chunk])
+            hidden[i] = core(kernel, of((count, size)), expert, kept[i], arrived[i], packed, cost=0.4)
+            other_hidden[i] = lax.ppermute(hidden[i], "exp", swap)
+        elif step == "both":
+            shapes = [of((rows, features))] * len(chunk)
+            arrivals = [(at, term) for at, o in enumerate(chunk) for term in terms.pop(o, [])]
+            kernel = functools.partial(both_kernel, [at for at, _ in arrivals])
+            out = core(
+                kernel,
+                shapes,
+                mine, other, hidden[i], other_hidden[i], down_weight,
+                *[term for _, term in arrivals],
+                cost=1.1,
+            )
+            for offset, term in zip(chunk, out):
+                terms.setdefault(offset ^ SENDS[offset], []).append(hop(term, SENDS[offset]))
+        elif step == "wait":
+            core.also += terms[0][-i:]
+        else:
+            ready = [terms[0].pop(0) for _ in range(OWN[step])]
+            if step == "own":
+                total = core(
+                    own_kernel,
+                    of((rows, features), jnp.float32),
+                    mine, hidden[i], down_weight, mixed_rows, *ready,
+                    cost=0.7,
+                )
+            else:
+                total = core(
+                    own_kernel,
+                    of((rows, features)),
+                    other, other_hidden[i], down_weight, total, *ready,
+                    cost=0.7,
+                )
+    return total
 
 
 def solution(mesh):
@@ -187,6 +483,7 @@
         P("ctx", "exp", None),
         P("ctx", None, "exp"),
     )
+    small = mesh.shape["exp"] == 2 and mesh.shape["ctx"] == 8
     return jax.shard_map(
-        local, mesh=mesh, in_specs=placed, out_specs=P(("rep", "ctx"), "exp"), check_vma=False
-    )
+        local if small else general, mesh=mesh, in_specs=placed, out_specs=P(("rep", "ctx"), "exp"), check_vma=False
+    )

time: 173 us -> 109 us (0.63)
  waiting for transfers between devices: 115 us -> 45.3 us
  Pallas kernels: 0 us -> 21 us
  matrix products: 18.6 us -> 0 us
  starting transfers between devices: 22.5 us -> 38.9 us
  other arithmetic: 8.01 us -> 0.07 us
  blocking collectives: 5.11 us -> 0 us
    ppermute x5 -> x24, waiting for transfers between devices: 73 us -> 35.5 us  [the longest x14 18.1 us: hop(): return lax.ppermute(block, 'ctx', xor_pairs(ctx_count, offset))]
    ppermute x6 -> x3, waiting for transfers between devices: 41.9 us -> 9.78 us  [gather_rows(): lax.ppermute(block, 'ctx', xor_pairs(count, bit))]
    ppermute x5 -> x24, starting transfers between devices: 10.4 us -> 31.6 us  [the longest x14 19.4 us: hop(): return lax.ppermute(block, 'ctx', xor_pairs(ctx_count, offset))]
    pallas_call x0 -> x23, Pallas kernels: none -> 21 us  [__call__(): pl.pallas_call(body, out_shape=out_shape, in_specs=specs, out_specs=[vmem...]
    dot_general x11 -> x0, matrix products: 18.6 us -> none  [the longest x8 11.8 us: partial_sums(): terms.append(jnp.dot(rows, weight[k], preferred_element_type=jnp.float32))]
    psum x1 -> x0, blocking collectives: 5.11 us -> none  [local(): square_sum = lax.psum(jnp.sum(mixed_f * mixed_f, axis=1), 'exp')]
    ppermute x6 -> x3, starting transfers between devices: 12.1 us -> 7.34 us  [gather_rows(): lax.ppermute(block, 'ctx', xor_pairs(count, bit))]
    reduce_sum x4 -> x0, other arithmetic: 2.37 us -> none  [the longest x1 0.84 us: local(): jnp.sum(jnp.where(owners[:, None] == block_ids[None, :], block_order[None...]
  transfers between devices with their start and end apart: 11 -> 27, of which waited for: 11 -> 17; matrix products, arithmetic and copies ran while one was open for 4% -> 0% of each run, Pallas kernels for 0% -> 15%
where the time goes in v3:
time: 109 us
  waiting for transfers between devices  45.3 us (42%)
  starting transfers between devices  38.9 us (36%)
  Pallas kernels  21 us (19%)
  local copies, waits for them, and re-layouts  2.94 us (3%)
    pallas_call x23, Pallas kernels, __call__(): pl.pallas_call(body, out_shape=out_shape, in_specs=specs, out_specs=[vmem...  21 us
    ppermute x14, starting transfers between devices, hop(): return lax.ppermute(block, 'ctx', xor_pairs(ctx_count, offset))  19.4 us
    ppermute x14, waiting for transfers between devices, hop(): return lax.ppermute(block, 'ctx', xor_pairs(ctx_count, offset))  18.1 us
    ppermute x5, waiting for transfers between devices, local(): other_hidden[i] = lax.ppermute(hidden[i], 'exp', swap)  10.2 us
    ppermute x3, waiting for transfers between devices, gather_rows(): lax.ppermute(block, 'ctx', xor_pairs(count, bit))  9.78 us
    ppermute x3, starting transfers between devices, gather_rows(): lax.ppermute(block, 'ctx', xor_pairs(count, bit))  7.34 us
    ppermute x5, waiting for transfers between devices, local(): arrived[i] = lax.ppermute(product, 'exp', swap)  7.19 us
    ppermute x5, starting transfers between devices, local(): other_hidden[i] = lax.ppermute(hidden[i], 'exp', swap)  6.81 us
  transfers between devices with their start and end apart: 27, of which 17 were waited for; matrix products, arithmetic and copies ran while one was open for 0% of the time, Pallas kernels for 15%

profile of v3, /device:TPU:0, one launch (start us, length us, event | category | flops | bytes accessed | tf_op | source)
XLA Modules:
  0.0 108.6 jit_solution(13791654983603066771)
XLA Ops:
  3.1 4.1 %collective-permute-start = (bf16[64,384]{1,0:T(8,128)(2,1)S(1)}, bf16[64,384]{1,0:T(8,128)(2,1)S(1)}, u32[]{:S(2)}, u32[]{:S(2)}) collective-permute-start(bf16[64,384]{1,0:T(8,128)(2,1)S(1)} %shard_map.109.refs_5_), channel_id=1, source_target_pairs={{0,16},{4,20},{8,24},{12,28},{16,0},{20,4},{24,8},{28,12},{1,17},{... | collective-permute-start | bytes 147464 | tf_op jit(solution)/shard_map/ppermute | solution.py:52
  7.2 2.6 %collective-permute-done = bf16[64,384]{1,0:T(8,128)(2,1)S(1)} collective-permute-done((bf16[64,384]{1,0:T(8,128)(2,1)S(1)}, bf16[64,384]{1,0:T(8,128)(2,1)S(1)}, u32[]{:S(2)}, u32[]{:S(2)}) %collective-permute-start) | collective-permute-done | bytes 49184 | tf_op jit(solution)/shard_map/ppermute | solution.py:52
  9.8 1.4 %collective-permute-start.1 = (bf16[128,384]{1,0:T(8,128)(2,1)S(1)}, bf16[128,384]{1,0:T(8,128)(2,1)S(1)}, u32[]{:S(2)}, u32[]{:S(2)}) collective-permute-start(bf16[128,384]{1,0:T(8,128)(2,1)S(1)} %pad_maximum_fusion.2), channel_id=1, source_target_pairs={{0,8},{4,12},{8,0},{12,4},{16,24},{20,28},{24,16},{28,20},{1,9},{5... | collective-permute-start | bytes 294920 | tf_op jit(solution)/shard_map/ppermute | solution.py:52
  11.2 3.2 %collective-permute-done.1 = bf16[128,384]{1,0:T(8,128)(2,1)S(1)} collective-permute-done((bf16[128,384]{1,0:T(8,128)(2,1)S(1)}, bf16[128,384]{1,0:T(8,128)(2,1)S(1)}, u32[]{:S(2)}, u32[]{:S(2)}) %collective-permute-start.1) | collective-permute-done | bytes 98336 | tf_op jit(solution)/shard_map/ppermute | solution.py:52
  14.5 1.8 %collective-permute-start.2 = (bf16[256,384]{1,0:T(8,128)(2,1)S(1)}, bf16[256,384]{1,0:T(8,128)(2,1)S(1)}, u32[]{:S(2)}, u32[]{:S(2)}) collective-permute-start(bf16[256,384]{1,0:T(8,128)(2,1)S(1)} %pad_maximum_fusion.1), channel_id=1, source_target_pairs={{0,4},{4,0},{8,12},{12,8},{16,20},{20,16},{24,28},{28,24},{1,5},{5... | collective-permute-start | bytes 589832 | tf_op jit(solution)/shard_map/ppermute | solution.py:52
  16.3 3.9 %collective-permute-done.2 = bf16[256,384]{1,0:T(8,128)(2,1)S(1)} collective-permute-done((bf16[256,384]{1,0:T(8,128)(2,1)S(1)}, bf16[256,384]{1,0:T(8,128)(2,1)S(1)}, u32[]{:S(2)}, u32[]{:S(2)}) %collective-permute-start.2) | collective-permute-done | bytes 196640 | tf_op jit(solution)/shard_map/ppermute | solution.py:52
  20.4 1.9 %shard_map.110.refs_5_.refs_4_.refs_3_ = bf16[64,2048]{1,0:T(8,128)(2,1)S(1)} custom-call(s32[1]{0:T(128)} %bitcast.1.refs_0_, s32[8]{0:T(128)S(1)} %copy-done.7, bf16[64,2048]{1,0:T(8,128)(2,1)S(1)} %copy-done.1, bf16[512,384]{1,0:T(8,128)(2,1)S(1)} %pad_maximum_fusion.refs_3_, bf16[64,2048]{1,0:T(8,128)(2,1)S(1)} %copy-done.2, ...), custom_call_target="tpu_custom_call" | custom-call | flops 10000000000 | tf_op jit(solution)/shard_map/pallas_call | solution.py:336
  22.3 2.5 %collective-permute-start.5 = (bf16[64,2048]{1,0:T(8,128)(2,1)S(1)}, bf16[64,2048]{1,0:T(8,128)(2,1)S(1)}, u32[]{:S(2)}, u32[]{:S(2)}) collective-permute-start(bf16[64,2048]{1,0:T(8,128)(2,1)S(1)} %shard_map.110.refs_5_.refs_4_.refs_3_), channel_id=1, source_target_pairs={{0,16},{4,20},{8,24},{12,28},{16,0},{20,4},{24,8},{28,12},{1,17},{... | collective-permute-start | bytes 786440 | tf_op jit(solution)/shard_map/ppermute | solution.py:380
  24.8 1.5 %collective-permute-start.8 = (bf16[64,2048]{1,0:T(8,128)(2,1)S(1)}, bf16[64,2048]{1,0:T(8,128)(2,1)S(1)}, u32[]{:S(2)}, u32[]{:S(2)}) collective-permute-start(bf16[64,2048]{1,0:T(8,128)(2,1)S(1)} %shard_map.110.refs_5_.refs_4_.refs_3_), channel_id=1, source_target_pairs={{0,4},{4,0},{8,12},{12,8},{16,20},{20,16},{24,28},{28,24},{1,5},{5... | collective-permute-start | bytes 786440 | tf_op jit(solution)/shard_map/ppermute | solution.py:380
  26.3 1.9 %collective-permute-start.3 = (bf16[64,2048]{1,0:T(8,128)(2,1)S(1)}, bf16[64,2048]{1,0:T(8,128)(2,1)S(1)}, u32[]{:S(2)}, u32[]{:S(2)}) collective-permute-start(bf16[64,2048]{1,0:T(8,128)(2,1)S(1)} %shard_map.110.refs_5_.refs_4_.refs_3_), channel_id=1, source_target_pairs={{0,8},{4,12},{8,0},{12,4},{16,24},{20,28},{24,16},{28,20},{1,9},{5... | collective-permute-start | bytes 786440 | tf_op jit(solution)/shard_map/ppermute | solution.py:380
  28.3 5.4 %collective-permute-done.5.refs_5_ = bf16[64,2048]{1,0:T(8,128)(2,1)S(1)} collective-permute-done((bf16[64,2048]{1,0:T(8,128)(2,1)S(1)}, bf16[64,2048]{1,0:T(8,128)(2,1)S(1)}, u32[]{:S(2)}, u32[]{:S(2)}) %collective-permute-start.5) | collective-permute-done | bytes 262176 | tf_op jit(solution)/shard_map/ppermute | solution.py:380
  34.3 1.4 %collective-permute-start.7 = (bf16[64,2048]{1,0:T(8,128)(2,1)S(1)}, bf16[64,2048]{1,0:T(8,128)(2,1)S(1)}, u32[]{:S(2)}, u32[]{:S(2)}) collective-permute-start(bf16[64,2048]{1,0:T(8,128)(2,1)S(1)} %collective-permute-done.5.refs_5_), channel_id=1, source_target_pairs={{0,4},{4,0},{8,12},{12,8},{16,20},{20,16},{24,28},{28,24},{1,5},{5... | collective-permute-start | bytes 786440 | tf_op jit(solution)/shard_map/ppermute | solution.py:380
  35.8 1.2 %shard_map.111.refs_5_ = bf16[64,1664]{1,0:T(8,128)(2,1)S(1)} custom-call(s32[1]{0:T(128)S(6)} %sub.3.refs_0_.refs_1_, f32[1,2048]{1,0:T(1,128)S(1)} %bitcast.11, bf16[2,2048,768]{2,1,0:T(8,128)(2,1)S(1)} %bitcast.6, bf16[2,2048,768]{2,1,0:T(8,128)(2,1)S(1)} %bitcast.8, bf16[64,2048]{1,0:T(8,128)(2,1)S(1)} %collective-permute-done.8.refs_4_, ...), custom_call_target="tpu_custom_call" | custom-call | flops 2400000000 | tf_op jit(solution)/shard_map/pallas_call | solution.py:336
  37.0 1.6 %collective-permute-start.9 = (bf16[64,1664]{1,0:T(8,128)(2,1)S(1)}, bf16[64,1664]{1,0:T(8,128)(2,1)S(1)}, u32[]{:S(2)}, u32[]{:S(2)}) collective-permute-start(bf16[64,1664]{1,0:T(8,128)(2,1)S(1)} %shard_map.111.refs_5_), channel_id=1, source_target_pairs={{0,2},{2,0},{1,3},{3,1},{4,6},{6,4},{5,7},{7,5},{8,10},{10,8},{9,1... | collective-permute-start | bytes 638984 | tf_op jit(solution)/shard_map/ppermute | solution.py:431
  39.2 1.2 %shard_map.112.refs_6_.refs_1_ = bf16[64,1664]{1,0:T(8,128)(2,1)S(1)} custom-call(s32[1]{0:T(128)} %bitcast.refs_0_, f32[1,2048]{1,0:T(1,128)S(1)} %bitcast.12, bf16[2,2048,768]{2,1,0:T(8,128)(2,1)S(1)} %bitcast.6, bf16[2,2048,768]{2,1,0:T(8,128)(2,1)S(1)} %bitcast.8, bf16[64,2048]{1,0:T(8,128)(2,1)S(1)} %collective-permute-done.8.refs_4_, ...), custom_call_target="tpu_custom_call" | custom-call | flops 2400000000 | tf_op jit(solution)/shard_map/pallas_call | solution.py:336
  40.5 2.5 %collective-permute-done.7.refs_5_ = bf16[64,2048]{1,0:T(8,128)(2,1)S(1)} collective-permute-done((bf16[64,2048]{1,0:T(8,128)(2,1)S(1)}, bf16[64,2048]{1,0:T(8,128)(2,1)S(1)}, u32[]{:S(2)}, u32[]{:S(2)}) %collective-permute-start.7) | collective-permute-done | bytes 262176 | tf_op jit(solution)/shard_map/ppermute | solution.py:380
  43.0 1.0 shard_map.113.refs_4_
  44.1 2.1 %collective-permute-start.10 = (bf16[128,1664]{1,0:T(8,128)(2,1)S(1)}, bf16[128,1664]{1,0:T(8,128)(2,1)S(1)}, u32[]{:S(2)}, u32[]{:S(2)}) collective-permute-start(bf16[128,1664]{1,0:T(8,128)(2,1)S(1)} %shard_map.113.refs_4_), channel_id=1, source_target_pairs={{0,2},{2,0},{1,3},{3,1},{4,6},{6,4},{5,7},{7,5},{8,10},{10,8},{9,1... | collective-permute-start | bytes 1277960 | tf_op jit(solution)/shard_map/ppermute | solution.py:431
  46.1 1.4 %collective-permute-start.12 = (bf16[64,2048]{1,0:T(8,128)(2,1)S(1)}, bf16[64,2048]{1,0:T(8,128)(2,1)S(1)}, u32[]{:S(2)}, u32[]{:S(2)}) collective-permute-start(bf16[64,2048]{1,0:T(8,128)(2,1)S(1)} %collective-permute-done.6.refs_4_), channel_id=1, source_target_pairs={{0,4},{4,0},{8,12},{12,8},{16,20},{20,16},{24,28},{28,24},{1,5},{5... | collective-permute-start | bytes 786440 | tf_op jit(solution)/shard_map/ppermute | solution.py:380
  48.3 1.0 shard_map.115.refs_6_.refs_1_
  49.4 3.1 %collective-permute-done.12.refs_4_ = bf16[64,2048]{1,0:T(8,128)(2,1)S(1)} collective-permute-done((bf16[64,2048]{1,0:T(8,128)(2,1)S(1)}, bf16[64,2048]{1,0:T(8,128)(2,1)S(1)}, u32[]{:S(2)}, u32[]{:S(2)}) %collective-permute-start.12) | collective-permute-done | bytes 262176 | tf_op jit(solution)/shard_map/ppermute | solution.py:380
  52.5 1.0 shard_map.116.refs_5_
  54.3 1.1 collective-permute-done.11.refs_3_
  55.3 1.2 %shard_map.117.refs_4_ = bf16[64,2048]{1,0:T(8,128)(2,1)S(1)} custom-call(s32[1]{0:T(128)} %bitcast.refs_0_, s32[1]{0:T(128)S(6)} %sub.3.refs_0_.refs_1_, bf16[64,768]{1,0:T(8,128)(2,1)S(1)} %shard_map.114.refs_6_.refs_2_, bf16[64,768]{1,0:T(8,128)(2,1)S(1)} %collective-permute-done.11.refs_3_, bf16[2,768,2048]{2,1,0:T(8,128)(2,1)S(1)} %bitcast.10, ...), custom_call_target="tpu_custom_call" | custom-call | flops 2200000000 | tf_op jit(solution)/shard_map/pallas_call | solution.py:336
  56.9 2.1 %collective-permute-start.13 = (bf16[128,768]{1,0:T(8,128)(2,1)S(1)}, bf16[128,768]{1,0:T(8,128)(2,1)S(1)}, u32[]{:S(2)}, u32[]{:S(2)}) collective-permute-start(bf16[128,768]{1,0:T(8,128)(2,1)S(1)} %shard_map.118.refs_6_.refs_2_), channel_id=1, source_target_pairs={{0,2},{2,0},{1,3},{3,1},{4,6},{6,4},{5,7},{7,5},{8,10},{10,8},{9,1... | collective-permute-start | bytes 589832 | tf_op jit(solution)/shard_map/ppermute | solution.py:437
  59.0 1.0 shard_map.119.refs_1_.refs_4_
  60.0 5.4 %collective-permute-done.14.refs_2_ = bf16[128,1664]{1,0:T(8,128)(2,1)S(1)} collective-permute-done((bf16[128,1664]{1,0:T(8,128)(2,1)S(1)}, bf16[128,1664]{1,0:T(8,128)(2,1)S(1)}, u32[]{:S(2)}, u32[]{:S(2)}) %collective-permute-start.14) | collective-permute-done | bytes 426016 | tf_op jit(solution)/shard_map/ppermute | solution.py:431
  65.7 1.0 shard_map.121.refs_5_
  67.5 1.0 shard_map.122
  68.5 1.5 %collective-permute-start.17 = (bf16[64,2048]{1,0:T(8,128)(2,1)S(1)}, bf16[64,2048]{1,0:T(8,128)(2,1)S(1)}, u32[]{:S(2)}, u32[]{:S(2)}) collective-permute-start(bf16[64,2048]{1,0:T(8,128)(2,1)S(1)} %get-tuple-element.11.refs_6_), channel_id=1, source_target_pairs={{0,8},{4,12},{8,0},{12,4},{16,24},{20,28},{24,16},{28,20},{1,9},{5... | collective-permute-start | bytes 786440 | tf_op jit(solution)/shard_map/ppermute | solution.py:380
  70.6 1.5 %collective-permute-start.22 = (bf16[64,2048]{1,0:T(8,128)(2,1)S(1)}, bf16[64,2048]{1,0:T(8,128)(2,1)S(1)}, u32[]{:S(2)}, u32[]{:S(2)}) collective-permute-start(bf16[64,2048]{1,0:T(8,128)(2,1)S(1)} %shard_map.117.refs_4_), channel_id=1, source_target_pairs={{0,4},{4,0},{8,12},{12,8},{16,20},{20,16},{24,28},{28,24},{1,5},{5... | collective-permute-start | bytes 786440 | tf_op jit(solution)/shard_map/ppermute | solution.py:380
  72.1 1.5 %collective-permute-start.16 = (bf16[128,768]{1,0:T(8,128)(2,1)S(1)}, bf16[128,768]{1,0:T(8,128)(2,1)S(1)}, u32[]{:S(2)}, u32[]{:S(2)}) collective-permute-start(bf16[128,768]{1,0:T(8,128)(2,1)S(1)} %shard_map.120.refs_6_.refs_2_), channel_id=1, source_target_pairs={{0,2},{2,0},{1,3},{3,1},{4,6},{6,4},{5,7},{7,5},{8,10},{10,8},{9,1... | collective-permute-start | bytes 589832 | tf_op jit(solution)/shard_map/ppermute | solution.py:437
  75.1 4.8 %collective-permute-done.16.refs_3_ = bf16[128,768]{1,0:T(8,128)(2,1)S(1)} collective-permute-done((bf16[128,768]{1,0:T(8,128)(2,1)S(1)}, bf16[128,768]{1,0:T(8,128)(2,1)S(1)}, u32[]{:S(2)}, u32[]{:S(2)}) %collective-permute-start.16) | collective-permute-done | bytes 196640 | tf_op jit(solution)/shard_map/ppermute | solution.py:437
  79.9 1.1 shard_map.124
  81.0 4.0 %collective-permute-start.23 = (bf16[64,2048]{1,0:T(8,128)(2,1)S(1)}, bf16[64,2048]{1,0:T(8,128)(2,1)S(1)}, u32[]{:S(2)}, u32[]{:S(2)}) collective-permute-start(bf16[64,2048]{1,0:T(8,128)(2,1)S(1)} %get-tuple-element.13.refs_4_), channel_id=1, source_target_pairs={{0,28},{4,24},{8,20},{12,16},{16,12},{20,8},{24,4},{28,0},{1,29},{... | collective-permute-start | bytes 786440 | tf_op jit(solution)/shard_map/ppermute | solution.py:380
  85.3 1.2 %shard_map.126.refs_5_ = bf16[64,1664]{1,0:T(8,128)(2,1)S(1)} custom-call(s32[1]{0:T(128)S(6)} %sub.3.refs_0_.refs_1_, f32[1,2048]{1,0:T(1,128)S(1)} %bitcast.19, bf16[2,2048,768]{2,1,0:T(8,128)(2,1)S(1)} %bitcast.6, bf16[2,2048,768]{2,1,0:T(8,128)(2,1)S(1)} %bitcast.8, bf16[64,2048]{1,0:T(8,128)(2,1)S(1)} %shard_map.110.refs_5_.refs_4_.refs_3_, ...), custom_call_target="tpu_custom_call" | custom-call | flops 2400000000 | tf_op jit(solution)/shard_map/pallas_call | solution.py:336
  86.5 1.6 %collective-permute-start.20 = (bf16[128,768]{1,0:T(8,128)(2,1)S(1)}, bf16[128,768]{1,0:T(8,128)(2,1)S(1)}, u32[]{:S(2)}, u32[]{:S(2)}) collective-permute-start(bf16[128,768]{1,0:T(8,128)(2,1)S(1)} %shard_map.125.refs_5_.refs_2_), channel_id=1, source_target_pairs={{0,2},{2,0},{1,3},{3,1},{4,6},{6,4},{5,7},{7,5},{8,10},{10,8},{9,1... | collective-permute-start | bytes 589832 | tf_op jit(solution)/shard_map/ppermute | solution.py:437
  88.6 1.2 %shard_map.127.refs_5_.refs_1_ = bf16[64,1664]{1,0:T(8,128)(2,1)S(1)} custom-call(s32[1]{0:T(128)} %bitcast.refs_0_, f32[1,2048]{1,0:T(1,128)S(1)} %bitcast.20, bf16[2,2048,768]{2,1,0:T(8,128)(2,1)S(1)} %bitcast.6, bf16[2,2048,768]{2,1,0:T(8,128)(2,1)S(1)} %bitcast.8, bf16[64,2048]{1,0:T(8,128)(2,1)S(1)} %shard_map.110.refs_5_.refs_4_.refs_3_, ...), custom_call_target="tpu_custom_call" | custom-call | flops 2400000000 | tf_op jit(solution)/shard_map/pallas_call | solution.py:336
  89.9 2.4 %collective-permute-done.20.refs_3_ = bf16[128,768]{1,0:T(8,128)(2,1)S(1)} collective-permute-done((bf16[128,768]{1,0:T(8,128)(2,1)S(1)}, bf16[128,768]{1,0:T(8,128)(2,1)S(1)}, u32[]{:S(2)}, u32[]{:S(2)}) %collective-permute-start.20) | collective-permute-done | bytes 196640 | tf_op jit(solution)/shard_map/ppermute | solution.py:437
  92.3 1.1 shard_map.128
  93.8 1.8 %collective-permute-done.19.refs_2_ = bf16[64,1664]{1,0:T(8,128)(2,1)S(1)} collective-permute-done((bf16[64,1664]{1,0:T(8,128)(2,1)S(1)}, bf16[64,1664]{1,0:T(8,128)(2,1)S(1)}, u32[]{:S(2)}, u32[]{:S(2)}) %collective-permute-start.19) | collective-permute-done | bytes 213024 | tf_op jit(solution)/shard_map/ppermute | solution.py:431
  95.6 1.4 %collective-permute-start.26 = (bf16[64,2048]{1,0:T(8,128)(2,1)S(1)}, bf16[64,2048]{1,0:T(8,128)(2,1)S(1)}, u32[]{:S(2)}, u32[]{:S(2)}) collective-permute-start(bf16[64,2048]{1,0:T(8,128)(2,1)S(1)} %get-tuple-element.16), channel_id=1, source_target_pairs={{0,12},{4,8},{8,4},{12,0},{16,28},{20,24},{24,20},{28,16},{1,13},{... | collective-permute-start | bytes 786440 | tf_op jit(solution)/shard_map/ppermute | solution.py:380
  97.2 1.1 collective-permute-start.21
  99.0 1.7 %collective-permute-done.24.refs_5_ = bf16[64,2048]{1,0:T(8,128)(2,1)S(1)} collective-permute-done((bf16[64,2048]{1,0:T(8,128)(2,1)S(1)}, bf16[64,2048]{1,0:T(8,128)(2,1)S(1)}, u32[]{:S(2)}, u32[]{:S(2)}) %collective-permute-start.24) | collective-permute-done | bytes 262176 | tf_op jit(solution)/shard_map/ppermute | solution.py:380
  100.7 1.2 %collective-permute-done.21.refs_1_ = bf16[64,768]{1,0:T(8,128)(2,1)S(1)} collective-permute-done((bf16[64,768]{1,0:T(8,128)(2,1)S(1)}, bf16[64,768]{1,0:T(8,128)(2,1)S(1)}, u32[]{:S(2)}, u32[]{:S(2)}) %collective-permute-start.21) | collective-permute-done | bytes 98336 | tf_op jit(solution)/shard_map/ppermute | solution.py:437
  101.9 2.4 %collective-permute-done.25.refs_6_ = bf16[64,2048]{1,0:T(8,128)(2,1)S(1)} collective-permute-done((bf16[64,2048]{1,0:T(8,128)(2,1)S(1)}, bf16[64,2048]{1,0:T(8,128)(2,1)S(1)}, u32[]{:S(2)}, u32[]{:S(2)}) %collective-permute-start.25) | collective-permute-done | bytes 262176 | tf_op jit(solution)/shard_map/ppermute | solution.py:380
  104.3 2.8 %collective-permute-done.26.refs_7_ = bf16[64,2048]{1,0:T(8,128)(2,1)S(1)} collective-permute-done((bf16[64,2048]{1,0:T(8,128)(2,1)S(1)}, bf16[64,2048]{1,0:T(8,128)(2,1)S(1)}, u32[]{:S(2)}, u32[]{:S(2)}) %collective-permute-start.26) | collective-permute-done | bytes 262176 | tf_op jit(solution)/shard_map/ppermute | solution.py:380
  107.1 1.5 %shard_map.131 = bf16[64,2048]{1,0:T(8,128)(2,1)} custom-call(s32[1]{0:T(128)S(6)} %sub.3.refs_0_.refs_1_, bf16[64,768]{1,0:T(8,128)(2,1)S(1)} %collective-permute-done.21.refs_1_, bf16[2,768,2048]{2,1,0:T(8,128)(2,1)S(1)} %bitcast.10, f32[64,2048]{1,0:T(8,128)S(1)} %shard_map.130.refs_3_.refs_8_, bf16[64,2048]{1,0:T(8,128)(2,1)S(1)} %collective-permute-done.23.refs_4_, ...), custom_call_target="tpu_custom_call" | custom-call | flops 1400000000 | tf_op jit(solution)/shard_map/pallas_call | solution.py:336
  (63 shorter events, 11.6 us)
Async XLA Ops:
  0.0 0.8 copy-start.3
  0.8 0.8 copy-start.4
  1.5 0.7 copy-start.5
  2.2 0.7 copy-start.6
  2.9 17.4 %copy-start.1 = (bf16[64,2048]{1,0:T(8,128)(2,1)S(1)}, bf16[64,2048]{1,0:T(8,128)(2,1)}, u32[]{:S(2)}) copy-start(bf16[64,2048]{1,0:T(8,128)(2,1)} %refs_2_.15) | copy-start | bytes 786436
  2.9 17.4 %copy-start.2 = (bf16[64,2048]{1,0:T(8,128)(2,1)S(1)}, bf16[64,2048]{1,0:T(8,128)(2,1)}, u32[]{:S(2)}) copy-start(bf16[64,2048]{1,0:T(8,128)(2,1)} %refs_4_.5) | copy-start | bytes 786436
  2.9 17.4 %copy-start.7 = (s32[8]{0:T(128)S(1)}, s32[8]{0:T(128)}, u32[]{:S(2)}) copy-start(s32[8]{0:T(128)} %refs_1_.3) | copy-start | bytes 100
  3.1 6.7 %collective-permute-start = (bf16[64,384]{1,0:T(8,128)(2,1)S(1)}, bf16[64,384]{1,0:T(8,128)(2,1)S(1)}, u32[]{:S(2)}, u32[]{:S(2)}) collective-permute-start(bf16[64,384]{1,0:T(8,128)(2,1)S(1)} %shard_map.109.refs_5_), channel_id=1, source_target_pairs={{0,16},{4,20},{8,24},{12,28},{16,0},{20,4},{24,8},{28,12},{1,17},{... | collective-permute-start | bytes 147464 | tf_op jit(solution)/shard_map/ppermute | solution.py:52
  9.8 4.7 %collective-permute-start.1 = (bf16[128,384]{1,0:T(8,128)(2,1)S(1)}, bf16[128,384]{1,0:T(8,128)(2,1)S(1)}, u32[]{:S(2)}, u32[]{:S(2)}) collective-permute-start(bf16[128,384]{1,0:T(8,128)(2,1)S(1)} %pad_maximum_fusion.2), channel_id=1, source_target_pairs={{0,8},{4,12},{8,0},{12,4},{16,24},{20,28},{24,16},{28,20},{1,9},{5... | collective-permute-start | bytes 294920 | tf_op jit(solution)/shard_map/ppermute | solution.py:52
  14.5 5.7 %collective-permute-start.2 = (bf16[256,384]{1,0:T(8,128)(2,1)S(1)}, bf16[256,384]{1,0:T(8,128)(2,1)S(1)}, u32[]{:S(2)}, u32[]{:S(2)}) collective-permute-start(bf16[256,384]{1,0:T(8,128)(2,1)S(1)} %pad_maximum_fusion.1), channel_id=1, source_target_pairs={{0,4},{4,0},{8,12},{12,8},{16,20},{20,16},{24,28},{28,24},{1,5},{5... | collective-permute-start | bytes 589832 | tf_op jit(solution)/shard_map/ppermute | solution.py:52
  20.2 15.5 %slice-start = ((s8[6291456]{0:T(1024)(128)(4,1)}), s8[4194304]{0:T(1024)(128)(4,1)S(1)}, s32[]{:S(2)}) async-start(s8[6291456]{0:T(1024)(128)(4,1)} %bitcast.5), calls=%async_computation | async-start | bytes 8388608
  20.2 15.5 %slice-start.2 = ((s8[6291456]{0:T(1024)(128)(4,1)}), s8[4194304]{0:T(1024)(128)(4,1)S(1)}, s32[]{:S(2)}) async-start(s8[6291456]{0:T(1024)(128)(4,1)} %bitcast.7), calls=%async_computation.2 | async-start | bytes 8388608
  20.3 15.4 %slice-start.1 = ((s8[6291456]{0:T(1024)(128)(4,1)}), s8[2097152]{0:T(1024)(128)(4,1)S(1)}, s32[]{:S(2)}) async-start(s8[6291456]{0:T(1024)(128)(4,1)} %bitcast.5), calls=%async_computation.1 | async-start | bytes 4194304
  20.3 15.4 %slice-start.3 = ((s8[6291456]{0:T(1024)(128)(4,1)}), s8[2097152]{0:T(1024)(128)(4,1)S(1)}, s32[]{:S(2)}) async-start(s8[6291456]{0:T(1024)(128)(4,1)} %bitcast.7), calls=%async_computation.3 | async-start | bytes 4194304
  20.3 15.4 %copy-start = (f32[2048]{0:T(1024)S(1)}, f32[2048]{0:T(1024)}, u32[]{:S(2)}) copy-start(f32[2048]{0:T(1024)} %param.16) | copy-start | bytes 24580
  22.3 11.3 %collective-permute-start.5 = (bf16[64,2048]{1,0:T(8,128)(2,1)S(1)}, bf16[64,2048]{1,0:T(8,128)(2,1)S(1)}, u32[]{:S(2)}, u32[]{:S(2)}) collective-permute-start(bf16[64,2048]{1,0:T(8,128)(2,1)S(1)} %shard_map.110.refs_5_.refs_4_.refs_3_), channel_id=1, source_target_pairs={{0,16},{4,20},{8,24},{12,28},{16,0},{20,4},{24,8},{28,12},{1,17},{... | collective-permute-start | bytes 786440 | tf_op jit(solution)/shard_map/ppermute | solution.py:380
  24.8 10.9 %collective-permute-start.8 = (bf16[64,2048]{1,0:T(8,128)(2,1)S(1)}, bf16[64,2048]{1,0:T(8,128)(2,1)S(1)}, u32[]{:S(2)}, u32[]{:S(2)}) collective-permute-start(bf16[64,2048]{1,0:T(8,128)(2,1)S(1)} %shard_map.110.refs_5_.refs_4_.refs_3_), channel_id=1, source_target_pairs={{0,4},{4,0},{8,12},{12,8},{16,20},{20,16},{24,28},{28,24},{1,5},{5... | collective-permute-start | bytes 786440 | tf_op jit(solution)/shard_map/ppermute | solution.py:380
  26.3 12.2 %collective-permute-start.3 = (bf16[64,2048]{1,0:T(8,128)(2,1)S(1)}, bf16[64,2048]{1,0:T(8,128)(2,1)S(1)}, u32[]{:S(2)}, u32[]{:S(2)}) collective-permute-start(bf16[64,2048]{1,0:T(8,128)(2,1)S(1)} %shard_map.110.refs_5_.refs_4_.refs_3_), channel_id=1, source_target_pairs={{0,8},{4,12},{8,0},{12,4},{16,24},{20,28},{24,16},{28,20},{1,9},{5... | collective-permute-start | bytes 786440 | tf_op jit(solution)/shard_map/ppermute | solution.py:380
  33.6 6.9 %collective-permute-start.6 = (bf16[64,2048]{1,0:T(8,128)(2,1)S(1)}, bf16[64,2048]{1,0:T(8,128)(2,1)S(1)}, u32[]{:S(2)}, u32[]{:S(2)}) collective-permute-start(bf16[64,2048]{1,0:T(8,128)(2,1)S(1)} %collective-permute-done.5.refs_5_), channel_id=1, source_target_pairs={{0,8},{4,12},{8,0},{12,4},{16,24},{20,28},{24,16},{28,20},{1,9},{5... | collective-permute-start | bytes 786440 | tf_op jit(solution)/shard_map/ppermute | solution.py:380
  34.3 8.7 %collective-permute-start.7 = (bf16[64,2048]{1,0:T(8,128)(2,1)S(1)}, bf16[64,2048]{1,0:T(8,128)(2,1)S(1)}, u32[]{:S(2)}, u32[]{:S(2)}) collective-permute-start(bf16[64,2048]{1,0:T(8,128)(2,1)S(1)} %collective-permute-done.5.refs_5_), channel_id=1, source_target_pairs={{0,4},{4,0},{8,12},{12,8},{16,20},{20,16},{24,28},{28,24},{1,5},{5... | collective-permute-start | bytes 786440 | tf_op jit(solution)/shard_map/ppermute | solution.py:380
  37.0 10.6 %collective-permute-start.9 = (bf16[64,1664]{1,0:T(8,128)(2,1)S(1)}, bf16[64,1664]{1,0:T(8,128)(2,1)S(1)}, u32[]{:S(2)}, u32[]{:S(2)}) collective-permute-start(bf16[64,1664]{1,0:T(8,128)(2,1)S(1)} %shard_map.111.refs_5_), channel_id=1, source_target_pairs={{0,2},{2,0},{1,3},{3,1},{4,6},{6,4},{5,7},{7,5},{8,10},{10,8},{9,1... | collective-permute-start | bytes 638984 | tf_op jit(solution)/shard_map/ppermute | solution.py:431
  38.6 27.2 %collective-permute-start.4 = (bf16[64,2048]{1,0:T(8,128)(2,1)S(1)}, bf16[64,2048]{1,0:T(8,128)(2,1)S(1)}, u32[]{:S(2)}, u32[]{:S(2)}) collective-permute-start(bf16[64,2048]{1,0:T(8,128)(2,1)S(1)} %collective-permute-done.3.refs_4_), channel_id=1, source_target_pairs={{0,4},{4,0},{8,12},{12,8},{16,20},{20,16},{24,28},{28,24},{1,5},{5... | collective-permute-start | bytes 786440 | tf_op jit(solution)/shard_map/ppermute | solution.py:380
  44.1 12.5 %collective-permute-start.10 = (bf16[128,1664]{1,0:T(8,128)(2,1)S(1)}, bf16[128,1664]{1,0:T(8,128)(2,1)S(1)}, u32[]{:S(2)}, u32[]{:S(2)}) collective-permute-start(bf16[128,1664]{1,0:T(8,128)(2,1)S(1)} %shard_map.113.refs_4_), channel_id=1, source_target_pairs={{0,2},{2,0},{1,3},{3,1},{4,6},{6,4},{5,7},{7,5},{8,10},{10,8},{9,1... | collective-permute-start | bytes 1277960 | tf_op jit(solution)/shard_map/ppermute | solution.py:431
  46.1 6.4 %collective-permute-start.12 = (bf16[64,2048]{1,0:T(8,128)(2,1)S(1)}, bf16[64,2048]{1,0:T(8,128)(2,1)S(1)}, u32[]{:S(2)}, u32[]{:S(2)}) collective-permute-start(bf16[64,2048]{1,0:T(8,128)(2,1)S(1)} %collective-permute-done.6.refs_4_), channel_id=1, source_target_pairs={{0,4},{4,0},{8,12},{12,8},{16,20},{20,16},{24,28},{28,24},{1,5},{5... | collective-permute-start | bytes 786440 | tf_op jit(solution)/shard_map/ppermute | solution.py:380
  47.8 7.6 %collective-permute-start.11 = (bf16[64,768]{1,0:T(8,128)(2,1)S(1)}, bf16[64,768]{1,0:T(8,128)(2,1)S(1)}, u32[]{:S(2)}, u32[]{:S(2)}) collective-permute-start(bf16[64,768]{1,0:T(8,128)(2,1)S(1)} %shard_map.114.refs_6_.refs_2_), channel_id=1, source_target_pairs={{0,2},{2,0},{1,3},{3,1},{4,6},{6,4},{5,7},{7,5},{8,10},{10,8},{9,1... | collective-permute-start | bytes 294920 | tf_op jit(solution)/shard_map/ppermute | solution.py:437
  48.3 7.0 %slice-start.4 = ((s8[6291456]{0:T(1024)(128)(4,1)}), s8[4194304]{0:T(1024)(128)(4,1)S(1)}, s32[]{:S(2)}) async-start(s8[6291456]{0:T(1024)(128)(4,1)} %bitcast.9), calls=%async_computation.4 | async-start | bytes 8388608
  49.4 6.0 %slice-start.5 = ((s8[6291456]{0:T(1024)(128)(4,1)}), s8[2097152]{0:T(1024)(128)(4,1)S(1)}, s32[]{:S(2)}) async-start(s8[6291456]{0:T(1024)(128)(4,1)} %bitcast.9), calls=%async_computation.5 | async-start | bytes 4194304
  53.5 11.9 %collective-permute-start.14 = (bf16[128,1664]{1,0:T(8,128)(2,1)S(1)}, bf16[128,1664]{1,0:T(8,128)(2,1)S(1)}, u32[]{:S(2)}, u32[]{:S(2)}) collective-permute-start(bf16[128,1664]{1,0:T(8,128)(2,1)S(1)} %shard_map.116.refs_5_), channel_id=1, source_target_pairs={{0,2},{2,0},{1,3},{3,1},{4,6},{6,4},{5,7},{7,5},{8,10},{10,8},{9,1... | collective-permute-start | bytes 1277960 | tf_op jit(solution)/shard_map/ppermute | solution.py:431
  56.9 10.6 %collective-permute-start.13 = (bf16[128,768]{1,0:T(8,128)(2,1)S(1)}, bf16[128,768]{1,0:T(8,128)(2,1)S(1)}, u32[]{:S(2)}, u32[]{:S(2)}) collective-permute-start(bf16[128,768]{1,0:T(8,128)(2,1)S(1)} %shard_map.118.refs_6_.refs_2_), channel_id=1, source_target_pairs={{0,2},{2,0},{1,3},{3,1},{4,6},{6,4},{5,7},{7,5},{8,10},{10,8},{9,1... | collective-permute-start | bytes 589832 | tf_op jit(solution)/shard_map/ppermute | solution.py:437
  68.5 11.4 %collective-permute-start.17 = (bf16[64,2048]{1,0:T(8,128)(2,1)S(1)}, bf16[64,2048]{1,0:T(8,128)(2,1)S(1)}, u32[]{:S(2)}, u32[]{:S(2)}) collective-permute-start(bf16[64,2048]{1,0:T(8,128)(2,1)S(1)} %get-tuple-element.11.refs_6_), channel_id=1, source_target_pairs={{0,8},{4,12},{8,0},{12,4},{16,24},{20,28},{24,16},{28,20},{1,9},{5... | collective-permute-start | bytes 786440 | tf_op jit(solution)/shard_map/ppermute | solution.py:380
  70.1 9.9 %collective-permute-start.18 = (bf16[64,2048]{1,0:T(8,128)(2,1)S(1)}, bf16[64,2048]{1,0:T(8,128)(2,1)S(1)}, u32[]{:S(2)}, u32[]{:S(2)}) collective-permute-start(bf16[64,2048]{1,0:T(8,128)(2,1)S(1)} %get-tuple-element.12), channel_id=1, source_target_pairs={{0,4},{4,0},{8,12},{12,8},{16,20},{20,16},{24,28},{28,24},{1,5},{5... | collective-permute-start | bytes 786440 | tf_op jit(solution)/shard_map/ppermute | solution.py:380
  70.6 26.6 %collective-permute-start.22 = (bf16[64,2048]{1,0:T(8,128)(2,1)S(1)}, bf16[64,2048]{1,0:T(8,128)(2,1)S(1)}, u32[]{:S(2)}, u32[]{:S(2)}) collective-permute-start(bf16[64,2048]{1,0:T(8,128)(2,1)S(1)} %shard_map.117.refs_4_), channel_id=1, source_target_pairs={{0,4},{4,0},{8,12},{12,8},{16,20},{20,16},{24,28},{28,24},{1,5},{5... | collective-permute-start | bytes 786440 | tf_op jit(solution)/shard_map/ppermute | solution.py:380
  72.1 7.8 %collective-permute-start.16 = (bf16[128,768]{1,0:T(8,128)(2,1)S(1)}, bf16[128,768]{1,0:T(8,128)(2,1)S(1)}, u32[]{:S(2)}, u32[]{:S(2)}) collective-permute-start(bf16[128,768]{1,0:T(8,128)(2,1)S(1)} %shard_map.120.refs_6_.refs_2_), channel_id=1, source_target_pairs={{0,2},{2,0},{1,3},{3,1},{4,6},{6,4},{5,7},{7,5},{8,10},{10,8},{9,1... | collective-permute-start | bytes 589832 | tf_op jit(solution)/shard_map/ppermute | solution.py:437
  73.6 11.4 %collective-permute-start.15 = (bf16[128,1664]{1,0:T(8,128)(2,1)S(1)}, bf16[128,1664]{1,0:T(8,128)(2,1)S(1)}, u32[]{:S(2)}, u32[]{:S(2)}) collective-permute-start(bf16[128,1664]{1,0:T(8,128)(2,1)S(1)} %shard_map.121.refs_5_), channel_id=1, source_target_pairs={{0,2},{2,0},{1,3},{3,1},{4,6},{6,4},{5,7},{7,5},{8,10},{10,8},{9,1... | collective-permute-start | bytes 1277960 | tf_op jit(solution)/shard_map/ppermute | solution.py:431
  81.0 18.0 %collective-permute-start.23 = (bf16[64,2048]{1,0:T(8,128)(2,1)S(1)}, bf16[64,2048]{1,0:T(8,128)(2,1)S(1)}, u32[]{:S(2)}, u32[]{:S(2)}) collective-permute-start(bf16[64,2048]{1,0:T(8,128)(2,1)S(1)} %get-tuple-element.13.refs_4_), channel_id=1, source_target_pairs={{0,28},{4,24},{8,20},{12,16},{16,12},{20,8},{24,4},{28,0},{1,29},{... | collective-permute-start | bytes 786440 | tf_op jit(solution)/shard_map/ppermute | solution.py:380
  85.0 15.7 %collective-permute-start.24 = (bf16[64,2048]{1,0:T(8,128)(2,1)S(1)}, bf16[64,2048]{1,0:T(8,128)(2,1)S(1)}, u32[]{:S(2)}, u32[]{:S(2)}) collective-permute-start(bf16[64,2048]{1,0:T(8,128)(2,1)S(1)} %get-tuple-element.15), channel_id=1, source_target_pairs={{0,16},{4,20},{8,24},{12,28},{16,0},{20,4},{24,8},{28,12},{1,17},{... | collective-permute-start | bytes 786440 | tf_op jit(solution)/shard_map/ppermute | solution.py:380
  86.5 5.7 %collective-permute-start.20 = (bf16[128,768]{1,0:T(8,128)(2,1)S(1)}, bf16[128,768]{1,0:T(8,128)(2,1)S(1)}, u32[]{:S(2)}, u32[]{:S(2)}) collective-permute-start(bf16[128,768]{1,0:T(8,128)(2,1)S(1)} %shard_map.125.refs_5_.refs_2_), channel_id=1, source_target_pairs={{0,2},{2,0},{1,3},{3,1},{4,6},{6,4},{5,7},{7,5},{8,10},{10,8},{9,1... | collective-permute-start | bytes 589832 | tf_op jit(solution)/shard_map/ppermute | solution.py:437
  88.2 7.4 %collective-permute-start.19 = (bf16[64,1664]{1,0:T(8,128)(2,1)S(1)}, bf16[64,1664]{1,0:T(8,128)(2,1)S(1)}, u32[]{:S(2)}, u32[]{:S(2)}) collective-permute-start(bf16[64,1664]{1,0:T(8,128)(2,1)S(1)} %shard_map.126.refs_5_), channel_id=1, source_target_pairs={{0,2},{2,0},{1,3},{3,1},{4,6},{6,4},{5,7},{7,5},{8,10},{10,8},{9,1... | collective-permute-start | bytes 638984 | tf_op jit(solution)/shard_map/ppermute | solution.py:431
  93.3 11.0 %collective-permute-start.25 = (bf16[64,2048]{1,0:T(8,128)(2,1)S(1)}, bf16[64,2048]{1,0:T(8,128)(2,1)S(1)}, u32[]{:S(2)}, u32[]{:S(2)}) collective-permute-start(bf16[64,2048]{1,0:T(8,128)(2,1)S(1)} %get-tuple-element.14.refs_4_), channel_id=1, source_target_pairs={{0,8},{4,12},{8,0},{12,4},{16,24},{20,28},{24,16},{28,20},{1,9},{5... | collective-permute-start | bytes 786440 | tf_op jit(solution)/shard_map/ppermute | solution.py:380
  95.6 11.5 %collective-permute-start.26 = (bf16[64,2048]{1,0:T(8,128)(2,1)S(1)}, bf16[64,2048]{1,0:T(8,128)(2,1)S(1)}, u32[]{:S(2)}, u32[]{:S(2)}) collective-permute-start(bf16[64,2048]{1,0:T(8,128)(2,1)S(1)} %get-tuple-element.16), channel_id=1, source_target_pairs={{0,12},{4,8},{8,4},{12,0},{16,28},{20,24},{24,20},{28,16},{1,13},{... | collective-permute-start | bytes 786440 | tf_op jit(solution)/shard_map/ppermute | solution.py:380
  97.2 4.7 %collective-permute-start.21 = (bf16[64,768]{1,0:T(8,128)(2,1)S(1)}, bf16[64,768]{1,0:T(8,128)(2,1)S(1)}, u32[]{:S(2)}, u32[]{:S(2)}) collective-permute-start(bf16[64,768]{1,0:T(8,128)(2,1)S(1)} %shard_map.129.refs_1_.refs_5_), channel_id=1, source_target_pairs={{0,2},{2,0},{1,3},{3,1},{4,6},{6,4},{5,7},{7,5},{8,10},{10,8},{9,1... | collective-permute-start | bytes 294920 | tf_op jit(solution)/shard_map/ppermute | solution.py:437

commit v4 on v3

--- a/solution.py
+++ b/solution.py
@@ -23,17 +23,36 @@
 COST = 2e9
 PACK_COST = 5
 ATT_COST = 5
-HOPS = ((0, 1), (0, 4), (4, 2), (4, 1), (6, 1), (0, 2), (2, 1))
-CHUNKS = ((1,), (6, 5), (7, 4), (2, 3), (0,))
-SENDS = {1: 1, 2: 2, 3: 3, 4: 4, 5: 1, 6: 2, 7: 7}
+HOPS = ((0, 4), (0, 1), (4, 2), (4, 1), (6, 1), (0, 2), (2, 1))
+CHUNKS = ((0,), (2, 1), (6, 5), (7,), (4,), (3,))
+SENDS = {0: 0, 1: 1, 2: 2, 3: 3, 4: 4, 5: 1, 6: 2, 7: 3}
 STEPS = (
-    ("send", 0), ("keep", 0), ("send", 1), ("hidden", 0), ("keep", 1), ("send", 2),
-    ("both", 0), ("hidden", 1), ("keep", 2), ("hidden", 2), ("send", 3), ("both", 1), ("keep", 3),
-    ("both", 2), ("hidden", 3), ("send", 4), ("keep", 4), ("both", 3), ("hidden", 4), ("own", 4), ("end", 4),
+    ("send", 0),
+    ("keep", 0),
+    ("send", 1),
+    ("hidden", 0),
+    ("keep", 1),
+    ("send", 2),
+    ("both", 0),
+    ("hidden", 1),
+    ("keep", 2),
+    ("send", 3),
+    ("both", 1),
+    ("hidden", 2),
+    ("keep", 3),
+    ("hidden", 3),
+    ("send", 4),
+    ("both", 2),
+    ("both", 3),
+    ("keep", 4),
+    ("send", 5),
+    ("hidden", 4),
+    ("keep", 5),
+    ("both", 4),
+    ("hidden", 5),
+    ("both", 5),
+    ("sum", 0),
 )
-OWN = {"own": 1, "end": 4}
-
-
 def xor_pairs(count, bit):
     return [(i, i ^ bit) for i in range(count)]
 
@@ -181,32 +200,11 @@
     return (mixed_f + routed_sum).astype(jnp.bfloat16)
 
 
-def pack_kernel(head_ref, key_ref, value_ref, ids_ref, route_ref, out_ref, ids, weights, sems):
-    columns = pl.ds(pl.multiple_of(head_ref[0] * HEAD_SIZE, HEAD_SIZE), HEAD_SIZE)
-    copies = [
-        pltpu.make_async_copy(ids_ref, ids, sems.at[0]),
-        pltpu.make_async_copy(route_ref, weights, sems.at[1]),
-        pltpu.make_async_copy(key_ref.at[:, columns], out_ref.at[:, :HEAD_SIZE], sems.at[2]),
-        pltpu.make_async_copy(
-            value_ref.at[:, columns], out_ref.at[:, HEAD_SIZE : 2 * HEAD_SIZE], sems.at[3]
-        ),
-    ]
-    for copy in copies:
-        copy.start()
-    copies[0].wait()
-    copies[1].wait()
-    rows = out_ref.shape[0]
-    line = lax.broadcasted_iota(jnp.int32, (LANES, rows), 0)
-    expert = line % ROUTE_LANES
-    route = jnp.zeros(line.shape, jnp.float32)
-    for i in range(TOPK):
-        route = route + jnp.where(ids[i : i + 1, :] == expert, weights[i : i + 1, :], 0.0)
-    high = route.astype(jnp.bfloat16).astype(jnp.float32)
-    both = jnp.where(line < ROUTE_LANES, high, route - high)
-    both = jnp.concatenate([both, jnp.zeros((LANES, LANES - rows), jnp.float32)], axis=1)
-    out_ref[:, 2 * HEAD_SIZE :] = jnp.transpose(both)[:rows].astype(jnp.bfloat16)
-    copies[2].wait()
-    copies[3].wait()
+def pack_kernel(key_ref, value_ref, high_ref, low_ref, out_ref):
+    out_ref[:, :HEAD_SIZE] = key_ref[...]
+    out_ref[:, HEAD_SIZE : 2 * HEAD_SIZE] = value_ref[...]
+    out_ref[:, 2 * HEAD_SIZE : 2 * HEAD_SIZE + ROUTE_LANES] = high_ref[...]
+    out_ref[:, 2 * HEAD_SIZE + ROUTE_LANES : 2 * HEAD_SIZE + 2 * ROUTE_LANES] = low_ref[...]
 
 
 def attention_kernel(place_ref, order_ref, query_ref, packed_ref, residual_ref, out_ref):
@@ -247,6 +245,17 @@
         )
 
 
+def copy_kernel(block_ref, out_ref):
+    out_ref[...] = block_ref[...]
+
+
+def product(rows, weight):
+    count = rows.shape[0]
+    if count < LANES:
+        rows = jnp.concatenate([rows, rows], axis=0)
+    return jnp.dot(rows, weight, preferred_element_type=jnp.float32)[:count]
+
+
 def prepared(blocks, gain_ref):
     rows = jnp.concatenate([block[...] for block in blocks], axis=0).astype(jnp.float32)
     squares = jnp.sum(rows * rows, axis=1, keepdims=True)
@@ -258,9 +267,9 @@
     k = index_ref[0]
     size = gate_ref.shape[2]
     rows, squares = prepared(rest[:-1], gain_ref)
-    gate = jnp.dot(rows, gate_ref[k], preferred_element_type=jnp.float32)
+    gate = product(rows, gate_ref[k])
     out_ref[:, :size] = gate.astype(jnp.bfloat16)
-    up = jnp.dot(rows, up_ref[k], preferred_element_type=jnp.float32)
+    up = product(rows, up_ref[k])
     out_ref[:, size : 2 * size] = up.astype(jnp.bfloat16)
     high = squares.astype(jnp.bfloat16).astype(jnp.float32)
     lane = lax.broadcasted_iota(jnp.int32, (rows.shape[0], LANES), 1)
@@ -278,9 +287,8 @@
         [packed_ref[place * rows : (place + 1) * rows, 2 * HEAD_SIZE :] for place in places], axis=0
     ).astype(jnp.float32)
     lane = lax.broadcasted_iota(jnp.int32, route.shape, 1)
-    route = jnp.sum(
-        jnp.where(lane % ROUTE_LANES == index_ref[0], route, 0.0), axis=1, keepdims=True
-    )
+    named = (lane == index_ref[0]) | (lane == index_ref[0] + ROUTE_LANES)
+    route = jnp.sum(jnp.where(named, route, 0.0), axis=1, keepdims=True)
     gate = kept_ref[:, :size].astype(jnp.float32) + arrived_ref[:, :size].astype(jnp.float32)
     up = kept_ref[:, size : 2 * size].astype(jnp.float32) + arrived_ref[
         :, size : 2 * size
@@ -290,21 +298,16 @@
     out_ref[...] = (gate / (1.0 + jnp.exp(-gate)) * up).astype(jnp.bfloat16)
 
 
-def own_kernel(index_ref, hidden_ref, down_ref, mixed_ref, *rest):
-    out_ref = rest[-1]
-    total = mixed_ref[...].astype(jnp.float32) + jnp.dot(
-        hidden_ref[...], down_ref[index_ref[0]], preferred_element_type=jnp.float32
-    )
-    for term in rest[:-1]:
-        total = total + term[...].astype(jnp.float32)
-    out_ref[...] = total.astype(out_ref.dtype)
+def sum_kernel(mixed_ref, *rest):
+    total = mixed_ref[...].astype(jnp.float32)
+    for term_ref in rest[:-1]:
+        total = total + term_ref[...].astype(jnp.float32)
+    rest[-1][...] = total.astype(rest[-1].dtype)
 
 
 def both_kernel(places, mine_ref, other_ref, hidden_ref, other_hidden_ref, down_ref, *rest):
-    both = jnp.dot(hidden_ref[...], down_ref[mine_ref[0]], preferred_element_type=jnp.float32)
-    both = both + jnp.dot(
-        other_hidden_ref[...], down_ref[other_ref[0]], preferred_element_type=jnp.float32
-    )
+    both = product(hidden_ref[...], down_ref[mine_ref[0]])
+    both = both + product(other_hidden_ref[...], down_ref[other_ref[0]])
     rows = rest[-1].shape[0]
     for i, out_ref in enumerate(rest[len(places) :]):
         term = both[i * rows : (i + 1) * rows]
@@ -319,10 +322,10 @@
         self.before = None
         self.also = []
 
-    def __call__(self, kernel, out_shape, *args, held=(), cost=0, scratch=(), space=pltpu.VMEM):
+    def __call__(self, kernel, out_shape, *args, held=(), cost=0):
         vmem = pl.BlockSpec(memory_space=pltpu.VMEM)
         specs = [
-            pl.BlockSpec(memory_space=pltpu.SMEM if arg.ndim == 1 else space) for arg in args
+            pl.BlockSpec(memory_space=pltpu.SMEM) if arg.ndim == 1 else vmem for arg in args
         ]
         unread = list(held) + ([] if self.before is None else [self.before]) + self.also
         self.also = []
@@ -338,7 +341,6 @@
             out_shape=out_shape,
             in_specs=specs,
             out_specs=[vmem] * len(out_shape) if many else vmem,
-            scratch_shapes=list(scratch),
             compiler_params=pltpu.CompilerParams(vmem_limit_bytes=KERNEL_BYTES),
             cost_estimate=pl.CostEstimate(
                 flops=int(cost * COST), bytes_accessed=0, transcendentals=0
@@ -379,21 +381,19 @@
     def hop(block, offset):
         return lax.ppermute(block, "ctx", xor_pairs(ctx_count, offset))
 
+    columns = mine[0] * HEAD_SIZE
+    experts = jnp.arange(ROUTE_LANES, dtype=jnp.int32)
+    named = expert_ids[:, :, None] == experts[None, None, :]
+    route = jnp.sum(jnp.where(named, route_weight[:, :, None], 0.0), axis=1)
+    high = lax.reduce_precision(route, 8, 7)
     packed = core(
         pack_kernel,
         of((rows, 2 * HEAD_SIZE + LANES)),
-        mine,
-        key_rows,
-        value_head_rows,
-        expert_ids.T,
-        route_weight.T,
+        lax.dynamic_slice_in_dim(key_rows, columns, HEAD_SIZE, 1),
+        lax.dynamic_slice_in_dim(value_head_rows, columns, HEAD_SIZE, 1),
+        high.astype(jnp.bfloat16),
+        (route - high).astype(jnp.bfloat16),
         cost=PACK_COST,
-        space=pl.ANY,
-        scratch=(
-            pltpu.VMEM((TOPK, rows), jnp.int32),
-            pltpu.VMEM((TOPK, rows), jnp.float32),
-            pltpu.SemaphoreType.DMA((4,)),
-        ),
     )
     packed = gather_rows(packed, ctx_count)
     mixed_rows = core(
@@ -414,6 +414,21 @@
 
     kept, arrived, hidden, other_hidden, terms = {}, {}, {}, {}, {}
     for step, i in STEPS:
+        if step == "hop":
+            source, offset = i
+            again = core(copy_kernel, of((rows, features)), block[source], cost=0.2)
+            block[source ^ offset] = hop(again, offset)
+            continue
+        if step == "sum":
+            total = core(sum_kernel, of((rows, features)), mixed_rows, *terms[0])
+            continue
+        if step == "pin":
+            core.also.append(other_hidden[i])
+            continue
+        if step == "on":
+            source, offset = i
+            block[source ^ offset] = hop(block[source], offset)
+            continue
         chunk = CHUNKS[i % len(CHUNKS)]
         count = len(chunk) * rows
         if step in ("send", "keep"):
@@ -435,8 +450,8 @@
             kernel = functools.partial(hidden_kernel, [position[offset] for offset in chunk])
             hidden[i] = core(kernel, of((count, size)), expert, kept[i], arrived[i], packed, cost=0.4)
             other_hidden[i] = lax.ppermute(hidden[i], "exp", swap)
-        elif step == "both":
-            shapes = [of((rows, features))] * len(chunk)
+        else:
+            shapes = [of((rows, features), jnp.bfloat16 if o else jnp.float32) for o in chunk]
             arrivals = [(at, term) for at, o in enumerate(chunk) for term in terms.pop(o, [])]
             kernel = functools.partial(both_kernel, [at for at, _ in arrivals])
             out = core(
@@ -447,25 +462,8 @@
                 cost=1.1,
             )
             for offset, term in zip(chunk, out):
-                terms.setdefault(offset ^ SENDS[offset], []).append(hop(term, SENDS[offset]))
-        elif step == "wait":
-            core.also += terms[0][-i:]
-        else:
-            ready = [terms[0].pop(0) for _ in range(OWN[step])]
-            if step == "own":
-                total = core(
-                    own_kernel,
-                    of((rows, features), jnp.float32),
-                    mine, hidden[i], down_weight, mixed_rows, *ready,
-                    cost=0.7,
-                )
-            else:
-                total = core(
-                    own_kernel,
-                    of((rows, features)),
-                    other, other_hidden[i], down_weight, total, *ready,
-                    cost=0.7,
-                )
+                term = hop(term, SENDS[offset]) if offset else term
+                terms.setdefault(offset ^ SENDS[offset], []).append(term)
     return total
 
 

time: 109 us -> 102 us (0.936)
  waiting for transfers between devices: 45.3 us -> 33.9 us
  starting transfers between devices: 38.9 us -> 42.9 us
  local copies, waits for them, and re-layouts: 2.94 us -> 0.96 us
  Pallas kernels: 21 us -> 22.6 us
    ppermute x5 -> x6, waiting for transfers between devices: 7.19 us -> 0.73 us  [local(): arrived[i] = lax.ppermute(product, 'exp', swap)]
    ppermute x14, waiting for transfers between devices: 18.1 us -> 11.9 us  [hop(): return lax.ppermute(block, 'ctx', xor_pairs(ctx_count, offset))]
    unnamed x28 -> x20, local copies, waits for them, and re-layouts: 2.94 us -> 0.05 us
    ppermute x14, starting transfers between devices: 19.4 us -> 21.9 us  [hop(): return lax.ppermute(block, 'ctx', xor_pairs(ctx_count, offset))]
    pallas_call x23 -> x27, Pallas kernels: 21 us -> 22.6 us  [__call__(): pl.pallas_call(body, out_shape=out_shape, in_specs=specs, out_specs=[vmem...]
    ppermute x5 -> x6, waiting for transfers between devices: 10.2 us -> 11.5 us  [local(): other_hidden[i] = lax.ppermute(hidden[i], 'exp', swap)]
    ppermute x5 -> x6, starting transfers between devices: 6.81 us -> 7.96 us  [local(): other_hidden[i] = lax.ppermute(hidden[i], 'exp', swap)]
    ppermute x5 -> x6, starting transfers between devices: 5.34 us -> 5.82 us  [local(): arrived[i] = lax.ppermute(product, 'exp', swap)]
  transfers between devices with their start and end apart: 27 -> 29, of which waited for: 17 -> 14; matrix products, arithmetic and copies ran while one was open for 0% -> 0% of each run, Pallas kernels for 15% -> 19%
where the time goes in v4:
time: 102 us
  starting transfers between devices  42.9 us (42%)
  waiting for transfers between devices  33.9 us (33%)
  Pallas kernels  22.6 us (22%)
    pallas_call x27, Pallas kernels, __call__(): pl.pallas_call(body, out_shape=out_shape, in_specs=specs, out_specs=[vmem...  22.6 us
    ppermute x14, starting transfers between devices, hop(): return lax.ppermute(block, 'ctx', xor_pairs(ctx_count, offset))  21.9 us
    ppermute x14, waiting for transfers between devices, hop(): return lax.ppermute(block, 'ctx', xor_pairs(ctx_count, offset))  11.9 us
    ppermute x6, waiting for transfers between devices, local(): other_hidden[i] = lax.ppermute(hidden[i], 'exp', swap)  11.5 us
    ppermute x3, waiting for transfers between devices, gather_rows(): lax.ppermute(block, 'ctx', xor_pairs(count, bit))  9.78 us
    ppermute x6, starting transfers between devices, local(): other_hidden[i] = lax.ppermute(hidden[i], 'exp', swap)  7.96 us
    ppermute x3, starting transfers between devices, gather_rows(): lax.ppermute(block, 'ctx', xor_pairs(count, bit))  7.29 us
    ppermute x6, starting transfers between devices, local(): arrived[i] = lax.ppermute(product, 'exp', swap)  5.82 us
  transfers between devices with their start and end apart: 29, of which 14 were waited for; matrix products, arithmetic and copies ran while one was open for 0% of the time, Pallas kernels for 19%

profile of v4, /device:TPU:0, one launch (start us, length us, event | category | flops | bytes accessed | tf_op | source)
XLA Modules:
  0.0 101.6 jit_solution(11077719381088931467)
XLA Ops:
  1.7 4.0 %collective-permute-start = (bf16[64,384]{1,0:T(8,128)(2,1)S(1)}, bf16[64,384]{1,0:T(8,128)(2,1)S(1)}, u32[]{:S(2)}, u32[]{:S(2)}) collective-permute-start(bf16[64,384]{1,0:T(8,128)(2,1)S(1)} %shard_map.109.refs_5_), channel_id=1, source_target_pairs={{0,16},{4,20},{8,24},{12,28},{16,0},{20,4},{24,8},{28,12},{1,17},{... | collective-permute-start | bytes 147464 | tf_op jit(solution)/shard_map/ppermute | solution.py:71
  5.8 2.6 %collective-permute-done = bf16[64,384]{1,0:T(8,128)(2,1)S(1)} collective-permute-done((bf16[64,384]{1,0:T(8,128)(2,1)S(1)}, bf16[64,384]{1,0:T(8,128)(2,1)S(1)}, u32[]{:S(2)}, u32[]{:S(2)}) %collective-permute-start) | collective-permute-done | bytes 49184 | tf_op jit(solution)/shard_map/ppermute | solution.py:71
  8.4 1.4 %collective-permute-start.1 = (bf16[128,384]{1,0:T(8,128)(2,1)S(1)}, bf16[128,384]{1,0:T(8,128)(2,1)S(1)}, u32[]{:S(2)}, u32[]{:S(2)}) collective-permute-start(bf16[128,384]{1,0:T(8,128)(2,1)S(1)} %pad_maximum_fusion.2), channel_id=1, source_target_pairs={{0,8},{4,12},{8,0},{12,4},{16,24},{20,28},{24,16},{28,20},{1,9},{5... | collective-permute-start | bytes 294920 | tf_op jit(solution)/shard_map/ppermute | solution.py:71
  9.9 3.2 %collective-permute-done.1 = bf16[128,384]{1,0:T(8,128)(2,1)S(1)} collective-permute-done((bf16[128,384]{1,0:T(8,128)(2,1)S(1)}, bf16[128,384]{1,0:T(8,128)(2,1)S(1)}, u32[]{:S(2)}, u32[]{:S(2)}) %collective-permute-start.1) | collective-permute-done | bytes 98336 | tf_op jit(solution)/shard_map/ppermute | solution.py:71
  13.1 1.8 %collective-permute-start.2 = (bf16[256,384]{1,0:T(8,128)(2,1)S(1)}, bf16[256,384]{1,0:T(8,128)(2,1)S(1)}, u32[]{:S(2)}, u32[]{:S(2)}) collective-permute-start(bf16[256,384]{1,0:T(8,128)(2,1)S(1)} %pad_maximum_fusion.1), channel_id=1, source_target_pairs={{0,4},{4,0},{8,12},{12,8},{16,20},{20,16},{24,28},{28,24},{1,5},{5... | collective-permute-start | bytes 589832 | tf_op jit(solution)/shard_map/ppermute | solution.py:71
  14.9 3.9 %collective-permute-done.2 = bf16[256,384]{1,0:T(8,128)(2,1)S(1)} collective-permute-done((bf16[256,384]{1,0:T(8,128)(2,1)S(1)}, bf16[256,384]{1,0:T(8,128)(2,1)S(1)}, u32[]{:S(2)}, u32[]{:S(2)}) %collective-permute-start.2) | collective-permute-done | bytes 196640 | tf_op jit(solution)/shard_map/ppermute | solution.py:71
  19.0 1.9 %shard_map.110.refs_4_.refs_5_.refs_0_ = bf16[64,2048]{1,0:T(8,128)(2,1)S(1)} custom-call(s32[1]{0:T(128)} %bitcast.refs_0_, s32[8]{0:T(128)S(1)} %copy-done.3, bf16[64,2048]{1,0:T(8,128)(2,1)S(1)} %copy-done.1, bf16[512,384]{1,0:T(8,128)(2,1)S(1)} %pad_maximum_fusion.refs_3_, bf16[64,2048]{1,0:T(8,128)(2,1)S(1)} %copy-done.2, ...), custom_call_target="tpu_custom_call" | custom-call | flops 10000000000 | tf_op jit(solution)/shard_map/pallas_call | solution.py:339
  20.9 1.4 %collective-permute-start.4 = (bf16[64,2048]{1,0:T(8,128)(2,1)S(1)}, bf16[64,2048]{1,0:T(8,128)(2,1)S(1)}, u32[]{:S(2)}, u32[]{:S(2)}) collective-permute-start(bf16[64,2048]{1,0:T(8,128)(2,1)S(1)} %shard_map.110.refs_4_.refs_5_.refs_0_), channel_id=1, source_target_pairs={{0,8},{4,12},{8,0},{12,4},{16,24},{20,28},{24,16},{28,20},{1,9},{5... | collective-permute-start | bytes 786440 | tf_op jit(solution)/shard_map/ppermute | solution.py:382
  22.4 1.5 %collective-permute-start.5 = (bf16[64,2048]{1,0:T(8,128)(2,1)S(1)}, bf16[64,2048]{1,0:T(8,128)(2,1)S(1)}, u32[]{:S(2)}, u32[]{:S(2)}) collective-permute-start(bf16[64,2048]{1,0:T(8,128)(2,1)S(1)} %shard_map.110.refs_4_.refs_5_.refs_0_), channel_id=1, source_target_pairs={{0,4},{4,0},{8,12},{12,8},{16,20},{20,16},{24,28},{28,24},{1,5},{5... | collective-permute-start | bytes 786440 | tf_op jit(solution)/shard_map/ppermute | solution.py:382
  23.9 3.0 %collective-permute-start.7 = (bf16[64,2048]{1,0:T(8,128)(2,1)S(1)}, bf16[64,2048]{1,0:T(8,128)(2,1)S(1)}, u32[]{:S(2)}, u32[]{:S(2)}) collective-permute-start(bf16[64,2048]{1,0:T(8,128)(2,1)S(1)} %shard_map.110.refs_4_.refs_5_.refs_0_), channel_id=1, source_target_pairs={{0,16},{4,20},{8,24},{12,28},{16,0},{20,4},{24,8},{28,12},{1,17},{... | collective-permute-start | bytes 786440 | tf_op jit(solution)/shard_map/ppermute | solution.py:382
  26.9 1.0 shard_map.111.refs_5_
  27.9 1.0 shard_map.112.refs_6_.refs_1_
  29.0 1.6 %collective-permute-start.3 = (bf16[64,1664]{1,0:T(8,128)(2,1)S(1)}, bf16[64,1664]{1,0:T(8,128)(2,1)S(1)}, u32[]{:S(2)}, u32[]{:S(2)}) collective-permute-start(bf16[64,1664]{1,0:T(8,128)(2,1)S(1)} %shard_map.111.refs_5_), channel_id=1, source_target_pairs={{0,2},{2,0},{1,3},{3,1},{4,6},{6,4},{5,7},{7,5},{8,10},{10,8},{9,1... | collective-permute-start | bytes 638984 | tf_op jit(solution)/shard_map/ppermute | solution.py:446
  30.5 1.0 %shard_map.113.refs_4_ = bf16[128,1664]{1,0:T(8,128)(2,1)S(1)} custom-call(s32[1]{0:T(128)S(6)} %sub.7.refs_0_.refs_1_, f32[1,2048]{1,0:T(1,128)S(1)} %bitcast.9, bf16[2,2048,768]{2,1,0:T(8,128)(2,1)S(1)} %bitcast.4, bf16[2,2048,768]{2,1,0:T(8,128)(2,1)S(1)} %bitcast.6, bf16[64,2048]{1,0:T(8,128)(2,1)S(1)} %collective-permute-done.4.refs_4_, ...), custom_call_target="tpu_custom_call" | custom-call | flops 2400000000 | tf_op jit(solution)/shard_map/pallas_call | solution.py:339
  32.2 2.8 %collective-permute-done.7.refs_4_ = bf16[64,2048]{1,0:T(8,128)(2,1)S(1)} collective-permute-done((bf16[64,2048]{1,0:T(8,128)(2,1)S(1)}, bf16[64,2048]{1,0:T(8,128)(2,1)S(1)}, u32[]{:S(2)}, u32[]{:S(2)}) %collective-permute-start.7) | collective-permute-done | bytes 262176 | tf_op jit(solution)/shard_map/ppermute | solution.py:382
  34.9 1.6 %collective-permute-start.9 = (bf16[64,2048]{1,0:T(8,128)(2,1)S(1)}, bf16[64,2048]{1,0:T(8,128)(2,1)S(1)}, u32[]{:S(2)}, u32[]{:S(2)}) collective-permute-start(bf16[64,2048]{1,0:T(8,128)(2,1)S(1)} %collective-permute-done.7.refs_4_), channel_id=1, source_target_pairs={{0,4},{4,0},{8,12},{12,8},{16,20},{20,16},{24,28},{28,24},{1,5},{5... | collective-permute-start | bytes 786440 | tf_op jit(solution)/shard_map/ppermute | solution.py:382
  37.4 1.6 %collective-permute-start.6 = (bf16[64,768]{1,0:T(8,128)(2,1)S(1)}, bf16[64,768]{1,0:T(8,128)(2,1)S(1)}, u32[]{:S(2)}, u32[]{:S(2)}) collective-permute-start(bf16[64,768]{1,0:T(8,128)(2,1)S(1)} %shard_map.114.refs_6_.refs_2_), channel_id=1, source_target_pairs={{0,2},{2,0},{1,3},{3,1},{4,6},{6,4},{5,7},{7,5},{8,10},{10,8},{9,1... | collective-permute-start | bytes 294920 | tf_op jit(solution)/shard_map/ppermute | solution.py:452
  39.5 1.0 %shard_map.115.refs_6_.refs_1_ = bf16[128,1664]{1,0:T(8,128)(2,1)S(1)} custom-call(s32[1]{0:T(128)} %bitcast.1.refs_0_, f32[1,2048]{1,0:T(1,128)S(1)} %bitcast.10, bf16[2,2048,768]{2,1,0:T(8,128)(2,1)S(1)} %bitcast.4, bf16[2,2048,768]{2,1,0:T(8,128)(2,1)S(1)} %bitcast.6, bf16[64,2048]{1,0:T(8,128)(2,1)S(1)} %collective-permute-done.4.refs_4_, ...), custom_call_target="tpu_custom_call" | custom-call | flops 2400000000 | tf_op jit(solution)/shard_map/pallas_call | solution.py:339
  41.4 1.0 shard_map.116.refs_5_
  42.4 2.6 %collective-permute-start.15 = (bf16[128,1664]{1,0:T(8,128)(2,1)S(1)}, bf16[128,1664]{1,0:T(8,128)(2,1)S(1)}, u32[]{:S(2)}, u32[]{:S(2)}) collective-permute-start(bf16[128,1664]{1,0:T(8,128)(2,1)S(1)} %shard_map.116.refs_5_), channel_id=1, source_target_pairs={{0,2},{2,0},{1,3},{3,1},{4,6},{6,4},{5,7},{7,5},{8,10},{10,8},{9,1... | collective-permute-start | bytes 1277960 | tf_op jit(solution)/shard_map/ppermute | solution.py:446
  45.0 2.5 %collective-permute-start.12 = (bf16[64,2048]{1,0:T(8,128)(2,1)S(1)}, bf16[64,2048]{1,0:T(8,128)(2,1)S(1)}, u32[]{:S(2)}, u32[]{:S(2)}) collective-permute-start(bf16[64,2048]{1,0:T(8,128)(2,1)S(1)} %collective-permute-done.8.refs_4_), channel_id=1, source_target_pairs={{0,4},{4,0},{8,12},{12,8},{16,20},{20,16},{24,28},{28,24},{1,5},{5... | collective-permute-start | bytes 786440 | tf_op jit(solution)/shard_map/ppermute | solution.py:382
  47.5 1.0 shard_map.117.refs_4_.refs_1_
  49.0 1.0 shard_map.119.refs_5_.refs_1_
  50.0 1.8 %collective-permute-done.12.refs_4_ = bf16[64,2048]{1,0:T(8,128)(2,1)S(1)} collective-permute-done((bf16[64,2048]{1,0:T(8,128)(2,1)S(1)}, bf16[64,2048]{1,0:T(8,128)(2,1)S(1)}, u32[]{:S(2)}, u32[]{:S(2)}) %collective-permute-start.12) | collective-permute-done | bytes 262176 | tf_op jit(solution)/shard_map/ppermute | solution.py:382
  51.8 1.0 shard_map.120.refs_5_
  53.1 6.9 %collective-permute-done.11.refs_3_ = bf16[128,768]{1,0:T(8,128)(2,1)S(1)} collective-permute-done((bf16[128,768]{1,0:T(8,128)(2,1)S(1)}, bf16[128,768]{1,0:T(8,128)(2,1)S(1)}, u32[]{:S(2)}, u32[]{:S(2)}) %collective-permute-start.11) | collective-permute-done | bytes 196640 | tf_op jit(solution)/shard_map/ppermute | solution.py:452
  60.0 1.0 %shard_map.121 = (bf16[64,2048]{1,0:T(8,128)(2,1)S(1)}, bf16[64,2048]{1,0:T(8,128)(2,1)S(1)}) custom-call(s32[1]{0:T(128)} %bitcast.1.refs_0_, s32[1]{0:T(128)S(6)} %sub.7.refs_0_.refs_1_, bf16[128,768]{1,0:T(8,128)(2,1)S(1)} %shard_map.118.refs_6_.refs_2_, bf16[128,768]{1,0:T(8,128)(2,1)S(1)} %collective-permute-done.11.refs_3_, ...), custom_call_target="tpu_custom_call" | custom-call | flops 2200000000 | tf_op jit(solution)/shard_map/pallas_call | solution.py:339
  61.3 2.3 %collective-permute-start.18 = (bf16[128,768]{1,0:T(8,128)(2,1)S(1)}, bf16[128,768]{1,0:T(8,128)(2,1)S(1)}, u32[]{:S(2)}, u32[]{:S(2)}) collective-permute-start(bf16[128,768]{1,0:T(8,128)(2,1)S(1)} %shard_map.122.refs_5_.refs_2_), channel_id=1, source_target_pairs={{0,2},{2,0},{1,3},{3,1},{4,6},{6,4},{5,7},{7,5},{8,10},{10,8},{9,1... | collective-permute-start | bytes 589832 | tf_op jit(solution)/shard_map/ppermute | solution.py:452
  63.6 1.0 shard_map.123.refs_1_.refs_4_
  64.8 2.0 %collective-permute-start.17 = (bf16[64,768]{1,0:T(8,128)(2,1)S(1)}, bf16[64,768]{1,0:T(8,128)(2,1)S(1)}, u32[]{:S(2)}, u32[]{:S(2)}) collective-permute-start(bf16[64,768]{1,0:T(8,128)(2,1)S(1)} %shard_map.124.refs_5_.refs_2_), channel_id=1, source_target_pairs={{0,2},{2,0},{1,3},{3,1},{4,6},{6,4},{5,7},{7,5},{8,10},{10,8},{9,1... | collective-permute-start | bytes 294920 | tf_op jit(solution)/shard_map/ppermute | solution.py:452
  66.8 1.0 shard_map.125.refs_5_
  68.4 1.0 %shard_map.126 = (bf16[64,2048]{1,0:T(8,128)(2,1)S(1)}, bf16[64,2048]{1,0:T(8,128)(2,1)S(1)}) custom-call(s32[1]{0:T(128)} %bitcast.1.refs_0_, s32[1]{0:T(128)S(6)} %sub.7.refs_0_.refs_1_, bf16[128,768]{1,0:T(8,128)(2,1)S(1)} %shard_map.122.refs_5_.refs_2_, bf16[128,768]{1,0:T(8,128)(2,1)S(1)} %collective-permute-done.18.refs_3_, ...), custom_call_target="tpu_custom_call" | custom-call | flops 2200000000 | tf_op jit(solution)/shard_map/pallas_call | solution.py:339
  69.5 2.9 %collective-permute-start.22 = (bf16[64,2048]{1,0:T(8,128)(2,1)S(1)}, bf16[64,2048]{1,0:T(8,128)(2,1)S(1)}, u32[]{:S(2)}, u32[]{:S(2)}) collective-permute-start(bf16[64,2048]{1,0:T(8,128)(2,1)S(1)} %get-tuple-element.11.refs_5_), channel_id=1, source_target_pairs={{0,8},{4,12},{8,0},{12,4},{16,24},{20,28},{24,16},{28,20},{1,9},{5... | collective-permute-start | bytes 786440 | tf_op jit(solution)/shard_map/ppermute | solution.py:382
  72.4 1.0 shard_map.127.refs_5_
  74.2 1.6 %collective-permute-start.23 = (bf16[64,2048]{1,0:T(8,128)(2,1)S(1)}, bf16[64,2048]{1,0:T(8,128)(2,1)S(1)}, u32[]{:S(2)}, u32[]{:S(2)}) collective-permute-start(bf16[64,2048]{1,0:T(8,128)(2,1)S(1)} %get-tuple-element.12), channel_id=1, source_target_pairs={{0,4},{4,0},{8,12},{12,8},{16,20},{20,16},{24,28},{28,24},{1,5},{5... | collective-permute-start | bytes 786440 | tf_op jit(solution)/shard_map/ppermute | solution.py:382
  75.8 1.0 shard_map.128.refs_5_.refs_1_
  76.8 1.0 shard_map.129.refs_4_
  78.7 1.5 %collective-permute-start.21 = (bf16[64,768]{1,0:T(8,128)(2,1)S(1)}, bf16[64,768]{1,0:T(8,128)(2,1)S(1)}, u32[]{:S(2)}, u32[]{:S(2)}) collective-permute-start(bf16[64,768]{1,0:T(8,128)(2,1)S(1)} %shard_map.130.refs_5_.refs_2_), channel_id=1, source_target_pairs={{0,2},{2,0},{1,3},{3,1},{4,6},{6,4},{5,7},{7,5},{8,10},{10,8},{9,1... | collective-permute-start | bytes 294920 | tf_op jit(solution)/shard_map/ppermute | solution.py:452
  80.2 1.0 shard_map.131.refs_8_.refs_1_
  81.2 4.0 %collective-permute-done.21.refs_3_ = bf16[64,768]{1,0:T(8,128)(2,1)S(1)} collective-permute-done((bf16[64,768]{1,0:T(8,128)(2,1)S(1)}, bf16[64,768]{1,0:T(8,128)(2,1)S(1)}, u32[]{:S(2)}, u32[]{:S(2)}) %collective-permute-start.21) | collective-permute-done | bytes 98336 | tf_op jit(solution)/shard_map/ppermute | solution.py:452
  85.3 1.1 %shard_map.132.refs_4_ = bf16[64,2048]{1,0:T(8,128)(2,1)S(1)} custom-call(s32[1]{0:T(128)} %bitcast.1.refs_0_, s32[1]{0:T(128)S(6)} %sub.7.refs_0_.refs_1_, bf16[64,768]{1,0:T(8,128)(2,1)S(1)} %shard_map.130.refs_5_.refs_2_, bf16[64,768]{1,0:T(8,128)(2,1)S(1)} %collective-permute-done.21.refs_3_, bf16[2,768,2048]{2,1,0:T(8,128)(2,1)S(1)} %bitcast.20, ...), custom_call_target="tpu_custom_call" | custom-call | flops 2200000000 | tf_op jit(solution)/shard_map/pallas_call | solution.py:339
  87.0 1.8 %collective-permute-start.13 = (bf16[64,2048]{1,0:T(8,128)(2,1)S(1)}, bf16[64,2048]{1,0:T(8,128)(2,1)S(1)}, u32[]{:S(2)}, u32[]{:S(2)}) collective-permute-start(bf16[64,2048]{1,0:T(8,128)(2,1)S(1)} %get-tuple-element.9.refs_4_), channel_id=1, source_target_pairs={{0,8},{4,12},{8,0},{12,4},{16,24},{20,28},{24,16},{28,20},{1,9},{5... | collective-permute-start | bytes 786440 | tf_op jit(solution)/shard_map/ppermute | solution.py:382
  88.8 1.7 %collective-permute-start.14 = (bf16[64,2048]{1,0:T(8,128)(2,1)S(1)}, bf16[64,2048]{1,0:T(8,128)(2,1)S(1)}, u32[]{:S(2)}, u32[]{:S(2)}) collective-permute-start(bf16[64,2048]{1,0:T(8,128)(2,1)S(1)} %get-tuple-element.10), channel_id=1, source_target_pairs={{0,4},{4,0},{8,12},{12,8},{16,20},{20,16},{24,28},{28,24},{1,5},{5... | collective-permute-start | bytes 786440 | tf_op jit(solution)/shard_map/ppermute | solution.py:382
  91.2 1.0 shard_map.134.refs_6_
  92.2 2.0 %collective-permute-start.28 = (bf16[64,2048]{1,0:T(8,128)(2,1)S(1)}, bf16[64,2048]{1,0:T(8,128)(2,1)S(1)}, u32[]{:S(2)}, u32[]{:S(2)}) collective-permute-start(bf16[64,2048]{1,0:T(8,128)(2,1)S(1)} %shard_map.134.refs_6_), channel_id=1, source_target_pairs={{0,12},{4,8},{8,4},{12,0},{16,28},{20,24},{24,20},{28,16},{1,13},{... | collective-permute-start | bytes 786440 | tf_op jit(solution)/shard_map/ppermute | solution.py:382
  94.2 0.9 collective-permute-done.14.refs_3_
  95.2 5.5 %collective-permute-done.25.refs_4_ = bf16[64,2048]{1,0:T(8,128)(2,1)S(1)} collective-permute-done((bf16[64,2048]{1,0:T(8,128)(2,1)S(1)}, bf16[64,2048]{1,0:T(8,128)(2,1)S(1)}, u32[]{:S(2)}, u32[]{:S(2)}) %collective-permute-start.25) | collective-permute-done | bytes 262176 | tf_op jit(solution)/shard_map/ppermute | solution.py:382
  100.7 0.9 shard_map.135
  (69 shorter events, 9.6 us)
Async XLA Ops:
  1.7 17.2 %copy-start.1 = (bf16[64,2048]{1,0:T(8,128)(2,1)S(1)}, bf16[64,2048]{1,0:T(8,128)(2,1)}, u32[]{:S(2)}) copy-start(bf16[64,2048]{1,0:T(8,128)(2,1)} %refs_2_.13) | copy-start | bytes 786436
  1.7 17.2 %copy-start.2 = (bf16[64,2048]{1,0:T(8,128)(2,1)S(1)}, bf16[64,2048]{1,0:T(8,128)(2,1)}, u32[]{:S(2)}) copy-start(bf16[64,2048]{1,0:T(8,128)(2,1)} %refs_4_.7) | copy-start | bytes 786436
  1.7 17.3 %copy-start.3 = (s32[8]{0:T(128)S(1)}, s32[8]{0:T(128)}, u32[]{:S(2)}) copy-start(s32[8]{0:T(128)} %refs_1_.1) | copy-start | bytes 100
  1.7 6.6 %collective-permute-start = (bf16[64,384]{1,0:T(8,128)(2,1)S(1)}, bf16[64,384]{1,0:T(8,128)(2,1)S(1)}, u32[]{:S(2)}, u32[]{:S(2)}) collective-permute-start(bf16[64,384]{1,0:T(8,128)(2,1)S(1)} %shard_map.109.refs_5_), channel_id=1, source_target_pairs={{0,16},{4,20},{8,24},{12,28},{16,0},{20,4},{24,8},{28,12},{1,17},{... | collective-permute-start | bytes 147464 | tf_op jit(solution)/shard_map/ppermute | solution.py:71
  8.4 4.7 %collective-permute-start.1 = (bf16[128,384]{1,0:T(8,128)(2,1)S(1)}, bf16[128,384]{1,0:T(8,128)(2,1)S(1)}, u32[]{:S(2)}, u32[]{:S(2)}) collective-permute-start(bf16[128,384]{1,0:T(8,128)(2,1)S(1)} %pad_maximum_fusion.2), channel_id=1, source_target_pairs={{0,8},{4,12},{8,0},{12,4},{16,24},{20,28},{24,16},{28,20},{1,9},{5... | collective-permute-start | bytes 294920 | tf_op jit(solution)/shard_map/ppermute | solution.py:71
  13.1 5.7 %collective-permute-start.2 = (bf16[256,384]{1,0:T(8,128)(2,1)S(1)}, bf16[256,384]{1,0:T(8,128)(2,1)S(1)}, u32[]{:S(2)}, u32[]{:S(2)}) collective-permute-start(bf16[256,384]{1,0:T(8,128)(2,1)S(1)} %pad_maximum_fusion.1), channel_id=1, source_target_pairs={{0,4},{4,0},{8,12},{12,8},{16,20},{20,16},{24,28},{28,24},{1,5},{5... | collective-permute-start | bytes 589832 | tf_op jit(solution)/shard_map/ppermute | solution.py:71
  18.9 8.0 %slice-start = ((s8[6291456]{0:T(1024)(128)(4,1)}), s8[4194304]{0:T(1024)(128)(4,1)S(1)}, s32[]{:S(2)}) async-start(s8[6291456]{0:T(1024)(128)(4,1)} %bitcast.3), calls=%async_computation | async-start | bytes 8388608
  18.9 8.0 %slice-start.2 = ((s8[6291456]{0:T(1024)(128)(4,1)}), s8[4194304]{0:T(1024)(128)(4,1)S(1)}, s32[]{:S(2)}) async-start(s8[6291456]{0:T(1024)(128)(4,1)} %bitcast.5), calls=%async_computation.2 | async-start | bytes 8388608
  18.9 8.0 %slice-start.1 = ((s8[6291456]{0:T(1024)(128)(4,1)}), s8[2097152]{0:T(1024)(128)(4,1)S(1)}, s32[]{:S(2)}) async-start(s8[6291456]{0:T(1024)(128)(4,1)} %bitcast.3), calls=%async_computation.1 | async-start | bytes 4194304
  18.9 8.0 %slice-start.3 = ((s8[6291456]{0:T(1024)(128)(4,1)}), s8[2097152]{0:T(1024)(128)(4,1)S(1)}, s32[]{:S(2)}) async-start(s8[6291456]{0:T(1024)(128)(4,1)} %bitcast.5), calls=%async_computation.3 | async-start | bytes 4194304
  19.0 7.9 %copy-start = (f32[2048]{0:T(1024)S(1)}, f32[2048]{0:T(1024)}, u32[]{:S(2)}) copy-start(f32[2048]{0:T(1024)} %param.16) | copy-start | bytes 24580
  20.9 9.6 %collective-permute-start.4 = (bf16[64,2048]{1,0:T(8,128)(2,1)S(1)}, bf16[64,2048]{1,0:T(8,128)(2,1)S(1)}, u32[]{:S(2)}, u32[]{:S(2)}) collective-permute-start(bf16[64,2048]{1,0:T(8,128)(2,1)S(1)} %shard_map.110.refs_4_.refs_5_.refs_0_), channel_id=1, source_target_pairs={{0,8},{4,12},{8,0},{12,4},{16,24},{20,28},{24,16},{28,20},{1,9},{5... | collective-permute-start | bytes 786440 | tf_op jit(solution)/shard_map/ppermute | solution.py:382
  22.4 8.1 %collective-permute-start.5 = (bf16[64,2048]{1,0:T(8,128)(2,1)S(1)}, bf16[64,2048]{1,0:T(8,128)(2,1)S(1)}, u32[]{:S(2)}, u32[]{:S(2)}) collective-permute-start(bf16[64,2048]{1,0:T(8,128)(2,1)S(1)} %shard_map.110.refs_4_.refs_5_.refs_0_), channel_id=1, source_target_pairs={{0,4},{4,0},{8,12},{12,8},{16,20},{20,16},{24,28},{28,24},{1,5},{5... | collective-permute-start | bytes 786440 | tf_op jit(solution)/shard_map/ppermute | solution.py:382
  23.9 11.0 %collective-permute-start.7 = (bf16[64,2048]{1,0:T(8,128)(2,1)S(1)}, bf16[64,2048]{1,0:T(8,128)(2,1)S(1)}, u32[]{:S(2)}, u32[]{:S(2)}) collective-permute-start(bf16[64,2048]{1,0:T(8,128)(2,1)S(1)} %shard_map.110.refs_4_.refs_5_.refs_0_), channel_id=1, source_target_pairs={{0,16},{4,20},{8,24},{12,28},{16,0},{20,4},{24,8},{28,12},{1,17},{... | collective-permute-start | bytes 786440 | tf_op jit(solution)/shard_map/ppermute | solution.py:382
  29.0 8.3 %collective-permute-start.3 = (bf16[64,1664]{1,0:T(8,128)(2,1)S(1)}, bf16[64,1664]{1,0:T(8,128)(2,1)S(1)}, u32[]{:S(2)}, u32[]{:S(2)}) collective-permute-start(bf16[64,1664]{1,0:T(8,128)(2,1)S(1)} %shard_map.111.refs_5_), channel_id=1, source_target_pairs={{0,2},{2,0},{1,3},{3,1},{4,6},{6,4},{5,7},{7,5},{8,10},{10,8},{9,1... | collective-permute-start | bytes 638984 | tf_op jit(solution)/shard_map/ppermute | solution.py:446
  31.5 17.0 %collective-permute-start.10 = (bf16[128,1664]{1,0:T(8,128)(2,1)S(1)}, bf16[128,1664]{1,0:T(8,128)(2,1)S(1)}, u32[]{:S(2)}, u32[]{:S(2)}) collective-permute-start(bf16[128,1664]{1,0:T(8,128)(2,1)S(1)} %shard_map.113.refs_4_), channel_id=1, source_target_pairs={{0,2},{2,0},{1,3},{3,1},{4,6},{6,4},{5,7},{7,5},{8,10},{10,8},{9,1... | collective-permute-start | bytes 1277960 | tf_op jit(solution)/shard_map/ppermute | solution.py:446
  34.9 6.4 %collective-permute-start.8 = (bf16[64,2048]{1,0:T(8,128)(2,1)S(1)}, bf16[64,2048]{1,0:T(8,128)(2,1)S(1)}, u32[]{:S(2)}, u32[]{:S(2)}) collective-permute-start(bf16[64,2048]{1,0:T(8,128)(2,1)S(1)} %collective-permute-done.7.refs_4_), channel_id=1, source_target_pairs={{0,8},{4,12},{8,0},{12,4},{16,24},{20,28},{24,16},{28,20},{1,9},{5... | collective-permute-start | bytes 786440 | tf_op jit(solution)/shard_map/ppermute | solution.py:382
  34.9 6.5 %collective-permute-start.9 = (bf16[64,2048]{1,0:T(8,128)(2,1)S(1)}, bf16[64,2048]{1,0:T(8,128)(2,1)S(1)}, u32[]{:S(2)}, u32[]{:S(2)}) collective-permute-start(bf16[64,2048]{1,0:T(8,128)(2,1)S(1)} %collective-permute-done.7.refs_4_), channel_id=1, source_target_pairs={{0,4},{4,0},{8,12},{12,8},{16,20},{20,16},{24,28},{28,24},{1,5},{5... | collective-permute-start | bytes 786440 | tf_op jit(solution)/shard_map/ppermute | solution.py:382
  37.4 10.1 %collective-permute-start.6 = (bf16[64,768]{1,0:T(8,128)(2,1)S(1)}, bf16[64,768]{1,0:T(8,128)(2,1)S(1)}, u32[]{:S(2)}, u32[]{:S(2)}) collective-permute-start(bf16[64,768]{1,0:T(8,128)(2,1)S(1)} %shard_map.114.refs_6_.refs_2_), channel_id=1, source_target_pairs={{0,2},{2,0},{1,3},{3,1},{4,6},{6,4},{5,7},{7,5},{8,10},{10,8},{9,1... | collective-permute-start | bytes 294920 | tf_op jit(solution)/shard_map/ppermute | solution.py:452
  39.0 37.8 %collective-permute-start.20 = (bf16[64,2048]{1,0:T(8,128)(2,1)S(1)}, bf16[64,2048]{1,0:T(8,128)(2,1)S(1)}, u32[]{:S(2)}, u32[]{:S(2)}) collective-permute-start(bf16[64,2048]{1,0:T(8,128)(2,1)S(1)} %collective-permute-done.4.refs_4_), channel_id=1, source_target_pairs={{0,4},{4,0},{8,12},{12,8},{16,20},{20,16},{24,28},{28,24},{1,5},{5... | collective-permute-start | bytes 786440 | tf_op jit(solution)/shard_map/ppermute | solution.py:382
  39.5 8.0 %slice-start.4 = ((s8[6291456]{0:T(1024)(128)(4,1)}), s8[4194304]{0:T(1024)(128)(4,1)S(1)}, s32[]{:S(2)}) async-start(s8[6291456]{0:T(1024)(128)(4,1)} %bitcast.19), calls=%async_computation.4 | async-start | bytes 8388608
  40.5 7.0 %slice-start.5 = ((s8[6291456]{0:T(1024)(128)(4,1)}), s8[2097152]{0:T(1024)(128)(4,1)S(1)}, s32[]{:S(2)}) async-start(s8[6291456]{0:T(1024)(128)(4,1)} %bitcast.19), calls=%async_computation.5 | async-start | bytes 4194304
  42.4 18.6 %collective-permute-start.15 = (bf16[128,1664]{1,0:T(8,128)(2,1)S(1)}, bf16[128,1664]{1,0:T(8,128)(2,1)S(1)}, u32[]{:S(2)}, u32[]{:S(2)}) collective-permute-start(bf16[128,1664]{1,0:T(8,128)(2,1)S(1)} %shard_map.116.refs_5_), channel_id=1, source_target_pairs={{0,2},{2,0},{1,3},{3,1},{4,6},{6,4},{5,7},{7,5},{8,10},{10,8},{9,1... | collective-permute-start | bytes 1277960 | tf_op jit(solution)/shard_map/ppermute | solution.py:446
  45.0 6.8 %collective-permute-start.12 = (bf16[64,2048]{1,0:T(8,128)(2,1)S(1)}, bf16[64,2048]{1,0:T(8,128)(2,1)S(1)}, u32[]{:S(2)}, u32[]{:S(2)}) collective-permute-start(bf16[64,2048]{1,0:T(8,128)(2,1)S(1)} %collective-permute-done.8.refs_4_), channel_id=1, source_target_pairs={{0,4},{4,0},{8,12},{12,8},{16,20},{20,16},{24,28},{28,24},{1,5},{5... | collective-permute-start | bytes 786440 | tf_op jit(solution)/shard_map/ppermute | solution.py:382
  48.9 11.1 %collective-permute-start.11 = (bf16[128,768]{1,0:T(8,128)(2,1)S(1)}, bf16[128,768]{1,0:T(8,128)(2,1)S(1)}, u32[]{:S(2)}, u32[]{:S(2)}) collective-permute-start(bf16[128,768]{1,0:T(8,128)(2,1)S(1)} %shard_map.118.refs_6_.refs_2_), channel_id=1, source_target_pairs={{0,2},{2,0},{1,3},{3,1},{4,6},{6,4},{5,7},{7,5},{8,10},{10,8},{9,1... | collective-permute-start | bytes 589832 | tf_op jit(solution)/shard_map/ppermute | solution.py:452
  52.9 11.8 %collective-permute-start.16 = (bf16[64,1664]{1,0:T(8,128)(2,1)S(1)}, bf16[64,1664]{1,0:T(8,128)(2,1)S(1)}, u32[]{:S(2)}, u32[]{:S(2)}) collective-permute-start(bf16[64,1664]{1,0:T(8,128)(2,1)S(1)} %shard_map.120.refs_5_), channel_id=1, source_target_pairs={{0,2},{2,0},{1,3},{3,1},{4,6},{6,4},{5,7},{7,5},{8,10},{10,8},{9,1... | collective-permute-start | bytes 638984 | tf_op jit(solution)/shard_map/ppermute | solution.py:446
  61.3 7.1 %collective-permute-start.18 = (bf16[128,768]{1,0:T(8,128)(2,1)S(1)}, bf16[128,768]{1,0:T(8,128)(2,1)S(1)}, u32[]{:S(2)}, u32[]{:S(2)}) collective-permute-start(bf16[128,768]{1,0:T(8,128)(2,1)S(1)} %shard_map.122.refs_5_.refs_2_), channel_id=1, source_target_pairs={{0,2},{2,0},{1,3},{3,1},{4,6},{6,4},{5,7},{7,5},{8,10},{10,8},{9,1... | collective-permute-start | bytes 589832 | tf_op jit(solution)/shard_map/ppermute | solution.py:452
  64.8 7.6 %collective-permute-start.17 = (bf16[64,768]{1,0:T(8,128)(2,1)S(1)}, bf16[64,768]{1,0:T(8,128)(2,1)S(1)}, u32[]{:S(2)}, u32[]{:S(2)}) collective-permute-start(bf16[64,768]{1,0:T(8,128)(2,1)S(1)} %shard_map.124.refs_5_.refs_2_), channel_id=1, source_target_pairs={{0,2},{2,0},{1,3},{3,1},{4,6},{6,4},{5,7},{7,5},{8,10},{10,8},{9,1... | collective-permute-start | bytes 294920 | tf_op jit(solution)/shard_map/ppermute | solution.py:452
  67.8 10.6 %collective-permute-start.19 = (bf16[64,1664]{1,0:T(8,128)(2,1)S(1)}, bf16[64,1664]{1,0:T(8,128)(2,1)S(1)}, u32[]{:S(2)}, u32[]{:S(2)}) collective-permute-start(bf16[64,1664]{1,0:T(8,128)(2,1)S(1)} %shard_map.125.refs_5_), channel_id=1, source_target_pairs={{0,2},{2,0},{1,3},{3,1},{4,6},{6,4},{5,7},{7,5},{8,10},{10,8},{9,1... | collective-permute-start | bytes 638984 | tf_op jit(solution)/shard_map/ppermute | solution.py:446
  69.5 15.8 %collective-permute-start.22 = (bf16[64,2048]{1,0:T(8,128)(2,1)S(1)}, bf16[64,2048]{1,0:T(8,128)(2,1)S(1)}, u32[]{:S(2)}, u32[]{:S(2)}) collective-permute-start(bf16[64,2048]{1,0:T(8,128)(2,1)S(1)} %get-tuple-element.11.refs_5_), channel_id=1, source_target_pairs={{0,8},{4,12},{8,0},{12,4},{16,24},{20,28},{24,16},{28,20},{1,9},{5... | collective-permute-start | bytes 786440 | tf_op jit(solution)/shard_map/ppermute | solution.py:382
  73.4 11.8 %collective-permute-start.24 = (bf16[64,2048]{1,0:T(8,128)(2,1)S(1)}, bf16[64,2048]{1,0:T(8,128)(2,1)S(1)}, u32[]{:S(2)}, u32[]{:S(2)}) collective-permute-start(bf16[64,2048]{1,0:T(8,128)(2,1)S(1)} %shard_map.127.refs_5_), channel_id=1, source_target_pairs={{0,12},{4,8},{8,4},{12,0},{16,28},{20,24},{24,20},{28,16},{1,13},{... | collective-permute-start | bytes 786440 | tf_op jit(solution)/shard_map/ppermute | solution.py:382
  74.2 11.1 %collective-permute-start.23 = (bf16[64,2048]{1,0:T(8,128)(2,1)S(1)}, bf16[64,2048]{1,0:T(8,128)(2,1)S(1)}, u32[]{:S(2)}, u32[]{:S(2)}) collective-permute-start(bf16[64,2048]{1,0:T(8,128)(2,1)S(1)} %get-tuple-element.12), channel_id=1, source_target_pairs={{0,4},{4,0},{8,12},{12,8},{16,20},{20,16},{24,28},{28,24},{1,5},{5... | collective-permute-start | bytes 786440 | tf_op jit(solution)/shard_map/ppermute | solution.py:382
  77.8 8.5 %collective-permute-start.26 = (bf16[64,1664]{1,0:T(8,128)(2,1)S(1)}, bf16[64,1664]{1,0:T(8,128)(2,1)S(1)}, u32[]{:S(2)}, u32[]{:S(2)}) collective-permute-start(bf16[64,1664]{1,0:T(8,128)(2,1)S(1)} %shard_map.129.refs_4_), channel_id=1, source_target_pairs={{0,2},{2,0},{1,3},{3,1},{4,6},{6,4},{5,7},{7,5},{8,10},{10,8},{9,1... | collective-permute-start | bytes 638984 | tf_op jit(solution)/shard_map/ppermute | solution.py:446
  78.7 6.6 %collective-permute-start.21 = (bf16[64,768]{1,0:T(8,128)(2,1)S(1)}, bf16[64,768]{1,0:T(8,128)(2,1)S(1)}, u32[]{:S(2)}, u32[]{:S(2)}) collective-permute-start(bf16[64,768]{1,0:T(8,128)(2,1)S(1)} %shard_map.130.refs_5_.refs_2_), channel_id=1, source_target_pairs={{0,2},{2,0},{1,3},{3,1},{4,6},{6,4},{5,7},{7,5},{8,10},{10,8},{9,1... | collective-permute-start | bytes 294920 | tf_op jit(solution)/shard_map/ppermute | solution.py:452
  86.6 4.7 %collective-permute-start.27 = (bf16[64,768]{1,0:T(8,128)(2,1)S(1)}, bf16[64,768]{1,0:T(8,128)(2,1)S(1)}, u32[]{:S(2)}, u32[]{:S(2)}) collective-permute-start(bf16[64,768]{1,0:T(8,128)(2,1)S(1)} %shard_map.133.refs_2_.refs_5_), channel_id=1, source_target_pairs={{0,2},{2,0},{1,3},{3,1},{4,6},{6,4},{5,7},{7,5},{8,10},{10,8},{9,1... | collective-permute-start | bytes 294920 | tf_op jit(solution)/shard_map/ppermute | solution.py:452
  87.0 7.2 %collective-permute-start.13 = (bf16[64,2048]{1,0:T(8,128)(2,1)S(1)}, bf16[64,2048]{1,0:T(8,128)(2,1)S(1)}, u32[]{:S(2)}, u32[]{:S(2)}) collective-permute-start(bf16[64,2048]{1,0:T(8,128)(2,1)S(1)} %get-tuple-element.9.refs_4_), channel_id=1, source_target_pairs={{0,8},{4,12},{8,0},{12,4},{16,24},{20,28},{24,16},{28,20},{1,9},{5... | collective-permute-start | bytes 786440 | tf_op jit(solution)/shard_map/ppermute | solution.py:382
  88.8 6.4 %collective-permute-start.14 = (bf16[64,2048]{1,0:T(8,128)(2,1)S(1)}, bf16[64,2048]{1,0:T(8,128)(2,1)S(1)}, u32[]{:S(2)}, u32[]{:S(2)}) collective-permute-start(bf16[64,2048]{1,0:T(8,128)(2,1)S(1)} %get-tuple-element.10), channel_id=1, source_target_pairs={{0,4},{4,0},{8,12},{12,8},{16,20},{20,16},{24,28},{28,24},{1,5},{5... | collective-permute-start | bytes 786440 | tf_op jit(solution)/shard_map/ppermute | solution.py:382
  90.5 10.2 %collective-permute-start.25 = (bf16[64,2048]{1,0:T(8,128)(2,1)S(1)}, bf16[64,2048]{1,0:T(8,128)(2,1)S(1)}, u32[]{:S(2)}, u32[]{:S(2)}) collective-permute-start(bf16[64,2048]{1,0:T(8,128)(2,1)S(1)} %shard_map.132.refs_4_), channel_id=1, source_target_pairs={{0,16},{4,20},{8,24},{12,28},{16,0},{20,4},{24,8},{28,12},{1,17},{... | collective-permute-start | bytes 786440 | tf_op jit(solution)/shard_map/ppermute | solution.py:382
  92.2 8.5 %collective-permute-start.28 = (bf16[64,2048]{1,0:T(8,128)(2,1)S(1)}, bf16[64,2048]{1,0:T(8,128)(2,1)S(1)}, u32[]{:S(2)}, u32[]{:S(2)}) collective-permute-start(bf16[64,2048]{1,0:T(8,128)(2,1)S(1)} %shard_map.134.refs_6_), channel_id=1, source_target_pairs={{0,12},{4,8},{8,4},{12,0},{16,28},{20,24},{24,20},{28,16},{1,13},{... | collective-permute-start | bytes 786440 | tf_op jit(solution)/shard_map/ppermute | solution.py:382

commit v5 on v4

--- a/solution.py
+++ b/solution.py
@@ -18,12 +18,17 @@
 NORM_EPS = 1e-06
 LANES = 128
 KERNEL_BYTES = 16 * 1024 * 1024
-ROUTE_LANES = 16
+EXPERT_ROWS = 16
 HELD = False
 COST = 2e9
-PACK_COST = 5
+FIRST_COST = 1.2
+HIDDEN_COST = 0.4
+BOTH_COST = 1.1
+PACK_COST = 10
 ATT_COST = 5
 HOPS = ((0, 4), (0, 1), (4, 2), (4, 1), (6, 1), (0, 2), (2, 1))
+COSTS = {}
+LATER = (2,)
 CHUNKS = ((0,), (2, 1), (6, 5), (7,), (4,), (3,))
 SENDS = {0: 0, 1: 1, 2: 2, 3: 3, 4: 4, 5: 1, 6: 2, 7: 3}
 STEPS = (
@@ -37,16 +42,18 @@
     ("hidden", 1),
     ("keep", 2),
     ("send", 3),
+    ("hidden", 2),
     ("both", 1),
-    ("hidden", 2),
     ("keep", 3),
     ("hidden", 3),
     ("send", 4),
     ("both", 2),
     ("both", 3),
+    ("got", 1),
+    ("got", 2),
     ("keep", 4),
+    ("hidden", 4),
     ("send", 5),
-    ("hidden", 4),
     ("keep", 5),
     ("both", 4),
     ("hidden", 5),
@@ -200,23 +207,27 @@
     return (mixed_f + routed_sum).astype(jnp.bfloat16)
 
 
-def pack_kernel(key_ref, value_ref, high_ref, low_ref, out_ref):
-    out_ref[:, :HEAD_SIZE] = key_ref[...]
-    out_ref[:, HEAD_SIZE : 2 * HEAD_SIZE] = value_ref[...]
-    out_ref[:, 2 * HEAD_SIZE : 2 * HEAD_SIZE + ROUTE_LANES] = high_ref[...]
-    out_ref[:, 2 * HEAD_SIZE + ROUTE_LANES : 2 * HEAD_SIZE + 2 * ROUTE_LANES] = low_ref[...]
+def pack_kernel(key_ref, value_ref, route_ref, out_ref):
+    rows = key_ref.shape[0]
+    out_ref[:rows] = key_ref[...]
+    out_ref[rows : 2 * rows] = value_ref[...]
+    out_ref[2 * rows :] = route_ref[...]
 
 
 def attention_kernel(place_ref, order_ref, query_ref, packed_ref, residual_ref, out_ref):
     rows = query_ref.shape[0]
     heads = query_ref.shape[1] // HEAD_SIZE
-    count = packed_ref.shape[0]
+    block = 2 * rows + EXPERT_ROWS
+    starts = range(0, packed_ref.shape[0], block)
+    count = len(starts) * rows
+    keys = jnp.concatenate([packed_ref[i : i + rows] for i in starts], axis=0)
+    values = jnp.concatenate([packed_ref[i + rows : i + 2 * rows] for i in starts], axis=0)
     queries = jnp.concatenate(
         [query_ref[:, h * HEAD_SIZE : (h + 1) * HEAD_SIZE] for h in range(heads)], axis=0
     )
     scores = lax.dot_general(
         queries,
-        packed_ref[:, :HEAD_SIZE],
+        keys,
         (((1,), (1,)), ((), ())),
         preferred_element_type=jnp.float32,
     ) * (1.0 / math.sqrt(HEAD_SIZE))
@@ -233,7 +244,7 @@
     weight_sum = jnp.sum(weights, axis=1, keepdims=True)
     weighted = jnp.dot(
         weights.astype(jnp.bfloat16),
-        packed_ref[:, HEAD_SIZE : 2 * HEAD_SIZE],
+        values,
         preferred_element_type=jnp.float32,
     )
     attention = (weighted / weight_sum).astype(jnp.bfloat16)
@@ -283,12 +294,16 @@
         jnp.float32
     )
     scale = lax.rsqrt((tail[:, :1] + tail[:, 1:2]) / D + NORM_EPS)
-    route = jnp.concatenate(
-        [packed_ref[place * rows : (place + 1) * rows, 2 * HEAD_SIZE :] for place in places], axis=0
-    ).astype(jnp.float32)
-    lane = lax.broadcasted_iota(jnp.int32, route.shape, 1)
-    named = (lane == index_ref[0]) | (lane == index_ref[0] + ROUTE_LANES)
-    route = jnp.sum(jnp.where(named, route, 0.0), axis=1, keepdims=True)
+    block = 2 * rows + EXPERT_ROWS
+    expert = lax.broadcasted_iota(jnp.int32, (EXPERT_ROWS, 2 * rows), 0)
+    row = lax.broadcasted_iota(jnp.int32, (rows, 2 * rows), 0)
+    lane = lax.broadcasted_iota(jnp.int32, (rows, 2 * rows), 1)
+    columns = []
+    for place in places:
+        part = packed_ref[place * block + 2 * rows : (place + 1) * block].astype(jnp.float32)
+        line = jnp.sum(jnp.where(expert == index_ref[0], part, 0.0), axis=0, keepdims=True)
+        columns.append(jnp.sum(jnp.where(lane % rows == row, line, 0.0), axis=1, keepdims=True))
+    route = jnp.concatenate(columns, axis=0)
     gate = kept_ref[:, :size].astype(jnp.float32) + arrived_ref[:, :size].astype(jnp.float32)
     up = kept_ref[:, size : 2 * size].astype(jnp.float32) + arrived_ref[
         :, size : 2 * size
@@ -382,17 +397,16 @@
         return lax.ppermute(block, "ctx", xor_pairs(ctx_count, offset))
 
     columns = mine[0] * HEAD_SIZE
-    experts = jnp.arange(ROUTE_LANES, dtype=jnp.int32)
-    named = expert_ids[:, :, None] == experts[None, None, :]
-    route = jnp.sum(jnp.where(named, route_weight[:, :, None], 0.0), axis=1)
+    experts = jnp.arange(EXPERT_ROWS, dtype=jnp.int32)
+    named = expert_ids.T[:, None, :] == experts[None, :, None]
+    route = jnp.sum(jnp.where(named, route_weight.T[:, None, :], 0.0), axis=0)
     high = lax.reduce_precision(route, 8, 7)
     packed = core(
         pack_kernel,
-        of((rows, 2 * HEAD_SIZE + LANES)),
+        of((2 * rows + EXPERT_ROWS, HEAD_SIZE)),
         lax.dynamic_slice_in_dim(key_rows, columns, HEAD_SIZE, 1),
         lax.dynamic_slice_in_dim(value_head_rows, columns, HEAD_SIZE, 1),
-        high.astype(jnp.bfloat16),
-        (route - high).astype(jnp.bfloat16),
+        jnp.concatenate([high, route - high], axis=1).astype(jnp.bfloat16),
         cost=PACK_COST,
     )
     packed = gather_rows(packed, ctx_count)
@@ -422,8 +436,19 @@
         if step == "sum":
             total = core(sum_kernel, of((rows, features)), mixed_rows, *terms[0])
             continue
+        if step == "got":
+            core.also.append(terms[0][i])
+            continue
         if step == "pin":
             core.also.append(other_hidden[i])
+            continue
+        if step == "later":
+            again = core(copy_kernel, of((rows, features)), block[0], cost=0.2)
+            for offset in LATER:
+                block[offset] = hop(again, offset)
+            continue
+        if step == "need":
+            core.also.append(block[i])
             continue
         if step == "on":
             source, offset = i
@@ -440,7 +465,7 @@
                 gate_weight,
                 up_weight,
                 *[block[offset] for offset in chunk],
-                cost=1.2,
+                cost=COSTS.get((step, i), FIRST_COST),
             )
             if step == "send":
                 arrived[i] = lax.ppermute(product, "exp", swap)
@@ -448,7 +473,7 @@
                 kept[i] = product
         elif step == "hidden":
             kernel = functools.partial(hidden_kernel, [position[offset] for offset in chunk])
-            hidden[i] = core(kernel, of((count, size)), expert, kept[i], arrived[i], packed, cost=0.4)
+            hidden[i] = core(kernel, of((count, size)), expert, kept[i], arrived[i], packed, cost=HIDDEN_COST)
             other_hidden[i] = lax.ppermute(hidden[i], "exp", swap)
         else:
             shapes = [of((rows, features), jnp.bfloat16 if o else jnp.float32) for o in chunk]
@@ -459,7 +484,7 @@
                 shapes,
                 mine, other, hidden[i], other_hidden[i], down_weight,
                 *[term for _, term in arrivals],
-                cost=1.1,
+                cost=BOTH_COST,
             )
             for offset, term in zip(chunk, out):
                 term = hop(term, SENDS[offset]) if offset else term

time: 102 us -> 100 us (0.980)
    ppermute x6, waiting for transfers between devices: 11.5 us -> 5.68 us  [local(): other_hidden[i] = lax.ppermute(hidden[i], 'exp', swap)]
    ppermute x6, waiting for transfers between devices: 0.73 us -> 4.41 us  [local(): arrived[i] = lax.ppermute(product, 'exp', swap)]
    ppermute x14, starting transfers between devices: 21.9 us -> 18.6 us  [hop(): return lax.ppermute(block, 'ctx', xor_pairs(ctx_count, offset))]
    ppermute x14, waiting for transfers between devices: 11.9 us -> 14.6 us  [hop(): return lax.ppermute(block, 'ctx', xor_pairs(ctx_count, offset))]
    ppermute x6, starting transfers between devices: 7.96 us -> 9.51 us  [local(): other_hidden[i] = lax.ppermute(hidden[i], 'exp', swap)]
    ppermute x3, waiting for transfers between devices: 9.78 us -> 8.59 us  [gather_rows(): lax.ppermute(block, 'ctx', xor_pairs(count, bit))]
    ppermute x6, starting transfers between devices: 5.82 us -> 6.88 us  [local(): arrived[i] = lax.ppermute(product, 'exp', swap)]
  transfers between devices with their start and end apart: 29 -> 29, of which waited for: 14 -> 16; matrix products, arithmetic and copies ran while one was open for 0% -> 0% of each run, Pallas kernels for 19% -> 19%
where the time goes in v5:
time: 100 us
  starting transfers between devices  42.4 us (42%)
  waiting for transfers between devices  33.3 us (33%)
  Pallas kernels  22.5 us (22%)
    pallas_call x27, Pallas kernels, __call__(): pl.pallas_call(body, out_shape=out_shape, in_specs=specs, out_specs=[vmem...  22.5 us
    ppermute x14, starting transfers between devices, hop(): return lax.ppermute(block, 'ctx', xor_pairs(ctx_count, offset))  18.6 us
    ppermute x14, waiting for transfers between devices, hop(): return lax.ppermute(block, 'ctx', xor_pairs(ctx_count, offset))  14.6 us
    ppermute x6, starting transfers between devices, local(): other_hidden[i] = lax.ppermute(hidden[i], 'exp', swap)  9.51 us
    ppermute x3, waiting for transfers between devices, gather_rows(): lax.ppermute(block, 'ctx', xor_pairs(count, bit))  8.59 us
    ppermute x3, starting transfers between devices, gather_rows(): lax.ppermute(block, 'ctx', xor_pairs(count, bit))  7.41 us
    ppermute x6, starting transfers between devices, local(): arrived[i] = lax.ppermute(product, 'exp', swap)  6.88 us
    ppermute x6, waiting for transfers between devices, local(): other_hidden[i] = lax.ppermute(hidden[i], 'exp', swap)  5.68 us
  transfers between devices with their start and end apart: 29, of which 16 were waited for; matrix products, arithmetic and copies ran while one was open for 0% of the time, Pallas kernels for 19%

profile of v5, /device:TPU:0, one launch (start us, length us, event | category | flops | bytes accessed | tf_op | source)
XLA Modules:
  0.0 100.2 jit_solution(6753004029655391268)
XLA Ops:
  1.6 4.1 %collective-permute-start = (bf16[144,128]{1,0:T(8,128)(2,1)S(1)}, bf16[144,128]{1,0:T(8,128)(2,1)S(1)}, u32[]{:S(2)}, u32[]{:S(2)}) collective-permute-start(bf16[144,128]{1,0:T(8,128)(2,1)S(1)} %shard_map.109.refs_5_), channel_id=1, source_target_pairs={{0,16},{4,20},{8,24},{12,28},{16,0},{20,4},{24,8},{28,12},{1,17},{... | collective-permute-start | bytes 110600 | tf_op jit(solution)/shard_map/ppermute | solution.py:78
  5.7 2.3 %collective-permute-done = bf16[144,128]{1,0:T(8,128)(2,1)S(1)} collective-permute-done((bf16[144,128]{1,0:T(8,128)(2,1)S(1)}, bf16[144,128]{1,0:T(8,128)(2,1)S(1)}, u32[]{:S(2)}, u32[]{:S(2)}) %collective-permute-start) | collective-permute-done | bytes 36896 | tf_op jit(solution)/shard_map/ppermute | solution.py:78
  8.0 1.5 %collective-permute-start.1 = (bf16[288,128]{1,0:T(8,128)(2,1)S(1)}, bf16[288,128]{1,0:T(8,128)(2,1)S(1)}, u32[]{:S(2)}, u32[]{:S(2)}) collective-permute-start(bf16[288,128]{1,0:T(8,128)(2,1)S(1)} %pad_maximum_fusion.2), channel_id=1, source_target_pairs={{0,8},{4,12},{8,0},{12,4},{16,24},{20,28},{24,16},{28,20},{1,9},{5... | collective-permute-start | bytes 221192 | tf_op jit(solution)/shard_map/ppermute | solution.py:78
  9.5 2.8 %collective-permute-done.1 = bf16[288,128]{1,0:T(8,128)(2,1)S(1)} collective-permute-done((bf16[288,128]{1,0:T(8,128)(2,1)S(1)}, bf16[288,128]{1,0:T(8,128)(2,1)S(1)}, u32[]{:S(2)}, u32[]{:S(2)}) %collective-permute-start.1) | collective-permute-done | bytes 73760 | tf_op jit(solution)/shard_map/ppermute | solution.py:78
  12.4 1.8 %collective-permute-start.2 = (bf16[576,128]{1,0:T(8,128)(2,1)S(1)}, bf16[576,128]{1,0:T(8,128)(2,1)S(1)}, u32[]{:S(2)}, u32[]{:S(2)}) collective-permute-start(bf16[576,128]{1,0:T(8,128)(2,1)S(1)} %pad_maximum_fusion.1), channel_id=1, source_target_pairs={{0,4},{4,0},{8,12},{12,8},{16,20},{20,16},{24,28},{28,24},{1,5},{5... | collective-permute-start | bytes 442376 | tf_op jit(solution)/shard_map/ppermute | solution.py:78
  14.2 3.4 %collective-permute-done.2 = bf16[576,128]{1,0:T(8,128)(2,1)S(1)} collective-permute-done((bf16[576,128]{1,0:T(8,128)(2,1)S(1)}, bf16[576,128]{1,0:T(8,128)(2,1)S(1)}, u32[]{:S(2)}, u32[]{:S(2)}) %collective-permute-start.2) | collective-permute-done | bytes 147488 | tf_op jit(solution)/shard_map/ppermute | solution.py:78
  17.7 2.0 %shard_map.110.refs_4_.refs_5_.refs_0_ = bf16[64,2048]{1,0:T(8,128)(2,1)S(1)} custom-call(s32[1]{0:T(128)} %bitcast.refs_0_, s32[8]{0:T(128)S(1)} %copy-done.5, bf16[64,2048]{1,0:T(8,128)(2,1)S(1)} %copy-done.3, bf16[1152,128]{1,0:T(8,128)(2,1)S(1)} %pad_maximum_fusion.refs_3_, bf16[64,2048]{1,0:T(8,128)(2,1)S(1)} %copy-done.4, ...), custom_call_target="tpu_custom_call" | custom-call | flops 10000000000 | tf_op jit(solution)/shard_map/pallas_call | solution.py:354
  19.6 1.6 %collective-permute-start.4 = (bf16[64,2048]{1,0:T(8,128)(2,1)S(1)}, bf16[64,2048]{1,0:T(8,128)(2,1)S(1)}, u32[]{:S(2)}, u32[]{:S(2)}) collective-permute-start(bf16[64,2048]{1,0:T(8,128)(2,1)S(1)} %shard_map.110.refs_4_.refs_5_.refs_0_), channel_id=1, source_target_pairs={{0,8},{4,12},{8,0},{12,4},{16,24},{20,28},{24,16},{28,20},{1,9},{5... | collective-permute-start | bytes 786440 | tf_op jit(solution)/shard_map/ppermute | solution.py:397
  21.2 1.5 %collective-permute-start.5 = (bf16[64,2048]{1,0:T(8,128)(2,1)S(1)}, bf16[64,2048]{1,0:T(8,128)(2,1)S(1)}, u32[]{:S(2)}, u32[]{:S(2)}) collective-permute-start(bf16[64,2048]{1,0:T(8,128)(2,1)S(1)} %shard_map.110.refs_4_.refs_5_.refs_0_), channel_id=1, source_target_pairs={{0,4},{4,0},{8,12},{12,8},{16,20},{20,16},{24,28},{28,24},{1,5},{5... | collective-permute-start | bytes 786440 | tf_op jit(solution)/shard_map/ppermute | solution.py:397
  22.7 2.9 %collective-permute-start.7 = (bf16[64,2048]{1,0:T(8,128)(2,1)S(1)}, bf16[64,2048]{1,0:T(8,128)(2,1)S(1)}, u32[]{:S(2)}, u32[]{:S(2)}) collective-permute-start(bf16[64,2048]{1,0:T(8,128)(2,1)S(1)} %shard_map.110.refs_4_.refs_5_.refs_0_), channel_id=1, source_target_pairs={{0,16},{4,20},{8,24},{12,28},{16,0},{20,4},{24,8},{28,12},{1,17},{... | collective-permute-start | bytes 786440 | tf_op jit(solution)/shard_map/ppermute | solution.py:397
  25.6 1.0 shard_map.111.refs_5_
  26.6 1.0 %shard_map.112.refs_6_.refs_1_ = bf16[64,1664]{1,0:T(8,128)(2,1)S(1)} custom-call(s32[1]{0:T(128)} %bitcast.3.refs_0_, f32[1,2048]{1,0:T(1,128)S(1)} %bitcast.6, bf16[2,2048,768]{2,1,0:T(8,128)(2,1)S(1)} %copy-done, bf16[2,2048,768]{2,1,0:T(8,128)(2,1)S(1)} %copy-done.1, bf16[64,2048]{1,0:T(8,128)(2,1)S(1)} %shard_map.110.refs_4_.refs_5_.refs_0_, ...), custom_call_target="tpu_custom_call" | custom-call | flops 2400000000 | tf_op jit(solution)/shard_map/pallas_call | solution.py:354
  27.6 1.6 %collective-permute-start.3 = (bf16[64,1664]{1,0:T(8,128)(2,1)S(1)}, bf16[64,1664]{1,0:T(8,128)(2,1)S(1)}, u32[]{:S(2)}, u32[]{:S(2)}) collective-permute-start(bf16[64,1664]{1,0:T(8,128)(2,1)S(1)} %shard_map.111.refs_5_), channel_id=1, source_target_pairs={{0,2},{2,0},{1,3},{3,1},{4,6},{6,4},{5,7},{7,5},{8,10},{10,8},{9,1... | collective-permute-start | bytes 638984 | tf_op jit(solution)/shard_map/ppermute | solution.py:471
  29.2 1.0 %shard_map.113.refs_4_ = bf16[128,1664]{1,0:T(8,128)(2,1)S(1)} custom-call(s32[1]{0:T(128)S(6)} %sub.7.refs_0_.refs_1_, f32[1,2048]{1,0:T(1,128)S(1)} %bitcast.7, bf16[2,2048,768]{2,1,0:T(8,128)(2,1)S(1)} %copy-done, bf16[2,2048,768]{2,1,0:T(8,128)(2,1)S(1)} %copy-done.1, bf16[64,2048]{1,0:T(8,128)(2,1)S(1)} %collective-permute-done.4.refs_4_, ...), custom_call_target="tpu_custom_call" | custom-call | flops 2400000000 | tf_op jit(solution)/shard_map/pallas_call | solution.py:354
  30.8 2.8 %collective-permute-done.7.refs_4_ = bf16[64,2048]{1,0:T(8,128)(2,1)S(1)} collective-permute-done((bf16[64,2048]{1,0:T(8,128)(2,1)S(1)}, bf16[64,2048]{1,0:T(8,128)(2,1)S(1)}, u32[]{:S(2)}, u32[]{:S(2)}) %collective-permute-start.7) | collective-permute-done | bytes 262176 | tf_op jit(solution)/shard_map/ppermute | solution.py:397
  33.6 1.6 %collective-permute-start.9 = (bf16[64,2048]{1,0:T(8,128)(2,1)S(1)}, bf16[64,2048]{1,0:T(8,128)(2,1)S(1)}, u32[]{:S(2)}, u32[]{:S(2)}) collective-permute-start(bf16[64,2048]{1,0:T(8,128)(2,1)S(1)} %collective-permute-done.7.refs_4_), channel_id=1, source_target_pairs={{0,4},{4,0},{8,12},{12,8},{16,20},{20,16},{24,28},{28,24},{1,5},{5... | collective-permute-start | bytes 786440 | tf_op jit(solution)/shard_map/ppermute | solution.py:397
  36.1 1.6 %collective-permute-start.6 = (bf16[64,768]{1,0:T(8,128)(2,1)S(1)}, bf16[64,768]{1,0:T(8,128)(2,1)S(1)}, u32[]{:S(2)}, u32[]{:S(2)}) collective-permute-start(bf16[64,768]{1,0:T(8,128)(2,1)S(1)} %shard_map.114.refs_6_.refs_2_), channel_id=1, source_target_pairs={{0,2},{2,0},{1,3},{3,1},{4,6},{6,4},{5,7},{7,5},{8,10},{10,8},{9,1... | collective-permute-start | bytes 294920 | tf_op jit(solution)/shard_map/ppermute | solution.py:477
  38.2 1.0 %shard_map.115.refs_6_.refs_1_ = bf16[128,1664]{1,0:T(8,128)(2,1)S(1)} custom-call(s32[1]{0:T(128)} %bitcast.3.refs_0_, f32[1,2048]{1,0:T(1,128)S(1)} %bitcast.8, bf16[2,2048,768]{2,1,0:T(8,128)(2,1)S(1)} %copy-done, bf16[2,2048,768]{2,1,0:T(8,128)(2,1)S(1)} %copy-done.1, bf16[64,2048]{1,0:T(8,128)(2,1)S(1)} %collective-permute-done.4.refs_4_, ...), custom_call_target="tpu_custom_call" | custom-call | flops 2400000000 | tf_op jit(solution)/shard_map/pallas_call | solution.py:354
  40.1 1.0 %shard_map.116.refs_5_ = bf16[128,1664]{1,0:T(8,128)(2,1)S(1)} custom-call(s32[1]{0:T(128)S(6)} %sub.7.refs_0_.refs_1_, f32[1,2048]{1,0:T(1,128)S(1)} %bitcast.9, bf16[2,2048,768]{2,1,0:T(8,128)(2,1)S(1)} %copy-done, bf16[2,2048,768]{2,1,0:T(8,128)(2,1)S(1)} %copy-done.1, bf16[64,2048]{1,0:T(8,128)(2,1)S(1)} %collective-permute-done.8.refs_4_, ...), custom_call_target="tpu_custom_call" | custom-call | flops 2400000000 | tf_op jit(solution)/shard_map/pallas_call | solution.py:354
  41.1 2.6 %collective-permute-start.12 = (bf16[128,1664]{1,0:T(8,128)(2,1)S(1)}, bf16[128,1664]{1,0:T(8,128)(2,1)S(1)}, u32[]{:S(2)}, u32[]{:S(2)}) collective-permute-start(bf16[128,1664]{1,0:T(8,128)(2,1)S(1)} %shard_map.116.refs_5_), channel_id=1, source_target_pairs={{0,2},{2,0},{1,3},{3,1},{4,6},{6,4},{5,7},{7,5},{8,10},{10,8},{9,1... | collective-permute-start | bytes 1277960 | tf_op jit(solution)/shard_map/ppermute | solution.py:471
  43.7 2.5 %collective-permute-start.13 = (bf16[64,2048]{1,0:T(8,128)(2,1)S(1)}, bf16[64,2048]{1,0:T(8,128)(2,1)S(1)}, u32[]{:S(2)}, u32[]{:S(2)}) collective-permute-start(bf16[64,2048]{1,0:T(8,128)(2,1)S(1)} %collective-permute-done.8.refs_4_), channel_id=1, source_target_pairs={{0,4},{4,0},{8,12},{12,8},{16,20},{20,16},{24,28},{28,24},{1,5},{5... | collective-permute-start | bytes 786440 | tf_op jit(solution)/shard_map/ppermute | solution.py:397
  46.2 1.0 shard_map.117.refs_4_.refs_1_
  47.7 1.0 %shard_map.119.refs_5_.refs_1_ = bf16[128,1664]{1,0:T(8,128)(2,1)S(1)} custom-call(s32[1]{0:T(128)} %bitcast.3.refs_0_, f32[1,2048]{1,0:T(1,128)S(1)} %bitcast.10, bf16[2,2048,768]{2,1,0:T(8,128)(2,1)S(1)} %copy-done, bf16[2,2048,768]{2,1,0:T(8,128)(2,1)S(1)} %copy-done.1, bf16[64,2048]{1,0:T(8,128)(2,1)S(1)} %collective-permute-done.8.refs_4_, ...), custom_call_target="tpu_custom_call" | custom-call | flops 2400000000 | tf_op jit(solution)/shard_map/pallas_call | solution.py:354
  48.7 1.8 %collective-permute-done.13.refs_4_ = bf16[64,2048]{1,0:T(8,128)(2,1)S(1)} collective-permute-done((bf16[64,2048]{1,0:T(8,128)(2,1)S(1)}, bf16[64,2048]{1,0:T(8,128)(2,1)S(1)}, u32[]{:S(2)}, u32[]{:S(2)}) %collective-permute-start.13) | collective-permute-done | bytes 262176 | tf_op jit(solution)/shard_map/ppermute | solution.py:397
  50.5 1.0 shard_map.120.refs_4_
  51.8 2.7 %collective-permute-done.12.refs_2_ = bf16[128,1664]{1,0:T(8,128)(2,1)S(1)} collective-permute-done((bf16[128,1664]{1,0:T(8,128)(2,1)S(1)}, bf16[128,1664]{1,0:T(8,128)(2,1)S(1)}, u32[]{:S(2)}, u32[]{:S(2)}) %collective-permute-start.12) | collective-permute-done | bytes 426016 | tf_op jit(solution)/shard_map/ppermute | solution.py:471
  54.8 2.1 %collective-permute-start.18 = (bf16[128,768]{1,0:T(8,128)(2,1)S(1)}, bf16[128,768]{1,0:T(8,128)(2,1)S(1)}, u32[]{:S(2)}, u32[]{:S(2)}) collective-permute-start(bf16[128,768]{1,0:T(8,128)(2,1)S(1)} %shard_map.121.refs_5_.refs_2_), channel_id=1, source_target_pairs={{0,2},{2,0},{1,3},{3,1},{4,6},{6,4},{5,7},{7,5},{8,10},{10,8},{9,1... | collective-permute-start | bytes 589832 | tf_op jit(solution)/shard_map/ppermute | solution.py:477
  56.9 1.8 %collective-permute-done.11.refs_3_ = bf16[128,768]{1,0:T(8,128)(2,1)S(1)} collective-permute-done((bf16[128,768]{1,0:T(8,128)(2,1)S(1)}, bf16[128,768]{1,0:T(8,128)(2,1)S(1)}, u32[]{:S(2)}, u32[]{:S(2)}) %collective-permute-start.11) | collective-permute-done | bytes 196640 | tf_op jit(solution)/shard_map/ppermute | solution.py:477
  58.7 1.0 %shard_map.122 = (bf16[64,2048]{1,0:T(8,128)(2,1)S(1)}, bf16[64,2048]{1,0:T(8,128)(2,1)S(1)}) custom-call(s32[1]{0:T(128)} %bitcast.3.refs_0_, s32[1]{0:T(128)S(6)} %sub.7.refs_0_.refs_1_, bf16[128,768]{1,0:T(8,128)(2,1)S(1)} %shard_map.118.refs_6_.refs_2_, bf16[128,768]{1,0:T(8,128)(2,1)S(1)} %collective-permute-done.11.refs_3_, ...), custom_call_target="tpu_custom_call" | custom-call | flops 2200000000 | tf_op jit(solution)/shard_map/pallas_call | solution.py:354
  59.7 2.3 %collective-permute-start.14 = (bf16[64,2048]{1,0:T(8,128)(2,1)S(1)}, bf16[64,2048]{1,0:T(8,128)(2,1)S(1)}, u32[]{:S(2)}, u32[]{:S(2)}) collective-permute-start(bf16[64,2048]{1,0:T(8,128)(2,1)S(1)} %get-tuple-element.9.refs_5_), channel_id=1, source_target_pairs={{0,8},{4,12},{8,0},{12,4},{16,24},{20,28},{24,16},{28,20},{1,9},{5... | collective-permute-start | bytes 786440 | tf_op jit(solution)/shard_map/ppermute | solution.py:397
  62.5 1.0 %shard_map.123.refs_1_.refs_4_ = bf16[64,1664]{1,0:T(8,128)(2,1)S(1)} custom-call(s32[1]{0:T(128)} %bitcast.3.refs_0_, f32[1,2048]{1,0:T(1,128)S(1)} %bitcast.12, bf16[2,2048,768]{2,1,0:T(8,128)(2,1)S(1)} %copy-done, bf16[2,2048,768]{2,1,0:T(8,128)(2,1)S(1)} %copy-done.1, bf16[64,2048]{1,0:T(8,128)(2,1)S(1)} %collective-permute-done.13.refs_4_, ...), custom_call_target="tpu_custom_call" | custom-call | flops 2400000000 | tf_op jit(solution)/shard_map/pallas_call | solution.py:354
  63.7 2.1 %collective-permute-start.17 = (bf16[64,768]{1,0:T(8,128)(2,1)S(1)}, bf16[64,768]{1,0:T(8,128)(2,1)S(1)}, u32[]{:S(2)}, u32[]{:S(2)}) collective-permute-start(bf16[64,768]{1,0:T(8,128)(2,1)S(1)} %shard_map.124.refs_5_.refs_2_), channel_id=1, source_target_pairs={{0,2},{2,0},{1,3},{3,1},{4,6},{6,4},{5,7},{7,5},{8,10},{10,8},{9,1... | collective-permute-start | bytes 294920 | tf_op jit(solution)/shard_map/ppermute | solution.py:477
  66.8 1.8 %collective-permute-start.19 = (bf16[64,1664]{1,0:T(8,128)(2,1)S(1)}, bf16[64,1664]{1,0:T(8,128)(2,1)S(1)}, u32[]{:S(2)}, u32[]{:S(2)}) collective-permute-start(bf16[64,1664]{1,0:T(8,128)(2,1)S(1)} %shard_map.125.refs_5_), channel_id=1, source_target_pairs={{0,2},{2,0},{1,3},{3,1},{4,6},{6,4},{5,7},{7,5},{8,10},{10,8},{9,1... | collective-permute-start | bytes 638984 | tf_op jit(solution)/shard_map/ppermute | solution.py:471
  68.6 1.0 %shard_map.126 = (bf16[64,2048]{1,0:T(8,128)(2,1)S(1)}, bf16[64,2048]{1,0:T(8,128)(2,1)S(1)}) custom-call(s32[1]{0:T(128)} %bitcast.3.refs_0_, s32[1]{0:T(128)S(6)} %sub.7.refs_0_.refs_1_, bf16[128,768]{1,0:T(8,128)(2,1)S(1)} %shard_map.121.refs_5_.refs_2_, bf16[128,768]{1,0:T(8,128)(2,1)S(1)} %collective-permute-done.18.refs_3_, ...), custom_call_target="tpu_custom_call" | custom-call | flops 2200000000 | tf_op jit(solution)/shard_map/pallas_call | solution.py:354
  71.5 2.1 %collective-permute-start.23 = (bf16[64,2048]{1,0:T(8,128)(2,1)S(1)}, bf16[64,2048]{1,0:T(8,128)(2,1)S(1)}, u32[]{:S(2)}, u32[]{:S(2)}) collective-permute-start(bf16[64,2048]{1,0:T(8,128)(2,1)S(1)} %shard_map.127.refs_5_), channel_id=1, source_target_pairs={{0,12},{4,8},{8,4},{12,0},{16,28},{20,24},{24,20},{28,16},{1,13},{... | collective-permute-start | bytes 786440 | tf_op jit(solution)/shard_map/ppermute | solution.py:397
  74.3 1.0 %shard_map.128.refs_1_.refs_4_ = bf16[64,1664]{1,0:T(8,128)(2,1)S(1)} custom-call(s32[1]{0:T(128)} %bitcast.3.refs_0_, f32[1,2048]{1,0:T(1,128)S(1)} %bitcast.14, bf16[2,2048,768]{2,1,0:T(8,128)(2,1)S(1)} %copy-done, bf16[2,2048,768]{2,1,0:T(8,128)(2,1)S(1)} %copy-done.1, bf16[64,2048]{1,0:T(8,128)(2,1)S(1)} %collective-permute-done.7.refs_4_, ...), custom_call_target="tpu_custom_call" | custom-call | flops 2400000000 | tf_op jit(solution)/shard_map/pallas_call | solution.py:354
  75.5 2.1 %collective-permute-start.20 = (bf16[64,768]{1,0:T(8,128)(2,1)S(1)}, bf16[64,768]{1,0:T(8,128)(2,1)S(1)}, u32[]{:S(2)}, u32[]{:S(2)}) collective-permute-start(bf16[64,768]{1,0:T(8,128)(2,1)S(1)} %shard_map.129.refs_5_.refs_2_), channel_id=1, source_target_pairs={{0,2},{2,0},{1,3},{3,1},{4,6},{6,4},{5,7},{7,5},{8,10},{10,8},{9,1... | collective-permute-start | bytes 294920 | tf_op jit(solution)/shard_map/ppermute | solution.py:477
  77.6 1.0 shard_map.130.refs_5_
  79.8 1.1 %collective-permute-done.20.refs_3_ = bf16[64,768]{1,0:T(8,128)(2,1)S(1)} collective-permute-done((bf16[64,768]{1,0:T(8,128)(2,1)S(1)}, bf16[64,768]{1,0:T(8,128)(2,1)S(1)}, u32[]{:S(2)}, u32[]{:S(2)}) %collective-permute-start.20) | collective-permute-done | bytes 98336 | tf_op jit(solution)/shard_map/ppermute | solution.py:477
  80.9 1.6 %collective-permute-done.22.refs_6_ = bf16[64,2048]{1,0:T(8,128)(2,1)S(1)} collective-permute-done((bf16[64,2048]{1,0:T(8,128)(2,1)S(1)}, bf16[64,2048]{1,0:T(8,128)(2,1)S(1)}, u32[]{:S(2)}, u32[]{:S(2)}) %collective-permute-start.22) | collective-permute-done | bytes 262176 | tf_op jit(solution)/shard_map/ppermute | solution.py:397
  82.4 1.1 %shard_map.132.refs_4_ = bf16[64,2048]{1,0:T(8,128)(2,1)S(1)} custom-call(s32[1]{0:T(128)} %bitcast.3.refs_0_, s32[1]{0:T(128)S(6)} %sub.7.refs_0_.refs_1_, bf16[64,768]{1,0:T(8,128)(2,1)S(1)} %shard_map.129.refs_5_.refs_2_, bf16[64,768]{1,0:T(8,128)(2,1)S(1)} %collective-permute-done.20.refs_3_, bf16[2,768,2048]{2,1,0:T(8,128)(2,1)S(1)} %bitcast.18, ...), custom_call_target="tpu_custom_call" | custom-call | flops 2200000000 | tf_op jit(solution)/shard_map/pallas_call | solution.py:354
  83.5 1.1 %collective-permute-done.26.refs_2_ = bf16[64,1664]{1,0:T(8,128)(2,1)S(1)} collective-permute-done((bf16[64,1664]{1,0:T(8,128)(2,1)S(1)}, bf16[64,1664]{1,0:T(8,128)(2,1)S(1)}, u32[]{:S(2)}, u32[]{:S(2)}) %collective-permute-start.26) | collective-permute-done | bytes 213024 | tf_op jit(solution)/shard_map/ppermute | solution.py:471
  84.8 1.5 %collective-permute-start.27 = (bf16[64,768]{1,0:T(8,128)(2,1)S(1)}, bf16[64,768]{1,0:T(8,128)(2,1)S(1)}, u32[]{:S(2)}, u32[]{:S(2)}) collective-permute-start(bf16[64,768]{1,0:T(8,128)(2,1)S(1)} %shard_map.133.refs_2_.refs_5_), channel_id=1, source_target_pairs={{0,2},{2,0},{1,3},{3,1},{4,6},{6,4},{5,7},{7,5},{8,10},{10,8},{9,1... | collective-permute-start | bytes 294920 | tf_op jit(solution)/shard_map/ppermute | solution.py:477
  86.7 2.8 %collective-permute-done.27.refs_3_ = bf16[64,768]{1,0:T(8,128)(2,1)S(1)} collective-permute-done((bf16[64,768]{1,0:T(8,128)(2,1)S(1)}, bf16[64,768]{1,0:T(8,128)(2,1)S(1)}, u32[]{:S(2)}, u32[]{:S(2)}) %collective-permute-start.27) | collective-permute-done | bytes 98336 | tf_op jit(solution)/shard_map/ppermute | solution.py:477
  89.5 1.0 %shard_map.134.refs_6_ = bf16[64,2048]{1,0:T(8,128)(2,1)S(1)} custom-call(s32[1]{0:T(128)} %bitcast.3.refs_0_, s32[1]{0:T(128)S(6)} %sub.7.refs_0_.refs_1_, bf16[64,768]{1,0:T(8,128)(2,1)S(1)} %shard_map.133.refs_2_.refs_5_, bf16[64,768]{1,0:T(8,128)(2,1)S(1)} %collective-permute-done.27.refs_3_, bf16[2,768,2048]{2,1,0:T(8,128)(2,1)S(1)} %bitcast.18, ...), custom_call_target="tpu_custom_call" | custom-call | flops 2200000000 | tf_op jit(solution)/shard_map/pallas_call | solution.py:354
  90.5 1.2 %collective-permute-start.28 = (bf16[64,2048]{1,0:T(8,128)(2,1)S(1)}, bf16[64,2048]{1,0:T(8,128)(2,1)S(1)}, u32[]{:S(2)}, u32[]{:S(2)}) collective-permute-start(bf16[64,2048]{1,0:T(8,128)(2,1)S(1)} %shard_map.134.refs_6_), channel_id=1, source_target_pairs={{0,12},{4,8},{8,4},{12,0},{16,28},{20,24},{24,20},{28,16},{1,13},{... | collective-permute-start | bytes 786440 | tf_op jit(solution)/shard_map/ppermute | solution.py:397
  91.7 4.1 %collective-permute-done.25.refs_4_ = bf16[64,2048]{1,0:T(8,128)(2,1)S(1)} collective-permute-done((bf16[64,2048]{1,0:T(8,128)(2,1)S(1)}, bf16[64,2048]{1,0:T(8,128)(2,1)S(1)}, u32[]{:S(2)}, u32[]{:S(2)}) %collective-permute-start.25) | collective-permute-done | bytes 262176 | tf_op jit(solution)/shard_map/ppermute | solution.py:397
  95.8 3.5 %collective-permute-done.28.refs_5_ = bf16[64,2048]{1,0:T(8,128)(2,1)S(1)} collective-permute-done((bf16[64,2048]{1,0:T(8,128)(2,1)S(1)}, bf16[64,2048]{1,0:T(8,128)(2,1)S(1)}, u32[]{:S(2)}, u32[]{:S(2)}) %collective-permute-start.28) | collective-permute-done | bytes 262176 | tf_op jit(solution)/shard_map/ppermute | solution.py:397
  (61 shorter events, 12.5 us)
Async XLA Ops:
  1.6 16.1 %copy-start.3 = (bf16[64,2048]{1,0:T(8,128)(2,1)S(1)}, bf16[64,2048]{1,0:T(8,128)(2,1)}, u32[]{:S(2)}) copy-start(bf16[64,2048]{1,0:T(8,128)(2,1)} %refs_2_.13) | copy-start | bytes 786436
  1.6 16.1 %copy-start.4 = (bf16[64,2048]{1,0:T(8,128)(2,1)S(1)}, bf16[64,2048]{1,0:T(8,128)(2,1)}, u32[]{:S(2)}) copy-start(bf16[64,2048]{1,0:T(8,128)(2,1)} %refs_4_.7) | copy-start | bytes 786436
  1.6 16.1 %copy-start.5 = (s32[8]{0:T(128)S(1)}, s32[8]{0:T(128)}, u32[]{:S(2)}) copy-start(s32[8]{0:T(128)} %refs_1_.1) | copy-start | bytes 100
  1.6 6.4 %collective-permute-start = (bf16[144,128]{1,0:T(8,128)(2,1)S(1)}, bf16[144,128]{1,0:T(8,128)(2,1)S(1)}, u32[]{:S(2)}, u32[]{:S(2)}) collective-permute-start(bf16[144,128]{1,0:T(8,128)(2,1)S(1)} %shard_map.109.refs_5_), channel_id=1, source_target_pairs={{0,16},{4,20},{8,24},{12,28},{16,0},{20,4},{24,8},{28,12},{1,17},{... | collective-permute-start | bytes 110600 | tf_op jit(solution)/shard_map/ppermute | solution.py:78
  8.0 4.4 %collective-permute-start.1 = (bf16[288,128]{1,0:T(8,128)(2,1)S(1)}, bf16[288,128]{1,0:T(8,128)(2,1)S(1)}, u32[]{:S(2)}, u32[]{:S(2)}) collective-permute-start(bf16[288,128]{1,0:T(8,128)(2,1)S(1)} %pad_maximum_fusion.2), channel_id=1, source_target_pairs={{0,8},{4,12},{8,0},{12,4},{16,24},{20,28},{24,16},{28,20},{1,9},{5... | collective-permute-start | bytes 221192 | tf_op jit(solution)/shard_map/ppermute | solution.py:78
  12.4 5.2 %collective-permute-start.2 = (bf16[576,128]{1,0:T(8,128)(2,1)S(1)}, bf16[576,128]{1,0:T(8,128)(2,1)S(1)}, u32[]{:S(2)}, u32[]{:S(2)}) collective-permute-start(bf16[576,128]{1,0:T(8,128)(2,1)S(1)} %pad_maximum_fusion.1), channel_id=1, source_target_pairs={{0,4},{4,0},{8,12},{12,8},{16,20},{20,16},{24,28},{28,24},{1,5},{5... | collective-permute-start | bytes 442376 | tf_op jit(solution)/shard_map/ppermute | solution.py:78
  17.6 8.0 %copy-start = (bf16[2,2048,768]{2,1,0:T(8,128)(2,1)S(1)}, bf16[2,2048,768]{2,1,0:T(8,128)(2,1)}, u32[]{:S(2)}) copy-start(bf16[2,2048,768]{2,1,0:T(8,128)(2,1)} %refs_2_.25) | copy-start | bytes 18874372
  17.7 8.0 %copy-start.1 = (bf16[2,2048,768]{2,1,0:T(8,128)(2,1)S(1)}, bf16[2,2048,768]{2,1,0:T(8,128)(2,1)}, u32[]{:S(2)}) copy-start(bf16[2,2048,768]{2,1,0:T(8,128)(2,1)} %refs_3_.23) | copy-start | bytes 18874372
  17.7 7.9 %copy-start.2 = (f32[2048]{0:T(1024)S(1)}, f32[2048]{0:T(1024)}, u32[]{:S(2)}) copy-start(f32[2048]{0:T(1024)} %param.16) | copy-start | bytes 24580
  19.6 9.6 %collective-permute-start.4 = (bf16[64,2048]{1,0:T(8,128)(2,1)S(1)}, bf16[64,2048]{1,0:T(8,128)(2,1)S(1)}, u32[]{:S(2)}, u32[]{:S(2)}) collective-permute-start(bf16[64,2048]{1,0:T(8,128)(2,1)S(1)} %shard_map.110.refs_4_.refs_5_.refs_0_), channel_id=1, source_target_pairs={{0,8},{4,12},{8,0},{12,4},{16,24},{20,28},{24,16},{28,20},{1,9},{5... | collective-permute-start | bytes 786440 | tf_op jit(solution)/shard_map/ppermute | solution.py:397
  21.2 8.0 %collective-permute-start.5 = (bf16[64,2048]{1,0:T(8,128)(2,1)S(1)}, bf16[64,2048]{1,0:T(8,128)(2,1)S(1)}, u32[]{:S(2)}, u32[]{:S(2)}) collective-permute-start(bf16[64,2048]{1,0:T(8,128)(2,1)S(1)} %shard_map.110.refs_4_.refs_5_.refs_0_), channel_id=1, source_target_pairs={{0,4},{4,0},{8,12},{12,8},{16,20},{20,16},{24,28},{28,24},{1,5},{5... | collective-permute-start | bytes 786440 | tf_op jit(solution)/shard_map/ppermute | solution.py:397
  22.7 10.9 %collective-permute-start.7 = (bf16[64,2048]{1,0:T(8,128)(2,1)S(1)}, bf16[64,2048]{1,0:T(8,128)(2,1)S(1)}, u32[]{:S(2)}, u32[]{:S(2)}) collective-permute-start(bf16[64,2048]{1,0:T(8,128)(2,1)S(1)} %shard_map.110.refs_4_.refs_5_.refs_0_), channel_id=1, source_target_pairs={{0,16},{4,20},{8,24},{12,28},{16,0},{20,4},{24,8},{28,12},{1,17},{... | collective-permute-start | bytes 786440 | tf_op jit(solution)/shard_map/ppermute | solution.py:397
  27.6 8.3 %collective-permute-start.3 = (bf16[64,1664]{1,0:T(8,128)(2,1)S(1)}, bf16[64,1664]{1,0:T(8,128)(2,1)S(1)}, u32[]{:S(2)}, u32[]{:S(2)}) collective-permute-start(bf16[64,1664]{1,0:T(8,128)(2,1)S(1)} %shard_map.111.refs_5_), channel_id=1, source_target_pairs={{0,2},{2,0},{1,3},{3,1},{4,6},{6,4},{5,7},{7,5},{8,10},{10,8},{9,1... | collective-permute-start | bytes 638984 | tf_op jit(solution)/shard_map/ppermute | solution.py:471
  30.2 17.0 %collective-permute-start.10 = (bf16[128,1664]{1,0:T(8,128)(2,1)S(1)}, bf16[128,1664]{1,0:T(8,128)(2,1)S(1)}, u32[]{:S(2)}, u32[]{:S(2)}) collective-permute-start(bf16[128,1664]{1,0:T(8,128)(2,1)S(1)} %shard_map.113.refs_4_), channel_id=1, source_target_pairs={{0,2},{2,0},{1,3},{3,1},{4,6},{6,4},{5,7},{7,5},{8,10},{10,8},{9,1... | collective-permute-start | bytes 1277960 | tf_op jit(solution)/shard_map/ppermute | solution.py:471
  33.6 6.4 %collective-permute-start.8 = (bf16[64,2048]{1,0:T(8,128)(2,1)S(1)}, bf16[64,2048]{1,0:T(8,128)(2,1)S(1)}, u32[]{:S(2)}, u32[]{:S(2)}) collective-permute-start(bf16[64,2048]{1,0:T(8,128)(2,1)S(1)} %collective-permute-done.7.refs_4_), channel_id=1, source_target_pairs={{0,8},{4,12},{8,0},{12,4},{16,24},{20,28},{24,16},{28,20},{1,9},{5... | collective-permute-start | bytes 786440 | tf_op jit(solution)/shard_map/ppermute | solution.py:397
  33.6 6.4 %collective-permute-start.9 = (bf16[64,2048]{1,0:T(8,128)(2,1)S(1)}, bf16[64,2048]{1,0:T(8,128)(2,1)S(1)}, u32[]{:S(2)}, u32[]{:S(2)}) collective-permute-start(bf16[64,2048]{1,0:T(8,128)(2,1)S(1)} %collective-permute-done.7.refs_4_), channel_id=1, source_target_pairs={{0,4},{4,0},{8,12},{12,8},{16,20},{20,16},{24,28},{28,24},{1,5},{5... | collective-permute-start | bytes 786440 | tf_op jit(solution)/shard_map/ppermute | solution.py:397
  36.1 10.1 %collective-permute-start.6 = (bf16[64,768]{1,0:T(8,128)(2,1)S(1)}, bf16[64,768]{1,0:T(8,128)(2,1)S(1)}, u32[]{:S(2)}, u32[]{:S(2)}) collective-permute-start(bf16[64,768]{1,0:T(8,128)(2,1)S(1)} %shard_map.114.refs_6_.refs_2_), channel_id=1, source_target_pairs={{0,2},{2,0},{1,3},{3,1},{4,6},{6,4},{5,7},{7,5},{8,10},{10,8},{9,1... | collective-permute-start | bytes 294920 | tf_op jit(solution)/shard_map/ppermute | solution.py:477
  37.7 40.0 %collective-permute-start.24 = (bf16[64,2048]{1,0:T(8,128)(2,1)S(1)}, bf16[64,2048]{1,0:T(8,128)(2,1)S(1)}, u32[]{:S(2)}, u32[]{:S(2)}) collective-permute-start(bf16[64,2048]{1,0:T(8,128)(2,1)S(1)} %collective-permute-done.4.refs_4_), channel_id=1, source_target_pairs={{0,4},{4,0},{8,12},{12,8},{16,20},{20,16},{24,28},{28,24},{1,5},{5... | collective-permute-start | bytes 786440 | tf_op jit(solution)/shard_map/ppermute | solution.py:397
  38.2 8.0 %slice-start = ((s8[6291456]{0:T(1024)(128)(4,1)}), s8[4194304]{0:T(1024)(128)(4,1)S(1)}, s32[]{:S(2)}) async-start(s8[6291456]{0:T(1024)(128)(4,1)} %bitcast.17), calls=%async_computation | async-start | bytes 8388608
  39.2 7.0 %slice-start.1 = ((s8[6291456]{0:T(1024)(128)(4,1)}), s8[2097152]{0:T(1024)(128)(4,1)S(1)}, s32[]{:S(2)}) async-start(s8[6291456]{0:T(1024)(128)(4,1)} %bitcast.17), calls=%async_computation.1 | async-start | bytes 4194304
  41.1 13.4 %collective-permute-start.12 = (bf16[128,1664]{1,0:T(8,128)(2,1)S(1)}, bf16[128,1664]{1,0:T(8,128)(2,1)S(1)}, u32[]{:S(2)}, u32[]{:S(2)}) collective-permute-start(bf16[128,1664]{1,0:T(8,128)(2,1)S(1)} %shard_map.116.refs_5_), channel_id=1, source_target_pairs={{0,2},{2,0},{1,3},{3,1},{4,6},{6,4},{5,7},{7,5},{8,10},{10,8},{9,1... | collective-permute-start | bytes 1277960 | tf_op jit(solution)/shard_map/ppermute | solution.py:471
  43.7 6.8 %collective-permute-start.13 = (bf16[64,2048]{1,0:T(8,128)(2,1)S(1)}, bf16[64,2048]{1,0:T(8,128)(2,1)S(1)}, u32[]{:S(2)}, u32[]{:S(2)}) collective-permute-start(bf16[64,2048]{1,0:T(8,128)(2,1)S(1)} %collective-permute-done.8.refs_4_), channel_id=1, source_target_pairs={{0,4},{4,0},{8,12},{12,8},{16,20},{20,16},{24,28},{28,24},{1,5},{5... | collective-permute-start | bytes 786440 | tf_op jit(solution)/shard_map/ppermute | solution.py:397
  47.6 11.1 %collective-permute-start.11 = (bf16[128,768]{1,0:T(8,128)(2,1)S(1)}, bf16[128,768]{1,0:T(8,128)(2,1)S(1)}, u32[]{:S(2)}, u32[]{:S(2)}) collective-permute-start(bf16[128,768]{1,0:T(8,128)(2,1)S(1)} %shard_map.118.refs_6_.refs_2_), channel_id=1, source_target_pairs={{0,2},{2,0},{1,3},{3,1},{4,6},{6,4},{5,7},{7,5},{8,10},{10,8},{9,1... | collective-permute-start | bytes 589832 | tf_op jit(solution)/shard_map/ppermute | solution.py:477
  51.5 11.9 %collective-permute-start.16 = (bf16[64,1664]{1,0:T(8,128)(2,1)S(1)}, bf16[64,1664]{1,0:T(8,128)(2,1)S(1)}, u32[]{:S(2)}, u32[]{:S(2)}) collective-permute-start(bf16[64,1664]{1,0:T(8,128)(2,1)S(1)} %shard_map.120.refs_4_), channel_id=1, source_target_pairs={{0,2},{2,0},{1,3},{3,1},{4,6},{6,4},{5,7},{7,5},{8,10},{10,8},{9,1... | collective-permute-start | bytes 638984 | tf_op jit(solution)/shard_map/ppermute | solution.py:471
  54.8 12.0 %collective-permute-start.18 = (bf16[128,768]{1,0:T(8,128)(2,1)S(1)}, bf16[128,768]{1,0:T(8,128)(2,1)S(1)}, u32[]{:S(2)}, u32[]{:S(2)}) collective-permute-start(bf16[128,768]{1,0:T(8,128)(2,1)S(1)} %shard_map.121.refs_5_.refs_2_), channel_id=1, source_target_pairs={{0,2},{2,0},{1,3},{3,1},{4,6},{6,4},{5,7},{7,5},{8,10},{10,8},{9,1... | collective-permute-start | bytes 589832 | tf_op jit(solution)/shard_map/ppermute | solution.py:477
  59.7 11.8 %collective-permute-start.14 = (bf16[64,2048]{1,0:T(8,128)(2,1)S(1)}, bf16[64,2048]{1,0:T(8,128)(2,1)S(1)}, u32[]{:S(2)}, u32[]{:S(2)}) collective-permute-start(bf16[64,2048]{1,0:T(8,128)(2,1)S(1)} %get-tuple-element.9.refs_5_), channel_id=1, source_target_pairs={{0,8},{4,12},{8,0},{12,4},{16,24},{20,28},{24,16},{28,20},{1,9},{5... | collective-permute-start | bytes 786440 | tf_op jit(solution)/shard_map/ppermute | solution.py:397
  62.0 11.5 %collective-permute-start.15 = (bf16[64,2048]{1,0:T(8,128)(2,1)S(1)}, bf16[64,2048]{1,0:T(8,128)(2,1)S(1)}, u32[]{:S(2)}, u32[]{:S(2)}) collective-permute-start(bf16[64,2048]{1,0:T(8,128)(2,1)S(1)} %get-tuple-element.10), channel_id=1, source_target_pairs={{0,4},{4,0},{8,12},{12,8},{16,20},{20,16},{24,28},{28,24},{1,5},{5... | collective-permute-start | bytes 786440 | tf_op jit(solution)/shard_map/ppermute | solution.py:397
  63.7 5.9 %collective-permute-start.17 = (bf16[64,768]{1,0:T(8,128)(2,1)S(1)}, bf16[64,768]{1,0:T(8,128)(2,1)S(1)}, u32[]{:S(2)}, u32[]{:S(2)}) collective-permute-start(bf16[64,768]{1,0:T(8,128)(2,1)S(1)} %shard_map.124.refs_5_.refs_2_), channel_id=1, source_target_pairs={{0,2},{2,0},{1,3},{3,1},{4,6},{6,4},{5,7},{7,5},{8,10},{10,8},{9,1... | collective-permute-start | bytes 294920 | tf_op jit(solution)/shard_map/ppermute | solution.py:477
  66.8 8.5 %collective-permute-start.19 = (bf16[64,1664]{1,0:T(8,128)(2,1)S(1)}, bf16[64,1664]{1,0:T(8,128)(2,1)S(1)}, u32[]{:S(2)}, u32[]{:S(2)}) collective-permute-start(bf16[64,1664]{1,0:T(8,128)(2,1)S(1)} %shard_map.125.refs_5_), channel_id=1, source_target_pairs={{0,2},{2,0},{1,3},{3,1},{4,6},{6,4},{5,7},{7,5},{8,10},{10,8},{9,1... | collective-permute-start | bytes 638984 | tf_op jit(solution)/shard_map/ppermute | solution.py:471
  69.6 11.2 %collective-permute-start.21 = (bf16[64,2048]{1,0:T(8,128)(2,1)S(1)}, bf16[64,2048]{1,0:T(8,128)(2,1)S(1)}, u32[]{:S(2)}, u32[]{:S(2)}) collective-permute-start(bf16[64,2048]{1,0:T(8,128)(2,1)S(1)} %get-tuple-element.11.refs_5_), channel_id=1, source_target_pairs={{0,8},{4,12},{8,0},{12,4},{16,24},{20,28},{24,16},{28,20},{1,9},{5... | collective-permute-start | bytes 786440 | tf_op jit(solution)/shard_map/ppermute | solution.py:397
  71.5 9.4 %collective-permute-start.23 = (bf16[64,2048]{1,0:T(8,128)(2,1)S(1)}, bf16[64,2048]{1,0:T(8,128)(2,1)S(1)}, u32[]{:S(2)}, u32[]{:S(2)}) collective-permute-start(bf16[64,2048]{1,0:T(8,128)(2,1)S(1)} %shard_map.127.refs_5_), channel_id=1, source_target_pairs={{0,12},{4,8},{8,4},{12,0},{16,28},{20,24},{24,20},{28,16},{1,13},{... | collective-permute-start | bytes 786440 | tf_op jit(solution)/shard_map/ppermute | solution.py:397
  73.6 8.9 %collective-permute-start.22 = (bf16[64,2048]{1,0:T(8,128)(2,1)S(1)}, bf16[64,2048]{1,0:T(8,128)(2,1)S(1)}, u32[]{:S(2)}, u32[]{:S(2)}) collective-permute-start(bf16[64,2048]{1,0:T(8,128)(2,1)S(1)} %get-tuple-element.12), channel_id=1, source_target_pairs={{0,4},{4,0},{8,12},{12,8},{16,20},{20,16},{24,28},{28,24},{1,5},{5... | collective-permute-start | bytes 786440 | tf_op jit(solution)/shard_map/ppermute | solution.py:397
  75.5 5.3 %collective-permute-start.20 = (bf16[64,768]{1,0:T(8,128)(2,1)S(1)}, bf16[64,768]{1,0:T(8,128)(2,1)S(1)}, u32[]{:S(2)}, u32[]{:S(2)}) collective-permute-start(bf16[64,768]{1,0:T(8,128)(2,1)S(1)} %shard_map.129.refs_5_.refs_2_), channel_id=1, source_target_pairs={{0,2},{2,0},{1,3},{3,1},{4,6},{6,4},{5,7},{7,5},{8,10},{10,8},{9,1... | collective-permute-start | bytes 294920 | tf_op jit(solution)/shard_map/ppermute | solution.py:477
  78.7 5.9 %collective-permute-start.26 = (bf16[64,1664]{1,0:T(8,128)(2,1)S(1)}, bf16[64,1664]{1,0:T(8,128)(2,1)S(1)}, u32[]{:S(2)}, u32[]{:S(2)}) collective-permute-start(bf16[64,1664]{1,0:T(8,128)(2,1)S(1)} %shard_map.130.refs_5_), channel_id=1, source_target_pairs={{0,2},{2,0},{1,3},{3,1},{4,6},{6,4},{5,7},{7,5},{8,10},{10,8},{9,1... | collective-permute-start | bytes 638984 | tf_op jit(solution)/shard_map/ppermute | solution.py:471
  84.8 4.7 %collective-permute-start.27 = (bf16[64,768]{1,0:T(8,128)(2,1)S(1)}, bf16[64,768]{1,0:T(8,128)(2,1)S(1)}, u32[]{:S(2)}, u32[]{:S(2)}) collective-permute-start(bf16[64,768]{1,0:T(8,128)(2,1)S(1)} %shard_map.133.refs_2_.refs_5_), channel_id=1, source_target_pairs={{0,2},{2,0},{1,3},{3,1},{4,6},{6,4},{5,7},{7,5},{8,10},{10,8},{9,1... | collective-permute-start | bytes 294920 | tf_op jit(solution)/shard_map/ppermute | solution.py:477
  86.3 9.5 %collective-permute-start.25 = (bf16[64,2048]{1,0:T(8,128)(2,1)S(1)}, bf16[64,2048]{1,0:T(8,128)(2,1)S(1)}, u32[]{:S(2)}, u32[]{:S(2)}) collective-permute-start(bf16[64,2048]{1,0:T(8,128)(2,1)S(1)} %shard_map.132.refs_4_), channel_id=1, source_target_pairs={{0,16},{4,20},{8,24},{12,28},{16,0},{20,4},{24,8},{28,12},{1,17},{... | collective-permute-start | bytes 786440 | tf_op jit(solution)/shard_map/ppermute | solution.py:397
  90.5 8.8 %collective-permute-start.28 = (bf16[64,2048]{1,0:T(8,128)(2,1)S(1)}, bf16[64,2048]{1,0:T(8,128)(2,1)S(1)}, u32[]{:S(2)}, u32[]{:S(2)}) collective-permute-start(bf16[64,2048]{1,0:T(8,128)(2,1)S(1)} %shard_map.134.refs_6_), channel_id=1, source_target_pairs={{0,12},{4,8},{8,4},{12,0},{16,28},{20,24},{24,20},{28,16},{1,13},{... | collective-permute-start | bytes 786440 | tf_op jit(solution)/shard_map/ppermute | solution.py:397

commit v6 on v5

--- a/solution.py
+++ b/solution.py
@@ -26,7 +26,7 @@
 BOTH_COST = 1.1
 PACK_COST = 10
 ATT_COST = 5
-HOPS = ((0, 4), (0, 1), (4, 2), (4, 1), (6, 1), (0, 2), (2, 1))
+HOPS = ((0, 4), (0, 1), (4, 2), (4, 1), (5, 2), (0, 2), (2, 1))
 COSTS = {}
 LATER = (2,)
 CHUNKS = ((0,), (2, 1), (6, 5), (7,), (4,), (3,))
@@ -54,8 +54,8 @@
     ("keep", 4),
     ("hidden", 4),
     ("send", 5),
+    ("both", 4),
     ("keep", 5),
-    ("both", 4),
     ("hidden", 5),
     ("both", 5),
     ("sum", 0),
@@ -237,10 +237,10 @@
     for i, offset in enumerate(offsets(count // rows)):
         key_pos = key_pos + jnp.where(column // rows == i, order_ref[me ^ offset] * rows, 0)
     query_pos = order_ref[me] * rows + lax.broadcasted_iota(jnp.int32, (rows, count), 0)
-    visible = jnp.concatenate([key_pos <= query_pos] * heads, axis=0)
-    scores = jnp.where(visible, scores, MASKED_SCORE)
+    hidden_score = jnp.where(key_pos <= query_pos, 0.0, MASKED_SCORE)
+    scores = scores + jnp.concatenate([hidden_score] * heads, axis=0)
     largest = jnp.max(scores, axis=1, keepdims=True)
-    weights = jnp.where(visible, jnp.exp(scores - largest), 0.0)
+    weights = jnp.exp(scores - largest)
     weight_sum = jnp.sum(weights, axis=1, keepdims=True)
     weighted = jnp.dot(
         weights.astype(jnp.bfloat16),

time: 100 us -> 99.1 us (level)
  starting transfers between devices: 42.4 us -> 41.4 us
    ppermute x14, waiting for transfers between devices: 14.6 us -> 13.1 us  [hop(): return lax.ppermute(block, 'ctx', xor_pairs(ctx_count, offset))]
    ppermute x6, waiting for transfers between devices: 5.68 us -> 7.16 us  [local(): other_hidden[i] = lax.ppermute(hidden[i], 'exp', swap)]
  transfers between devices with their start and end apart: 29 -> 29, of which waited for: 16 -> 16; matrix products, arithmetic and copies ran while one was open for 0% -> 0% of each run, Pallas kernels for 19% -> 20%
where the time goes in v6:
time: 99.1 us; the launch traced here: 98.8 us
  starting transfers between devices  41.4 us (42%)
  waiting for transfers between devices  32.8 us (33%)
  Pallas kernels  22.6 us (23%)
    pallas_call x27, Pallas kernels, __call__(): pl.pallas_call(body, out_shape=out_shape, in_specs=specs, out_specs=[vmem...  22.6 us
    ppermute x14, starting transfers between devices, hop(): return lax.ppermute(block, 'ctx', xor_pairs(ctx_count, offset))  18.3 us
    ppermute x14, waiting for transfers between devices, hop(): return lax.ppermute(block, 'ctx', xor_pairs(ctx_count, offset))  13.1 us
    ppermute x3, waiting for transfers between devices, gather_rows(): lax.ppermute(block, 'ctx', xor_pairs(count, bit))  8.59 us
    ppermute x6, starting transfers between devices, local(): other_hidden[i] = lax.ppermute(hidden[i], 'exp', swap)  8.54 us
    ppermute x3, starting transfers between devices, gather_rows(): lax.ppermute(block, 'ctx', xor_pairs(count, bit))  7.41 us
    ppermute x6, starting transfers between devices, local(): arrived[i] = lax.ppermute(product, 'exp', swap)  7.18 us
    ppermute x6, waiting for transfers between devices, local(): other_hidden[i] = lax.ppermute(hidden[i], 'exp', swap)  7.16 us
  transfers between devices with their start and end apart: 29, of which 16 were waited for; matrix products, arithmetic and copies ran while one was open for 0% of the time, Pallas kernels for 20%

profile of v6, /device:TPU:0, one launch (start us, length us, event | category | flops | bytes accessed | tf_op | source)
XLA Modules:
  0.0 98.8 jit_solution(13477494486161940809)
XLA Ops:
  1.6 4.1 %collective-permute-start = (bf16[144,128]{1,0:T(8,128)(2,1)S(1)}, bf16[144,128]{1,0:T(8,128)(2,1)S(1)}, u32[]{:S(2)}, u32[]{:S(2)}) collective-permute-start(bf16[144,128]{1,0:T(8,128)(2,1)S(1)} %shard_map.109.refs_5_), channel_id=1, source_target_pairs={{0,16},{4,20},{8,24},{12,28},{16,0},{20,4},{24,8},{28,12},{1,17},{... | collective-permute-start | bytes 110600 | tf_op jit(solution)/shard_map/ppermute | solution.py:78
  5.7 2.3 %collective-permute-done = bf16[144,128]{1,0:T(8,128)(2,1)S(1)} collective-permute-done((bf16[144,128]{1,0:T(8,128)(2,1)S(1)}, bf16[144,128]{1,0:T(8,128)(2,1)S(1)}, u32[]{:S(2)}, u32[]{:S(2)}) %collective-permute-start) | collective-permute-done | bytes 36896 | tf_op jit(solution)/shard_map/ppermute | solution.py:78
  8.0 1.5 %collective-permute-start.1 = (bf16[288,128]{1,0:T(8,128)(2,1)S(1)}, bf16[288,128]{1,0:T(8,128)(2,1)S(1)}, u32[]{:S(2)}, u32[]{:S(2)}) collective-permute-start(bf16[288,128]{1,0:T(8,128)(2,1)S(1)} %pad_maximum_fusion.2), channel_id=1, source_target_pairs={{0,8},{4,12},{8,0},{12,4},{16,24},{20,28},{24,16},{28,20},{1,9},{5... | collective-permute-start | bytes 221192 | tf_op jit(solution)/shard_map/ppermute | solution.py:78
  9.5 2.8 %collective-permute-done.1 = bf16[288,128]{1,0:T(8,128)(2,1)S(1)} collective-permute-done((bf16[288,128]{1,0:T(8,128)(2,1)S(1)}, bf16[288,128]{1,0:T(8,128)(2,1)S(1)}, u32[]{:S(2)}, u32[]{:S(2)}) %collective-permute-start.1) | collective-permute-done | bytes 73760 | tf_op jit(solution)/shard_map/ppermute | solution.py:78
  12.4 1.8 %collective-permute-start.2 = (bf16[576,128]{1,0:T(8,128)(2,1)S(1)}, bf16[576,128]{1,0:T(8,128)(2,1)S(1)}, u32[]{:S(2)}, u32[]{:S(2)}) collective-permute-start(bf16[576,128]{1,0:T(8,128)(2,1)S(1)} %pad_maximum_fusion.1), channel_id=1, source_target_pairs={{0,4},{4,0},{8,12},{12,8},{16,20},{20,16},{24,28},{28,24},{1,5},{5... | collective-permute-start | bytes 442376 | tf_op jit(solution)/shard_map/ppermute | solution.py:78
  14.2 3.4 %collective-permute-done.2 = bf16[576,128]{1,0:T(8,128)(2,1)S(1)} collective-permute-done((bf16[576,128]{1,0:T(8,128)(2,1)S(1)}, bf16[576,128]{1,0:T(8,128)(2,1)S(1)}, u32[]{:S(2)}, u32[]{:S(2)}) %collective-permute-start.2) | collective-permute-done | bytes 147488 | tf_op jit(solution)/shard_map/ppermute | solution.py:78
  17.7 1.8 %shard_map.110.refs_4_.refs_5_.refs_0_ = bf16[64,2048]{1,0:T(8,128)(2,1)S(1)} custom-call(s32[1]{0:T(128)} %bitcast.refs_0_, s32[8]{0:T(128)S(1)} %copy-done.5, bf16[64,2048]{1,0:T(8,128)(2,1)S(1)} %copy-done.3, bf16[1152,128]{1,0:T(8,128)(2,1)S(1)} %pad_maximum_fusion.refs_3_, bf16[64,2048]{1,0:T(8,128)(2,1)S(1)} %copy-done.4, ...), custom_call_target="tpu_custom_call" | custom-call | flops 10000000000 | tf_op jit(solution)/shard_map/pallas_call | solution.py:354
  19.5 1.6 %collective-permute-start.4 = (bf16[64,2048]{1,0:T(8,128)(2,1)S(1)}, bf16[64,2048]{1,0:T(8,128)(2,1)S(1)}, u32[]{:S(2)}, u32[]{:S(2)}) collective-permute-start(bf16[64,2048]{1,0:T(8,128)(2,1)S(1)} %shard_map.110.refs_4_.refs_5_.refs_0_), channel_id=1, source_target_pairs={{0,8},{4,12},{8,0},{12,4},{16,24},{20,28},{24,16},{28,20},{1,9},{5... | collective-permute-start | bytes 786440 | tf_op jit(solution)/shard_map/ppermute | solution.py:397
  21.1 1.5 %collective-permute-start.5 = (bf16[64,2048]{1,0:T(8,128)(2,1)S(1)}, bf16[64,2048]{1,0:T(8,128)(2,1)S(1)}, u32[]{:S(2)}, u32[]{:S(2)}) collective-permute-start(bf16[64,2048]{1,0:T(8,128)(2,1)S(1)} %shard_map.110.refs_4_.refs_5_.refs_0_), channel_id=1, source_target_pairs={{0,4},{4,0},{8,12},{12,8},{16,20},{20,16},{24,28},{28,24},{1,5},{5... | collective-permute-start | bytes 786440 | tf_op jit(solution)/shard_map/ppermute | solution.py:397
  22.6 2.9 %collective-permute-start.7 = (bf16[64,2048]{1,0:T(8,128)(2,1)S(1)}, bf16[64,2048]{1,0:T(8,128)(2,1)S(1)}, u32[]{:S(2)}, u32[]{:S(2)}) collective-permute-start(bf16[64,2048]{1,0:T(8,128)(2,1)S(1)} %shard_map.110.refs_4_.refs_5_.refs_0_), channel_id=1, source_target_pairs={{0,16},{4,20},{8,24},{12,28},{16,0},{20,4},{24,8},{28,12},{1,17},{... | collective-permute-start | bytes 786440 | tf_op jit(solution)/shard_map/ppermute | solution.py:397
  25.5 1.0 %shard_map.111.refs_5_ = bf16[64,1664]{1,0:T(8,128)(2,1)S(1)} custom-call(s32[1]{0:T(128)S(6)} %sub.7.refs_0_.refs_1_, f32[1,2048]{1,0:T(1,128)S(1)} %bitcast.5, bf16[2,2048,768]{2,1,0:T(8,128)(2,1)S(1)} %copy-done, bf16[2,2048,768]{2,1,0:T(8,128)(2,1)S(1)} %copy-done.1, bf16[64,2048]{1,0:T(8,128)(2,1)S(1)} %shard_map.110.refs_4_.refs_5_.refs_0_, ...), custom_call_target="tpu_custom_call" | custom-call | flops 2400000000 | tf_op jit(solution)/shard_map/pallas_call | solution.py:354
  26.5 1.0 %shard_map.112.refs_6_.refs_1_ = bf16[64,1664]{1,0:T(8,128)(2,1)S(1)} custom-call(s32[1]{0:T(128)} %bitcast.3.refs_0_, f32[1,2048]{1,0:T(1,128)S(1)} %bitcast.6, bf16[2,2048,768]{2,1,0:T(8,128)(2,1)S(1)} %copy-done, bf16[2,2048,768]{2,1,0:T(8,128)(2,1)S(1)} %copy-done.1, bf16[64,2048]{1,0:T(8,128)(2,1)S(1)} %shard_map.110.refs_4_.refs_5_.refs_0_, ...), custom_call_target="tpu_custom_call" | custom-call | flops 2400000000 | tf_op jit(solution)/shard_map/pallas_call | solution.py:354
  27.5 1.6 %collective-permute-start.3 = (bf16[64,1664]{1,0:T(8,128)(2,1)S(1)}, bf16[64,1664]{1,0:T(8,128)(2,1)S(1)}, u32[]{:S(2)}, u32[]{:S(2)}) collective-permute-start(bf16[64,1664]{1,0:T(8,128)(2,1)S(1)} %shard_map.111.refs_5_), channel_id=1, source_target_pairs={{0,2},{2,0},{1,3},{3,1},{4,6},{6,4},{5,7},{7,5},{8,10},{10,8},{9,1... | collective-permute-start | bytes 638984 | tf_op jit(solution)/shard_map/ppermute | solution.py:471
  29.0 1.0 %shard_map.113.refs_4_ = bf16[128,1664]{1,0:T(8,128)(2,1)S(1)} custom-call(s32[1]{0:T(128)S(6)} %sub.7.refs_0_.refs_1_, f32[1,2048]{1,0:T(1,128)S(1)} %bitcast.7, bf16[2,2048,768]{2,1,0:T(8,128)(2,1)S(1)} %copy-done, bf16[2,2048,768]{2,1,0:T(8,128)(2,1)S(1)} %copy-done.1, bf16[64,2048]{1,0:T(8,128)(2,1)S(1)} %collective-permute-done.4.refs_4_, ...), custom_call_target="tpu_custom_call" | custom-call | flops 2400000000 | tf_op jit(solution)/shard_map/pallas_call | solution.py:354
  30.7 2.8 %collective-permute-done.7.refs_4_ = bf16[64,2048]{1,0:T(8,128)(2,1)S(1)} collective-permute-done((bf16[64,2048]{1,0:T(8,128)(2,1)S(1)}, bf16[64,2048]{1,0:T(8,128)(2,1)S(1)}, u32[]{:S(2)}, u32[]{:S(2)}) %collective-permute-start.7) | collective-permute-done | bytes 262176 | tf_op jit(solution)/shard_map/ppermute | solution.py:397
  33.5 1.6 %collective-permute-start.9 = (bf16[64,2048]{1,0:T(8,128)(2,1)S(1)}, bf16[64,2048]{1,0:T(8,128)(2,1)S(1)}, u32[]{:S(2)}, u32[]{:S(2)}) collective-permute-start(bf16[64,2048]{1,0:T(8,128)(2,1)S(1)} %collective-permute-done.7.refs_4_), channel_id=1, source_target_pairs={{0,4},{4,0},{8,12},{12,8},{16,20},{20,16},{24,28},{28,24},{1,5},{5... | collective-permute-start | bytes 786440 | tf_op jit(solution)/shard_map/ppermute | solution.py:397
  35.9 1.6 %collective-permute-start.6 = (bf16[64,768]{1,0:T(8,128)(2,1)S(1)}, bf16[64,768]{1,0:T(8,128)(2,1)S(1)}, u32[]{:S(2)}, u32[]{:S(2)}) collective-permute-start(bf16[64,768]{1,0:T(8,128)(2,1)S(1)} %shard_map.114.refs_6_.refs_2_), channel_id=1, source_target_pairs={{0,2},{2,0},{1,3},{3,1},{4,6},{6,4},{5,7},{7,5},{8,10},{10,8},{9,1... | collective-permute-start | bytes 294920 | tf_op jit(solution)/shard_map/ppermute | solution.py:477
  38.0 1.0 %shard_map.115.refs_6_.refs_1_ = bf16[128,1664]{1,0:T(8,128)(2,1)S(1)} custom-call(s32[1]{0:T(128)} %bitcast.3.refs_0_, f32[1,2048]{1,0:T(1,128)S(1)} %bitcast.8, bf16[2,2048,768]{2,1,0:T(8,128)(2,1)S(1)} %copy-done, bf16[2,2048,768]{2,1,0:T(8,128)(2,1)S(1)} %copy-done.1, bf16[64,2048]{1,0:T(8,128)(2,1)S(1)} %collective-permute-done.4.refs_4_, ...), custom_call_target="tpu_custom_call" | custom-call | flops 2400000000 | tf_op jit(solution)/shard_map/pallas_call | solution.py:354
  39.8 1.0 %shard_map.116.refs_5_ = bf16[128,1664]{1,0:T(8,128)(2,1)S(1)} custom-call(s32[1]{0:T(128)S(6)} %sub.7.refs_0_.refs_1_, f32[1,2048]{1,0:T(1,128)S(1)} %bitcast.9, bf16[2,2048,768]{2,1,0:T(8,128)(2,1)S(1)} %copy-done, bf16[2,2048,768]{2,1,0:T(8,128)(2,1)S(1)} %copy-done.1, bf16[64,2048]{1,0:T(8,128)(2,1)S(1)} %collective-permute-done.8.refs_4_, ...), custom_call_target="tpu_custom_call" | custom-call | flops 2400000000 | tf_op jit(solution)/shard_map/pallas_call | solution.py:354
  40.9 2.2 %collective-permute-start.12 = (bf16[128,1664]{1,0:T(8,128)(2,1)S(1)}, bf16[128,1664]{1,0:T(8,128)(2,1)S(1)}, u32[]{:S(2)}, u32[]{:S(2)}) collective-permute-start(bf16[128,1664]{1,0:T(8,128)(2,1)S(1)} %shard_map.116.refs_5_), channel_id=1, source_target_pairs={{0,2},{2,0},{1,3},{3,1},{4,6},{6,4},{5,7},{7,5},{8,10},{10,8},{9,1... | collective-permute-start | bytes 1277960 | tf_op jit(solution)/shard_map/ppermute | solution.py:471
  43.0 1.4 %collective-permute-start.13 = (bf16[64,2048]{1,0:T(8,128)(2,1)S(1)}, bf16[64,2048]{1,0:T(8,128)(2,1)S(1)}, u32[]{:S(2)}, u32[]{:S(2)}) collective-permute-start(bf16[64,2048]{1,0:T(8,128)(2,1)S(1)} %collective-permute-done.9.refs_5_), channel_id=1, source_target_pairs={{0,8},{4,12},{8,0},{12,4},{16,24},{20,28},{24,16},{28,20},{1,9},{5... | collective-permute-start | bytes 786440 | tf_op jit(solution)/shard_map/ppermute | solution.py:397
  44.5 1.0 %shard_map.117.refs_4_.refs_1_ = f32[64,2048]{1,0:T(8,128)S(1)} custom-call(s32[1]{0:T(128)} %bitcast.3.refs_0_, s32[1]{0:T(128)S(6)} %sub.7.refs_0_.refs_1_, bf16[64,768]{1,0:T(8,128)(2,1)S(1)} %shard_map.114.refs_6_.refs_2_, bf16[64,768]{1,0:T(8,128)(2,1)S(1)} %collective-permute-done.6.refs_3_, bf16[2,768,2048]{2,1,0:T(8,128)(2,1)S(1)} %bitcast.18, ...), custom_call_target="tpu_custom_call" | custom-call | flops 2200000000 | tf_op jit(solution)/shard_map/pallas_call | solution.py:354
  45.8 1.1 %collective-permute-start.11 = (bf16[128,768]{1,0:T(8,128)(2,1)S(1)}, bf16[128,768]{1,0:T(8,128)(2,1)S(1)}, u32[]{:S(2)}, u32[]{:S(2)}) collective-permute-start(bf16[128,768]{1,0:T(8,128)(2,1)S(1)} %shard_map.118.refs_6_.refs_2_), channel_id=1, source_target_pairs={{0,2},{2,0},{1,3},{3,1},{4,6},{6,4},{5,7},{7,5},{8,10},{10,8},{9,1... | collective-permute-start | bytes 589832 | tf_op jit(solution)/shard_map/ppermute | solution.py:477
  46.9 1.0 %shard_map.119.refs_5_.refs_1_ = bf16[128,1664]{1,0:T(8,128)(2,1)S(1)} custom-call(s32[1]{0:T(128)} %bitcast.3.refs_0_, f32[1,2048]{1,0:T(1,128)S(1)} %bitcast.10, bf16[2,2048,768]{2,1,0:T(8,128)(2,1)S(1)} %copy-done, bf16[2,2048,768]{2,1,0:T(8,128)(2,1)S(1)} %copy-done.1, bf16[64,2048]{1,0:T(8,128)(2,1)S(1)} %collective-permute-done.8.refs_4_, ...), custom_call_target="tpu_custom_call" | custom-call | flops 2400000000 | tf_op jit(solution)/shard_map/pallas_call | solution.py:354
  47.9 1.5 %collective-permute-done.13.refs_4_ = bf16[64,2048]{1,0:T(8,128)(2,1)S(1)} collective-permute-done((bf16[64,2048]{1,0:T(8,128)(2,1)S(1)}, bf16[64,2048]{1,0:T(8,128)(2,1)S(1)}, u32[]{:S(2)}, u32[]{:S(2)}) %collective-permute-start.13) | collective-permute-done | bytes 262176 | tf_op jit(solution)/shard_map/ppermute | solution.py:397
  49.4 1.0 %shard_map.120.refs_4_ = bf16[64,1664]{1,0:T(8,128)(2,1)S(1)} custom-call(s32[1]{0:T(128)S(6)} %sub.7.refs_0_.refs_1_, f32[1,2048]{1,0:T(1,128)S(1)} %bitcast.11, bf16[2,2048,768]{2,1,0:T(8,128)(2,1)S(1)} %copy-done, bf16[2,2048,768]{2,1,0:T(8,128)(2,1)S(1)} %copy-done.1, bf16[64,2048]{1,0:T(8,128)(2,1)S(1)} %collective-permute-done.13.refs_4_, ...), custom_call_target="tpu_custom_call" | custom-call | flops 2400000000 | tf_op jit(solution)/shard_map/pallas_call | solution.py:354
  50.6 3.2 %collective-permute-done.12.refs_2_ = bf16[128,1664]{1,0:T(8,128)(2,1)S(1)} collective-permute-done((bf16[128,1664]{1,0:T(8,128)(2,1)S(1)}, bf16[128,1664]{1,0:T(8,128)(2,1)S(1)}, u32[]{:S(2)}, u32[]{:S(2)}) %collective-permute-start.12) | collective-permute-done | bytes 426016 | tf_op jit(solution)/shard_map/ppermute | solution.py:471
  54.1 2.1 %collective-permute-start.18 = (bf16[128,768]{1,0:T(8,128)(2,1)S(1)}, bf16[128,768]{1,0:T(8,128)(2,1)S(1)}, u32[]{:S(2)}, u32[]{:S(2)}) collective-permute-start(bf16[128,768]{1,0:T(8,128)(2,1)S(1)} %shard_map.121.refs_5_.refs_2_), channel_id=1, source_target_pairs={{0,2},{2,0},{1,3},{3,1},{4,6},{6,4},{5,7},{7,5},{8,10},{10,8},{9,1... | collective-permute-start | bytes 589832 | tf_op jit(solution)/shard_map/ppermute | solution.py:477
  56.2 1.8 %collective-permute-done.11.refs_3_ = bf16[128,768]{1,0:T(8,128)(2,1)S(1)} collective-permute-done((bf16[128,768]{1,0:T(8,128)(2,1)S(1)}, bf16[128,768]{1,0:T(8,128)(2,1)S(1)}, u32[]{:S(2)}, u32[]{:S(2)}) %collective-permute-start.11) | collective-permute-done | bytes 196640 | tf_op jit(solution)/shard_map/ppermute | solution.py:477
  58.0 1.0 %shard_map.122 = (bf16[64,2048]{1,0:T(8,128)(2,1)S(1)}, bf16[64,2048]{1,0:T(8,128)(2,1)S(1)}) custom-call(s32[1]{0:T(128)} %bitcast.3.refs_0_, s32[1]{0:T(128)S(6)} %sub.7.refs_0_.refs_1_, bf16[128,768]{1,0:T(8,128)(2,1)S(1)} %shard_map.118.refs_6_.refs_2_, bf16[128,768]{1,0:T(8,128)(2,1)S(1)} %collective-permute-done.11.refs_3_, ...), custom_call_target="tpu_custom_call" | custom-call | flops 2200000000 | tf_op jit(solution)/shard_map/pallas_call | solution.py:354
  59.0 2.0 %collective-permute-start.14 = (bf16[64,2048]{1,0:T(8,128)(2,1)S(1)}, bf16[64,2048]{1,0:T(8,128)(2,1)S(1)}, u32[]{:S(2)}, u32[]{:S(2)}) collective-permute-start(bf16[64,2048]{1,0:T(8,128)(2,1)S(1)} %get-tuple-element.9.refs_5_), channel_id=1, source_target_pairs={{0,8},{4,12},{8,0},{12,4},{16,24},{20,28},{24,16},{28,20},{1,9},{5... | collective-permute-start | bytes 786440 | tf_op jit(solution)/shard_map/ppermute | solution.py:397
  61.2 1.2 %shard_map.123.refs_1_.refs_4_ = bf16[64,1664]{1,0:T(8,128)(2,1)S(1)} custom-call(s32[1]{0:T(128)} %bitcast.3.refs_0_, f32[1,2048]{1,0:T(1,128)S(1)} %bitcast.12, bf16[2,2048,768]{2,1,0:T(8,128)(2,1)S(1)} %copy-done, bf16[2,2048,768]{2,1,0:T(8,128)(2,1)S(1)} %copy-done.1, bf16[64,2048]{1,0:T(8,128)(2,1)S(1)} %collective-permute-done.13.refs_4_, ...), custom_call_target="tpu_custom_call" | custom-call | flops 2400000000 | tf_op jit(solution)/shard_map/pallas_call | solution.py:354
  62.8 1.6 %collective-permute-start.17 = (bf16[64,768]{1,0:T(8,128)(2,1)S(1)}, bf16[64,768]{1,0:T(8,128)(2,1)S(1)}, u32[]{:S(2)}, u32[]{:S(2)}) collective-permute-start(bf16[64,768]{1,0:T(8,128)(2,1)S(1)} %shard_map.124.refs_5_.refs_2_), channel_id=1, source_target_pairs={{0,2},{2,0},{1,3},{3,1},{4,6},{6,4},{5,7},{7,5},{8,10},{10,8},{9,1... | collective-permute-start | bytes 294920 | tf_op jit(solution)/shard_map/ppermute | solution.py:477
  64.3 1.0 %shard_map.125.refs_5_ = bf16[64,1664]{1,0:T(8,128)(2,1)S(1)} custom-call(s32[1]{0:T(128)S(6)} %sub.7.refs_0_.refs_1_, f32[1,2048]{1,0:T(1,128)S(1)} %bitcast.13, bf16[2,2048,768]{2,1,0:T(8,128)(2,1)S(1)} %copy-done, bf16[2,2048,768]{2,1,0:T(8,128)(2,1)S(1)} %copy-done.1, bf16[64,2048]{1,0:T(8,128)(2,1)S(1)} %collective-permute-done.7.refs_4_, ...), custom_call_target="tpu_custom_call" | custom-call | flops 2400000000 | tf_op jit(solution)/shard_map/pallas_call | solution.py:354
  66.1 2.0 %collective-permute-start.19 = (bf16[64,1664]{1,0:T(8,128)(2,1)S(1)}, bf16[64,1664]{1,0:T(8,128)(2,1)S(1)}, u32[]{:S(2)}, u32[]{:S(2)}) collective-permute-start(bf16[64,1664]{1,0:T(8,128)(2,1)S(1)} %shard_map.125.refs_5_), channel_id=1, source_target_pairs={{0,2},{2,0},{1,3},{3,1},{4,6},{6,4},{5,7},{7,5},{8,10},{10,8},{9,1... | collective-permute-start | bytes 638984 | tf_op jit(solution)/shard_map/ppermute | solution.py:471
  68.1 1.0 %shard_map.126 = (bf16[64,2048]{1,0:T(8,128)(2,1)S(1)}, bf16[64,2048]{1,0:T(8,128)(2,1)S(1)}) custom-call(s32[1]{0:T(128)} %bitcast.3.refs_0_, s32[1]{0:T(128)S(6)} %sub.7.refs_0_.refs_1_, bf16[128,768]{1,0:T(8,128)(2,1)S(1)} %shard_map.121.refs_5_.refs_2_, bf16[128,768]{1,0:T(8,128)(2,1)S(1)} %collective-permute-done.18.refs_3_, ...), custom_call_target="tpu_custom_call" | custom-call | flops 2200000000 | tf_op jit(solution)/shard_map/pallas_call | solution.py:354
  70.9 1.8 %collective-permute-start.23 = (bf16[64,2048]{1,0:T(8,128)(2,1)S(1)}, bf16[64,2048]{1,0:T(8,128)(2,1)S(1)}, u32[]{:S(2)}, u32[]{:S(2)}) collective-permute-start(bf16[64,2048]{1,0:T(8,128)(2,1)S(1)} %shard_map.127.refs_5_), channel_id=1, source_target_pairs={{0,12},{4,8},{8,4},{12,0},{16,28},{20,24},{24,20},{28,16},{1,13},{... | collective-permute-start | bytes 786440 | tf_op jit(solution)/shard_map/ppermute | solution.py:397
  72.7 1.1 %collective-permute-start.22 = (bf16[64,2048]{1,0:T(8,128)(2,1)S(1)}, bf16[64,2048]{1,0:T(8,128)(2,1)S(1)}, u32[]{:S(2)}, u32[]{:S(2)}) collective-permute-start(bf16[64,2048]{1,0:T(8,128)(2,1)S(1)} %get-tuple-element.12), channel_id=1, source_target_pairs={{0,4},{4,0},{8,12},{12,8},{16,20},{20,16},{24,28},{28,24},{1,5},{5... | collective-permute-start | bytes 786440 | tf_op jit(solution)/shard_map/ppermute | solution.py:397
  75.0 1.5 %collective-permute-start.20 = (bf16[64,768]{1,0:T(8,128)(2,1)S(1)}, bf16[64,768]{1,0:T(8,128)(2,1)S(1)}, u32[]{:S(2)}, u32[]{:S(2)}) collective-permute-start(bf16[64,768]{1,0:T(8,128)(2,1)S(1)} %shard_map.129.refs_5_.refs_2_), channel_id=1, source_target_pairs={{0,2},{2,0},{1,3},{3,1},{4,6},{6,4},{5,7},{7,5},{8,10},{10,8},{9,1... | collective-permute-start | bytes 294920 | tf_op jit(solution)/shard_map/ppermute | solution.py:477
  76.5 1.0 %shard_map.130.refs_8_ = bf16[64,1664]{1,0:T(8,128)(2,1)S(1)} custom-call(s32[1]{0:T(128)S(6)} %sub.7.refs_0_.refs_1_, f32[1,2048]{1,0:T(1,128)S(1)} %bitcast.15, bf16[2,2048,768]{2,1,0:T(8,128)(2,1)S(1)} %copy-done, bf16[2,2048,768]{2,1,0:T(8,128)(2,1)S(1)} %copy-done.1, bf16[64,2048]{1,0:T(8,128)(2,1)S(1)} %collective-permute-done.24.refs_4_, ...), custom_call_target="tpu_custom_call" | custom-call | flops 2400000000 | tf_op jit(solution)/shard_map/pallas_call | solution.py:354
  78.2 2.5 %collective-permute-done.20.refs_3_ = bf16[64,768]{1,0:T(8,128)(2,1)S(1)} collective-permute-done((bf16[64,768]{1,0:T(8,128)(2,1)S(1)}, bf16[64,768]{1,0:T(8,128)(2,1)S(1)}, u32[]{:S(2)}, u32[]{:S(2)}) %collective-permute-start.20) | collective-permute-done | bytes 98336 | tf_op jit(solution)/shard_map/ppermute | solution.py:477
  81.6 1.1 %shard_map.131.refs_5_ = bf16[64,2048]{1,0:T(8,128)(2,1)S(1)} custom-call(s32[1]{0:T(128)} %bitcast.3.refs_0_, s32[1]{0:T(128)S(6)} %sub.7.refs_0_.refs_1_, bf16[64,768]{1,0:T(8,128)(2,1)S(1)} %shard_map.129.refs_5_.refs_2_, bf16[64,768]{1,0:T(8,128)(2,1)S(1)} %collective-permute-done.20.refs_3_, bf16[2,768,2048]{2,1,0:T(8,128)(2,1)S(1)} %bitcast.18, ...), custom_call_target="tpu_custom_call" | custom-call | flops 2200000000 | tf_op jit(solution)/shard_map/pallas_call | solution.py:354
  82.7 1.0 %shard_map.132.refs_1_.refs_4_ = bf16[64,1664]{1,0:T(8,128)(2,1)S(1)} custom-call(s32[1]{0:T(128)} %bitcast.3.refs_0_, f32[1,2048]{1,0:T(1,128)S(1)} %bitcast.16, bf16[2,2048,768]{2,1,0:T(8,128)(2,1)S(1)} %copy-done, bf16[2,2048,768]{2,1,0:T(8,128)(2,1)S(1)} %copy-done.1, bf16[64,2048]{1,0:T(8,128)(2,1)S(1)} %collective-permute-done.24.refs_4_, ...), custom_call_target="tpu_custom_call" | custom-call | flops 2400000000 | tf_op jit(solution)/shard_map/pallas_call | solution.py:354
  84.7 1.7 %collective-permute-start.25 = (bf16[64,2048]{1,0:T(8,128)(2,1)S(1)}, bf16[64,2048]{1,0:T(8,128)(2,1)S(1)}, u32[]{:S(2)}, u32[]{:S(2)}) collective-permute-start(bf16[64,2048]{1,0:T(8,128)(2,1)S(1)} %shard_map.131.refs_5_), channel_id=1, source_target_pairs={{0,16},{4,20},{8,24},{12,28},{16,0},{20,4},{24,8},{28,12},{1,17},{... | collective-permute-start | bytes 786440 | tf_op jit(solution)/shard_map/ppermute | solution.py:397
  86.5 2.1 %collective-permute-done.27.refs_3_ = bf16[64,768]{1,0:T(8,128)(2,1)S(1)} collective-permute-done((bf16[64,768]{1,0:T(8,128)(2,1)S(1)}, bf16[64,768]{1,0:T(8,128)(2,1)S(1)}, u32[]{:S(2)}, u32[]{:S(2)}) %collective-permute-start.27) | collective-permute-done | bytes 98336 | tf_op jit(solution)/shard_map/ppermute | solution.py:477
  89.6 1.3 %collective-permute-start.28 = (bf16[64,2048]{1,0:T(8,128)(2,1)S(1)}, bf16[64,2048]{1,0:T(8,128)(2,1)S(1)}, u32[]{:S(2)}, u32[]{:S(2)}) collective-permute-start(bf16[64,2048]{1,0:T(8,128)(2,1)S(1)} %shard_map.134.refs_6_), channel_id=1, source_target_pairs={{0,12},{4,8},{8,4},{12,0},{16,28},{20,24},{24,20},{28,16},{1,13},{... | collective-permute-start | bytes 786440 | tf_op jit(solution)/shard_map/ppermute | solution.py:397
  90.8 3.8 %collective-permute-done.25.refs_4_ = bf16[64,2048]{1,0:T(8,128)(2,1)S(1)} collective-permute-done((bf16[64,2048]{1,0:T(8,128)(2,1)S(1)}, bf16[64,2048]{1,0:T(8,128)(2,1)S(1)}, u32[]{:S(2)}, u32[]{:S(2)}) %collective-permute-start.25) | collective-permute-done | bytes 262176 | tf_op jit(solution)/shard_map/ppermute | solution.py:397
  94.7 3.2 %collective-permute-done.28.refs_5_ = bf16[64,2048]{1,0:T(8,128)(2,1)S(1)} collective-permute-done((bf16[64,2048]{1,0:T(8,128)(2,1)S(1)}, bf16[64,2048]{1,0:T(8,128)(2,1)S(1)}, u32[]{:S(2)}, u32[]{:S(2)}) %collective-permute-start.28) | collective-permute-done | bytes 262176 | tf_op jit(solution)/shard_map/ppermute | solution.py:397
  (61 shorter events, 14.0 us)
Async XLA Ops:
  1.6 16.1 %copy-start.3 = (bf16[64,2048]{1,0:T(8,128)(2,1)S(1)}, bf16[64,2048]{1,0:T(8,128)(2,1)}, u32[]{:S(2)}) copy-start(bf16[64,2048]{1,0:T(8,128)(2,1)} %refs_2_.13) | copy-start | bytes 786436
  1.6 16.1 %copy-start.4 = (bf16[64,2048]{1,0:T(8,128)(2,1)S(1)}, bf16[64,2048]{1,0:T(8,128)(2,1)}, u32[]{:S(2)}) copy-start(bf16[64,2048]{1,0:T(8,128)(2,1)} %refs_4_.7) | copy-start | bytes 786436
  1.6 16.1 %copy-start.5 = (s32[8]{0:T(128)S(1)}, s32[8]{0:T(128)}, u32[]{:S(2)}) copy-start(s32[8]{0:T(128)} %refs_1_.1) | copy-start | bytes 100
  1.6 6.4 %collective-permute-start = (bf16[144,128]{1,0:T(8,128)(2,1)S(1)}, bf16[144,128]{1,0:T(8,128)(2,1)S(1)}, u32[]{:S(2)}, u32[]{:S(2)}) collective-permute-start(bf16[144,128]{1,0:T(8,128)(2,1)S(1)} %shard_map.109.refs_5_), channel_id=1, source_target_pairs={{0,16},{4,20},{8,24},{12,28},{16,0},{20,4},{24,8},{28,12},{1,17},{... | collective-permute-start | bytes 110600 | tf_op jit(solution)/shard_map/ppermute | solution.py:78
  8.0 4.4 %collective-permute-start.1 = (bf16[288,128]{1,0:T(8,128)(2,1)S(1)}, bf16[288,128]{1,0:T(8,128)(2,1)S(1)}, u32[]{:S(2)}, u32[]{:S(2)}) collective-permute-start(bf16[288,128]{1,0:T(8,128)(2,1)S(1)} %pad_maximum_fusion.2), channel_id=1, source_target_pairs={{0,8},{4,12},{8,0},{12,4},{16,24},{20,28},{24,16},{28,20},{1,9},{5... | collective-permute-start | bytes 221192 | tf_op jit(solution)/shard_map/ppermute | solution.py:78
  12.4 5.2 %collective-permute-start.2 = (bf16[576,128]{1,0:T(8,128)(2,1)S(1)}, bf16[576,128]{1,0:T(8,128)(2,1)S(1)}, u32[]{:S(2)}, u32[]{:S(2)}) collective-permute-start(bf16[576,128]{1,0:T(8,128)(2,1)S(1)} %pad_maximum_fusion.1), channel_id=1, source_target_pairs={{0,4},{4,0},{8,12},{12,8},{16,20},{20,16},{24,28},{28,24},{1,5},{5... | collective-permute-start | bytes 442376 | tf_op jit(solution)/shard_map/ppermute | solution.py:78
  17.6 7.8 %copy-start = (bf16[2,2048,768]{2,1,0:T(8,128)(2,1)S(1)}, bf16[2,2048,768]{2,1,0:T(8,128)(2,1)}, u32[]{:S(2)}) copy-start(bf16[2,2048,768]{2,1,0:T(8,128)(2,1)} %refs_2_.25) | copy-start | bytes 18874372
  17.7 7.8 %copy-start.1 = (bf16[2,2048,768]{2,1,0:T(8,128)(2,1)S(1)}, bf16[2,2048,768]{2,1,0:T(8,128)(2,1)}, u32[]{:S(2)}) copy-start(bf16[2,2048,768]{2,1,0:T(8,128)(2,1)} %refs_3_.23) | copy-start | bytes 18874372
  17.7 7.8 %copy-start.2 = (f32[2048]{0:T(1024)S(1)}, f32[2048]{0:T(1024)}, u32[]{:S(2)}) copy-start(f32[2048]{0:T(1024)} %param.16) | copy-start | bytes 24580
  19.5 9.6 %collective-permute-start.4 = (bf16[64,2048]{1,0:T(8,128)(2,1)S(1)}, bf16[64,2048]{1,0:T(8,128)(2,1)S(1)}, u32[]{:S(2)}, u32[]{:S(2)}) collective-permute-start(bf16[64,2048]{1,0:T(8,128)(2,1)S(1)} %shard_map.110.refs_4_.refs_5_.refs_0_), channel_id=1, source_target_pairs={{0,8},{4,12},{8,0},{12,4},{16,24},{20,28},{24,16},{28,20},{1,9},{5... | collective-permute-start | bytes 786440 | tf_op jit(solution)/shard_map/ppermute | solution.py:397
  21.1 8.0 %collective-permute-start.5 = (bf16[64,2048]{1,0:T(8,128)(2,1)S(1)}, bf16[64,2048]{1,0:T(8,128)(2,1)S(1)}, u32[]{:S(2)}, u32[]{:S(2)}) collective-permute-start(bf16[64,2048]{1,0:T(8,128)(2,1)S(1)} %shard_map.110.refs_4_.refs_5_.refs_0_), channel_id=1, source_target_pairs={{0,4},{4,0},{8,12},{12,8},{16,20},{20,16},{24,28},{28,24},{1,5},{5... | collective-permute-start | bytes 786440 | tf_op jit(solution)/shard_map/ppermute | solution.py:397
  22.6 10.9 %collective-permute-start.7 = (bf16[64,2048]{1,0:T(8,128)(2,1)S(1)}, bf16[64,2048]{1,0:T(8,128)(2,1)S(1)}, u32[]{:S(2)}, u32[]{:S(2)}) collective-permute-start(bf16[64,2048]{1,0:T(8,128)(2,1)S(1)} %shard_map.110.refs_4_.refs_5_.refs_0_), channel_id=1, source_target_pairs={{0,16},{4,20},{8,24},{12,28},{16,0},{20,4},{24,8},{28,12},{1,17},{... | collective-permute-start | bytes 786440 | tf_op jit(solution)/shard_map/ppermute | solution.py:397
  27.5 8.3 %collective-permute-start.3 = (bf16[64,1664]{1,0:T(8,128)(2,1)S(1)}, bf16[64,1664]{1,0:T(8,128)(2,1)S(1)}, u32[]{:S(2)}, u32[]{:S(2)}) collective-permute-start(bf16[64,1664]{1,0:T(8,128)(2,1)S(1)} %shard_map.111.refs_5_), channel_id=1, source_target_pairs={{0,2},{2,0},{1,3},{3,1},{4,6},{6,4},{5,7},{7,5},{8,10},{10,8},{9,1... | collective-permute-start | bytes 638984 | tf_op jit(solution)/shard_map/ppermute | solution.py:471
  30.1 15.4 %collective-permute-start.10 = (bf16[128,1664]{1,0:T(8,128)(2,1)S(1)}, bf16[128,1664]{1,0:T(8,128)(2,1)S(1)}, u32[]{:S(2)}, u32[]{:S(2)}) collective-permute-start(bf16[128,1664]{1,0:T(8,128)(2,1)S(1)} %shard_map.113.refs_4_), channel_id=1, source_target_pairs={{0,2},{2,0},{1,3},{3,1},{4,6},{6,4},{5,7},{7,5},{8,10},{10,8},{9,1... | collective-permute-start | bytes 1277960 | tf_op jit(solution)/shard_map/ppermute | solution.py:471
  33.5 6.4 %collective-permute-start.8 = (bf16[64,2048]{1,0:T(8,128)(2,1)S(1)}, bf16[64,2048]{1,0:T(8,128)(2,1)S(1)}, u32[]{:S(2)}, u32[]{:S(2)}) collective-permute-start(bf16[64,2048]{1,0:T(8,128)(2,1)S(1)} %collective-permute-done.7.refs_4_), channel_id=1, source_target_pairs={{0,8},{4,12},{8,0},{12,4},{16,24},{20,28},{24,16},{28,20},{1,9},{5... | collective-permute-start | bytes 786440 | tf_op jit(solution)/shard_map/ppermute | solution.py:397
  33.5 6.4 %collective-permute-start.9 = (bf16[64,2048]{1,0:T(8,128)(2,1)S(1)}, bf16[64,2048]{1,0:T(8,128)(2,1)S(1)}, u32[]{:S(2)}, u32[]{:S(2)}) collective-permute-start(bf16[64,2048]{1,0:T(8,128)(2,1)S(1)} %collective-permute-done.7.refs_4_), channel_id=1, source_target_pairs={{0,4},{4,0},{8,12},{12,8},{16,20},{20,16},{24,28},{28,24},{1,5},{5... | collective-permute-start | bytes 786440 | tf_op jit(solution)/shard_map/ppermute | solution.py:397
  35.9 8.5 %collective-permute-start.6 = (bf16[64,768]{1,0:T(8,128)(2,1)S(1)}, bf16[64,768]{1,0:T(8,128)(2,1)S(1)}, u32[]{:S(2)}, u32[]{:S(2)}) collective-permute-start(bf16[64,768]{1,0:T(8,128)(2,1)S(1)} %shard_map.114.refs_6_.refs_2_), channel_id=1, source_target_pairs={{0,2},{2,0},{1,3},{3,1},{4,6},{6,4},{5,7},{7,5},{8,10},{10,8},{9,1... | collective-permute-start | bytes 294920 | tf_op jit(solution)/shard_map/ppermute | solution.py:477
  37.5 39.0 %collective-permute-start.24 = (bf16[64,2048]{1,0:T(8,128)(2,1)S(1)}, bf16[64,2048]{1,0:T(8,128)(2,1)S(1)}, u32[]{:S(2)}, u32[]{:S(2)}) collective-permute-start(bf16[64,2048]{1,0:T(8,128)(2,1)S(1)} %collective-permute-done.4.refs_4_), channel_id=1, source_target_pairs={{0,4},{4,0},{8,12},{12,8},{16,20},{20,16},{24,28},{28,24},{1,5},{5... | collective-permute-start | bytes 786440 | tf_op jit(solution)/shard_map/ppermute | solution.py:397
  38.0 6.4 %slice-start = ((s8[6291456]{0:T(1024)(128)(4,1)}), s8[4194304]{0:T(1024)(128)(4,1)S(1)}, s32[]{:S(2)}) async-start(s8[6291456]{0:T(1024)(128)(4,1)} %bitcast.17), calls=%async_computation | async-start | bytes 8388608
  39.1 5.4 %slice-start.1 = ((s8[6291456]{0:T(1024)(128)(4,1)}), s8[2097152]{0:T(1024)(128)(4,1)S(1)}, s32[]{:S(2)}) async-start(s8[6291456]{0:T(1024)(128)(4,1)} %bitcast.17), calls=%async_computation.1 | async-start | bytes 4194304
  40.9 12.9 %collective-permute-start.12 = (bf16[128,1664]{1,0:T(8,128)(2,1)S(1)}, bf16[128,1664]{1,0:T(8,128)(2,1)S(1)}, u32[]{:S(2)}, u32[]{:S(2)}) collective-permute-start(bf16[128,1664]{1,0:T(8,128)(2,1)S(1)} %shard_map.116.refs_5_), channel_id=1, source_target_pairs={{0,2},{2,0},{1,3},{3,1},{4,6},{6,4},{5,7},{7,5},{8,10},{10,8},{9,1... | collective-permute-start | bytes 1277960 | tf_op jit(solution)/shard_map/ppermute | solution.py:471
  43.0 6.4 %collective-permute-start.13 = (bf16[64,2048]{1,0:T(8,128)(2,1)S(1)}, bf16[64,2048]{1,0:T(8,128)(2,1)S(1)}, u32[]{:S(2)}, u32[]{:S(2)}) collective-permute-start(bf16[64,2048]{1,0:T(8,128)(2,1)S(1)} %collective-permute-done.9.refs_5_), channel_id=1, source_target_pairs={{0,8},{4,12},{8,0},{12,4},{16,24},{20,28},{24,16},{28,20},{1,9},{5... | collective-permute-start | bytes 786440 | tf_op jit(solution)/shard_map/ppermute | solution.py:397
  45.8 12.2 %collective-permute-start.11 = (bf16[128,768]{1,0:T(8,128)(2,1)S(1)}, bf16[128,768]{1,0:T(8,128)(2,1)S(1)}, u32[]{:S(2)}, u32[]{:S(2)}) collective-permute-start(bf16[128,768]{1,0:T(8,128)(2,1)S(1)} %shard_map.118.refs_6_.refs_2_), channel_id=1, source_target_pairs={{0,2},{2,0},{1,3},{3,1},{4,6},{6,4},{5,7},{7,5},{8,10},{10,8},{9,1... | collective-permute-start | bytes 589832 | tf_op jit(solution)/shard_map/ppermute | solution.py:477
  50.4 12.1 %collective-permute-start.16 = (bf16[64,1664]{1,0:T(8,128)(2,1)S(1)}, bf16[64,1664]{1,0:T(8,128)(2,1)S(1)}, u32[]{:S(2)}, u32[]{:S(2)}) collective-permute-start(bf16[64,1664]{1,0:T(8,128)(2,1)S(1)} %shard_map.120.refs_4_), channel_id=1, source_target_pairs={{0,2},{2,0},{1,3},{3,1},{4,6},{6,4},{5,7},{7,5},{8,10},{10,8},{9,1... | collective-permute-start | bytes 638984 | tf_op jit(solution)/shard_map/ppermute | solution.py:471
  54.1 12.0 %collective-permute-start.18 = (bf16[128,768]{1,0:T(8,128)(2,1)S(1)}, bf16[128,768]{1,0:T(8,128)(2,1)S(1)}, u32[]{:S(2)}, u32[]{:S(2)}) collective-permute-start(bf16[128,768]{1,0:T(8,128)(2,1)S(1)} %shard_map.121.refs_5_.refs_2_), channel_id=1, source_target_pairs={{0,2},{2,0},{1,3},{3,1},{4,6},{6,4},{5,7},{7,5},{8,10},{10,8},{9,1... | collective-permute-start | bytes 589832 | tf_op jit(solution)/shard_map/ppermute | solution.py:477
  59.0 11.9 %collective-permute-start.14 = (bf16[64,2048]{1,0:T(8,128)(2,1)S(1)}, bf16[64,2048]{1,0:T(8,128)(2,1)S(1)}, u32[]{:S(2)}, u32[]{:S(2)}) collective-permute-start(bf16[64,2048]{1,0:T(8,128)(2,1)S(1)} %get-tuple-element.9.refs_5_), channel_id=1, source_target_pairs={{0,8},{4,12},{8,0},{12,4},{16,24},{20,28},{24,16},{28,20},{1,9},{5... | collective-permute-start | bytes 786440 | tf_op jit(solution)/shard_map/ppermute | solution.py:397
  61.0 11.7 %collective-permute-start.15 = (bf16[64,2048]{1,0:T(8,128)(2,1)S(1)}, bf16[64,2048]{1,0:T(8,128)(2,1)S(1)}, u32[]{:S(2)}, u32[]{:S(2)}) collective-permute-start(bf16[64,2048]{1,0:T(8,128)(2,1)S(1)} %get-tuple-element.10), channel_id=1, source_target_pairs={{0,4},{4,0},{8,12},{12,8},{16,20},{20,16},{24,28},{28,24},{1,5},{5... | collective-permute-start | bytes 786440 | tf_op jit(solution)/shard_map/ppermute | solution.py:397
  62.8 6.4 %collective-permute-start.17 = (bf16[64,768]{1,0:T(8,128)(2,1)S(1)}, bf16[64,768]{1,0:T(8,128)(2,1)S(1)}, u32[]{:S(2)}, u32[]{:S(2)}) collective-permute-start(bf16[64,768]{1,0:T(8,128)(2,1)S(1)} %shard_map.124.refs_5_.refs_2_), channel_id=1, source_target_pairs={{0,2},{2,0},{1,3},{3,1},{4,6},{6,4},{5,7},{7,5},{8,10},{10,8},{9,1... | collective-permute-start | bytes 294920 | tf_op jit(solution)/shard_map/ppermute | solution.py:477
  66.1 8.7 %collective-permute-start.19 = (bf16[64,1664]{1,0:T(8,128)(2,1)S(1)}, bf16[64,1664]{1,0:T(8,128)(2,1)S(1)}, u32[]{:S(2)}, u32[]{:S(2)}) collective-permute-start(bf16[64,1664]{1,0:T(8,128)(2,1)S(1)} %shard_map.125.refs_5_), channel_id=1, source_target_pairs={{0,2},{2,0},{1,3},{3,1},{4,6},{6,4},{5,7},{7,5},{8,10},{10,8},{9,1... | collective-permute-start | bytes 638984 | tf_op jit(solution)/shard_map/ppermute | solution.py:471
  69.1 11.5 %collective-permute-start.21 = (bf16[64,2048]{1,0:T(8,128)(2,1)S(1)}, bf16[64,2048]{1,0:T(8,128)(2,1)S(1)}, u32[]{:S(2)}, u32[]{:S(2)}) collective-permute-start(bf16[64,2048]{1,0:T(8,128)(2,1)S(1)} %get-tuple-element.11.refs_5_), channel_id=1, source_target_pairs={{0,8},{4,12},{8,0},{12,4},{16,24},{20,28},{24,16},{28,20},{1,9},{5... | collective-permute-start | bytes 786440 | tf_op jit(solution)/shard_map/ppermute | solution.py:397
  70.9 9.8 %collective-permute-start.23 = (bf16[64,2048]{1,0:T(8,128)(2,1)S(1)}, bf16[64,2048]{1,0:T(8,128)(2,1)S(1)}, u32[]{:S(2)}, u32[]{:S(2)}) collective-permute-start(bf16[64,2048]{1,0:T(8,128)(2,1)S(1)} %shard_map.127.refs_5_), channel_id=1, source_target_pairs={{0,12},{4,8},{8,4},{12,0},{16,28},{20,24},{24,20},{28,16},{1,13},{... | collective-permute-start | bytes 786440 | tf_op jit(solution)/shard_map/ppermute | solution.py:397
  72.7 8.9 %collective-permute-start.22 = (bf16[64,2048]{1,0:T(8,128)(2,1)S(1)}, bf16[64,2048]{1,0:T(8,128)(2,1)S(1)}, u32[]{:S(2)}, u32[]{:S(2)}) collective-permute-start(bf16[64,2048]{1,0:T(8,128)(2,1)S(1)} %get-tuple-element.12), channel_id=1, source_target_pairs={{0,4},{4,0},{8,12},{12,8},{16,20},{20,16},{24,28},{28,24},{1,5},{5... | collective-permute-start | bytes 786440 | tf_op jit(solution)/shard_map/ppermute | solution.py:397
  75.0 5.6 %collective-permute-start.20 = (bf16[64,768]{1,0:T(8,128)(2,1)S(1)}, bf16[64,768]{1,0:T(8,128)(2,1)S(1)}, u32[]{:S(2)}, u32[]{:S(2)}) collective-permute-start(bf16[64,768]{1,0:T(8,128)(2,1)S(1)} %shard_map.129.refs_5_.refs_2_), channel_id=1, source_target_pairs={{0,2},{2,0},{1,3},{3,1},{4,6},{6,4},{5,7},{7,5},{8,10},{10,8},{9,1... | collective-permute-start | bytes 294920 | tf_op jit(solution)/shard_map/ppermute | solution.py:477
  77.5 6.2 %collective-permute-start.26 = (bf16[64,1664]{1,0:T(8,128)(2,1)S(1)}, bf16[64,1664]{1,0:T(8,128)(2,1)S(1)}, u32[]{:S(2)}, u32[]{:S(2)}) collective-permute-start(bf16[64,1664]{1,0:T(8,128)(2,1)S(1)} %shard_map.130.refs_8_), channel_id=1, source_target_pairs={{0,2},{2,0},{1,3},{3,1},{4,6},{6,4},{5,7},{7,5},{8,10},{10,8},{9,1... | collective-permute-start | bytes 638984 | tf_op jit(solution)/shard_map/ppermute | solution.py:471
  83.9 4.7 %collective-permute-start.27 = (bf16[64,768]{1,0:T(8,128)(2,1)S(1)}, bf16[64,768]{1,0:T(8,128)(2,1)S(1)}, u32[]{:S(2)}, u32[]{:S(2)}) collective-permute-start(bf16[64,768]{1,0:T(8,128)(2,1)S(1)} %shard_map.133.refs_2_.refs_5_), channel_id=1, source_target_pairs={{0,2},{2,0},{1,3},{3,1},{4,6},{6,4},{5,7},{7,5},{8,10},{10,8},{9,1... | collective-permute-start | bytes 294920 | tf_op jit(solution)/shard_map/ppermute | solution.py:477
  84.7 10.0 %collective-permute-start.25 = (bf16[64,2048]{1,0:T(8,128)(2,1)S(1)}, bf16[64,2048]{1,0:T(8,128)(2,1)S(1)}, u32[]{:S(2)}, u32[]{:S(2)}) collective-permute-start(bf16[64,2048]{1,0:T(8,128)(2,1)S(1)} %shard_map.131.refs_5_), channel_id=1, source_target_pairs={{0,16},{4,20},{8,24},{12,28},{16,0},{20,4},{24,8},{28,12},{1,17},{... | collective-permute-start | bytes 786440 | tf_op jit(solution)/shard_map/ppermute | solution.py:397
  89.6 8.4 %collective-permute-start.28 = (bf16[64,2048]{1,0:T(8,128)(2,1)S(1)}, bf16[64,2048]{1,0:T(8,128)(2,1)S(1)}, u32[]{:S(2)}, u32[]{:S(2)}) collective-permute-start(bf16[64,2048]{1,0:T(8,128)(2,1)S(1)} %shard_map.134.refs_6_), channel_id=1, source_target_pairs={{0,12},{4,8},{8,4},{12,0},{16,28},{20,24},{24,20},{28,16},{1,13},{... | collective-permute-start | bytes 786440 | tf_op jit(solution)/shard_map/ppermute | solution.py:397

commit v7 on v6

--- a/solution.py
+++ b/solution.py
@@ -43,8 +43,8 @@
     ("keep", 2),
     ("send", 3),
     ("hidden", 2),
+    ("keep", 3),
     ("both", 1),
-    ("keep", 3),
     ("hidden", 3),
     ("send", 4),
     ("both", 2),
@@ -54,8 +54,8 @@
     ("keep", 4),
     ("hidden", 4),
     ("send", 5),
+    ("keep", 5),
     ("both", 4),
-    ("keep", 5),
     ("hidden", 5),
     ("both", 5),
     ("sum", 0),

time: 99.1 us -> 98.5 us (level)
    ppermute x6, waiting for transfers between devices: 7.16 us -> 5.72 us  [local(): other_hidden[i] = lax.ppermute(hidden[i], 'exp', swap)]
    ppermute x6, waiting for transfers between devices: 4.03 us -> 5.43 us  [local(): arrived[i] = lax.ppermute(product, 'exp', swap)]
    ppermute x14, starting transfers between devices: 18.3 us -> 17.1 us  [hop(): return lax.ppermute(block, 'ctx', xor_pairs(ctx_count, offset))]
  transfers between devices with their start and end apart: 29 -> 29, of which waited for: 16 -> 17; matrix products, arithmetic and copies ran while one was open for 0% -> 0% of each run, Pallas kernels for 20% -> 20%
where the time goes in v7:
time: 98.5 us; the launch traced here: 98.2 us
  starting transfers between devices  40.5 us (41%)
  waiting for transfers between devices  33.2 us (34%)
  Pallas kernels  22.5 us (23%)
    pallas_call x27, Pallas kernels, __call__(): pl.pallas_call(body, out_shape=out_shape, in_specs=specs, out_specs=[vmem...  22.5 us
    ppermute x14, starting transfers between devices, hop(): return lax.ppermute(block, 'ctx', xor_pairs(ctx_count, offset))  17.1 us
    ppermute x14, waiting for transfers between devices, hop(): return lax.ppermute(block, 'ctx', xor_pairs(ctx_count, offset))  13.4 us
    ppermute x6, starting transfers between devices, local(): other_hidden[i] = lax.ppermute(hidden[i], 'exp', swap)  8.83 us
    ppermute x3, waiting for transfers between devices, gather_rows(): lax.ppermute(block, 'ctx', xor_pairs(count, bit))  8.59 us
    ppermute x3, starting transfers between devices, gather_rows(): lax.ppermute(block, 'ctx', xor_pairs(count, bit))  7.41 us
    ppermute x6, starting transfers between devices, local(): arrived[i] = lax.ppermute(product, 'exp', swap)  7.19 us
    ppermute x6, waiting for transfers between devices, local(): other_hidden[i] = lax.ppermute(hidden[i], 'exp', swap)  5.72 us
  transfers between devices with their start and end apart: 29, of which 17 were waited for; matrix products, arithmetic and copies ran while one was open for 0% of the time, Pallas kernels for 20%

profile of v7, /device:TPU:0, one launch (start us, length us, event | category | flops | bytes accessed | tf_op | source)
XLA Modules:
  0.0 98.2 jit_solution(4232389520626429942)
XLA Ops:
  1.6 4.1 %collective-permute-start = (bf16[144,128]{1,0:T(8,128)(2,1)S(1)}, bf16[144,128]{1,0:T(8,128)(2,1)S(1)}, u32[]{:S(2)}, u32[]{:S(2)}) collective-permute-start(bf16[144,128]{1,0:T(8,128)(2,1)S(1)} %shard_map.109.refs_5_), channel_id=1, source_target_pairs={{0,16},{4,20},{8,24},{12,28},{16,0},{20,4},{24,8},{28,12},{1,17},{... | collective-permute-start | bytes 110600 | tf_op jit(solution)/shard_map/ppermute | solution.py:78
  5.7 2.3 %collective-permute-done = bf16[144,128]{1,0:T(8,128)(2,1)S(1)} collective-permute-done((bf16[144,128]{1,0:T(8,128)(2,1)S(1)}, bf16[144,128]{1,0:T(8,128)(2,1)S(1)}, u32[]{:S(2)}, u32[]{:S(2)}) %collective-permute-start) | collective-permute-done | bytes 36896 | tf_op jit(solution)/shard_map/ppermute | solution.py:78
  8.0 1.5 %collective-permute-start.1 = (bf16[288,128]{1,0:T(8,128)(2,1)S(1)}, bf16[288,128]{1,0:T(8,128)(2,1)S(1)}, u32[]{:S(2)}, u32[]{:S(2)}) collective-permute-start(bf16[288,128]{1,0:T(8,128)(2,1)S(1)} %pad_maximum_fusion.2), channel_id=1, source_target_pairs={{0,8},{4,12},{8,0},{12,4},{16,24},{20,28},{24,16},{28,20},{1,9},{5... | collective-permute-start | bytes 221192 | tf_op jit(solution)/shard_map/ppermute | solution.py:78
  9.5 2.8 %collective-permute-done.1 = bf16[288,128]{1,0:T(8,128)(2,1)S(1)} collective-permute-done((bf16[288,128]{1,0:T(8,128)(2,1)S(1)}, bf16[288,128]{1,0:T(8,128)(2,1)S(1)}, u32[]{:S(2)}, u32[]{:S(2)}) %collective-permute-start.1) | collective-permute-done | bytes 73760 | tf_op jit(solution)/shard_map/ppermute | solution.py:78
  12.4 1.8 %collective-permute-start.2 = (bf16[576,128]{1,0:T(8,128)(2,1)S(1)}, bf16[576,128]{1,0:T(8,128)(2,1)S(1)}, u32[]{:S(2)}, u32[]{:S(2)}) collective-permute-start(bf16[576,128]{1,0:T(8,128)(2,1)S(1)} %pad_maximum_fusion.1), channel_id=1, source_target_pairs={{0,4},{4,0},{8,12},{12,8},{16,20},{20,16},{24,28},{28,24},{1,5},{5... | collective-permute-start | bytes 442376 | tf_op jit(solution)/shard_map/ppermute | solution.py:78
  14.2 3.4 %collective-permute-done.2 = bf16[576,128]{1,0:T(8,128)(2,1)S(1)} collective-permute-done((bf16[576,128]{1,0:T(8,128)(2,1)S(1)}, bf16[576,128]{1,0:T(8,128)(2,1)S(1)}, u32[]{:S(2)}, u32[]{:S(2)}) %collective-permute-start.2) | collective-permute-done | bytes 147488 | tf_op jit(solution)/shard_map/ppermute | solution.py:78
  17.7 1.8 %shard_map.110.refs_4_.refs_5_.refs_0_ = bf16[64,2048]{1,0:T(8,128)(2,1)S(1)} custom-call(s32[1]{0:T(128)} %bitcast.refs_0_, s32[8]{0:T(128)S(1)} %copy-done.5, bf16[64,2048]{1,0:T(8,128)(2,1)S(1)} %copy-done.3, bf16[1152,128]{1,0:T(8,128)(2,1)S(1)} %pad_maximum_fusion.refs_3_, bf16[64,2048]{1,0:T(8,128)(2,1)S(1)} %copy-done.4, ...), custom_call_target="tpu_custom_call" | custom-call | flops 10000000000 | tf_op jit(solution)/shard_map/pallas_call | solution.py:354
  19.5 1.6 %collective-permute-start.4 = (bf16[64,2048]{1,0:T(8,128)(2,1)S(1)}, bf16[64,2048]{1,0:T(8,128)(2,1)S(1)}, u32[]{:S(2)}, u32[]{:S(2)}) collective-permute-start(bf16[64,2048]{1,0:T(8,128)(2,1)S(1)} %shard_map.110.refs_4_.refs_5_.refs_0_), channel_id=1, source_target_pairs={{0,8},{4,12},{8,0},{12,4},{16,24},{20,28},{24,16},{28,20},{1,9},{5... | collective-permute-start | bytes 786440 | tf_op jit(solution)/shard_map/ppermute | solution.py:397
  21.1 1.5 %collective-permute-start.5 = (bf16[64,2048]{1,0:T(8,128)(2,1)S(1)}, bf16[64,2048]{1,0:T(8,128)(2,1)S(1)}, u32[]{:S(2)}, u32[]{:S(2)}) collective-permute-start(bf16[64,2048]{1,0:T(8,128)(2,1)S(1)} %shard_map.110.refs_4_.refs_5_.refs_0_), channel_id=1, source_target_pairs={{0,4},{4,0},{8,12},{12,8},{16,20},{20,16},{24,28},{28,24},{1,5},{5... | collective-permute-start | bytes 786440 | tf_op jit(solution)/shard_map/ppermute | solution.py:397
  22.6 2.9 %collective-permute-start.7 = (bf16[64,2048]{1,0:T(8,128)(2,1)S(1)}, bf16[64,2048]{1,0:T(8,128)(2,1)S(1)}, u32[]{:S(2)}, u32[]{:S(2)}) collective-permute-start(bf16[64,2048]{1,0:T(8,128)(2,1)S(1)} %shard_map.110.refs_4_.refs_5_.refs_0_), channel_id=1, source_target_pairs={{0,16},{4,20},{8,24},{12,28},{16,0},{20,4},{24,8},{28,12},{1,17},{... | collective-permute-start | bytes 786440 | tf_op jit(solution)/shard_map/ppermute | solution.py:397
  25.5 1.0 %shard_map.111.refs_5_ = bf16[64,1664]{1,0:T(8,128)(2,1)S(1)} custom-call(s32[1]{0:T(128)S(6)} %sub.7.refs_0_.refs_1_, f32[1,2048]{1,0:T(1,128)S(1)} %bitcast.5, bf16[2,2048,768]{2,1,0:T(8,128)(2,1)S(1)} %copy-done, bf16[2,2048,768]{2,1,0:T(8,128)(2,1)S(1)} %copy-done.1, bf16[64,2048]{1,0:T(8,128)(2,1)S(1)} %shard_map.110.refs_4_.refs_5_.refs_0_, ...), custom_call_target="tpu_custom_call" | custom-call | flops 2400000000 | tf_op jit(solution)/shard_map/pallas_call | solution.py:354
  26.5 1.0 %shard_map.112.refs_6_.refs_1_ = bf16[64,1664]{1,0:T(8,128)(2,1)S(1)} custom-call(s32[1]{0:T(128)} %bitcast.3.refs_0_, f32[1,2048]{1,0:T(1,128)S(1)} %bitcast.6, bf16[2,2048,768]{2,1,0:T(8,128)(2,1)S(1)} %copy-done, bf16[2,2048,768]{2,1,0:T(8,128)(2,1)S(1)} %copy-done.1, bf16[64,2048]{1,0:T(8,128)(2,1)S(1)} %shard_map.110.refs_4_.refs_5_.refs_0_, ...), custom_call_target="tpu_custom_call" | custom-call | flops 2400000000 | tf_op jit(solution)/shard_map/pallas_call | solution.py:354
  27.5 1.6 %collective-permute-start.3 = (bf16[64,1664]{1,0:T(8,128)(2,1)S(1)}, bf16[64,1664]{1,0:T(8,128)(2,1)S(1)}, u32[]{:S(2)}, u32[]{:S(2)}) collective-permute-start(bf16[64,1664]{1,0:T(8,128)(2,1)S(1)} %shard_map.111.refs_5_), channel_id=1, source_target_pairs={{0,2},{2,0},{1,3},{3,1},{4,6},{6,4},{5,7},{7,5},{8,10},{10,8},{9,1... | collective-permute-start | bytes 638984 | tf_op jit(solution)/shard_map/ppermute | solution.py:471
  29.0 1.0 %shard_map.113.refs_4_ = bf16[128,1664]{1,0:T(8,128)(2,1)S(1)} custom-call(s32[1]{0:T(128)S(6)} %sub.7.refs_0_.refs_1_, f32[1,2048]{1,0:T(1,128)S(1)} %bitcast.7, bf16[2,2048,768]{2,1,0:T(8,128)(2,1)S(1)} %copy-done, bf16[2,2048,768]{2,1,0:T(8,128)(2,1)S(1)} %copy-done.1, bf16[64,2048]{1,0:T(8,128)(2,1)S(1)} %collective-permute-done.4.refs_4_, ...), custom_call_target="tpu_custom_call" | custom-call | flops 2400000000 | tf_op jit(solution)/shard_map/pallas_call | solution.py:354
  30.7 2.8 %collective-permute-done.7.refs_4_ = bf16[64,2048]{1,0:T(8,128)(2,1)S(1)} collective-permute-done((bf16[64,2048]{1,0:T(8,128)(2,1)S(1)}, bf16[64,2048]{1,0:T(8,128)(2,1)S(1)}, u32[]{:S(2)}, u32[]{:S(2)}) %collective-permute-start.7) | collective-permute-done | bytes 262176 | tf_op jit(solution)/shard_map/ppermute | solution.py:397
  33.5 1.6 %collective-permute-start.9 = (bf16[64,2048]{1,0:T(8,128)(2,1)S(1)}, bf16[64,2048]{1,0:T(8,128)(2,1)S(1)}, u32[]{:S(2)}, u32[]{:S(2)}) collective-permute-start(bf16[64,2048]{1,0:T(8,128)(2,1)S(1)} %collective-permute-done.7.refs_4_), channel_id=1, source_target_pairs={{0,4},{4,0},{8,12},{12,8},{16,20},{20,16},{24,28},{28,24},{1,5},{5... | collective-permute-start | bytes 786440 | tf_op jit(solution)/shard_map/ppermute | solution.py:397
  36.0 1.6 %collective-permute-start.6 = (bf16[64,768]{1,0:T(8,128)(2,1)S(1)}, bf16[64,768]{1,0:T(8,128)(2,1)S(1)}, u32[]{:S(2)}, u32[]{:S(2)}) collective-permute-start(bf16[64,768]{1,0:T(8,128)(2,1)S(1)} %shard_map.114.refs_6_.refs_2_), channel_id=1, source_target_pairs={{0,2},{2,0},{1,3},{3,1},{4,6},{6,4},{5,7},{7,5},{8,10},{10,8},{9,1... | collective-permute-start | bytes 294920 | tf_op jit(solution)/shard_map/ppermute | solution.py:477
  38.0 1.0 %shard_map.115.refs_6_.refs_1_ = bf16[128,1664]{1,0:T(8,128)(2,1)S(1)} custom-call(s32[1]{0:T(128)} %bitcast.3.refs_0_, f32[1,2048]{1,0:T(1,128)S(1)} %bitcast.8, bf16[2,2048,768]{2,1,0:T(8,128)(2,1)S(1)} %copy-done, bf16[2,2048,768]{2,1,0:T(8,128)(2,1)S(1)} %copy-done.1, bf16[64,2048]{1,0:T(8,128)(2,1)S(1)} %collective-permute-done.4.refs_4_, ...), custom_call_target="tpu_custom_call" | custom-call | flops 2400000000 | tf_op jit(solution)/shard_map/pallas_call | solution.py:354
  39.8 1.0 %shard_map.116.refs_5_ = bf16[128,1664]{1,0:T(8,128)(2,1)S(1)} custom-call(s32[1]{0:T(128)S(6)} %sub.7.refs_0_.refs_1_, f32[1,2048]{1,0:T(1,128)S(1)} %bitcast.9, bf16[2,2048,768]{2,1,0:T(8,128)(2,1)S(1)} %copy-done, bf16[2,2048,768]{2,1,0:T(8,128)(2,1)S(1)} %copy-done.1, bf16[64,2048]{1,0:T(8,128)(2,1)S(1)} %collective-permute-done.8.refs_4_, ...), custom_call_target="tpu_custom_call" | custom-call | flops 2400000000 | tf_op jit(solution)/shard_map/pallas_call | solution.py:354
  40.9 2.2 %collective-permute-start.13 = (bf16[128,1664]{1,0:T(8,128)(2,1)S(1)}, bf16[128,1664]{1,0:T(8,128)(2,1)S(1)}, u32[]{:S(2)}, u32[]{:S(2)}) collective-permute-start(bf16[128,1664]{1,0:T(8,128)(2,1)S(1)} %shard_map.116.refs_5_), channel_id=1, source_target_pairs={{0,2},{2,0},{1,3},{3,1},{4,6},{6,4},{5,7},{7,5},{8,10},{10,8},{9,1... | collective-permute-start | bytes 1277960 | tf_op jit(solution)/shard_map/ppermute | solution.py:471
  43.0 1.4 %collective-permute-start.12 = (bf16[64,2048]{1,0:T(8,128)(2,1)S(1)}, bf16[64,2048]{1,0:T(8,128)(2,1)S(1)}, u32[]{:S(2)}, u32[]{:S(2)}) collective-permute-start(bf16[64,2048]{1,0:T(8,128)(2,1)S(1)} %collective-permute-done.9.refs_5_), channel_id=1, source_target_pairs={{0,8},{4,12},{8,0},{12,4},{16,24},{20,28},{24,16},{28,20},{1,9},{5... | collective-permute-start | bytes 786440 | tf_op jit(solution)/shard_map/ppermute | solution.py:397
  45.8 1.1 %collective-permute-start.11 = (bf16[128,768]{1,0:T(8,128)(2,1)S(1)}, bf16[128,768]{1,0:T(8,128)(2,1)S(1)}, u32[]{:S(2)}, u32[]{:S(2)}) collective-permute-start(bf16[128,768]{1,0:T(8,128)(2,1)S(1)} %shard_map.118.refs_6_.refs_2_), channel_id=1, source_target_pairs={{0,2},{2,0},{1,3},{3,1},{4,6},{6,4},{5,7},{7,5},{8,10},{10,8},{9,1... | collective-permute-start | bytes 589832 | tf_op jit(solution)/shard_map/ppermute | solution.py:477
  46.9 1.0 %shard_map.119.refs_5_.refs_1_ = bf16[128,1664]{1,0:T(8,128)(2,1)S(1)} custom-call(s32[1]{0:T(128)} %bitcast.3.refs_0_, f32[1,2048]{1,0:T(1,128)S(1)} %bitcast.10, bf16[2,2048,768]{2,1,0:T(8,128)(2,1)S(1)} %copy-done, bf16[2,2048,768]{2,1,0:T(8,128)(2,1)S(1)} %copy-done.1, bf16[64,2048]{1,0:T(8,128)(2,1)S(1)} %collective-permute-done.8.refs_4_, ...), custom_call_target="tpu_custom_call" | custom-call | flops 2400000000 | tf_op jit(solution)/shard_map/pallas_call | solution.py:354
  47.9 1.5 %collective-permute-done.12.refs_4_ = bf16[64,2048]{1,0:T(8,128)(2,1)S(1)} collective-permute-done((bf16[64,2048]{1,0:T(8,128)(2,1)S(1)}, bf16[64,2048]{1,0:T(8,128)(2,1)S(1)}, u32[]{:S(2)}, u32[]{:S(2)}) %collective-permute-start.12) | collective-permute-done | bytes 262176 | tf_op jit(solution)/shard_map/ppermute | solution.py:397
  49.4 1.0 %shard_map.120.refs_4_ = bf16[64,1664]{1,0:T(8,128)(2,1)S(1)} custom-call(s32[1]{0:T(128)S(6)} %sub.7.refs_0_.refs_1_, f32[1,2048]{1,0:T(1,128)S(1)} %bitcast.11, bf16[2,2048,768]{2,1,0:T(8,128)(2,1)S(1)} %copy-done, bf16[2,2048,768]{2,1,0:T(8,128)(2,1)S(1)} %copy-done.1, bf16[64,2048]{1,0:T(8,128)(2,1)S(1)} %collective-permute-done.12.refs_4_, ...), custom_call_target="tpu_custom_call" | custom-call | flops 2400000000 | tf_op jit(solution)/shard_map/pallas_call | solution.py:354
  50.6 3.2 %collective-permute-done.13.refs_2_ = bf16[128,1664]{1,0:T(8,128)(2,1)S(1)} collective-permute-done((bf16[128,1664]{1,0:T(8,128)(2,1)S(1)}, bf16[128,1664]{1,0:T(8,128)(2,1)S(1)}, u32[]{:S(2)}, u32[]{:S(2)}) %collective-permute-start.13) | collective-permute-done | bytes 426016 | tf_op jit(solution)/shard_map/ppermute | solution.py:471
  54.1 2.1 %collective-permute-start.18 = (bf16[128,768]{1,0:T(8,128)(2,1)S(1)}, bf16[128,768]{1,0:T(8,128)(2,1)S(1)}, u32[]{:S(2)}, u32[]{:S(2)}) collective-permute-start(bf16[128,768]{1,0:T(8,128)(2,1)S(1)} %shard_map.121.refs_5_.refs_2_), channel_id=1, source_target_pairs={{0,2},{2,0},{1,3},{3,1},{4,6},{6,4},{5,7},{7,5},{8,10},{10,8},{9,1... | collective-permute-start | bytes 589832 | tf_op jit(solution)/shard_map/ppermute | solution.py:477
  56.2 1.0 %shard_map.122.refs_5_.refs_1_ = bf16[64,1664]{1,0:T(8,128)(2,1)S(1)} custom-call(s32[1]{0:T(128)} %bitcast.3.refs_0_, f32[1,2048]{1,0:T(1,128)S(1)} %bitcast.12, bf16[2,2048,768]{2,1,0:T(8,128)(2,1)S(1)} %copy-done, bf16[2,2048,768]{2,1,0:T(8,128)(2,1)S(1)} %copy-done.1, bf16[64,2048]{1,0:T(8,128)(2,1)S(1)} %collective-permute-done.12.refs_4_, ...), custom_call_target="tpu_custom_call" | custom-call | flops 2400000000 | tf_op jit(solution)/shard_map/pallas_call | solution.py:354
  58.0 1.2 %shard_map.123 = (bf16[64,2048]{1,0:T(8,128)(2,1)S(1)}, bf16[64,2048]{1,0:T(8,128)(2,1)S(1)}) custom-call(s32[1]{0:T(128)} %bitcast.3.refs_0_, s32[1]{0:T(128)S(6)} %sub.7.refs_0_.refs_1_, bf16[128,768]{1,0:T(8,128)(2,1)S(1)} %shard_map.118.refs_6_.refs_2_, bf16[128,768]{1,0:T(8,128)(2,1)S(1)} %collective-permute-done.11.refs_3_, ...), custom_call_target="tpu_custom_call" | custom-call | flops 2200000000 | tf_op jit(solution)/shard_map/pallas_call | solution.py:354
  59.2 2.0 %collective-permute-start.14 = (bf16[64,2048]{1,0:T(8,128)(2,1)S(1)}, bf16[64,2048]{1,0:T(8,128)(2,1)S(1)}, u32[]{:S(2)}, u32[]{:S(2)}) collective-permute-start(bf16[64,2048]{1,0:T(8,128)(2,1)S(1)} %get-tuple-element.9.refs_4_), channel_id=1, source_target_pairs={{0,8},{4,12},{8,0},{12,4},{16,24},{20,28},{24,16},{28,20},{1,9},{5... | collective-permute-start | bytes 786440 | tf_op jit(solution)/shard_map/ppermute | solution.py:397
  62.8 1.5 %collective-permute-start.17 = (bf16[64,768]{1,0:T(8,128)(2,1)S(1)}, bf16[64,768]{1,0:T(8,128)(2,1)S(1)}, u32[]{:S(2)}, u32[]{:S(2)}) collective-permute-start(bf16[64,768]{1,0:T(8,128)(2,1)S(1)} %shard_map.124.refs_5_.refs_2_), channel_id=1, source_target_pairs={{0,2},{2,0},{1,3},{3,1},{4,6},{6,4},{5,7},{7,5},{8,10},{10,8},{9,1... | collective-permute-start | bytes 294920 | tf_op jit(solution)/shard_map/ppermute | solution.py:477
  64.3 1.0 %shard_map.125.refs_5_ = bf16[64,1664]{1,0:T(8,128)(2,1)S(1)} custom-call(s32[1]{0:T(128)S(6)} %sub.7.refs_0_.refs_1_, f32[1,2048]{1,0:T(1,128)S(1)} %bitcast.13, bf16[2,2048,768]{2,1,0:T(8,128)(2,1)S(1)} %copy-done, bf16[2,2048,768]{2,1,0:T(8,128)(2,1)S(1)} %copy-done.1, bf16[64,2048]{1,0:T(8,128)(2,1)S(1)} %collective-permute-done.7.refs_4_, ...), custom_call_target="tpu_custom_call" | custom-call | flops 2400000000 | tf_op jit(solution)/shard_map/pallas_call | solution.py:354
  66.1 2.0 %collective-permute-start.19 = (bf16[64,1664]{1,0:T(8,128)(2,1)S(1)}, bf16[64,1664]{1,0:T(8,128)(2,1)S(1)}, u32[]{:S(2)}, u32[]{:S(2)}) collective-permute-start(bf16[64,1664]{1,0:T(8,128)(2,1)S(1)} %shard_map.125.refs_5_), channel_id=1, source_target_pairs={{0,2},{2,0},{1,3},{3,1},{4,6},{6,4},{5,7},{7,5},{8,10},{10,8},{9,1... | collective-permute-start | bytes 638984 | tf_op jit(solution)/shard_map/ppermute | solution.py:471
  68.1 1.0 %shard_map.126 = (bf16[64,2048]{1,0:T(8,128)(2,1)S(1)}, bf16[64,2048]{1,0:T(8,128)(2,1)S(1)}) custom-call(s32[1]{0:T(128)} %bitcast.3.refs_0_, s32[1]{0:T(128)S(6)} %sub.7.refs_0_.refs_1_, bf16[128,768]{1,0:T(8,128)(2,1)S(1)} %shard_map.121.refs_5_.refs_2_, bf16[128,768]{1,0:T(8,128)(2,1)S(1)} %collective-permute-done.18.refs_3_, ...), custom_call_target="tpu_custom_call" | custom-call | flops 2200000000 | tf_op jit(solution)/shard_map/pallas_call | solution.py:354
  69.9 1.0 %shard_map.127.refs_5_ = bf16[64,2048]{1,0:T(8,128)(2,1)S(1)} custom-call(s32[1]{0:T(128)} %bitcast.3.refs_0_, s32[1]{0:T(128)S(6)} %sub.7.refs_0_.refs_1_, bf16[64,768]{1,0:T(8,128)(2,1)S(1)} %shard_map.124.refs_5_.refs_2_, bf16[64,768]{1,0:T(8,128)(2,1)S(1)} %collective-permute-done.17.refs_3_, bf16[2,768,2048]{2,1,0:T(8,128)(2,1)S(1)} %bitcast.18, ...), custom_call_target="tpu_custom_call" | custom-call | flops 2200000000 | tf_op jit(solution)/shard_map/pallas_call | solution.py:354
  70.9 1.8 %collective-permute-start.23 = (bf16[64,2048]{1,0:T(8,128)(2,1)S(1)}, bf16[64,2048]{1,0:T(8,128)(2,1)S(1)}, u32[]{:S(2)}, u32[]{:S(2)}) collective-permute-start(bf16[64,2048]{1,0:T(8,128)(2,1)S(1)} %shard_map.127.refs_5_), channel_id=1, source_target_pairs={{0,12},{4,8},{8,4},{12,0},{16,28},{20,24},{24,20},{28,16},{1,13},{... | collective-permute-start | bytes 786440 | tf_op jit(solution)/shard_map/ppermute | solution.py:397
  72.7 1.1 %collective-permute-start.22 = (bf16[64,2048]{1,0:T(8,128)(2,1)S(1)}, bf16[64,2048]{1,0:T(8,128)(2,1)S(1)}, u32[]{:S(2)}, u32[]{:S(2)}) collective-permute-start(bf16[64,2048]{1,0:T(8,128)(2,1)S(1)} %get-tuple-element.12), channel_id=1, source_target_pairs={{0,4},{4,0},{8,12},{12,8},{16,20},{20,16},{24,28},{28,24},{1,5},{5... | collective-permute-start | bytes 786440 | tf_op jit(solution)/shard_map/ppermute | solution.py:397
  73.8 1.0 %shard_map.128.refs_1_.refs_4_ = bf16[64,1664]{1,0:T(8,128)(2,1)S(1)} custom-call(s32[1]{0:T(128)} %bitcast.3.refs_0_, f32[1,2048]{1,0:T(1,128)S(1)} %bitcast.14, bf16[2,2048,768]{2,1,0:T(8,128)(2,1)S(1)} %copy-done, bf16[2,2048,768]{2,1,0:T(8,128)(2,1)S(1)} %copy-done.1, bf16[64,2048]{1,0:T(8,128)(2,1)S(1)} %collective-permute-done.7.refs_4_, ...), custom_call_target="tpu_custom_call" | custom-call | flops 2400000000 | tf_op jit(solution)/shard_map/pallas_call | solution.py:354
  75.0 1.5 %collective-permute-start.20 = (bf16[64,768]{1,0:T(8,128)(2,1)S(1)}, bf16[64,768]{1,0:T(8,128)(2,1)S(1)}, u32[]{:S(2)}, u32[]{:S(2)}) collective-permute-start(bf16[64,768]{1,0:T(8,128)(2,1)S(1)} %shard_map.129.refs_5_.refs_2_), channel_id=1, source_target_pairs={{0,2},{2,0},{1,3},{3,1},{4,6},{6,4},{5,7},{7,5},{8,10},{10,8},{9,1... | collective-permute-start | bytes 294920 | tf_op jit(solution)/shard_map/ppermute | solution.py:477
  76.5 1.0 %shard_map.130.refs_5_ = bf16[64,1664]{1,0:T(8,128)(2,1)S(1)} custom-call(s32[1]{0:T(128)S(6)} %sub.7.refs_0_.refs_1_, f32[1,2048]{1,0:T(1,128)S(1)} %bitcast.15, bf16[2,2048,768]{2,1,0:T(8,128)(2,1)S(1)} %copy-done, bf16[2,2048,768]{2,1,0:T(8,128)(2,1)S(1)} %copy-done.1, bf16[64,2048]{1,0:T(8,128)(2,1)S(1)} %collective-permute-done.24.refs_4_, ...), custom_call_target="tpu_custom_call" | custom-call | flops 2400000000 | tf_op jit(solution)/shard_map/pallas_call | solution.py:354
  78.2 1.0 %shard_map.131.refs_8_.refs_1_ = bf16[64,1664]{1,0:T(8,128)(2,1)S(1)} custom-call(s32[1]{0:T(128)} %bitcast.3.refs_0_, f32[1,2048]{1,0:T(1,128)S(1)} %bitcast.16, bf16[2,2048,768]{2,1,0:T(8,128)(2,1)S(1)} %copy-done, bf16[2,2048,768]{2,1,0:T(8,128)(2,1)S(1)} %copy-done.1, bf16[64,2048]{1,0:T(8,128)(2,1)S(1)} %collective-permute-done.24.refs_4_, ...), custom_call_target="tpu_custom_call" | custom-call | flops 2400000000 | tf_op jit(solution)/shard_map/pallas_call | solution.py:354
  79.2 1.5 %collective-permute-done.20.refs_3_ = bf16[64,768]{1,0:T(8,128)(2,1)S(1)} collective-permute-done((bf16[64,768]{1,0:T(8,128)(2,1)S(1)}, bf16[64,768]{1,0:T(8,128)(2,1)S(1)}, u32[]{:S(2)}, u32[]{:S(2)}) %collective-permute-start.20) | collective-permute-done | bytes 98336 | tf_op jit(solution)/shard_map/ppermute | solution.py:477
  81.6 1.1 %shard_map.132.refs_4_ = bf16[64,2048]{1,0:T(8,128)(2,1)S(1)} custom-call(s32[1]{0:T(128)} %bitcast.3.refs_0_, s32[1]{0:T(128)S(6)} %sub.7.refs_0_.refs_1_, bf16[64,768]{1,0:T(8,128)(2,1)S(1)} %shard_map.129.refs_5_.refs_2_, bf16[64,768]{1,0:T(8,128)(2,1)S(1)} %collective-permute-done.20.refs_3_, bf16[2,768,2048]{2,1,0:T(8,128)(2,1)S(1)} %bitcast.18, ...), custom_call_target="tpu_custom_call" | custom-call | flops 2200000000 | tf_op jit(solution)/shard_map/pallas_call | solution.py:354
  83.7 1.1 %collective-permute-start.27 = (bf16[64,768]{1,0:T(8,128)(2,1)S(1)}, bf16[64,768]{1,0:T(8,128)(2,1)S(1)}, u32[]{:S(2)}, u32[]{:S(2)}) collective-permute-start(bf16[64,768]{1,0:T(8,128)(2,1)S(1)} %shard_map.133.refs_2_.refs_5_), channel_id=1, source_target_pairs={{0,2},{2,0},{1,3},{3,1},{4,6},{6,4},{5,7},{7,5},{8,10},{10,8},{9,1... | collective-permute-start | bytes 294920 | tf_op jit(solution)/shard_map/ppermute | solution.py:477
  85.6 2.7 %collective-permute-done.27.refs_3_ = bf16[64,768]{1,0:T(8,128)(2,1)S(1)} collective-permute-done((bf16[64,768]{1,0:T(8,128)(2,1)S(1)}, bf16[64,768]{1,0:T(8,128)(2,1)S(1)}, u32[]{:S(2)}, u32[]{:S(2)}) %collective-permute-start.27) | collective-permute-done | bytes 98336 | tf_op jit(solution)/shard_map/ppermute | solution.py:477
  88.3 1.0 %shard_map.134.refs_6_ = bf16[64,2048]{1,0:T(8,128)(2,1)S(1)} custom-call(s32[1]{0:T(128)} %bitcast.3.refs_0_, s32[1]{0:T(128)S(6)} %sub.7.refs_0_.refs_1_, bf16[64,768]{1,0:T(8,128)(2,1)S(1)} %shard_map.133.refs_2_.refs_5_, bf16[64,768]{1,0:T(8,128)(2,1)S(1)} %collective-permute-done.27.refs_3_, bf16[2,768,2048]{2,1,0:T(8,128)(2,1)S(1)} %bitcast.18, ...), custom_call_target="tpu_custom_call" | custom-call | flops 2200000000 | tf_op jit(solution)/shard_map/pallas_call | solution.py:354
  89.9 4.8 %collective-permute-done.25.refs_4_ = bf16[64,2048]{1,0:T(8,128)(2,1)S(1)} collective-permute-done((bf16[64,2048]{1,0:T(8,128)(2,1)S(1)}, bf16[64,2048]{1,0:T(8,128)(2,1)S(1)}, u32[]{:S(2)}, u32[]{:S(2)}) %collective-permute-start.25) | collective-permute-done | bytes 262176 | tf_op jit(solution)/shard_map/ppermute | solution.py:397
  94.6 2.7 %collective-permute-done.28.refs_5_ = bf16[64,2048]{1,0:T(8,128)(2,1)S(1)} collective-permute-done((bf16[64,2048]{1,0:T(8,128)(2,1)S(1)}, bf16[64,2048]{1,0:T(8,128)(2,1)S(1)}, u32[]{:S(2)}, u32[]{:S(2)}) %collective-permute-start.28) | collective-permute-done | bytes 262176 | tf_op jit(solution)/shard_map/ppermute | solution.py:397
  (61 shorter events, 15.2 us)
Async XLA Ops:
  1.6 16.1 %copy-start.3 = (bf16[64,2048]{1,0:T(8,128)(2,1)S(1)}, bf16[64,2048]{1,0:T(8,128)(2,1)}, u32[]{:S(2)}) copy-start(bf16[64,2048]{1,0:T(8,128)(2,1)} %refs_2_.13) | copy-start | bytes 786436
  1.6 16.1 %copy-start.4 = (bf16[64,2048]{1,0:T(8,128)(2,1)S(1)}, bf16[64,2048]{1,0:T(8,128)(2,1)}, u32[]{:S(2)}) copy-start(bf16[64,2048]{1,0:T(8,128)(2,1)} %refs_4_.7) | copy-start | bytes 786436
  1.6 16.1 %copy-start.5 = (s32[8]{0:T(128)S(1)}, s32[8]{0:T(128)}, u32[]{:S(2)}) copy-start(s32[8]{0:T(128)} %refs_1_.1) | copy-start | bytes 100
  1.6 6.4 %collective-permute-start = (bf16[144,128]{1,0:T(8,128)(2,1)S(1)}, bf16[144,128]{1,0:T(8,128)(2,1)S(1)}, u32[]{:S(2)}, u32[]{:S(2)}) collective-permute-start(bf16[144,128]{1,0:T(8,128)(2,1)S(1)} %shard_map.109.refs_5_), channel_id=1, source_target_pairs={{0,16},{4,20},{8,24},{12,28},{16,0},{20,4},{24,8},{28,12},{1,17},{... | collective-permute-start | bytes 110600 | tf_op jit(solution)/shard_map/ppermute | solution.py:78
  8.0 4.4 %collective-permute-start.1 = (bf16[288,128]{1,0:T(8,128)(2,1)S(1)}, bf16[288,128]{1,0:T(8,128)(2,1)S(1)}, u32[]{:S(2)}, u32[]{:S(2)}) collective-permute-start(bf16[288,128]{1,0:T(8,128)(2,1)S(1)} %pad_maximum_fusion.2), channel_id=1, source_target_pairs={{0,8},{4,12},{8,0},{12,4},{16,24},{20,28},{24,16},{28,20},{1,9},{5... | collective-permute-start | bytes 221192 | tf_op jit(solution)/shard_map/ppermute | solution.py:78
  12.4 5.2 %collective-permute-start.2 = (bf16[576,128]{1,0:T(8,128)(2,1)S(1)}, bf16[576,128]{1,0:T(8,128)(2,1)S(1)}, u32[]{:S(2)}, u32[]{:S(2)}) collective-permute-start(bf16[576,128]{1,0:T(8,128)(2,1)S(1)} %pad_maximum_fusion.1), channel_id=1, source_target_pairs={{0,4},{4,0},{8,12},{12,8},{16,20},{20,16},{24,28},{28,24},{1,5},{5... | collective-permute-start | bytes 442376 | tf_op jit(solution)/shard_map/ppermute | solution.py:78
  17.6 7.8 %copy-start = (bf16[2,2048,768]{2,1,0:T(8,128)(2,1)S(1)}, bf16[2,2048,768]{2,1,0:T(8,128)(2,1)}, u32[]{:S(2)}) copy-start(bf16[2,2048,768]{2,1,0:T(8,128)(2,1)} %refs_2_.25) | copy-start | bytes 18874372
  17.7 7.8 %copy-start.1 = (bf16[2,2048,768]{2,1,0:T(8,128)(2,1)S(1)}, bf16[2,2048,768]{2,1,0:T(8,128)(2,1)}, u32[]{:S(2)}) copy-start(bf16[2,2048,768]{2,1,0:T(8,128)(2,1)} %refs_3_.23) | copy-start | bytes 18874372
  17.7 7.8 %copy-start.2 = (f32[2048]{0:T(1024)S(1)}, f32[2048]{0:T(1024)}, u32[]{:S(2)}) copy-start(f32[2048]{0:T(1024)} %param.16) | copy-start | bytes 24580
  19.5 9.6 %collective-permute-start.4 = (bf16[64,2048]{1,0:T(8,128)(2,1)S(1)}, bf16[64,2048]{1,0:T(8,128)(2,1)S(1)}, u32[]{:S(2)}, u32[]{:S(2)}) collective-permute-start(bf16[64,2048]{1,0:T(8,128)(2,1)S(1)} %shard_map.110.refs_4_.refs_5_.refs_0_), channel_id=1, source_target_pairs={{0,8},{4,12},{8,0},{12,4},{16,24},{20,28},{24,16},{28,20},{1,9},{5... | collective-permute-start | bytes 786440 | tf_op jit(solution)/shard_map/ppermute | solution.py:397
  21.1 8.0 %collective-permute-start.5 = (bf16[64,2048]{1,0:T(8,128)(2,1)S(1)}, bf16[64,2048]{1,0:T(8,128)(2,1)S(1)}, u32[]{:S(2)}, u32[]{:S(2)}) collective-permute-start(bf16[64,2048]{1,0:T(8,128)(2,1)S(1)} %shard_map.110.refs_4_.refs_5_.refs_0_), channel_id=1, source_target_pairs={{0,4},{4,0},{8,12},{12,8},{16,20},{20,16},{24,28},{28,24},{1,5},{5... | collective-permute-start | bytes 786440 | tf_op jit(solution)/shard_map/ppermute | solution.py:397
  22.6 10.9 %collective-permute-start.7 = (bf16[64,2048]{1,0:T(8,128)(2,1)S(1)}, bf16[64,2048]{1,0:T(8,128)(2,1)S(1)}, u32[]{:S(2)}, u32[]{:S(2)}) collective-permute-start(bf16[64,2048]{1,0:T(8,128)(2,1)S(1)} %shard_map.110.refs_4_.refs_5_.refs_0_), channel_id=1, source_target_pairs={{0,16},{4,20},{8,24},{12,28},{16,0},{20,4},{24,8},{28,12},{1,17},{... | collective-permute-start | bytes 786440 | tf_op jit(solution)/shard_map/ppermute | solution.py:397
  27.5 8.3 %collective-permute-start.3 = (bf16[64,1664]{1,0:T(8,128)(2,1)S(1)}, bf16[64,1664]{1,0:T(8,128)(2,1)S(1)}, u32[]{:S(2)}, u32[]{:S(2)}) collective-permute-start(bf16[64,1664]{1,0:T(8,128)(2,1)S(1)} %shard_map.111.refs_5_), channel_id=1, source_target_pairs={{0,2},{2,0},{1,3},{3,1},{4,6},{6,4},{5,7},{7,5},{8,10},{10,8},{9,1... | collective-permute-start | bytes 638984 | tf_op jit(solution)/shard_map/ppermute | solution.py:471
  30.1 15.4 %collective-permute-start.10 = (bf16[128,1664]{1,0:T(8,128)(2,1)S(1)}, bf16[128,1664]{1,0:T(8,128)(2,1)S(1)}, u32[]{:S(2)}, u32[]{:S(2)}) collective-permute-start(bf16[128,1664]{1,0:T(8,128)(2,1)S(1)} %shard_map.113.refs_4_), channel_id=1, source_target_pairs={{0,2},{2,0},{1,3},{3,1},{4,6},{6,4},{5,7},{7,5},{8,10},{10,8},{9,1... | collective-permute-start | bytes 1277960 | tf_op jit(solution)/shard_map/ppermute | solution.py:471
  33.5 6.4 %collective-permute-start.8 = (bf16[64,2048]{1,0:T(8,128)(2,1)S(1)}, bf16[64,2048]{1,0:T(8,128)(2,1)S(1)}, u32[]{:S(2)}, u32[]{:S(2)}) collective-permute-start(bf16[64,2048]{1,0:T(8,128)(2,1)S(1)} %collective-permute-done.7.refs_4_), channel_id=1, source_target_pairs={{0,8},{4,12},{8,0},{12,4},{16,24},{20,28},{24,16},{28,20},{1,9},{5... | collective-permute-start | bytes 786440 | tf_op jit(solution)/shard_map/ppermute | solution.py:397
  33.5 6.4 %collective-permute-start.9 = (bf16[64,2048]{1,0:T(8,128)(2,1)S(1)}, bf16[64,2048]{1,0:T(8,128)(2,1)S(1)}, u32[]{:S(2)}, u32[]{:S(2)}) collective-permute-start(bf16[64,2048]{1,0:T(8,128)(2,1)S(1)} %collective-permute-done.7.refs_4_), channel_id=1, source_target_pairs={{0,4},{4,0},{8,12},{12,8},{16,20},{20,16},{24,28},{28,24},{1,5},{5... | collective-permute-start | bytes 786440 | tf_op jit(solution)/shard_map/ppermute | solution.py:397
  36.0 8.5 %collective-permute-start.6 = (bf16[64,768]{1,0:T(8,128)(2,1)S(1)}, bf16[64,768]{1,0:T(8,128)(2,1)S(1)}, u32[]{:S(2)}, u32[]{:S(2)}) collective-permute-start(bf16[64,768]{1,0:T(8,128)(2,1)S(1)} %shard_map.114.refs_6_.refs_2_), channel_id=1, source_target_pairs={{0,2},{2,0},{1,3},{3,1},{4,6},{6,4},{5,7},{7,5},{8,10},{10,8},{9,1... | collective-permute-start | bytes 294920 | tf_op jit(solution)/shard_map/ppermute | solution.py:477
  37.5 39.0 %collective-permute-start.24 = (bf16[64,2048]{1,0:T(8,128)(2,1)S(1)}, bf16[64,2048]{1,0:T(8,128)(2,1)S(1)}, u32[]{:S(2)}, u32[]{:S(2)}) collective-permute-start(bf16[64,2048]{1,0:T(8,128)(2,1)S(1)} %collective-permute-done.4.refs_4_), channel_id=1, source_target_pairs={{0,4},{4,0},{8,12},{12,8},{16,20},{20,16},{24,28},{28,24},{1,5},{5... | collective-permute-start | bytes 786440 | tf_op jit(solution)/shard_map/ppermute | solution.py:397
  38.0 6.4 %slice-start = ((s8[6291456]{0:T(1024)(128)(4,1)}), s8[4194304]{0:T(1024)(128)(4,1)S(1)}, s32[]{:S(2)}) async-start(s8[6291456]{0:T(1024)(128)(4,1)} %bitcast.17), calls=%async_computation | async-start | bytes 8388608
  39.1 5.4 %slice-start.1 = ((s8[6291456]{0:T(1024)(128)(4,1)}), s8[2097152]{0:T(1024)(128)(4,1)S(1)}, s32[]{:S(2)}) async-start(s8[6291456]{0:T(1024)(128)(4,1)} %bitcast.17), calls=%async_computation.1 | async-start | bytes 4194304
  40.9 12.9 %collective-permute-start.13 = (bf16[128,1664]{1,0:T(8,128)(2,1)S(1)}, bf16[128,1664]{1,0:T(8,128)(2,1)S(1)}, u32[]{:S(2)}, u32[]{:S(2)}) collective-permute-start(bf16[128,1664]{1,0:T(8,128)(2,1)S(1)} %shard_map.116.refs_5_), channel_id=1, source_target_pairs={{0,2},{2,0},{1,3},{3,1},{4,6},{6,4},{5,7},{7,5},{8,10},{10,8},{9,1... | collective-permute-start | bytes 1277960 | tf_op jit(solution)/shard_map/ppermute | solution.py:471
  43.0 6.4 %collective-permute-start.12 = (bf16[64,2048]{1,0:T(8,128)(2,1)S(1)}, bf16[64,2048]{1,0:T(8,128)(2,1)S(1)}, u32[]{:S(2)}, u32[]{:S(2)}) collective-permute-start(bf16[64,2048]{1,0:T(8,128)(2,1)S(1)} %collective-permute-done.9.refs_5_), channel_id=1, source_target_pairs={{0,8},{4,12},{8,0},{12,4},{16,24},{20,28},{24,16},{28,20},{1,9},{5... | collective-permute-start | bytes 786440 | tf_op jit(solution)/shard_map/ppermute | solution.py:397
  45.8 12.2 %collective-permute-start.11 = (bf16[128,768]{1,0:T(8,128)(2,1)S(1)}, bf16[128,768]{1,0:T(8,128)(2,1)S(1)}, u32[]{:S(2)}, u32[]{:S(2)}) collective-permute-start(bf16[128,768]{1,0:T(8,128)(2,1)S(1)} %shard_map.118.refs_6_.refs_2_), channel_id=1, source_target_pairs={{0,2},{2,0},{1,3},{3,1},{4,6},{6,4},{5,7},{7,5},{8,10},{10,8},{9,1... | collective-permute-start | bytes 589832 | tf_op jit(solution)/shard_map/ppermute | solution.py:477
  50.4 12.1 %collective-permute-start.16 = (bf16[64,1664]{1,0:T(8,128)(2,1)S(1)}, bf16[64,1664]{1,0:T(8,128)(2,1)S(1)}, u32[]{:S(2)}, u32[]{:S(2)}) collective-permute-start(bf16[64,1664]{1,0:T(8,128)(2,1)S(1)} %shard_map.120.refs_4_), channel_id=1, source_target_pairs={{0,2},{2,0},{1,3},{3,1},{4,6},{6,4},{5,7},{7,5},{8,10},{10,8},{9,1... | collective-permute-start | bytes 638984 | tf_op jit(solution)/shard_map/ppermute | solution.py:471
  54.1 12.0 %collective-permute-start.18 = (bf16[128,768]{1,0:T(8,128)(2,1)S(1)}, bf16[128,768]{1,0:T(8,128)(2,1)S(1)}, u32[]{:S(2)}, u32[]{:S(2)}) collective-permute-start(bf16[128,768]{1,0:T(8,128)(2,1)S(1)} %shard_map.121.refs_5_.refs_2_), channel_id=1, source_target_pairs={{0,2},{2,0},{1,3},{3,1},{4,6},{6,4},{5,7},{7,5},{8,10},{10,8},{9,1... | collective-permute-start | bytes 589832 | tf_op jit(solution)/shard_map/ppermute | solution.py:477
  59.2 11.7 %collective-permute-start.14 = (bf16[64,2048]{1,0:T(8,128)(2,1)S(1)}, bf16[64,2048]{1,0:T(8,128)(2,1)S(1)}, u32[]{:S(2)}, u32[]{:S(2)}) collective-permute-start(bf16[64,2048]{1,0:T(8,128)(2,1)S(1)} %get-tuple-element.9.refs_4_), channel_id=1, source_target_pairs={{0,8},{4,12},{8,0},{12,4},{16,24},{20,28},{24,16},{28,20},{1,9},{5... | collective-permute-start | bytes 786440 | tf_op jit(solution)/shard_map/ppermute | solution.py:397
  61.2 11.5 %collective-permute-start.15 = (bf16[64,2048]{1,0:T(8,128)(2,1)S(1)}, bf16[64,2048]{1,0:T(8,128)(2,1)S(1)}, u32[]{:S(2)}, u32[]{:S(2)}) collective-permute-start(bf16[64,2048]{1,0:T(8,128)(2,1)S(1)} %get-tuple-element.10), channel_id=1, source_target_pairs={{0,4},{4,0},{8,12},{12,8},{16,20},{20,16},{24,28},{28,24},{1,5},{5... | collective-permute-start | bytes 786440 | tf_op jit(solution)/shard_map/ppermute | solution.py:397
  62.8 6.4 %collective-permute-start.17 = (bf16[64,768]{1,0:T(8,128)(2,1)S(1)}, bf16[64,768]{1,0:T(8,128)(2,1)S(1)}, u32[]{:S(2)}, u32[]{:S(2)}) collective-permute-start(bf16[64,768]{1,0:T(8,128)(2,1)S(1)} %shard_map.124.refs_5_.refs_2_), channel_id=1, source_target_pairs={{0,2},{2,0},{1,3},{3,1},{4,6},{6,4},{5,7},{7,5},{8,10},{10,8},{9,1... | collective-permute-start | bytes 294920 | tf_op jit(solution)/shard_map/ppermute | solution.py:477
  66.1 8.7 %collective-permute-start.19 = (bf16[64,1664]{1,0:T(8,128)(2,1)S(1)}, bf16[64,1664]{1,0:T(8,128)(2,1)S(1)}, u32[]{:S(2)}, u32[]{:S(2)}) collective-permute-start(bf16[64,1664]{1,0:T(8,128)(2,1)S(1)} %shard_map.125.refs_5_), channel_id=1, source_target_pairs={{0,2},{2,0},{1,3},{3,1},{4,6},{6,4},{5,7},{7,5},{8,10},{10,8},{9,1... | collective-permute-start | bytes 638984 | tf_op jit(solution)/shard_map/ppermute | solution.py:471
  69.2 11.5 %collective-permute-start.21 = (bf16[64,2048]{1,0:T(8,128)(2,1)S(1)}, bf16[64,2048]{1,0:T(8,128)(2,1)S(1)}, u32[]{:S(2)}, u32[]{:S(2)}) collective-permute-start(bf16[64,2048]{1,0:T(8,128)(2,1)S(1)} %get-tuple-element.11.refs_5_), channel_id=1, source_target_pairs={{0,8},{4,12},{8,0},{12,4},{16,24},{20,28},{24,16},{28,20},{1,9},{5... | collective-permute-start | bytes 786440 | tf_op jit(solution)/shard_map/ppermute | solution.py:397
  70.9 9.8 %collective-permute-start.23 = (bf16[64,2048]{1,0:T(8,128)(2,1)S(1)}, bf16[64,2048]{1,0:T(8,128)(2,1)S(1)}, u32[]{:S(2)}, u32[]{:S(2)}) collective-permute-start(bf16[64,2048]{1,0:T(8,128)(2,1)S(1)} %shard_map.127.refs_5_), channel_id=1, source_target_pairs={{0,12},{4,8},{8,4},{12,0},{16,28},{20,24},{24,20},{28,16},{1,13},{... | collective-permute-start | bytes 786440 | tf_op jit(solution)/shard_map/ppermute | solution.py:397
  72.7 8.9 %collective-permute-start.22 = (bf16[64,2048]{1,0:T(8,128)(2,1)S(1)}, bf16[64,2048]{1,0:T(8,128)(2,1)S(1)}, u32[]{:S(2)}, u32[]{:S(2)}) collective-permute-start(bf16[64,2048]{1,0:T(8,128)(2,1)S(1)} %get-tuple-element.12), channel_id=1, source_target_pairs={{0,4},{4,0},{8,12},{12,8},{16,20},{20,16},{24,28},{28,24},{1,5},{5... | collective-permute-start | bytes 786440 | tf_op jit(solution)/shard_map/ppermute | solution.py:397
  75.0 5.6 %collective-permute-start.20 = (bf16[64,768]{1,0:T(8,128)(2,1)S(1)}, bf16[64,768]{1,0:T(8,128)(2,1)S(1)}, u32[]{:S(2)}, u32[]{:S(2)}) collective-permute-start(bf16[64,768]{1,0:T(8,128)(2,1)S(1)} %shard_map.129.refs_5_.refs_2_), channel_id=1, source_target_pairs={{0,2},{2,0},{1,3},{3,1},{4,6},{6,4},{5,7},{7,5},{8,10},{10,8},{9,1... | collective-permute-start | bytes 294920 | tf_op jit(solution)/shard_map/ppermute | solution.py:477
  77.5 5.9 %collective-permute-start.26 = (bf16[64,1664]{1,0:T(8,128)(2,1)S(1)}, bf16[64,1664]{1,0:T(8,128)(2,1)S(1)}, u32[]{:S(2)}, u32[]{:S(2)}) collective-permute-start(bf16[64,1664]{1,0:T(8,128)(2,1)S(1)} %shard_map.130.refs_5_), channel_id=1, source_target_pairs={{0,2},{2,0},{1,3},{3,1},{4,6},{6,4},{5,7},{7,5},{8,10},{10,8},{9,1... | collective-permute-start | bytes 638984 | tf_op jit(solution)/shard_map/ppermute | solution.py:471
  83.7 4.7 %collective-permute-start.27 = (bf16[64,768]{1,0:T(8,128)(2,1)S(1)}, bf16[64,768]{1,0:T(8,128)(2,1)S(1)}, u32[]{:S(2)}, u32[]{:S(2)}) collective-permute-start(bf16[64,768]{1,0:T(8,128)(2,1)S(1)} %shard_map.133.refs_2_.refs_5_), channel_id=1, source_target_pairs={{0,2},{2,0},{1,3},{3,1},{4,6},{6,4},{5,7},{7,5},{8,10},{10,8},{9,1... | collective-permute-start | bytes 294920 | tf_op jit(solution)/shard_map/ppermute | solution.py:477
  84.8 9.9 %collective-permute-start.25 = (bf16[64,2048]{1,0:T(8,128)(2,1)S(1)}, bf16[64,2048]{1,0:T(8,128)(2,1)S(1)}, u32[]{:S(2)}, u32[]{:S(2)}) collective-permute-start(bf16[64,2048]{1,0:T(8,128)(2,1)S(1)} %shard_map.132.refs_4_), channel_id=1, source_target_pairs={{0,16},{4,20},{8,24},{12,28},{16,0},{20,4},{24,8},{28,12},{1,17},{... | collective-permute-start | bytes 786440 | tf_op jit(solution)/shard_map/ppermute | solution.py:397
  89.3 8.0 %collective-permute-start.28 = (bf16[64,2048]{1,0:T(8,128)(2,1)S(1)}, bf16[64,2048]{1,0:T(8,128)(2,1)S(1)}, u32[]{:S(2)}, u32[]{:S(2)}) collective-permute-start(bf16[64,2048]{1,0:T(8,128)(2,1)S(1)} %shard_map.134.refs_6_), channel_id=1, source_target_pairs={{0,12},{4,8},{8,4},{12,0},{16,28},{20,24},{24,20},{28,16},{1,13},{... | collective-permute-start | bytes 786440 | tf_op jit(solution)/shard_map/ppermute | solution.py:397
